TPU v7x, 32 devices: a whole 2x2x4 slice. The times are simulated.
32 devices in a mesh: grp: 2 (over y), ctx: 8 (over z, x), head: 1, sub: 2 (over core).
Axes of the slice: x: 2, y: 2, z: 4, core: 2. Of those that a mesh axis runs over, the one named last changes fastest.
Arguments:
- queries: bfloat16 [32, 384, 2048], P(('grp', 'ctx', 'sub'), None, 'head'), parts along dimension 0, may hold values from -6 to 6
- keys: bfloat16 [32, 384, 2048], P(('grp', 'ctx', 'sub'), None, 'head'), parts along dimension 0, may hold values from -6 to 6
- values: bfloat16 [32, 384, 2048], P(('grp', 'ctx', 'sub'), None, 'head'), parts along dimension 0, may hold values from -6 to 6
- grad_out: bfloat16 [32, 384, 2048], P(('grp', 'ctx', 'sub'), None, 'head'), parts along dimension 0, may hold values from -6 to 6
- window_tiles: int32 [32, 6], P(('grp', 'ctx', 'sub')), parts along dimension 0, may hold values from 0 to 15, as said below
- window_count: int32 [32], P(('grp', 'ctx', 'sub')), parts along dimension 0, may hold values from 1 to 6
Outputs:
- attended: bfloat16 [32, 384, 2048], P(('grp', 'ctx', 'sub'), None, 'head'), parts along dimension 0
- grad_queries: bfloat16 [32, 384, 2048], P(('grp', 'ctx', 'sub'), None, 'head'), parts along dimension 0
- grad_keys: bfloat16 [32, 384, 2048], P(('grp', 'ctx', 'sub'), None, 'head'), parts along dimension 0
- grad_values: bfloat16 [32, 384, 2048], P(('grp', 'ctx', 'sub'), None, 'head'), parts along dimension 0
There are 2 independent parts, one for each index of `grp`. A program takes and returns all parts, laid end to end along the dimension named above; each array names one. Nothing has to cross between parts.
Inputs may be any that keep to these rules, and one draw needn't show every extreme that they name: `window_tiles`: tile i lies in tile column i // 16, time slab (i // 2) % 8 and tile row i % 2. The first window_count[i] entries of row i are distinct tiles whose column, slab and row each differ from tile i's by at most 1, tile i among them; the other entries equal i. Tile j is a live entry of tile i's list exactly when tile i is a live entry of tile j's list.
All inputs are finite; a program needn't handle non-finite values.
Results may differ from a plain program's by a relative error of at most 0.022.
Values may be sent and summed in bfloat16 or wider, within the bound.
No kernel may reach another device: no remote copies, remote signals or barrier semaphores. Data moves between devices by JAX's collectives and lax.ppermute only.
A program may use at most 256 MiB of HBM per device.

v0:
```python
import math

import jax
import jax.numpy as jnp
from jax import lax
from jax.sharding import PartitionSpec as P

HD = 128


def padded(value, sides, width):
    for axis, dim in sides:
        size, length = (lax.axis_size(axis), value.shape[dim])
        up = [(i, (i + 1) % size) for i in range(size - 1)]
        down = [(j, i) for i, j in up]
        last = lax.slice_in_dim(value, length - width, length, axis=dim)
        leading = lax.slice_in_dim(value, 0, width, axis=dim)
        before = lax.ppermute(last, axis, up)
        after = lax.ppermute(leading, axis, down)
        value = jnp.concatenate([before, value, after], axis=dim)
    return value


def region_slots(window_ids, my_slab, row_count):
    tile_slab = window_ids // row_count
    tile_row = window_ids % row_count
    return (tile_slab - my_slab + 1) * row_count + tile_row


def query_head(query_part, grad_part, key_part, value_part, live_keys, score_scale):
    scores = (
        jnp.einsum("qd,kd->qk", query_part, key_part, preferred_element_type=jnp.float32)
        * score_scale
    )
    scores = jnp.where(live_keys[None, :], scores, -jnp.inf)
    row_max = jnp.max(scores, axis=1, keepdims=True)
    expo = jnp.exp(scores - row_max)
    total = jnp.sum(expo, axis=1, keepdims=True)
    weights = expo / total
    weights_low = weights.astype(jnp.bfloat16)
    attended = jnp.dot(weights_low, value_part, preferred_element_type=jnp.float32).astype(
        jnp.bfloat16
    )
    offset = jnp.sum(
        grad_part.astype(jnp.float32) * attended.astype(jnp.float32), axis=1, keepdims=True
    )
    grad_weights = jnp.einsum(
        "qd,kd->qk", grad_part, value_part, preferred_element_type=jnp.float32
    )
    grad_scores = (weights * (grad_weights - offset) * score_scale).astype(jnp.bfloat16)
    grad_query = jnp.dot(grad_scores, key_part, preferred_element_type=jnp.float32).astype(
        jnp.bfloat16
    )
    log_total = row_max + jnp.log(total)
    return (attended, grad_query, grad_scores, weights_low, offset, log_total)


def body(queries, keys, values, grad_out, window_tiles, window_count):
    rows_here, tile_len, lane_width = queries.shape
    slot_count = window_tiles.shape[1]
    head_count = lane_width // HD
    row_count = lax.axis_size("sub")
    my_slab = lax.axis_index("ctx")
    score_scale = 1.0 / math.sqrt(HD)
    window_ids = window_tiles[0]
    slots = region_slots(window_ids, my_slab, row_count)
    live_slots = jnp.arange(slot_count) < window_count[0]
    live_keys = jnp.repeat(live_slots, tile_len)
    query_tile = queries[0]
    grad_tile = grad_out[0]
    kv_pair = jnp.stack([keys, values])
    slab_rows = lax.all_gather(kv_pair, "sub", axis=1, tiled=True)
    near = padded(slab_rows[:, None], (("ctx", 1),), 1)
    region = near.reshape(2, -1, tile_len, lane_width)
    key_rows = region[0][slots].reshape(slot_count * tile_len, lane_width)
    value_rows = region[1][slots].reshape(slot_count * tile_len, lane_width)
    head_outs = []
    head_dqs = []
    head_dks = []
    head_dvs = []
    for head_pos in range(head_count):
        lanes = slice(head_pos * HD, (head_pos + 1) * HD)
        query_part = query_tile[:, lanes]
        grad_part = grad_tile[:, lanes]
        attended, grad_query, grad_scores, weights_low, offset, log_total = query_head(
            query_part, grad_part, key_rows[:, lanes], value_rows[:, lanes], live_keys, score_scale
        )
        head_outs.append(attended)
        head_dqs.append(grad_query)
        head_dks.append(
            jnp.einsum("qk,qd->kd", grad_scores, query_part, preferred_element_type=jnp.float32)
        )
        head_dvs.append(
            jnp.einsum("qk,qd->kd", weights_low, grad_part, preferred_element_type=jnp.float32)
        )
    key_slots = jnp.concatenate(head_dks, axis=1).reshape(slot_count, tile_len, lane_width)
    value_slots = jnp.concatenate(head_dvs, axis=1).reshape(slot_count, tile_len, lane_width)
    partial_value = jnp.zeros((2, region.shape[1], tile_len, lane_width), jnp.float32)
    partial_value = partial_value.at[:, slots].add(jnp.stack([key_slots, value_slots]))
    column_terms = partial_value.reshape(2, 3, row_count, tile_len, lane_width)
    outward = jnp.stack([column_terms[:, 0], column_terms[:, 2]], axis=1)
    received = padded(outward.astype(jnp.bfloat16), (("ctx", 1),), 1).astype(outward.dtype)
    slab_total = column_terms[:, 1] + received[:, 0] + received[:, 3]
    own_rows = lax.psum_scatter(
        slab_total.astype(jnp.bfloat16), "sub", scatter_dimension=1, tiled=True
    ).astype(jnp.float32)
    grad_keys = own_rows[0].astype(jnp.bfloat16)
    grad_values = own_rows[1].astype(jnp.bfloat16)
    attended_all = jnp.concatenate(head_outs, axis=1)[None]
    grad_queries = jnp.concatenate(head_dqs, axis=1)[None]
    return (attended_all, grad_queries, grad_keys, grad_values)


def solution(mesh):
    return jax.shard_map(
        body,
        mesh=mesh,
        in_specs=(
            P(("grp", "ctx", "sub"), None, "head"),
            P(("grp", "ctx", "sub"), None, "head"),
            P(("grp", "ctx", "sub"), None, "head"),
            P(("grp", "ctx", "sub"), None, "head"),
            P(("grp", "ctx", "sub"), None),
            P(("grp", "ctx", "sub")),
        ),
        out_specs=(
            P(("grp", "ctx", "sub"), None, "head"),
            P(("grp", "ctx", "sub"), None, "head"),
            P(("grp", "ctx", "sub"), None, "head"),
            P(("grp", "ctx", "sub"), None, "head"),
        ),
        check_vma=False,
    )
```

profile of v0, /device:TPU:0, one launch (start us, length us, event | category | flops | bytes accessed | tf_op | source)
XLA Modules:
  0.0 1048.2 jit_solution(7883097710087489852)
XLA Ops:
  7.2 4.0 pad_maximum_fusion.4
  11.3 19.6 %all-gather.2.cloned.1.call-done = bf16[2,2,384,2048]{3,2,1,0:T(8,128)(2,1)} async-done(((bf16[2,1,384,2048]{3,2,1,0:T(8,128)(2,1)}), bf16[2,2,384,2048]{3,2,1,0:T(8,128)(2,1)}) %all-gather.2.cloned.1.call-update) | async-done | bytes 6291472 | tf_op jit(solution)/shard_map/all_gather | solution.py:72
  32.1 7.2 collective-permute-start
  41.7 129.1 %collective-permute-done.1 = bf16[2,1,2,384,2048]{4,3,2,0,1:T(8,128)(2,1)} collective-permute-done((bf16[2,1,2,384,2048]{4,3,2,0,1:T(8,128)(2,1)}, bf16[2,1,2,384,2048]{4,3,2,0,1:T(8,128)(2,1)}, u32[]{:S(2)}, u32[]{:S(2)}) %collective-permute-start.1) | collective-permute-done | bytes 6291488 | tf_op jit(solution)/shard_map/ppermute | solution.py:19
  170.8 135.0 %collective-permute-done = bf16[2,1,2,384,2048]{4,3,2,0,1:T(8,128)(2,1)} collective-permute-done((bf16[2,1,2,384,2048]{4,3,2,0,1:T(8,128)(2,1)}, bf16[2,1,2,384,2048]{4,3,2,0,1:T(8,128)(2,1)}, u32[]{:S(2)}, u32[]{:S(2)}) %collective-permute-start) | collective-permute-done | bytes 6291488 | tf_op jit(solution)/shard_map/ppermute | solution.py:18
  305.7 8.7 pad_maximum_fusion
  314.4 6.8 fusion.262
  321.2 9.1 gather_fusion
  330.3 2.7 fusion.278
  333.0 4.9 fusion.277
  337.8 4.2 fusion.276
  342.0 3.3 fusion.275
  345.3 3.3 fusion.274
  348.6 3.3 fusion.273
  351.8 3.3 fusion.272
  355.2 3.3 fusion.271
  358.5 3.3 fusion.270
  361.8 3.3 fusion.269
  365.1 3.3 fusion.268
  368.4 3.3 fusion.267
  371.7 3.6 fusion.266
  375.3 3.3 fusion.265
  378.6 2.7 fusion.264
  381.3 2.8 fusion.263
  384.1 9.2 gather_fusion.1
  403.7 1.8 fusion.118
  410.2 1.9 fusion.120
  413.5 1.8 fusion.121
  423.2 2.0 fusion.124
  429.7 1.8 fusion.126
  444.5 2.3 constant_dynamic-update-slice_fusion.15
  446.8 3.3 convolution_dynamic-update-slice_fusion.15
  460.6 2.4 constant_dynamic-update-slice_fusion.8
  463.0 1.9 constant_dynamic-update-slice_fusion.7
  476.0 4.5 fusion.64
  480.5 4.5 fusion.63
  485.0 4.4 fusion.62
  489.4 4.4 fusion.61
  493.8 3.3 fusion.60
  497.1 3.3 fusion.59
  500.4 3.5 fusion.65
  506.0 3.6 fusion.58
  529.9 1.9 convolution_dynamic-update-slice_fusion.25
  547.5 19.0 %copy.20 = f32[2304,2048]{1,0:T(8,128)} copy(f32[2304,2048]{0,1:T(8,128)} %convolution_dynamic-update-slice_fusion.16) | data formatting | bytes 37748736 | tf_op jit(solution)/shard_map/concatenate | solution.py:96
  566.5 3.3 convolution_dynamic-update-slice_fusion.14
  593.2 18.7 %copy.21 = f32[2304,2048]{1,0:T(8,128)} copy(f32[2304,2048]{0,1:T(8,128)} %convolution_dynamic-update-slice_fusion) | data formatting | bytes 37748736 | tf_op jit(solution)/shard_map/concatenate | solution.py:97
  611.9 13.6 %maximum_bitcast_fusion = f32[6,2,384,2048]{3,2,0,1:T(8,128)S(1)} fusion(f32[1,6,384,2048]{3,2,1,0:T(8,128)} %bitcast.115, f32[1,6,384,2048]{3,2,1,0:T(8,128)} %bitcast.114), kind=kLoop, calls=%fused_computation.3 | loop fusion | flops 9437184 | bytes 75497472 | tf_op jit(solution)/shard_map/stack | solution.py:99
  625.6 12.4 %copy.22 = f32[6,2,384,2048]{3,2,1,0:T(8,128)} copy(f32[6,2,384,2048]{3,2,0,1:T(8,128)S(1)} %maximum_bitcast_fusion) | data formatting | bytes 75497472 | tf_op jit(solution)/shard_map/stack | solution.py:99
  637.9 12.6 %broadcast_in_dim.147 = f32[2,6,384,2048]{3,2,1,0:T(8,128)} broadcast(f32[]{:T(128)} %constant.43.clone.1), dimensions={} | broadcast | bytes 37748740 | tf_op jit(solution)/shard_map/broadcast_in_dim | solution.py:98
  650.6 48.5 %scatter_fusion = f32[2,6,384,2048]{3,2,1,0:T(8,128)} fusion(f32[2,6,384,2048]{3,2,1,0:T(8,128)} %broadcast_in_dim.147, s32[6]{0:T(128)S(1)} %copy-done.126, f32[6,2,384,2048]{3,2,1,0:T(8,128)} %copy.22), kind=kCustom, calls=%fused_computation.2 | custom fusion | flops 9437184 | bytes 113246232 | tf_op jit(solution)/shard_map/scatter-add | solution.py:99
  699.1 13.6 %convert.8 = bf16[2,3,2,384,2048]{4,3,2,1,0:T(8,128)(2,1)S(1)} convert(f32[2,3,2,384,2048]{4,3,2,1,0:T(8,128)} %bitcast.112) | non-fusion elementwise | flops 9437184 | bytes 56623104 | tf_op jit(solution)/shard_map/convert.4
  714.5 4.8 collective-permute-start.2
  720.6 268.2 %collective-permute-done.2 = bf16[2,1,2,384,2048]{4,3,2,1,0:T(8,128)(2,1)S(1)} collective-permute-done((bf16[2,1,2,384,2048]{4,3,2,1,0:T(8,128)(2,1)S(1)}, bf16[2,1,2,384,2048]{4,3,2,1,0:T(8,128)(2,1)S(1)}, u32[]{:S(2)}, u32[]{:S(2)}) %collective-permute-start.2) | collective-permute-done | bytes 6291488 | tf_op jit(solution)/shard_map/ppermute | solution.py:18
  988.8 2.6 copy-done.49
  991.4 11.7 %fusion.2 = bf16[2,2,384,2048]{3,2,1,0:T(8,128)(2,1)} fusion(f32[2,3,2,384,2048]{4,3,2,1,0:T(8,128)} %bitcast.113, bf16[2,1,2,384,2048]{4,3,2,1,0:T(8,128)(2,1)} %collective-permute-done.3, bf16[2,1,2,384,2048]{4,3,2,1,0:T(8,128)(2,1)S(1)} %get-tuple-element.32, bf16[2,1,2,384,2048]{4,3,2,1,0:T(8,128)(2,1)S(1)} %get-tuple-element.33, ...), kind=kLoop, calls=%fused_computation.8 | loop fusion | flops 34603008 | bytes 44040192 | tf_op jit(solution)/shard_map/convert_element_type | solution.py:105
  1004.4 2.7 copy.23
  1007.0 2.2 fusion.99
  1009.3 1.9 fusion.100
  1011.3 2.2 fusion.101
  1013.5 2.2 fusion.102
  1015.8 2.6 fusion.103
  1029.1 2.7 copy.24
  1031.8 4.6 all-reduce.3.cloned.1.call-done
  1036.4 4.6 dynamic-slice_bitcast_fusion
  (376 shorter events, 142.5 us)
Async XLA Ops:
  7.2 23.7 %all-gather.2.cloned.1.call-start = ((), (), s32[]{:S(2)}) async-start(), calls=%async_computation | async-start | bytes 9437184 | tf_op jit(solution)/shard_map/all_gather | solution.py:72
  7.2 32.9 %copy-start.81 = (bf16[1,384,2048]{2,1,0:T(8,128)(2,1)S(1)}, bf16[1,384,2048]{2,1,0:T(8,128)(2,1)}, u32[]{:S(2)}) copy-start(bf16[1,384,2048]{2,1,0:T(8,128)(2,1)} %param.9) | copy-start | bytes 4718596
  11.2 30.4 %copy-start.127 = (s32[1,6]{1,0:T(1,128)S(1)}, s32[1,6]{1,0:T(1,128)}, u32[]{:S(2)}) copy-start(s32[1,6]{1,0:T(1,128)} %param.10) | copy-start | bytes 76
  11.2 1025.1 %all-reduce.3.cloned.1.call-start = ((), (), s32[]{:S(2)}) async-start(), calls=%async_computation.1 | async-start | bytes 12582912
  30.9 139.9 %collective-permute-start.1 = (bf16[2,1,2,384,2048]{4,3,2,0,1:T(8,128)(2,1)}, bf16[2,1,2,384,2048]{4,3,2,0,1:T(8,128)(2,1)}, u32[]{:S(2)}, u32[]{:S(2)}) collective-permute-start(bf16[2,1,2,384,2048]{4,3,2,0,1:T(8,128)(2,1)} %bitcast.220), channel_id=1, source_target_pairs={{2,0},{4,2},{6,4},{8,6},{10,8},{12,10},{14,12},{3,1},{5,3},{7,5},{... | collective-permute-start | bytes 18874376 | tf_op jit(solution)/shard_map/ppermute | solution.py:19
  32.1 273.6 %collective-permute-start = (bf16[2,1,2,384,2048]{4,3,2,0,1:T(8,128)(2,1)}, bf16[2,1,2,384,2048]{4,3,2,0,1:T(8,128)(2,1)}, u32[]{:S(2)}, u32[]{:S(2)}) collective-permute-start(bf16[2,1,2,384,2048]{4,3,2,0,1:T(8,128)(2,1)} %bitcast.221), channel_id=1, source_target_pairs={{0,2},{2,4},{4,6},{6,8},{8,10},{10,12},{12,14},{1,3},{3,5},{5,7},{... | collective-permute-start | bytes 18874376 | tf_op jit(solution)/shard_map/ppermute | solution.py:18
  41.7 272.8 %copy-start.125 = (s32[6]{0:T(128)}, s32[6]{0:T(128)S(1)}, u32[]{:S(2)}) copy-start(s32[6]{0:T(128)S(1)} %fusion.260) | copy-start | bytes 76
  41.7 279.5 %copy-start.124 = (s32[1024]{0:T(1024)}, s32[1024]{0:T(1024)S(1)}, u32[]{:S(2)}) copy-start(s32[1024]{0:T(1024)S(1)} %pad_clamp_fusion) | copy-start | bytes 12292
  330.3 11.7 %copy-start = (bf16[6,384,2048]{2,1,0:T(8,128)(2,1)S(1)}, bf16[6,384,2048]{2,1,0:T(8,128)(2,1)}, u32[]{:S(2)}) copy-start(bf16[6,384,2048]{2,1,0:T(8,128)(2,1)} %gather_fusion) | copy-start | bytes 28311556
  444.5 5.6 copy-start.46
  446.8 5.1 copy-start.44
  450.1 3.5 copy-start.42
  451.8 3.5 copy-start.40
  453.6 3.5 copy-start.38
  455.4 3.5 copy-start.36
  457.1 3.5 copy-start.34
  458.9 4.1 copy-start.32
  460.6 4.3 copy-start.30
  463.0 3.7 copy-start.28
  465.0 3.5 copy-start.26
  466.7 3.5 copy-start.24
  468.5 3.5 copy-start.22
  472.0 4.0 copy-start.123
  476.0 4.5 copy-start.121
  480.5 4.5 copy-start.119
  485.0 4.4 copy-start.117
  489.4 4.4 copy-start.115
  500.4 3.5 copy-start.18
  503.9 5.7 slice-start.3
  505.6 3.9 copy-start.82
  505.9 3.6 slice-start.4
  505.9 3.6 slice-start.5
  505.9 3.6 copy-start.107
  511.1 18.8 %copy-start.66 = (bf16[2304,384]{1,0:T(8,128)(2,1)}, bf16[2304,384]{1,0:T(8,128)(2,1)S(1)}, u32[]{:S(2)}) copy-start(bf16[2304,384]{1,0:T(8,128)(2,1)S(1)} %fusion.57) | copy-start | bytes 5308420
  512.2 16.1 %copy-start.68 = (bf16[2304,384]{1,0:T(8,128)(2,1)}, bf16[2304,384]{1,0:T(8,128)(2,1)S(1)}, u32[]{:S(2)}) copy-start(bf16[2304,384]{1,0:T(8,128)(2,1)S(1)} %fusion.56) | copy-start | bytes 5308420
  513.2 13.2 %copy-start.72 = (bf16[2304,384]{1,0:T(8,128)(2,1)}, bf16[2304,384]{1,0:T(8,128)(2,1)S(1)}, u32[]{:S(2)}) copy-start(bf16[2304,384]{1,0:T(8,128)(2,1)S(1)} %fusion.55) | copy-start | bytes 5308420
  514.3 10.4 copy-start.74
  515.4 7.6 copy-start.76
  516.5 4.8 copy-start.78
  519.5 26.3 %copy-start.70 = (bf16[2304,384]{1,0:T(8,128)(2,1)}, bf16[2304,384]{1,0:T(8,128)(2,1)S(1)}, u32[]{:S(2)}) copy-start(bf16[2304,384]{1,0:T(8,128)(2,1)S(1)} %fusion.66) | copy-start | bytes 5308420
  528.2 3.6 copy-start.64
  529.9 3.6 copy-start.62
  531.8 3.5 copy-start.60
  533.6 3.5 copy-start.56
  535.3 3.5 copy-start.54
  537.1 3.5 copy-start.52
  538.8 3.5 copy-start.50
  540.6 3.5 copy-start.58
  547.5 19.0 %copy-start.17 = (bf16[1,384,2048]{1,2,0:T(8,128)(2,1)S(1)}, bf16[1,384,2048]{1,2,0:T(8,128)(2,1)}, u32[]{:S(2)}) copy-start(bf16[1,384,2048]{1,2,0:T(8,128)(2,1)} %copy.19) | copy-start | bytes 4718596
  547.5 22.2 %copy-start.45 = (bf16[2304,384]{1,0:T(8,128)(2,1)S(1)}, bf16[2304,384]{1,0:T(8,128)(2,1)}, u32[]{:S(2)}) copy-start(bf16[2304,384]{1,0:T(8,128)(2,1)} %fusion.128) | copy-start | bytes 5308420
  566.5 4.9 copy-start.43
  576.4 3.5 copy-start.33
  637.9 12.7 %copy-start.126 = (s32[6]{0:T(128)S(1)}, s32[6]{0:T(128)}, u32[]{:S(2)}) copy-start(s32[6]{0:T(128)} %copy-done.125) | copy-start | bytes 76
  714.5 274.3 %collective-permute-start.2 = (bf16[2,1,2,384,2048]{4,3,2,1,0:T(8,128)(2,1)S(1)}, bf16[2,1,2,384,2048]{4,3,2,1,0:T(8,128)(2,1)S(1)}, u32[]{:S(2)}, u32[]{:S(2)}) collective-permute-start(bf16[2,1,2,384,2048]{4,3,2,1,0:T(8,128)(2,1)S(1)} %get-tuple-element.32), channel_id=1, source_target_pairs={{0,2},{2,4},{4,6},{6,8},{8,10},{10,12},{12,14},{1,3},{3,5},{5,7},{... | collective-permute-start | bytes 18874376 | tf_op jit(solution)/shard_map/ppermute | solution.py:18
  719.3 272.1 %collective-permute-start.3 = (bf16[2,1,2,384,2048]{4,3,2,1,0:T(8,128)(2,1)S(1)}, bf16[2,1,2,384,2048]{4,3,2,1,0:T(8,128)(2,1)}, u32[]{:S(2)}, u32[]{:S(2)}) collective-permute-start(bf16[2,1,2,384,2048]{4,3,2,1,0:T(8,128)(2,1)S(1)} %get-tuple-element.33), channel_id=1, source_target_pairs={{2,0},{4,2},{6,4},{8,6},{10,8},{12,10},{14,12},{3,1},{5,3},{7,5},{... | collective-permute-start | bytes 18874376 | tf_op jit(solution)/shard_map/ppermute | solution.py:19
  1003.1 6.2 copy-start.79
  1004.4 15.8 %slice-start = ((s8[9437184]{0:T(1024)(128)(4,1)}), s8[1048576]{0:T(1024)(128)(4,1)S(1)}, s32[]{:S(2)}) async-start(s8[9437184]{0:T(1024)(128)(4,1)} %bitcast.138), calls=%async_computation.2 | async-start | bytes 2097152
  1007.0 4.2 copy-start.77
  1009.3 4.2 copy-start.75
  1009.3 10.9 %slice-start.1 = ((s8[9437184]{0:T(1024)(128)(4,1)}), s8[4194304]{0:T(1024)(128)(4,1)S(1)}, s32[]{:S(2)}) async-start(s8[9437184]{0:T(1024)(128)(4,1)} %bitcast.138), calls=%async_computation.3 | async-start | bytes 8388608
  1011.3 4.5 copy-start.73
  1013.5 4.9 copy-start.69
  1013.5 6.6 slice-start.2
  1015.8 4.4 copy-start.67
  (77 other events, 187.2 us)
Sparse Core Ops, SparseCore 0:
  11.4 19.4 all-gather.1
  1003.2 33.1 all-reduce.2
where the time goes:
time: 1060 us; the launch traced here: 1050 us
  waiting for transfers between devices  556 us (52%)
  matrix products  199 us (19%)
  other arithmetic  140 us (13%)
  local copies, waits for them, and re-layouts  122 us (12%)
  between operations  16.3 us (2%)
  starting transfers between devices  14.6 us (1%)
    ppermute x2, waiting for transfers between devices, padded(): before = lax.ppermute(last, axis, up)  403 us
    ppermute x2, waiting for transfers between devices, padded(): after = lax.ppermute(leading, axis, down)  129 us
    dot_general x16, matrix products, query_head(): jnp.einsum('qd,kd->qk', query_part, key_part, preferred_element_type=jnp....  53.8 us
    scatter-add x1, other arithmetic, body(): partial_value.at[:, slots].add(jnp.stack([key_slots, value_slots]))  48.5 us
    dot_general x16, matrix products, query_head(): jnp.einsum('qd,kd->qk', grad_part, value_part, preferred_element_type=jnp...  40.2 us
    dot_general x16, matrix products, body(): jnp.einsum('qk,qd->kd', weights_low, grad_part, preferred_element_type=jn...  30 us
    convert_element_type x16, other arithmetic, query_head(): weights_low = weights.astype(jnp.bfloat16)  29 us
    dot_general x16, matrix products, query_head(): jnp.dot(weights_low, value_part, preferred_element_type=jnp.float32)  28.9 us
  transfers between devices with their start and end apart: 6, of which 5 were waited for; matrix products, arithmetic and copies ran while one was open for 2% of the time, Pallas kernels for 0%

commit v1 on v0

v1 whole, which is shorter than its diff:
```python
import functools
import math

import jax
import jax.numpy as jnp
from jax import lax
from jax.experimental import pallas as pl
from jax.experimental.pallas import tpu as pltpu
from jax.sharding import PartitionSpec as P

HD = 128
RING = ("ctx", "sub")
F32 = jnp.float32
BF16 = jnp.bfloat16
SCALE = 1.0 / math.sqrt(HD)
ANY = pl.BlockSpec(memory_space=pl.ANY)
VMEM = pl.BlockSpec(memory_space=pltpu.VMEM)
SMEM = pl.BlockSpec(memory_space=pltpu.SMEM)
VMEM_LIMIT = 48 * 1024 * 1024


def struct(shape, dtype):
    return jax.ShapeDtypeStruct(shape, dtype)


def run_copies(copies, sems):
    started = [pltpu.make_async_copy(src, dst, sems.at[n]) for n, (src, dst) in enumerate(copies)]
    for copy in started:
        copy.start()
    for copy in started:
        copy.wait()


def pack_kernel(team, cols_ref, q_ref, g_ref, k_ref, v_ref, *refs):
    outs, sems = refs[:team], refs[team]
    copies = []
    for d in range(team):
        lanes = pl.ds(pl.multiple_of(cols_ref[d], HD), HD)
        for n, ref in enumerate((q_ref, g_ref, k_ref, v_ref)):
            copies.append((ref.at[0, :, lanes], outs[d].at[n]))
    run_copies(copies, sems)


def pack(team, cols, q, g, k, v):
    tile = q.shape[1]
    return pl.pallas_call(
        functools.partial(pack_kernel, team),
        out_shape=[struct((4, tile, HD), BF16)] * team,
        in_specs=[SMEM] + [ANY] * 4,
        out_specs=[ANY] * team,
        scratch_shapes=[pltpu.SemaphoreType.DMA((4 * team,))],
        cost_estimate=pl.CostEstimate(
            flops=0, bytes_accessed=team * 4 * tile * HD * 4, transcendentals=0
        ),
        name="pack",
    )(cols, q, g, k, v)


def unpack_kernel(team, pieces_per, cols_ref, *refs):
    count = team * pieces_per
    pieces = refs[:count]
    outs = refs[-1 - 2 * pieces_per : -1]
    sems = refs[-1]
    copies = []
    for d in range(team):
        lanes = pl.ds(pl.multiple_of(cols_ref[d], HD), HD)
        for n in range(2 * pieces_per):
            src = pieces[pieces_per * d + n // 2].at[n % 2]
            copies.append((src, outs[n].at[0, :, lanes]))
    run_copies(copies, sems)


def unpack(team, cols, pieces, outs, shape):
    pieces_per = len(pieces[0])
    flat = [piece for row in pieces for piece in row]
    held = [] if outs is None else list(outs)
    tile = shape[1]
    return pl.pallas_call(
        functools.partial(unpack_kernel, team, pieces_per),
        out_shape=[struct(shape, BF16)] * (2 * pieces_per),
        in_specs=[SMEM] + [ANY] * (len(flat) + len(held)),
        out_specs=[ANY] * (2 * pieces_per),
        scratch_shapes=[pltpu.SemaphoreType.DMA((2 * pieces_per * team,))],
        input_output_aliases={1 + len(flat) + n: n for n in range(len(held))},
        cost_estimate=pl.CostEstimate(
            flops=0, bytes_accessed=2 * pieces_per * team * tile * HD * 4, transcendentals=0
        ),
        name="unpack",
    )(cols, *flat, *held)


def nt(a, b):
    return lax.dot_general(a, b, (((1,), (1,)), ((), ())), preferred_element_type=F32)


def nn(a, b):
    return jnp.dot(a, b, preferred_element_type=F32)


def attend_kernel(team, rows, wmax, tbl_ref, *refs):
    pieces = refs[:team]
    lo_ref, hi_ref = refs[team : team + 2]
    outs = refs[team + 2 : 2 * team + 2]
    loc_ref, glo_ref, ghi_ref = refs[2 * team + 2 : 2 * team + 5]
    qbuf, gbuf, kbuf, vbuf, kt, vt, dk, dv, s_buf, p_buf, ot, dqt, stat, sems = refs[2 * team + 5 :]
    tile = qbuf.shape[1]
    slots = team + 2 * rows
    copies = []
    for d in range(team):
        copies.append((pieces[d].at[0], qbuf.at[d]))
        copies.append((pieces[d].at[1], gbuf.at[d]))
        copies.append((pieces[d].at[2], kbuf.at[rows + d]))
        copies.append((pieces[d].at[3], vbuf.at[rows + d]))
    for r in range(rows):
        copies.append((lo_ref.at[r, 0], kbuf.at[r]))
        copies.append((lo_ref.at[r, 1], vbuf.at[r]))
        copies.append((hi_ref.at[r, 0], kbuf.at[rows + team + r]))
        copies.append((hi_ref.at[r, 1], vbuf.at[rows + team + r]))
    run_copies(copies, sems)

    def prepare(n, carry):
        kt[n] = kbuf[n].T
        vt[n] = vbuf[n].T
        dk[n] = jnp.zeros((tile, HD), F32)
        dv[n] = jnp.zeros((tile, HD), F32)
        return carry

    lax.fori_loop(0, slots, prepare, 0)
    factor = SCALE * math.log2(math.e)

    for d in range(team):
        count = tbl_ref[d, wmax]
        query = qbuf[d]
        grad = gbuf[d]

        def scores(w, top):
            s = nt(kbuf[tbl_ref[d, w]], query)
            s_buf[w] = s
            return jnp.maximum(top, jnp.max(s, axis=0, keepdims=True))

        top = lax.fori_loop(0, count, scores, jnp.full((1, tile), -jnp.inf, F32))

        ot[...] = jnp.zeros((HD, tile), F32)

        def expo(w, total):
            p = jnp.exp2((s_buf[w] - top) * factor)
            low = p.astype(BF16)
            p_buf[w] = low
            ot[...] += nn(vt[tbl_ref[d, w]], low)
            return total + jnp.sum(p, axis=0, keepdims=True)

        total = lax.fori_loop(0, count, expo, jnp.zeros((1, tile), F32))
        inv = 1.0 / total
        out_t = (ot[...] * inv).astype(BF16)
        grad_t = grad.T.astype(F32)
        offset = jnp.sum(grad_t * out_t.astype(F32), axis=0, keepdims=True)
        outs[d][0] = out_t.T
        grad_over = (grad_t * inv).astype(BF16).T
        query_over = (query.T.astype(F32) * inv).astype(BF16).T
        dqt[...] = jnp.zeros((HD, tile), F32)

        def backward(w, carry):
            slot = tbl_ref[d, w]
            low = p_buf[w]
            dp = nt(vbuf[slot], grad)
            ds = (low.astype(F32) * (dp - offset)).astype(BF16)
            dv[slot] += nn(low, grad_over)
            dk[slot] += nn(ds, query_over)
            dqt[...] += nn(kt[slot], ds)
            return carry

        lax.fori_loop(0, count, backward, 0)
        outs[d][1] = (dqt[...] * (inv * SCALE)).astype(BF16).T

    for d in range(team):
        loc_ref[d, 0] = dk[rows + d] * SCALE
        loc_ref[d, 1] = dv[rows + d]
    for r in range(rows):
        glo_ref[r, 0] = (dk[r] * SCALE).astype(BF16)
        glo_ref[r, 1] = dv[r].astype(BF16)
        ghi_ref[r, 0] = (dk[rows + team + r] * SCALE).astype(BF16)
        ghi_ref[r, 1] = dv[rows + team + r].astype(BF16)


def attend(team, rows, wmax, table, pieces, low_halo, high_halo):
    tile = pieces[0].shape[1]
    slots = team + 2 * rows
    pairs = team * wmax * tile * tile
    outs = pl.pallas_call(
        functools.partial(attend_kernel, team, rows, wmax),
        out_shape=[struct((2, tile, HD), BF16)] * team
        + [struct((team, 2, tile, HD), F32)]
        + [struct((rows, 2, tile, HD), BF16)] * 2,
        in_specs=[SMEM] + [ANY] * (team + 2),
        out_specs=[VMEM] * (team + 3),
        scratch_shapes=[
            pltpu.VMEM((team, tile, HD), BF16),
            pltpu.VMEM((team, tile, HD), BF16),
            pltpu.VMEM((slots, tile, HD), BF16),
            pltpu.VMEM((slots, tile, HD), BF16),
            pltpu.VMEM((slots, HD, tile), BF16),
            pltpu.VMEM((slots, HD, tile), BF16),
            pltpu.VMEM((slots, tile, HD), F32),
            pltpu.VMEM((slots, tile, HD), F32),
            pltpu.VMEM((wmax, tile, tile), F32),
            pltpu.VMEM((wmax, tile, tile), BF16),
            pltpu.VMEM((HD, tile), F32),
            pltpu.VMEM((HD, tile), F32),
            pltpu.VMEM((8, tile), F32),
            pltpu.SemaphoreType.DMA((4 * team + 4 * rows,)),
        ],
        cost_estimate=pl.CostEstimate(
            flops=12 * pairs * HD, bytes_accessed=8 * 1024 * 1024, transcendentals=pairs
        ),
        compiler_params=pltpu.CompilerParams(vmem_limit_bytes=VMEM_LIMIT),
        name="attend",
    )(table, *pieces, low_halo, high_halo)
    return outs[:team], outs[team], outs[team + 1], outs[team + 2]


def body(queries, keys, values, grad_out, window_tiles, window_count):
    rows_here, tile, lane_width = queries.shape
    wmax = window_tiles.shape[1]
    heads = lane_width // HD
    rows = lax.axis_size("sub")
    slabs = lax.axis_size("ctx")
    span = 2 if heads % (2 * rows) == 0 and slabs % 2 == 0 else 1
    team = span * rows
    per = heads // team
    size = slabs * rows
    slab = lax.axis_index("ctx")
    row = lax.axis_index("sub")
    me = (slab % span) * rows + row

    def swap(value, d):
        if d == 0:
            return value
        return lax.ppermute(value, RING, [(i, i - i % team + (i % team ^ d)) for i in range(size)])

    def up(value):
        return lax.ppermute(value, RING, [(i, i + team) for i in range(size - team)])

    def down(value):
        return lax.ppermute(value, RING, [(i + team, i) for i in range(size - team)])

    relative = (window_tiles[0] // rows - slab + 1) * rows + window_tiles[0] % rows
    place = relative + (slab % span) * rows
    entry = jnp.concatenate([place, window_count, jnp.zeros((1,), jnp.int32)])[None]
    entries = jnp.concatenate([swap(entry, d) for d in range(team)], axis=0)
    spot = entries[:, :wmax]
    inside = (spot >= rows) & (spot < rows + team)
    ordered = jnp.where(inside, rows + ((spot - rows) ^ me), spot ^ row)
    table = jnp.concatenate([ordered, entries[:, wmax:]], axis=1)

    partners = jnp.arange(team, dtype=jnp.int32) ^ me
    first = me < rows
    outs = None
    for c in range(per):
        cols = (partners * per + c) * HD
        packed = pack(team, cols, queries, grad_out, keys, values)
        pieces = [swap(packed[d], d) for d in range(team)]
        near = jnp.stack([piece[2:] for piece in pieces[:rows]])
        if span == 1:
            going_down = going_up = near
        else:
            far = jnp.stack([piece[2:] for piece in pieces[rows:]])
            going_down = jnp.where(first, near, far)
            going_up = jnp.where(first, far, near)
        high_halo = down(going_down)
        low_halo = up(going_up)
        done, local, grad_low, grad_high = attend(
            team, rows, wmax, table, pieces, low_halo, high_halo
        )
        from_above = down(grad_low)
        from_below = up(grad_high)
        home = []
        for d in range(team):
            e = d % rows
            if span == 1:
                extra = from_below[e].astype(F32) + from_above[e].astype(F32)
            else:
                mine = first if d < rows else jnp.logical_not(first)
                extra = jnp.where(mine, from_below[e], from_above[e]).astype(F32)
            home.append([swap(done[d], d), swap((local[d] + extra).astype(BF16), d)])
        outs = unpack(team, cols, home, outs, queries.shape)
    attended, grad_queries, grad_keys, grad_values = outs
    return (attended, grad_queries, grad_keys, grad_values)


def solution(mesh):
    spec = P(("grp", "ctx", "sub"), None, "head")
    return jax.shard_map(
        body,
        mesh=mesh,
        in_specs=(spec, spec, spec, spec, P(("grp", "ctx", "sub"), None), P(("grp", "ctx", "sub"))),
        out_specs=(spec, spec, spec, spec),
        check_vma=False,
    )
```

time: 1060 us -> 684 us (0.65); the launches traced: 1050 us -> 684 us
  Pallas kernels: 0 us -> 490 us
  waiting for transfers between devices: 556 us -> 72.7 us
  matrix products: 199 us -> 0 us
  other arithmetic: 140 us -> 6.85 us
  local copies, waits for them, and re-layouts: 122 us -> 19.6 us
  starting transfers between devices: 14.6 us -> 92 us
  between operations: 16.3 us -> 2.43 us
    pallas_call x0 -> x12, Pallas kernels: none -> 490 us  [the longest x4 198 us: pack(): pl.pallas_call(functools.partial(pack_kernel, team), out_shape=[struct((4...]
    ppermute x4 -> x55, waiting for transfers between devices: 532 us -> 72.7 us  [the longest x39 65 us: swap(): lax.ppermute(value, RING, [(i, i - i % team + (i % team ^ d)) for i in ra...]
    dot_general x96 -> x0, matrix products: 199 us -> none  [the longest x16 53.8 us: query_head(): jnp.einsum('qd,kd->qk', query_part, key_part, preferred_element_type=jnp....]
    ppermute x4 -> x55, starting transfers between devices: 14.5 us -> 92 us  [the longest x8 55.2 us: up(): lax.ppermute(value, RING, [(i, i + team) for i in range(size - team)])]
    scatter-add x1 -> x0, other arithmetic: 48.5 us -> none  [body(): partial_value.at[:, slots].add(jnp.stack([key_slots, value_slots]))]
    concatenate x2 -> x0, local copies, waits for them, and re-layouts: 37.7 us -> none  [the longest x1 19 us: body(): jnp.concatenate(head_dks, axis=1).reshape(slot_count, tile_len, lane_width)]
    convert_element_type x17 -> x4, other arithmetic: 40.7 us -> 3.58 us  [body(): home.append([swap(done[d], d), swap((local[d] + extra).astype(BF16), d)])]
    another operation x3 -> x0, other arithmetic: 31.2 us -> none  [the longest x1 13.6 us: body(): jnp.stack([key_slots, value_slots])]
  transfers between devices with their start and end apart: 6 -> 55, of which waited for: 5 -> 17; matrix products, arithmetic and copies ran while one was open for 2% -> 1% of each run, Pallas kernels for 0% -> 64%
where the time goes in v1:
time: 684 us
  Pallas kernels  490 us (72%)
  starting transfers between devices  92 us (13%)
  waiting for transfers between devices  72.7 us (11%)
  local copies, waits for them, and re-layouts  19.6 us (3%)
  other arithmetic  6.85 us (1%)
    pallas_call x4, Pallas kernels, pack(): pl.pallas_call(functools.partial(pack_kernel, team), out_shape=[struct((4...  198 us
    pallas_call x4, Pallas kernels, unpack(): pl.pallas_call(functools.partial(unpack_kernel, team, pieces_per), out_sh...  198 us
    pallas_call x4, Pallas kernels, attend(): pl.pallas_call(functools.partial(attend_kernel, team, rows, wmax), out_sh...  93.6 us
    ppermute x39, waiting for transfers between devices, swap(): lax.ppermute(value, RING, [(i, i - i % team + (i % team ^ d)) for i in ra...  65 us
    ppermute x8, starting transfers between devices, up(): lax.ppermute(value, RING, [(i, i + team) for i in range(size - team)])  55.2 us
    ppermute x39, starting transfers between devices, swap(): lax.ppermute(value, RING, [(i, i - i % team + (i % team ^ d)) for i in ra...  26.3 us
    unnamed x114, local copies, waits for them, and re-layouts  15.5 us
  transfers between devices with their start and end apart: 55, of which 17 were waited for; matrix products, arithmetic and copies ran while one was open for 1% of the time, Pallas kernels for 64%

profile of v1, /device:TPU:0, one launch (start us, length us, event | category | flops | bytes accessed | tf_op | source)
XLA Modules:
  0.0 683.7 jit_solution(16511314935110085019)
XLA Ops:
  2.5 2.6 collective-permute-start.1
  5.6 49.6 %pack.7 = (bf16[4,384,128]{2,1,0:T(8,128)(2,1)}, bf16[4,384,128]{2,1,0:T(8,128)(2,1)}, bf16[4,384,128]{2,1,0:T(8,128)(2,1)}, bf16[4,384,128]{2,1,0:T(8,128)(2,1)}) custom-call(s32[4]{0:T(128)} %fusion.18.cols_ref, bf16[1,384,2048]{2,1,0:T(8,128)(2,1)} %q_ref.7, bf16[1,384,2048]{2,1,0:T(8,128)(2,1)} %g_ref.7, bf16[1,384,2048]{2,1,0:T(8,128)(2,1)} %k_ref.7, ...), custom_call_target="tpu_custom_call" | custom-call | bytes 3145728 | tf_op jit(solution)/shard_map/pack/pallas_call | solution.py:46
  55.4 1.7 collective-permute-start.44
  58.7 0.9 slice_bitcast_fusion.12
  59.7 49.6 %pack.6 = (bf16[4,384,128]{2,1,0:T(8,128)(2,1)}, bf16[4,384,128]{2,1,0:T(8,128)(2,1)}, bf16[4,384,128]{2,1,0:T(8,128)(2,1)}, bf16[4,384,128]{2,1,0:T(8,128)(2,1)}) custom-call(s32[4]{0:T(128)} %add_multiply_fusion.cols_ref, bf16[1,384,2048]{2,1,0:T(8,128)(2,1)} %q_ref.7, bf16[1,384,2048]{2,1,0:T(8,128)(2,1)} %g_ref.7, bf16[1,384,2048]{2,1,0:T(8,128)(2,1)} %k_ref.7, ...), custom_call_target="tpu_custom_call" | custom-call | bytes 3145728 | tf_op jit(solution)/shard_map/pack/pallas_call | solution.py:46
  109.2 0.9 slice_bitcast_fusion.13
  110.2 49.6 %pack.5 = (bf16[4,384,128]{2,1,0:T(8,128)(2,1)}, bf16[4,384,128]{2,1,0:T(8,128)(2,1)}, bf16[4,384,128]{2,1,0:T(8,128)(2,1)}, bf16[4,384,128]{2,1,0:T(8,128)(2,1)}) custom-call(s32[4]{0:T(128)} %add_multiply_fusion.1.cols_ref, bf16[1,384,2048]{2,1,0:T(8,128)(2,1)} %q_ref.7, bf16[1,384,2048]{2,1,0:T(8,128)(2,1)} %g_ref.7, bf16[1,384,2048]{2,1,0:T(8,128)(2,1)} %k_ref.7, ...), custom_call_target="tpu_custom_call" | custom-call | bytes 3145728 | tf_op jit(solution)/shard_map/pack/pallas_call | solution.py:46
  159.7 0.9 slice_bitcast_fusion.14
  160.7 49.7 %pack.4 = (bf16[4,384,128]{2,1,0:T(8,128)(2,1)}, bf16[4,384,128]{2,1,0:T(8,128)(2,1)}, bf16[4,384,128]{2,1,0:T(8,128)(2,1)}, bf16[4,384,128]{2,1,0:T(8,128)(2,1)}) custom-call(s32[4]{0:T(128)} %add_multiply_fusion.2.cols_ref, bf16[1,384,2048]{2,1,0:T(8,128)(2,1)} %q_ref.7, bf16[1,384,2048]{2,1,0:T(8,128)(2,1)} %g_ref.7, bf16[1,384,2048]{2,1,0:T(8,128)(2,1)} %k_ref.7, ...), custom_call_target="tpu_custom_call" | custom-call | bytes 3145728 | tf_op jit(solution)/shard_map/pack/pallas_call | solution.py:46
  210.5 1.1 slice_bitcast_fusion.15
  212.1 1.7 collective-permute-start.31
  214.4 9.1 %collective-permute-done.43.refs_2_ = bf16[4,384,128]{2,1,0:T(8,128)(2,1)S(1)} collective-permute-done((bf16[4,384,128]{2,1,0:T(8,128)(2,1)S(1)}, bf16[4,384,128]{2,1,0:T(8,128)(2,1)S(1)}, u32[]{:S(2)}, u32[]{:S(2)}) %collective-permute-start.43) | collective-permute-done | bytes 393248 | tf_op jit(solution)/shard_map/ppermute | solution.py:238
  224.3 6.6 collective-permute-done.31.refs_3_
  231.7 8.7 %collective-permute-done.30.refs_2_ = bf16[4,384,128]{2,1,0:T(8,128)(2,1)S(1)} collective-permute-done((bf16[4,384,128]{2,1,0:T(8,128)(2,1)S(1)}, bf16[4,384,128]{2,1,0:T(8,128)(2,1)S(1)}, u32[]{:S(2)}, u32[]{:S(2)}) %collective-permute-start.30) | collective-permute-done | bytes 393248 | tf_op jit(solution)/shard_map/ppermute | solution.py:238
  240.9 6.8 collective-permute-done.18.refs_3_
  247.7 3.5 collective-permute-start.45
  251.2 6.0 collective-permute-done.17.refs_2_
  257.3 1.3 collective-permute-start.46
  258.7 5.9 collective-permute-done.5.refs_3_
  264.6 3.5 collective-permute-start.32
  268.1 5.5 collective-permute-done.4.refs_2_
  273.6 1.3 collective-permute-start.33
  275.0 4.6 collective-permute-start.19
  279.7 1.3 collective-permute-start.20
  281.0 4.7 collective-permute-start.6
  285.7 22.9 %attend.7 = (bf16[2,384,128]{2,1,0:T(8,128)(2,1)S(1)}, bf16[2,384,128]{2,1,0:T(8,128)(2,1)S(1)}, bf16[2,384,128]{2,1,0:T(8,128)(2,1)S(1)}, bf16[2,384,128]{2,1,0...) custom-call(s32[4,8]{1,0:T(4,128)S(1)} %pad_add_fusion.1.tbl_ref, ...), custom_call_target="tpu_custom_call" | custom-call | flops 5435817984 | bytes 8388608 | tf_op jit(solution)/shard_map/attend/pallas_call | solution.py:189
  310.8 1.3 collective-permute-start.7
  312.2 23.7 %attend.6 = (bf16[2,384,128]{2,1,0:T(8,128)(2,1)S(1)}, bf16[2,384,128]{2,1,0:T(8,128)(2,1)}, bf16[2,384,128]{2,1,0:T(8,128)(2,1)}, bf16[2,384,128]{2,1,0:T(8,128...) custom-call(s32[4,8]{1,0:T(4,128)S(1)} %pad_add_fusion.1.tbl_ref, ...), custom_call_target="tpu_custom_call" | custom-call | flops 5435817984 | bytes 8388608 | tf_op jit(solution)/shard_map/attend/pallas_call | solution.py:189
  338.4 1.5 collective-permute-start.53
  340.0 23.5 %attend.5 = (bf16[2,384,128]{2,1,0:T(8,128)(2,1)S(1)}, bf16[2,384,128]{2,1,0:T(8,128)(2,1)}, bf16[2,384,128]{2,1,0:T(8,128)(2,1)}, bf16[2,384,128]{2,1,0:T(8,128...) custom-call(s32[4,8]{1,0:T(4,128)S(1)} %pad_add_fusion.1.tbl_ref, ...), custom_call_target="tpu_custom_call" | custom-call | flops 5435817984 | bytes 8388608 | tf_op jit(solution)/shard_map/attend/pallas_call | solution.py:189
  368.5 1.2 collective-permute-start.40
  371.6 1.3 collective-permute-start.47
  372.9 3.3 collective-permute-done.38.refs_4_
  376.3 1.3 collective-permute-start.48
  377.5 1.5 collective-permute-done.40.refs_6_
  379.0 20.2 %collective-permute-start.34 = (bf16[2,2,384,128]{3,2,1,0:T(8,128)(2,1)}, bf16[2,2,384,128]{3,2,1,0:T(8,128)(2,1)S(1)}, u32[]{:S(2)}, u32[]{:S(2)}) collective-permute-start(bf16[2,2,384,128]{3,2,1,0:T(8,128)(2,1)} %copy-done.25), channel_id=1, source_target_pairs={{0,4},{1,5},{2,6},{3,7},{4,8},{5,9},{6,10},{7,11},{8,12},{9,13},{1... | collective-permute-start | bytes 1179656 | tf_op jit(solution)/shard_map/ppermute | solution.py:241
  399.2 1.3 collective-permute-start.35
  400.9 1.0 copy-done.8
  401.9 1.0 copy-done.10
  402.9 1.0 copy-done.13
  403.9 1.0 copy-done.24
  404.9 1.0 copy-done.27
  405.9 23.5 %attend.4 = (bf16[2,384,128]{2,1,0:T(8,128)(2,1)S(1)}, bf16[2,384,128]{2,1,0:T(8,128)(2,1)S(1)}, bf16[2,384,128]{2,1,0:T(8,128)(2,1)}, bf16[2,384,128]{2,1,0:T(8...) custom-call(s32[4,8]{1,0:T(4,128)S(1)} %pad_add_fusion.1.tbl_ref, ...), custom_call_target="tpu_custom_call" | custom-call | flops 5435817984 | bytes 8388608 | tf_op jit(solution)/shard_map/attend/pallas_call | solution.py:189
  429.5 5.1 collective-permute-start.21
  434.6 1.3 collective-permute-start.22
  435.9 12.3 %collective-permute-start.8 = (bf16[2,2,384,128]{3,2,1,0:T(8,128)(2,1)S(1)}, bf16[2,2,384,128]{3,2,1,0:T(8,128)(2,1)S(1)}, u32[]{:S(2)}, u32[]{:S(2)}) collective-permute-start(bf16[2,2,384,128]{3,2,1,0:T(8,128)(2,1)S(1)} %get-tuple-element.66), channel_id=1, source_target_pairs={{0,4},{1,5},{2,6},{3,7},{4,8},{5,9},{6,10},{7,11},{8,12},{9,13},{1... | collective-permute-start | bytes 1179656 | tf_op jit(solution)/shard_map/ppermute | solution.py:241
  449.2 1.5 collective-permute-start.9
  452.3 1.5 collective-permute-start.52
  453.8 2.4 collective-permute-done.22
  456.5 1.4 collective-permute-start.37
  458.8 5.0 collective-permute-done.9
  463.7 1.0 collective-permute-start.39
  464.8 1.1 collective-permute-start.24
  465.9 1.0 collective-permute-start.26
  468.2 3.3 collective-permute-done.39.refs_5_
  472.1 1.7 collective-permute-done.41.refs_7_
  473.9 1.9 collective-permute-start.14
  475.8 4.2 collective-permute-done.26.refs_5_
  480.6 1.7 collective-permute-done.28.refs_7_
  482.3 1.9 collective-permute-start.15
  484.2 49.6 %unpack.4 = (bf16[1,384,2048]{2,1,0:T(8,128)(2,1)}, bf16[1,384,2048]{2,1,0:T(8,128)(2,1)}, bf16[1,384,2048]{2,1,0:T(8,128)(2,1)}, bf16[1,384,2048]{2,1,0:T(8,128)(2,1)}) custom-call(s32[4]{0:T(128)} %fusion.18.cols_ref, bf16[2,384,128]{2,1,0:T(8,128)(2,1)} %copy-done.2, bf16[2,384,128]{2,1,0:T(8,128)(2,1)} %get-tuple-element.119.refs_1_, ...), custom_call_target="tpu_custom_call" | custom-call | bytes 3145728 | tf_op jit(solution)/shard_map/unpack/pallas_call | solution.py:78
  533.8 49.6 %unpack.5 = (bf16[1,384,2048]{2,1,0:T(8,128)(2,1)}, bf16[1,384,2048]{2,1,0:T(8,128)(2,1)}, bf16[1,384,2048]{2,1,0:T(8,128)(2,1)}, bf16[1,384,2048]{2,1,0:T(8,128)(2,1)}) custom-call(s32[4]{0:T(128)} %add_multiply_fusion.cols_ref, bf16[2,384,128]{2,1,0:T(8,128)(2,1)} %copy-done.3, ...), custom_call_target="tpu_custom_call", output_to_operand_aliasing={{0}: (9, {}), {1}: (10, {}), {2}: (11, {}), {3}: (12, {})} | custom-call | bytes 3145728 | tf_op jit(solution)/shard_map/unpack/pallas_call | solution.py:78
  583.4 49.6 %unpack.6 = (bf16[1,384,2048]{2,1,0:T(8,128)(2,1)}, bf16[1,384,2048]{2,1,0:T(8,128)(2,1)}, bf16[1,384,2048]{2,1,0:T(8,128)(2,1)}, bf16[1,384,2048]{2,1,0:T(8,128)(2,1)}) custom-call(s32[4]{0:T(128)} %add_multiply_fusion.1.cols_ref, bf16[2,384,128]{2,1,0:T(8,128)(2,1)} %copy-done.4, ...), custom_call_target="tpu_custom_call", output_to_operand_aliasing={{0}: (9, {}), {1}: (10, {}), {2}: (11, {}), {3}: (12, {})} | custom-call | bytes 3145728 | tf_op jit(solution)/shard_map/unpack/pallas_call | solution.py:78
  633.9 49.6 %unpack.7 = (bf16[1,384,2048]{2,1,0:T(8,128)(2,1)}, bf16[1,384,2048]{2,1,0:T(8,128)(2,1)}, bf16[1,384,2048]{2,1,0:T(8,128)(2,1)}, bf16[1,384,2048]{2,1,0:T(8,128)(2,1)}) custom-call(s32[4]{0:T(128)} %add_multiply_fusion.2.cols_ref, bf16[2,384,128]{2,1,0:T(8,128)(2,1)} %copy-done.5, ...), custom_call_target="tpu_custom_call", output_to_operand_aliasing={{0}: (9, {}), {1}: (10, {}), {2}: (11, {}), {3}: (12, {})} | custom-call | bytes 3145728 | tf_op jit(solution)/shard_map/unpack/pallas_call | solution.py:78
  (206 shorter events, 26.3 us)
Async XLA Ops:
  2.0 209.5 %collective-permute-start = (s32[1,8]{1,0:T(1,128)S(1)}, s32[1,8]{1,0:T(1,128)S(1)}, u32[]{:S(2)}, u32[]{:S(2)}) collective-permute-start(s32[1,8]{1,0:T(1,128)S(1)} %add_bitcast_fusion), channel_id=1, source_target_pairs={{0,1},{1,0},{2,3},{3,2},{4,5},{5,4},{6,7},{7,6},{8,9},{9,8},{10,11... | collective-permute-start | bytes 104 | tf_op jit(solution)/shard_map/ppermute | solution.py:238
  2.5 209.4 %collective-permute-start.1 = (s32[1,8]{1,0:T(1,128)S(1)}, s32[1,8]{1,0:T(1,128)S(1)}, u32[]{:S(2)}, u32[]{:S(2)}) collective-permute-start(s32[1,8]{1,0:T(1,128)S(1)} %add_bitcast_fusion), channel_id=1, source_target_pairs={{0,2},{1,3},{2,0},{3,1},{4,6},{5,7},{6,4},{7,5},{8,10},{9,11},{10,... | collective-permute-start | bytes 104 | tf_op jit(solution)/shard_map/ppermute | solution.py:238
  5.1 207.0 %collective-permute-start.2 = (s32[1,8]{1,0:T(1,128)S(1)}, s32[1,8]{1,0:T(1,128)S(1)}, u32[]{:S(2)}, u32[]{:S(2)}) collective-permute-start(s32[1,8]{1,0:T(1,128)S(1)} %add_bitcast_fusion), channel_id=1, source_target_pairs={{0,3},{1,2},{2,1},{3,0},{4,7},{5,6},{6,5},{7,4},{8,11},{9,10},{10,... | collective-permute-start | bytes 104 | tf_op jit(solution)/shard_map/ppermute | solution.py:238
  55.2 158.8 %collective-permute-start.42 = (bf16[4,384,128]{2,1,0:T(8,128)(2,1)}, bf16[4,384,128]{2,1,0:T(8,128)(2,1)S(1)}, u32[]{:S(2)}, u32[]{:S(2)}) collective-permute-start(bf16[4,384,128]{2,1,0:T(8,128)(2,1)} %get-tuple-element.94), channel_id=1, source_target_pairs={{0,1},{1,0},{2,3},{3,2},{4,5},{5,4},{6,7},{7,6},{8,9},{9,8},{10,11... | collective-permute-start | bytes 1179656 | tf_op jit(solution)/shard_map/ppermute | solution.py:238
  55.4 158.9 %collective-permute-start.44 = (bf16[4,384,128]{2,1,0:T(8,128)(2,1)}, bf16[4,384,128]{2,1,0:T(8,128)(2,1)S(1)}, u32[]{:S(2)}, u32[]{:S(2)}) collective-permute-start(bf16[4,384,128]{2,1,0:T(8,128)(2,1)} %get-tuple-element.96), channel_id=1, source_target_pairs={{0,3},{1,2},{2,1},{3,0},{4,7},{5,6},{6,5},{7,4},{8,11},{9,10},{10,... | collective-permute-start | bytes 1179656 | tf_op jit(solution)/shard_map/ppermute | solution.py:238
  160.7 53.3 %copy-start.54 = (bf16[4,384,128]{2,1,0:T(8,128)(2,1)S(1)}, bf16[4,384,128]{2,1,0:T(8,128)(2,1)}, u32[]{:S(2)}) copy-start(bf16[4,384,128]{2,1,0:T(8,128)(2,1)} %get-tuple-element.84) | copy-start | bytes 1179652
  160.7 53.6 %copy-start.53 = (bf16[4,384,128]{2,1,0:T(8,128)(2,1)S(1)}, bf16[4,384,128]{2,1,0:T(8,128)(2,1)}, u32[]{:S(2)}) copy-start(bf16[4,384,128]{2,1,0:T(8,128)(2,1)} %get-tuple-element.72) | copy-start | bytes 1179652
  160.7 62.8 %copy-start.52 = (bf16[4,384,128]{2,1,0:T(8,128)(2,1)S(1)}, bf16[4,384,128]{2,1,0:T(8,128)(2,1)}, u32[]{:S(2)}) copy-start(bf16[4,384,128]{2,1,0:T(8,128)(2,1)} %get-tuple-element.74) | copy-start | bytes 1179652
  211.6 12.0 %collective-permute-start.43 = (bf16[4,384,128]{2,1,0:T(8,128)(2,1)S(1)}, bf16[4,384,128]{2,1,0:T(8,128)(2,1)S(1)}, u32[]{:S(2)}, u32[]{:S(2)}) collective-permute-start(bf16[4,384,128]{2,1,0:T(8,128)(2,1)S(1)} %copy-done.56), channel_id=1, source_target_pairs={{0,2},{1,3},{2,0},{3,1},{4,6},{5,7},{6,4},{7,5},{8,10},{9,11},{10,... | collective-permute-start | bytes 1179656 | tf_op jit(solution)/shard_map/ppermute | solution.py:238
  211.9 11.7 %collective-permute-start.29 = (bf16[4,384,128]{2,1,0:T(8,128)(2,1)}, bf16[4,384,128]{2,1,0:T(8,128)(2,1)S(1)}, u32[]{:S(2)}, u32[]{:S(2)}) collective-permute-start(bf16[4,384,128]{2,1,0:T(8,128)(2,1)} %get-tuple-element.83), channel_id=1, source_target_pairs={{0,1},{1,0},{2,3},{3,2},{4,5},{5,4},{6,7},{7,6},{8,9},{9,8},{10,11... | collective-permute-start | bytes 1179656 | tf_op jit(solution)/shard_map/ppermute | solution.py:238
  212.1 18.8 %collective-permute-start.31 = (bf16[4,384,128]{2,1,0:T(8,128)(2,1)S(1)}, bf16[4,384,128]{2,1,0:T(8,128)(2,1)S(1)}, u32[]{:S(2)}, u32[]{:S(2)}) collective-permute-start(bf16[4,384,128]{2,1,0:T(8,128)(2,1)S(1)} %copy-done.55), channel_id=1, source_target_pairs={{0,3},{1,2},{2,1},{3,0},{4,7},{5,6},{6,5},{7,4},{8,11},{9,10},{10,... | collective-permute-start | bytes 1179656 | tf_op jit(solution)/shard_map/ppermute | solution.py:238
  214.0 26.4 %collective-permute-start.30 = (bf16[4,384,128]{2,1,0:T(8,128)(2,1)S(1)}, bf16[4,384,128]{2,1,0:T(8,128)(2,1)S(1)}, u32[]{:S(2)}, u32[]{:S(2)}) collective-permute-start(bf16[4,384,128]{2,1,0:T(8,128)(2,1)S(1)} %copy-done.54), channel_id=1, source_target_pairs={{0,2},{1,3},{2,0},{3,1},{4,6},{5,7},{6,4},{7,5},{8,10},{9,11},{10,... | collective-permute-start | bytes 1179656 | tf_op jit(solution)/shard_map/ppermute | solution.py:238
  214.3 26.4 %collective-permute-start.16 = (bf16[4,384,128]{2,1,0:T(8,128)(2,1)S(1)}, bf16[4,384,128]{2,1,0:T(8,128)(2,1)S(1)}, u32[]{:S(2)}, u32[]{:S(2)}) collective-permute-start(bf16[4,384,128]{2,1,0:T(8,128)(2,1)S(1)} %copy-done.53), channel_id=1, source_target_pairs={{0,1},{1,0},{2,3},{3,2},{4,5},{5,4},{6,7},{7,6},{8,9},{9,8},{10,11... | collective-permute-start | bytes 1179656 | tf_op jit(solution)/shard_map/ppermute | solution.py:238
  223.6 24.1 %collective-permute-start.18 = (bf16[4,384,128]{2,1,0:T(8,128)(2,1)S(1)}, bf16[4,384,128]{2,1,0:T(8,128)(2,1)S(1)}, u32[]{:S(2)}, u32[]{:S(2)}) collective-permute-start(bf16[4,384,128]{2,1,0:T(8,128)(2,1)S(1)} %copy-done.52), channel_id=1, source_target_pairs={{0,3},{1,2},{2,1},{3,0},{4,7},{5,6},{6,5},{7,4},{8,11},{9,10},{10,... | collective-permute-start | bytes 1179656 | tf_op jit(solution)/shard_map/ppermute | solution.py:238
  223.6 33.7 %collective-permute-start.17 = (bf16[4,384,128]{2,1,0:T(8,128)(2,1)S(1)}, bf16[4,384,128]{2,1,0:T(8,128)(2,1)S(1)}, u32[]{:S(2)}, u32[]{:S(2)}) collective-permute-start(bf16[4,384,128]{2,1,0:T(8,128)(2,1)S(1)} %copy-done.51), channel_id=1, source_target_pairs={{0,2},{1,3},{2,0},{3,1},{4,6},{5,7},{6,4},{7,5},{8,10},{9,11},{10,... | collective-permute-start | bytes 1179656 | tf_op jit(solution)/shard_map/ppermute | solution.py:238
  230.8 33.7 %collective-permute-start.5 = (bf16[4,384,128]{2,1,0:T(8,128)(2,1)S(1)}, bf16[4,384,128]{2,1,0:T(8,128)(2,1)S(1)}, u32[]{:S(2)}, u32[]{:S(2)}) collective-permute-start(bf16[4,384,128]{2,1,0:T(8,128)(2,1)S(1)} %copy-done.50), channel_id=1, source_target_pairs={{0,3},{1,2},{2,1},{3,0},{4,7},{5,6},{6,5},{7,4},{8,11},{9,10},{10,... | collective-permute-start | bytes 1179656 | tf_op jit(solution)/shard_map/ppermute | solution.py:238
  240.4 33.1 %collective-permute-start.4 = (bf16[4,384,128]{2,1,0:T(8,128)(2,1)S(1)}, bf16[4,384,128]{2,1,0:T(8,128)(2,1)S(1)}, u32[]{:S(2)}, u32[]{:S(2)}) collective-permute-start(bf16[4,384,128]{2,1,0:T(8,128)(2,1)S(1)} %copy-done.49), channel_id=1, source_target_pairs={{0,2},{1,3},{2,0},{3,1},{4,6},{5,7},{6,4},{7,5},{8,10},{9,11},{10,... | collective-permute-start | bytes 1179656 | tf_op jit(solution)/shard_map/ppermute | solution.py:238
  240.8 34.2 %collective-permute-start.3 = (bf16[4,384,128]{2,1,0:T(8,128)(2,1)S(1)}, bf16[4,384,128]{2,1,0:T(8,128)(2,1)S(1)}, u32[]{:S(2)}, u32[]{:S(2)}) collective-permute-start(bf16[4,384,128]{2,1,0:T(8,128)(2,1)S(1)} %copy-done.48), channel_id=1, source_target_pairs={{0,1},{1,0},{2,3},{3,2},{4,5},{5,4},{6,7},{7,6},{8,9},{9,8},{10,11... | collective-permute-start | bytes 1179656 | tf_op jit(solution)/shard_map/ppermute | solution.py:238
  247.7 32.0 %collective-permute-start.45 = (bf16[2,2,384,128]{3,2,1,0:T(8,128)(2,1)S(1)}, bf16[2,2,384,128]{3,2,1,0:T(8,128)(2,1)S(1)}, u32[]{:S(2)}, u32[]{:S(2)}) collective-permute-start(bf16[2,2,384,128]{3,2,1,0:T(8,128)(2,1)S(1)} %get-tuple-element.133), channel_id=1, source_target_pairs={{0,4},{1,5},{2,6},{3,7},{4,8},{5,9},{6,10},{7,11},{8,12},{9,13},{1... | collective-permute-start | bytes 1179656 | tf_op jit(solution)/shard_map/ppermute | solution.py:241
  257.3 23.7 %collective-permute-start.46 = (bf16[2,2,384,128]{3,2,1,0:T(8,128)(2,1)S(1)}, bf16[2,2,384,128]{3,2,1,0:T(8,128)(2,1)S(1)}, u32[]{:S(2)}, u32[]{:S(2)}) collective-permute-start(bf16[2,2,384,128]{3,2,1,0:T(8,128)(2,1)S(1)} %get-tuple-element.132), channel_id=1, source_target_pairs={{4,0},{5,1},{6,2},{7,3},{8,4},{9,5},{10,6},{11,7},{12,8},{13,9},{1... | collective-permute-start | bytes 1179656 | tf_op jit(solution)/shard_map/ppermute | solution.py:244
  264.6 46.3 %collective-permute-start.32 = (bf16[2,2,384,128]{3,2,1,0:T(8,128)(2,1)S(1)}, bf16[2,2,384,128]{3,2,1,0:T(8,128)(2,1)S(1)}, u32[]{:S(2)}, u32[]{:S(2)}) collective-permute-start(bf16[2,2,384,128]{3,2,1,0:T(8,128)(2,1)S(1)} %get-tuple-element.135), channel_id=1, source_target_pairs={{0,4},{1,5},{2,6},{3,7},{4,8},{5,9},{6,10},{7,11},{8,12},{9,13},{1... | collective-permute-start | bytes 1179656 | tf_op jit(solution)/shard_map/ppermute | solution.py:241
  273.6 38.6 %collective-permute-start.33 = (bf16[2,2,384,128]{3,2,1,0:T(8,128)(2,1)S(1)}, bf16[2,2,384,128]{3,2,1,0:T(8,128)(2,1)S(1)}, u32[]{:S(2)}, u32[]{:S(2)}) collective-permute-start(bf16[2,2,384,128]{3,2,1,0:T(8,128)(2,1)S(1)} %get-tuple-element.134), channel_id=1, source_target_pairs={{4,0},{5,1},{6,2},{7,3},{8,4},{9,5},{10,6},{11,7},{12,8},{13,9},{1... | collective-permute-start | bytes 1179656 | tf_op jit(solution)/shard_map/ppermute | solution.py:244
  275.0 63.2 %collective-permute-start.19 = (bf16[2,2,384,128]{3,2,1,0:T(8,128)(2,1)S(1)}, bf16[2,2,384,128]{3,2,1,0:T(8,128)(2,1)S(1)}, u32[]{:S(2)}, u32[]{:S(2)}) collective-permute-start(bf16[2,2,384,128]{3,2,1,0:T(8,128)(2,1)S(1)} %get-tuple-element.137), channel_id=1, source_target_pairs={{0,4},{1,5},{2,6},{3,7},{4,8},{5,9},{6,10},{7,11},{8,12},{9,13},{1... | collective-permute-start | bytes 1179656 | tf_op jit(solution)/shard_map/ppermute | solution.py:241
  279.7 58.7 %collective-permute-start.20 = (bf16[2,2,384,128]{3,2,1,0:T(8,128)(2,1)S(1)}, bf16[2,2,384,128]{3,2,1,0:T(8,128)(2,1)S(1)}, u32[]{:S(2)}, u32[]{:S(2)}) collective-permute-start(bf16[2,2,384,128]{3,2,1,0:T(8,128)(2,1)S(1)} %get-tuple-element.136), channel_id=1, source_target_pairs={{4,0},{5,1},{6,2},{7,3},{8,4},{9,5},{10,6},{11,7},{12,8},{13,9},{1... | collective-permute-start | bytes 1179656 | tf_op jit(solution)/shard_map/ppermute | solution.py:244
  281.0 85.3 %collective-permute-start.6 = (bf16[2,2,384,128]{3,2,1,0:T(8,128)(2,1)S(1)}, bf16[2,2,384,128]{3,2,1,0:T(8,128)(2,1)S(1)}, u32[]{:S(2)}, u32[]{:S(2)}) collective-permute-start(bf16[2,2,384,128]{3,2,1,0:T(8,128)(2,1)S(1)} %get-tuple-element.139), channel_id=1, source_target_pairs={{0,4},{1,5},{2,6},{3,7},{4,8},{5,9},{6,10},{7,11},{8,12},{9,13},{1... | collective-permute-start | bytes 1179656 | tf_op jit(solution)/shard_map/ppermute | solution.py:241
  310.8 56.6 %collective-permute-start.7 = (bf16[2,2,384,128]{3,2,1,0:T(8,128)(2,1)S(1)}, bf16[2,2,384,128]{3,2,1,0:T(8,128)(2,1)S(1)}, u32[]{:S(2)}, u32[]{:S(2)}) collective-permute-start(bf16[2,2,384,128]{3,2,1,0:T(8,128)(2,1)S(1)} %get-tuple-element.138), channel_id=1, source_target_pairs={{4,0},{5,1},{6,2},{7,3},{8,4},{9,5},{10,6},{11,7},{12,8},{13,9},{1... | collective-permute-start | bytes 1179656 | tf_op jit(solution)/shard_map/ppermute | solution.py:244
  312.1 56.4 %collective-permute-start.49 = (bf16[2,384,128]{2,1,0:T(8,128)(2,1)S(1)}, bf16[2,384,128]{2,1,0:T(8,128)(2,1)S(1)}, u32[]{:S(2)}, u32[]{:S(2)}) collective-permute-start(bf16[2,384,128]{2,1,0:T(8,128)(2,1)S(1)} %get-tuple-element.101), channel_id=1, source_target_pairs={{0,1},{1,0},{2,3},{3,2},{4,5},{5,4},{6,7},{7,6},{8,9},{9,8},{10,11... | collective-permute-start | bytes 589832 | tf_op jit(solution)/shard_map/ppermute | solution.py:238
  338.1 31.6 %collective-permute-start.51 = (bf16[2,384,128]{2,1,0:T(8,128)(2,1)S(1)}, bf16[2,384,128]{2,1,0:T(8,128)(2,1)S(1)}, u32[]{:S(2)}, u32[]{:S(2)}) collective-permute-start(bf16[2,384,128]{2,1,0:T(8,128)(2,1)S(1)} %get-tuple-element.102), channel_id=1, source_target_pairs={{0,2},{1,3},{2,0},{3,1},{4,6},{5,7},{6,4},{7,5},{8,10},{9,11},{10,... | collective-permute-start | bytes 589832 | tf_op jit(solution)/shard_map/ppermute | solution.py:238
  338.4 62.5 %copy-start.6 = (bf16[4,384,128]{2,1,0:T(8,128)(2,1)S(1)}, bf16[4,384,128]{2,1,0:T(8,128)(2,1)}, u32[]{:S(2)}) copy-start(bf16[4,384,128]{2,1,0:T(8,128)(2,1)} %get-tuple-element.60.refs_0_) | copy-start | bytes 1179652
  338.4 31.9 %collective-permute-start.53 = (bf16[2,384,128]{2,1,0:T(8,128)(2,1)S(1)}, bf16[2,384,128]{2,1,0:T(8,128)(2,1)S(1)}, u32[]{:S(2)}, u32[]{:S(2)}) collective-permute-start(bf16[2,384,128]{2,1,0:T(8,128)(2,1)S(1)} %get-tuple-element.103), channel_id=1, source_target_pairs={{0,3},{1,2},{2,1},{3,0},{4,7},{5,6},{6,5},{7,4},{8,11},{9,10},{10,... | collective-permute-start | bytes 589832 | tf_op jit(solution)/shard_map/ppermute | solution.py:238
  367.1 4.5 collective-permute-start.36
  368.2 8.1 %collective-permute-start.38 = (bf16[2,384,128]{2,1,0:T(8,128)(2,1)}, bf16[2,384,128]{2,1,0:T(8,128)(2,1)}, u32[]{:S(2)}, u32[]{:S(2)}) collective-permute-start(bf16[2,384,128]{2,1,0:T(8,128)(2,1)} %get-tuple-element.91), channel_id=1, source_target_pairs={{0,2},{1,3},{2,0},{3,1},{4,6},{5,7},{6,4},{7,5},{8,10},{9,11},{10,... | collective-permute-start | bytes 589832 | tf_op jit(solution)/shard_map/ppermute | solution.py:238
  368.5 10.5 %collective-permute-start.40 = (bf16[2,384,128]{2,1,0:T(8,128)(2,1)}, bf16[2,384,128]{2,1,0:T(8,128)(2,1)}, u32[]{:S(2)}, u32[]{:S(2)}) collective-permute-start(bf16[2,384,128]{2,1,0:T(8,128)(2,1)} %get-tuple-element.92), channel_id=1, source_target_pairs={{0,3},{1,2},{2,1},{3,0},{4,7},{5,6},{6,5},{7,4},{8,11},{9,10},{10,... | collective-permute-start | bytes 589832 | tf_op jit(solution)/shard_map/ppermute | solution.py:238
  369.8 29.4 %collective-permute-start.23 = (bf16[2,384,128]{2,1,0:T(8,128)(2,1)}, bf16[2,384,128]{2,1,0:T(8,128)(2,1)}, u32[]{:S(2)}, u32[]{:S(2)}) collective-permute-start(bf16[2,384,128]{2,1,0:T(8,128)(2,1)} %get-tuple-element.79), channel_id=1, source_target_pairs={{0,1},{1,0},{2,3},{3,2},{4,5},{5,4},{6,7},{7,6},{8,9},{9,8},{10,11... | collective-permute-start | bytes 589832 | tf_op jit(solution)/shard_map/ppermute | solution.py:238
  371.0 29.5 %collective-permute-start.25 = (bf16[2,384,128]{2,1,0:T(8,128)(2,1)}, bf16[2,384,128]{2,1,0:T(8,128)(2,1)}, u32[]{:S(2)}, u32[]{:S(2)}) collective-permute-start(bf16[2,384,128]{2,1,0:T(8,128)(2,1)} %get-tuple-element.80), channel_id=1, source_target_pairs={{0,2},{1,3},{2,0},{3,1},{4,6},{5,7},{6,4},{7,5},{8,10},{9,11},{10,... | collective-permute-start | bytes 589832 | tf_op jit(solution)/shard_map/ppermute | solution.py:238
  371.6 63.0 %collective-permute-start.47 = (bf16[2,2,384,128]{3,2,1,0:T(8,128)(2,1)}, bf16[2,2,384,128]{3,2,1,0:T(8,128)(2,1)S(1)}, u32[]{:S(2)}, u32[]{:S(2)}) collective-permute-start(bf16[2,2,384,128]{3,2,1,0:T(8,128)(2,1)} %copy-done.19), channel_id=1, source_target_pairs={{0,4},{1,5},{2,6},{3,7},{4,8},{5,9},{6,10},{7,11},{8,12},{9,13},{1... | collective-permute-start | bytes 1179656 | tf_op jit(solution)/shard_map/ppermute | solution.py:241
  376.3 59.7 %collective-permute-start.48 = (bf16[2,2,384,128]{3,2,1,0:T(8,128)(2,1)}, bf16[2,2,384,128]{3,2,1,0:T(8,128)(2,1)S(1)}, u32[]{:S(2)}, u32[]{:S(2)}) collective-permute-start(bf16[2,2,384,128]{3,2,1,0:T(8,128)(2,1)} %copy-done.16), channel_id=1, source_target_pairs={{4,0},{5,1},{6,2},{7,3},{8,4},{9,5},{10,6},{11,7},{12,8},{13,9},{1... | collective-permute-start | bytes 1179656 | tf_op jit(solution)/shard_map/ppermute | solution.py:244
  379.0 70.1 %collective-permute-start.34 = (bf16[2,2,384,128]{3,2,1,0:T(8,128)(2,1)}, bf16[2,2,384,128]{3,2,1,0:T(8,128)(2,1)S(1)}, u32[]{:S(2)}, u32[]{:S(2)}) collective-permute-start(bf16[2,2,384,128]{3,2,1,0:T(8,128)(2,1)} %copy-done.25), channel_id=1, source_target_pairs={{0,4},{1,5},{2,6},{3,7},{4,8},{5,9},{6,10},{7,11},{8,12},{9,13},{1... | collective-permute-start | bytes 1179656 | tf_op jit(solution)/shard_map/ppermute | solution.py:241
  399.2 51.4 %collective-permute-start.35 = (bf16[2,2,384,128]{3,2,1,0:T(8,128)(2,1)}, bf16[2,2,384,128]{3,2,1,0:T(8,128)(2,1)S(1)}, u32[]{:S(2)}, u32[]{:S(2)}) collective-permute-start(bf16[2,2,384,128]{3,2,1,0:T(8,128)(2,1)} %copy-done.20), channel_id=1, source_target_pairs={{4,0},{5,1},{6,2},{7,3},{8,4},{9,5},{10,6},{11,7},{12,8},{13,9},{1... | collective-permute-start | bytes 1179656 | tf_op jit(solution)/shard_map/ppermute | solution.py:244
  400.5 28.9 %collective-permute-start.27 = (bf16[2,384,128]{2,1,0:T(8,128)(2,1)}, bf16[2,384,128]{2,1,0:T(8,128)(2,1)S(1)}, u32[]{:S(2)}, u32[]{:S(2)}) collective-permute-start(bf16[2,384,128]{2,1,0:T(8,128)(2,1)} %copy-done.28), channel_id=1, source_target_pairs={{0,3},{1,2},{2,1},{3,0},{4,7},{5,6},{6,5},{7,4},{8,11},{9,10},{10,... | collective-permute-start | bytes 589832 | tf_op jit(solution)/shard_map/ppermute | solution.py:238
  429.5 22.9 %collective-permute-start.21 = (bf16[2,2,384,128]{3,2,1,0:T(8,128)(2,1)S(1)}, bf16[2,2,384,128]{3,2,1,0:T(8,128)(2,1)S(1)}, u32[]{:S(2)}, u32[]{:S(2)}) collective-permute-start(bf16[2,2,384,128]{3,2,1,0:T(8,128)(2,1)S(1)} %copy-done.22), channel_id=1, source_target_pairs={{0,4},{1,5},{2,6},{3,7},{4,8},{5,9},{6,10},{7,11},{8,12},{9,13},{1... | collective-permute-start | bytes 1179656 | tf_op jit(solution)/shard_map/ppermute | solution.py:241
  434.6 21.6 %collective-permute-start.22 = (bf16[2,2,384,128]{3,2,1,0:T(8,128)(2,1)S(1)}, bf16[2,2,384,128]{3,2,1,0:T(8,128)(2,1)S(1)}, u32[]{:S(2)}, u32[]{:S(2)}) collective-permute-start(bf16[2,2,384,128]{3,2,1,0:T(8,128)(2,1)S(1)} %copy-done.18), channel_id=1, source_target_pairs={{4,0},{5,1},{6,2},{7,3},{8,4},{9,5},{10,6},{11,7},{12,8},{13,9},{1... | collective-permute-start | bytes 1179656 | tf_op jit(solution)/shard_map/ppermute | solution.py:244
  435.9 20.6 %collective-permute-start.8 = (bf16[2,2,384,128]{3,2,1,0:T(8,128)(2,1)S(1)}, bf16[2,2,384,128]{3,2,1,0:T(8,128)(2,1)S(1)}, u32[]{:S(2)}, u32[]{:S(2)}) collective-permute-start(bf16[2,2,384,128]{3,2,1,0:T(8,128)(2,1)S(1)} %get-tuple-element.66), channel_id=1, source_target_pairs={{0,4},{1,5},{2,6},{3,7},{4,8},{5,9},{6,10},{7,11},{8,12},{9,13},{1... | collective-permute-start | bytes 1179656 | tf_op jit(solution)/shard_map/ppermute | solution.py:241
  449.2 14.6 %collective-permute-start.9 = (bf16[2,2,384,128]{3,2,1,0:T(8,128)(2,1)S(1)}, bf16[2,2,384,128]{3,2,1,0:T(8,128)(2,1)S(1)}, u32[]{:S(2)}, u32[]{:S(2)}) collective-permute-start(bf16[2,2,384,128]{3,2,1,0:T(8,128)(2,1)S(1)} %get-tuple-element.67), channel_id=1, source_target_pairs={{4,0},{5,1},{6,2},{7,3},{8,4},{9,5},{10,6},{11,7},{12,8},{13,9},{1... | collective-permute-start | bytes 1179656 | tf_op jit(solution)/shard_map/ppermute | solution.py:244
  450.7 1.5 collective-permute-start.10
  452.2 12.6 %collective-permute-start.50 = (bf16[2,384,128]{2,1,0:T(8,128)(2,1)S(1)}, bf16[2,384,128]{2,1,0:T(8,128)(2,1)S(1)}, u32[]{:S(2)}, u32[]{:S(2)}) collective-permute-start(bf16[2,384,128]{2,1,0:T(8,128)(2,1)S(1)} %get-tuple-element.118), channel_id=1, source_target_pairs={{0,1},{1,0},{2,3},{3,2},{4,5},{5,4},{6,7},{7,6},{8,9},{9,8},{10,11... | collective-permute-start | bytes 589832 | tf_op jit(solution)/shard_map/ppermute | solution.py:238
  452.3 12.4 %collective-permute-start.52 = (bf16[2,384,128]{2,1,0:T(8,128)(2,1)S(1)}, bf16[2,384,128]{2,1,0:T(8,128)(2,1)S(1)}, u32[]{:S(2)}, u32[]{:S(2)}) collective-permute-start(bf16[2,384,128]{2,1,0:T(8,128)(2,1)S(1)} %get-tuple-element.117), channel_id=1, source_target_pairs={{0,2},{1,3},{2,0},{3,1},{4,6},{5,7},{6,4},{7,5},{8,10},{9,11},{10,... | collective-permute-start | bytes 589832 | tf_op jit(solution)/shard_map/ppermute | solution.py:238
  456.2 9.7 %collective-permute-start.54 = (bf16[2,384,128]{2,1,0:T(8,128)(2,1)S(1)}, bf16[2,384,128]{2,1,0:T(8,128)(2,1)S(1)}, u32[]{:S(2)}, u32[]{:S(2)}) collective-permute-start(bf16[2,384,128]{2,1,0:T(8,128)(2,1)S(1)} %get-tuple-element.116), channel_id=1, source_target_pairs={{0,3},{1,2},{2,1},{3,0},{4,7},{5,6},{6,5},{7,4},{8,11},{9,10},{10,... | collective-permute-start | bytes 589832 | tf_op jit(solution)/shard_map/ppermute | solution.py:238
  456.5 10.4 %collective-permute-start.37 = (bf16[2,384,128]{2,1,0:T(8,128)(2,1)S(1)}, bf16[2,384,128]{2,1,0:T(8,128)(2,1)S(1)}, u32[]{:S(2)}, u32[]{:S(2)}) collective-permute-start(bf16[2,384,128]{2,1,0:T(8,128)(2,1)S(1)} %get-tuple-element.122), channel_id=1, source_target_pairs={{0,1},{1,0},{2,3},{3,2},{4,5},{5,4},{6,7},{7,6},{8,9},{9,8},{10,11... | collective-permute-start | bytes 589832 | tf_op jit(solution)/shard_map/ppermute | solution.py:238
  463.7 7.8 %collective-permute-start.39 = (bf16[2,384,128]{2,1,0:T(8,128)(2,1)S(1)}, bf16[2,384,128]{2,1,0:T(8,128)(2,1)S(1)}, u32[]{:S(2)}, u32[]{:S(2)}) collective-permute-start(bf16[2,384,128]{2,1,0:T(8,128)(2,1)S(1)} %get-tuple-element.121), channel_id=1, source_target_pairs={{0,2},{1,3},{2,0},{3,1},{4,6},{5,7},{6,4},{7,5},{8,10},{9,11},{10,... | collective-permute-start | bytes 589832 | tf_op jit(solution)/shard_map/ppermute | solution.py:238
  464.7 9.1 %collective-permute-start.41 = (bf16[2,384,128]{2,1,0:T(8,128)(2,1)S(1)}, bf16[2,384,128]{2,1,0:T(8,128)(2,1)S(1)}, u32[]{:S(2)}, u32[]{:S(2)}) collective-permute-start(bf16[2,384,128]{2,1,0:T(8,128)(2,1)S(1)} %get-tuple-element.120), channel_id=1, source_target_pairs={{0,3},{1,2},{2,1},{3,0},{4,7},{5,6},{6,5},{7,4},{8,11},{9,10},{10,... | collective-permute-start | bytes 589832 | tf_op jit(solution)/shard_map/ppermute | solution.py:238
  464.8 11.0 %collective-permute-start.24 = (bf16[2,384,128]{2,1,0:T(8,128)(2,1)S(1)}, bf16[2,384,128]{2,1,0:T(8,128)(2,1)S(1)}, u32[]{:S(2)}, u32[]{:S(2)}) collective-permute-start(bf16[2,384,128]{2,1,0:T(8,128)(2,1)S(1)} %get-tuple-element.126), channel_id=1, source_target_pairs={{0,1},{1,0},{2,3},{3,2},{4,5},{5,4},{6,7},{7,6},{8,9},{9,8},{10,11... | collective-permute-start | bytes 589832 | tf_op jit(solution)/shard_map/ppermute | solution.py:238
  465.9 14.1 %collective-permute-start.26 = (bf16[2,384,128]{2,1,0:T(8,128)(2,1)S(1)}, bf16[2,384,128]{2,1,0:T(8,128)(2,1)S(1)}, u32[]{:S(2)}, u32[]{:S(2)}) collective-permute-start(bf16[2,384,128]{2,1,0:T(8,128)(2,1)S(1)} %get-tuple-element.125), channel_id=1, source_target_pairs={{0,2},{1,3},{2,0},{3,1},{4,6},{5,7},{6,4},{7,5},{8,10},{9,11},{10,... | collective-permute-start | bytes 589832 | tf_op jit(solution)/shard_map/ppermute | solution.py:238
  466.9 15.4 %collective-permute-start.28 = (bf16[2,384,128]{2,1,0:T(8,128)(2,1)S(1)}, bf16[2,384,128]{2,1,0:T(8,128)(2,1)S(1)}, u32[]{:S(2)}, u32[]{:S(2)}) collective-permute-start(bf16[2,384,128]{2,1,0:T(8,128)(2,1)S(1)} %get-tuple-element.124), channel_id=1, source_target_pairs={{0,3},{1,2},{2,1},{3,0},{4,7},{5,6},{6,5},{7,4},{8,11},{9,10},{10,... | collective-permute-start | bytes 589832 | tf_op jit(solution)/shard_map/ppermute | solution.py:238
  471.6 62.2 %copy-start.41 = (bf16[2,384,128]{2,1,0:T(8,128)(2,1)}, bf16[2,384,128]{2,1,0:T(8,128)(2,1)S(1)}, u32[]{:S(2)}) copy-start(bf16[2,384,128]{2,1,0:T(8,128)(2,1)S(1)} %collective-permute-done.39.refs_5_) | copy-start | bytes 589828
  471.6 161.4 %collective-permute-start.12 = (bf16[2,384,128]{2,1,0:T(8,128)(2,1)}, bf16[2,384,128]{2,1,0:T(8,128)(2,1)S(1)}, u32[]{:S(2)}, u32[]{:S(2)}) collective-permute-start(bf16[2,384,128]{2,1,0:T(8,128)(2,1)} %get-tuple-element.69), channel_id=1, source_target_pairs={{0,2},{1,3},{2,0},{3,1},{4,6},{5,7},{6,4},{7,5},{8,10},{9,11},{10,... | collective-permute-start | bytes 589832 | tf_op jit(solution)/shard_map/ppermute | solution.py:238
  473.9 59.9 %copy-start.44 = (bf16[2,384,128]{2,1,0:T(8,128)(2,1)}, bf16[2,384,128]{2,1,0:T(8,128)(2,1)S(1)}, u32[]{:S(2)}) copy-start(bf16[2,384,128]{2,1,0:T(8,128)(2,1)S(1)} %collective-permute-done.41.refs_7_) | copy-start | bytes 589828
  473.9 159.1 %collective-permute-start.14 = (bf16[2,384,128]{2,1,0:T(8,128)(2,1)}, bf16[2,384,128]{2,1,0:T(8,128)(2,1)S(1)}, u32[]{:S(2)}, u32[]{:S(2)}) collective-permute-start(bf16[2,384,128]{2,1,0:T(8,128)(2,1)} %get-tuple-element.70), channel_id=1, source_target_pairs={{0,3},{1,2},{2,1},{3,0},{4,7},{5,6},{6,5},{7,4},{8,11},{9,10},{10,... | collective-permute-start | bytes 589832 | tf_op jit(solution)/shard_map/ppermute | solution.py:238
  475.8 107.6 %copy-start.39 = (bf16[2,384,128]{2,1,0:T(8,128)(2,1)}, bf16[2,384,128]{2,1,0:T(8,128)(2,1)S(1)}, u32[]{:S(2)}) copy-start(bf16[2,384,128]{2,1,0:T(8,128)(2,1)S(1)} %collective-permute-done.24.refs_3_) | copy-start | bytes 589828
  475.8 157.2 %collective-permute-start.11 = (bf16[2,384,128]{2,1,0:T(8,128)(2,1)S(1)}, bf16[2,384,128]{2,1,0:T(8,128)(2,1)S(1)}, u32[]{:S(2)}, u32[]{:S(2)}) collective-permute-start(bf16[2,384,128]{2,1,0:T(8,128)(2,1)S(1)} %get-tuple-element.130), channel_id=1, source_target_pairs={{0,1},{1,0},{2,3},{3,2},{4,5},{5,4},{6,7},{7,6},{8,9},{9,8},{10,11... | collective-permute-start | bytes 589832 | tf_op jit(solution)/shard_map/ppermute | solution.py:238
  480.0 103.4 %copy-start.42 = (bf16[2,384,128]{2,1,0:T(8,128)(2,1)}, bf16[2,384,128]{2,1,0:T(8,128)(2,1)S(1)}, u32[]{:S(2)}) copy-start(bf16[2,384,128]{2,1,0:T(8,128)(2,1)S(1)} %collective-permute-done.26.refs_5_) | copy-start | bytes 589828
  480.0 153.0 %collective-permute-start.13 = (bf16[2,384,128]{2,1,0:T(8,128)(2,1)S(1)}, bf16[2,384,128]{2,1,0:T(8,128)(2,1)S(1)}, u32[]{:S(2)}, u32[]{:S(2)}) collective-permute-start(bf16[2,384,128]{2,1,0:T(8,128)(2,1)S(1)} %get-tuple-element.129), channel_id=1, source_target_pairs={{0,2},{1,3},{2,0},{3,1},{4,6},{5,7},{6,4},{7,5},{8,10},{9,11},{10,... | collective-permute-start | bytes 589832 | tf_op jit(solution)/shard_map/ppermute | solution.py:238
  482.3 101.1 %copy-start.45 = (bf16[2,384,128]{2,1,0:T(8,128)(2,1)}, bf16[2,384,128]{2,1,0:T(8,128)(2,1)S(1)}, u32[]{:S(2)}) copy-start(bf16[2,384,128]{2,1,0:T(8,128)(2,1)S(1)} %collective-permute-done.28.refs_7_) | copy-start | bytes 589828
  482.3 150.8 %collective-permute-start.15 = (bf16[2,384,128]{2,1,0:T(8,128)(2,1)S(1)}, bf16[2,384,128]{2,1,0:T(8,128)(2,1)S(1)}, u32[]{:S(2)}, u32[]{:S(2)}) collective-permute-start(bf16[2,384,128]{2,1,0:T(8,128)(2,1)S(1)} %get-tuple-element.128), channel_id=1, source_target_pairs={{0,3},{1,2},{2,1},{3,0},{4,7},{5,6},{6,5},{7,4},{8,11},{9,10},{10,... | collective-permute-start | bytes 589832 | tf_op jit(solution)/shard_map/ppermute | solution.py:238
  (48 other events, 449.9 us)

commit v2 on v0

v2 whole, which is shorter than its diff:
```python
import functools
import math

import jax
import jax.numpy as jnp
from jax import lax
from jax.experimental import pallas as pl
from jax.experimental.pallas import tpu as pltpu
from jax.sharding import PartitionSpec as P

HD = 128
FLAG_ROWS = 16
RING = ("ctx", "sub")
F32 = jnp.float32
BF16 = jnp.bfloat16
SCALE = 1.0 / math.sqrt(HD)
FACTOR = SCALE * math.log2(math.e)
ANY = pl.BlockSpec(memory_space=pl.ANY)
VMEM = pl.BlockSpec(memory_space=pltpu.VMEM)
SMEM = pl.BlockSpec(memory_space=pltpu.SMEM)
PARAMS = pltpu.CompilerParams(vmem_limit_bytes=48 * 1024 * 1024)


def struct(shape, dtype):
    return jax.ShapeDtypeStruct(shape, dtype)


def moved(nbytes):
    return pl.CostEstimate(flops=0, bytes_accessed=nbytes, transcendentals=0)


def run_copies(copies, sems):
    started = [pltpu.make_async_copy(src, dst, sems.at[n]) for n, (src, dst) in enumerate(copies)]
    for copy in started:
        copy.start()
    for copy in started:
        copy.wait()


def pack_kernel(jobs, tile, cols_ref, flags_ref, *refs):
    sources, outs = refs[:4], refs[4 : 4 + len(jobs)]
    for out, (pieces, kinds, flagged) in zip(outs, jobs):
        at = 0
        for d, c in pieces:
            lanes = pl.ds(pl.multiple_of(cols_ref[c, d], HD), HD)
            for n in kinds:
                out[pl.ds(at, tile)] = sources[n][0, :, lanes]
                at += tile
        if flagged:
            lane = lax.broadcasted_iota(jnp.int32, (FLAG_ROWS, HD), 1)
            row = jnp.zeros((FLAG_ROWS, HD), F32)
            for w in range(flags_ref.shape[0]):
                row = jnp.where(lane == w, flags_ref[w].astype(F32), row)
            out[pl.ds(at, FLAG_ROWS)] = row.astype(BF16)


def pack(jobs, cols, flags, sources, after=()):
    tile = sources[0].shape[1]
    shapes = [
        (len(pieces) * len(kinds) * tile + (FLAG_ROWS if flagged else 0), HD)
        for pieces, kinds, flagged in jobs
    ]

    def kernel(cols_ref, flags_ref, *refs):
        pack_kernel(jobs, tile, cols_ref, flags_ref, *refs[:4], *refs[4 + len(after) :])

    return pl.pallas_call(
        kernel,
        out_shape=[struct(shape, BF16) for shape in shapes],
        in_specs=[SMEM, SMEM] + [VMEM] * 4 + [ANY] * len(after),
        out_specs=[VMEM] * len(jobs),
        cost_estimate=moved(sum(4 * HD * shape[0] for shape in shapes)),
        compiler_params=PARAMS,
        name="pack",
    )(cols, flags, *sources, *after)


def relay_kernel(rows, tile, *refs):
    pieces, out, sems = refs[:rows], refs[-2], refs[-1]
    run_copies(
        [
            (pieces[e].at[pl.ds(0, 2 * tile)], out.at[pl.ds(2 * tile * e, 2 * tile)])
            for e in range(rows)
        ],
        sems,
    )


def relay(rows, tile, pieces):
    return pl.pallas_call(
        functools.partial(relay_kernel, rows, tile),
        out_shape=struct((rows * 2 * tile, HD), BF16),
        in_specs=[ANY] * rows,
        out_specs=ANY,
        scratch_shapes=[pltpu.SemaphoreType.DMA((rows,))],
        cost_estimate=moved(rows * 8 * tile * HD),
        name="relay",
    )(*pieces)


def nt(a, b):
    return lax.dot_general(a, b, (((1,), (1,)), ((), ())), preferred_element_type=F32)


def nn(a, b):
    return jnp.dot(a, b, preferred_element_type=F32)


def attend_kernel(plan, rows, tile, live_ref, *refs):
    loads, windows, n_in, spare = plan
    slabs_here = len(windows)
    team = slabs_here * rows
    inputs = refs[:n_in]
    rest = refs[n_in + spare :]
    done, local, grads_one, grads_two = rest[:4]
    qbuf, gbuf, kbuf, vbuf, kt, vt, dk, dv, s_buf, p_buf, ds_buf, sems = rest[4:]
    targets = {"k": kbuf, "v": vbuf, "q": qbuf, "g": gbuf}
    run_copies(
        [
            (inputs[n].at[pl.ds(at, tile)], targets[kind].at[slab, pl.ds(e * tile, tile)])
            for n, at, kind, slab, e in loads
        ],
        sems,
    )
    width = rows * tile
    places = kbuf.shape[0]

    def prepare(n, carry):
        kt[n] = kbuf[n].T
        vt[n] = vbuf[n].T
        dk[n] = jnp.zeros((width, HD), F32)
        dv[n] = jnp.zeros((width, HD), F32)
        return carry

    lax.fori_loop(0, places, prepare, 0)
    lane = lax.broadcasted_iota(jnp.int32, (1, width), 1)

    for a, window in enumerate(windows):
        query = qbuf[a]
        grad = gbuf[a]

        def seen(b):
            total = 0
            for f in range(rows):
                for e in range(rows):
                    total = total + live_ref[a * rows + f, b * rows + e]
            return total > 0

        top = jnp.full((1, width), -jnp.inf, F32)
        for b, place in enumerate(window):

            def scores(_, b=b, place=place, top=top):
                best = top
                for e in range(rows):
                    keep = jnp.zeros((1, width), jnp.int32)
                    for f in range(rows):
                        inside = (lane >= f * tile) & (lane < (f + 1) * tile)
                        keep = jnp.where(inside, live_ref[a * rows + f, b * rows + e], keep)
                    mask = jnp.where(keep > 0, 0.0, -jnp.inf)
                    s = nt(kbuf[place, pl.ds(e * tile, tile)], query) + mask
                    s_buf[b, pl.ds(e * tile, tile)] = s
                    best = jnp.maximum(best, jnp.max(s, axis=0, keepdims=True))
                return best

            top = lax.cond(seen(b), scores, lambda _, top=top: top, 0)

        total = jnp.zeros((1, width), F32)
        out_t = jnp.zeros((HD, width), F32)
        for b, place in enumerate(window):

            def expo(_, b=b, place=place, total=total, out_t=out_t):
                for e in range(rows):
                    at = pl.ds(e * tile, tile)
                    p = jnp.exp2((s_buf[b, at] - top) * FACTOR)
                    total = total + jnp.sum(p, axis=0, keepdims=True)
                    p_buf[b, at] = p.astype(BF16)
                return total, out_t + nn(vt[place], p_buf[b])

            total, out_t = lax.cond(
                seen(b), expo, lambda _, total=total, out_t=out_t: (total, out_t), 0
            )

        inv = 1.0 / total
        low_t = (out_t * inv).astype(BF16)
        grad_t = grad.T.astype(F32)
        offset = jnp.sum(grad_t * low_t.astype(F32), axis=0, keepdims=True)
        grad_over = (grad_t * inv).astype(BF16).T
        query_over = (query.T.astype(F32) * inv).astype(BF16).T
        out = low_t.T
        dq_t = jnp.zeros((HD, width), F32)
        for b, place in enumerate(window):

            def backward(_, b=b, place=place, dq_t=dq_t):
                for e in range(rows):
                    at = pl.ds(e * tile, tile)
                    p = p_buf[b, at]
                    dp = nt(vbuf[place, at], grad)
                    ds = (p.astype(F32) * (dp - offset)).astype(BF16)
                    ds_buf[at] = ds
                    dv[place, at] += nn(p, grad_over)
                    dk[place, at] += nn(ds, query_over)
                return dq_t + nn(kt[place], ds_buf[...])

            dq_t = lax.cond(seen(b), backward, lambda _, dq_t=dq_t: dq_t, 0)
        dq = (dq_t * (inv * SCALE)).astype(BF16).T
        for f in range(rows):
            done[a * rows + f, 0] = out[f * tile : (f + 1) * tile]
            done[a * rows + f, 1] = dq[f * tile : (f + 1) * tile]

    for d in range(team):
        at = pl.ds(d % rows * tile, tile)
        local[d, 0] = dk[d // rows, at] * SCALE
        local[d, 1] = dv[d // rows, at]
    for n, grads in enumerate((grads_one, grads_two)):
        for e in range(rows):
            at = pl.ds(e * tile, tile)
            grads[e, 0] = (dk[slabs_here + n, at] * SCALE).astype(BF16)
            grads[e, 1] = dv[slabs_here + n, at].astype(BF16)


def attend(rows, tile, live, loads, windows, inputs, spare):
    places = len(windows) + 2
    team = len(windows) * rows
    width = rows * tile
    scores = 3 * len(windows) * width * width
    plan = (loads, windows, len(inputs), len(spare))
    return pl.pallas_call(
        functools.partial(attend_kernel, plan, rows, tile),
        out_shape=[
            struct((team, 2, tile, HD), BF16),
            struct((team, 2, tile, HD), F32),
            struct((rows, 2, tile, HD), BF16),
            struct((rows, 2, tile, HD), BF16),
        ],
        in_specs=[SMEM] + [ANY] * (len(inputs) + len(spare)),
        out_specs=[VMEM] * 4,
        scratch_shapes=[
            pltpu.VMEM((len(windows), width, HD), BF16),
            pltpu.VMEM((len(windows), width, HD), BF16),
            pltpu.VMEM((places, width, HD), BF16),
            pltpu.VMEM((places, width, HD), BF16),
            pltpu.VMEM((places, HD, width), BF16),
            pltpu.VMEM((places, HD, width), BF16),
            pltpu.VMEM((places, width, HD), F32),
            pltpu.VMEM((places, width, HD), F32),
            pltpu.VMEM((3, width, width), F32),
            pltpu.VMEM((3, width, width), BF16),
            pltpu.VMEM((width, width), BF16),
            pltpu.SemaphoreType.DMA((len(loads),)),
        ],
        cost_estimate=pl.CostEstimate(
            flops=12 * scores * HD, bytes_accessed=8 * 1024 * 1024, transcendentals=scores
        ),
        compiler_params=PARAMS,
        name="attend",
    )(live, *inputs, *spare)


def finish_kernel(team, rows, extras, done, local, *refs):
    grads, outs = refs[: len(extras)], refs[-team:]
    for d in range(team):
        for n in range(2):
            outs[d][n] = done[d, n]
            total = local[d, n]
            for grad, slab in zip(grads, extras):
                if d // rows == slab:
                    total = total + grad[d % rows, n].astype(F32)
            outs[d][2 + n] = total.astype(BF16)


def finish(team, rows, extras, done, local, grads, spare):
    tile = done.shape[2]
    return pl.pallas_call(
        functools.partial(finish_kernel, team, rows, extras),
        out_shape=[struct((4, tile, HD), BF16)] * team,
        in_specs=[VMEM] * (2 + len(grads)) + [ANY] * len(spare),
        out_specs=[VMEM] * team,
        cost_estimate=moved(team * 24 * tile * HD),
        compiler_params=PARAMS,
        name="finish",
    )(done, local, *grads, *spare)


def unpack_kernel(team, per, cols_ref, *refs):
    pieces, outs = refs[: team * per], refs[team * per :]
    for c in range(per):
        for d in range(team):
            lanes = pl.ds(pl.multiple_of(cols_ref[c, d], HD), HD)
            for n in range(4):
                outs[n][0, :, lanes] = pieces[c * team + d][n]


def unpack(team, per, cols, pieces, shape):
    tile = shape[1]
    step = tile // 4 if tile % 64 == 0 else tile
    return pl.pallas_call(
        functools.partial(unpack_kernel, team, per),
        grid=(tile // step,),
        out_shape=[struct(shape, BF16)] * 4,
        in_specs=[SMEM] + [pl.BlockSpec((4, step, HD), lambda i: (0, i, 0))] * len(pieces),
        out_specs=[pl.BlockSpec((1, step, shape[2]), lambda i: (0, i, 0))] * 4,
        cost_estimate=moved(len(pieces) * 16 * tile * HD),
        compiler_params=PARAMS,
        name="unpack",
    )(cols, *pieces)


def body(queries, keys, values, grad_out, window_tiles, window_count):
    rows_here, tile, lane_width = queries.shape
    wmax = window_tiles.shape[1]
    heads = lane_width // HD
    rows = lax.axis_size("sub")
    slabs = lax.axis_size("ctx")
    span = 2 if heads % (2 * rows) == 0 and slabs % 2 == 0 else 1
    team = span * rows
    per = heads // team
    size = slabs * rows
    slab = lax.axis_index("ctx")
    row = lax.axis_index("sub")
    odd = slab % span
    me = odd * rows + row

    def swap(value, d):
        if d == 0:
            return value
        return lax.ppermute(value, RING, [(i, i - i % team + (i % team ^ d)) for i in range(size)])

    def shift(value, way, flip=0):
        pairs = []
        for i in range(size):
            place = i % team // rows
            forward = (place == span - 1) if way == 0 else (place == 0)
            if span == 1:
                forward = way == 0
            j = i + team if forward else i - team
            if 0 <= j < size:
                pairs.append((i, j ^ flip))
        return lax.ppermute(value, RING, pairs)

    places = (window_tiles[0] // rows - slab + 1) * rows + window_tiles[0] % rows
    listed = jnp.arange(wmax) < window_count[0]
    flags = jnp.any(
        (places[None, :] == jnp.arange(3 * rows)[:, None]) & listed[None, :], axis=1
    ).astype(jnp.int32)

    partners = jnp.arange(team, dtype=jnp.int32) ^ me
    heads_of = (partners[None, :] * per + jnp.arange(per, dtype=jnp.int32)[:, None]) * HD
    sources = (keys, values, queries, grad_out)
    kinds = (0, 1, 2, 3)
    every = tuple(range(per))
    far = tuple(range(rows, team))

    sent = {}
    if far:
        first = pack([(((d, 0),), kinds, True) for d in far], heads_of, flags, sources)
        for d, value in zip(far, first):
            sent[0, d] = value
    jobs = [
        (tuple((0, c) for c in every), kinds, True),
        (tuple((1, c) for c in every), kinds, True),
        (tuple((0, c) for c in every), (0, 1), False),
        (tuple((1, c) for c in every), (0, 1), False),
    ]
    later = [(c, d) for c in every[1:] for d in far]
    jobs += [(((d, c),), kinds, False) for c, d in later]
    packed = pack(jobs, heads_of, flags, sources, after=tuple(sent.values())[:1])
    own, beside, own_kv, beside_kv = packed[:4]
    for key, value in zip(later, packed[4:]):
        sent[key] = value

    mates = [own, swap(beside, 1)]
    arrived = {}
    for c in every:
        for d in far:
            arrived[c, d] = swap(sent[c, d], d)
    near_one = [shift(own_kv, 0), shift(beside_kv, 0, flip=1)]
    if span == 1:
        near_two = [shift(own_kv, 1), shift(beside_kv, 1, flip=1)]

    lists = [mate[-FLAG_ROWS] for mate in mates] + [arrived[0, d][-FLAG_ROWS] for d in far]
    table = jnp.stack([value[: 3 * rows] for value in lists]).astype(jnp.int32)
    table = table.reshape(team, 3, rows)
    table = jnp.where(row == 0, table, table[:, :, ::-1])
    turned = table[:, ::-1]
    if span == 1:
        live = table
    else:
        live = jnp.concatenate(
            [
                jnp.where(odd == 0, table[:rows], turned[:rows]),
                jnp.where(odd == 0, turned[rows:], table[rows:]),
            ]
        )
    live = live.reshape(team, 3 * rows)

    if span == 1:
        windows = ((1, 0, 2),)
        extras = (0, 0)
    else:
        windows = ((3, 0, 1), (2, 1, 0))
        extras = (0, 1)

    two_bytes = 2 * tile
    pieces = []
    for c in every:
        inputs = [mates[0], mates[1]]
        loads = []
        for e in range(rows):
            for n, kind in enumerate("kvqg"):
                loads.append((e, (4 * c + n) * tile, kind, 0, e))
        for d in far:
            for n, kind in enumerate("kvqg"):
                loads.append((len(inputs), n * tile, kind, 1, d - rows))
            inputs.append(arrived[c, d])
        for e in range(rows):
            for n, kind in enumerate("kv"):
                loads.append((len(inputs), (2 * c + n) * tile, kind, span, e))
            inputs.append(near_one[e])
        if span == 1:
            for e in range(rows):
                for n, kind in enumerate("kv"):
                    loads.append((len(inputs), (2 * c + n) * tile, kind, span + 1, e))
                inputs.append(near_two[e])
        else:
            beyond = shift(relay(rows, tile, [arrived[c, d] for d in far]), 1)
            for e in range(rows):
                for n, kind in enumerate("kv"):
                    loads.append((len(inputs), (2 * e + n) * tile, kind, span + 1, e))
            inputs.append(beyond)
        done, local, grads_one, grads_two = attend(
            rows, tile, live, tuple(loads), windows, inputs, ()
        )
        back = (shift(grads_one, 1), shift(grads_two, 0))
        home = finish(team, rows, extras, done, local, back, ())
        pieces += [swap(home[d], d) for d in range(team)]
    grad_keys, grad_values = None, None
    attended, grad_queries, grad_keys, grad_values = unpack(
        team, per, heads_of, pieces, queries.shape
    )
    return (attended, grad_queries, grad_keys, grad_values)


def solution(mesh):
    spec = P(("grp", "ctx", "sub"), None, "head")
    return jax.shard_map(
        body,
        mesh=mesh,
        in_specs=(spec, spec, spec, spec, P(("grp", "ctx", "sub"), None), P(("grp", "ctx", "sub"))),
        out_specs=(spec, spec, spec, spec),
        check_vma=False,
    )
```

time: 1060 us -> 325 us (0.31)
  waiting for transfers between devices: 556 us -> 98.6 us
  matrix products: 199 us -> 0 us
  other arithmetic: 140 us -> 1.07 us
  Pallas kernels: 0 us -> 129 us
  local copies, waits for them, and re-layouts: 122 us -> 14.6 us
  starting transfers between devices: 14.6 us -> 74.8 us
  between operations: 16.3 us -> 2.29 us
    ppermute x4 -> x35, waiting for transfers between devices: 532 us -> 98.6 us  [the longest x21 88.8 us: swap(): lax.ppermute(value, RING, [(i, i - i % team + (i % team ^ d)) for i in ra...]
    dot_general x96 -> x0, matrix products: 199 us -> none  [the longest x16 53.8 us: query_head(): jnp.einsum('qd,kd->qk', query_part, key_part, preferred_element_type=jnp....]
    pallas_call x0 -> x15, Pallas kernels: none -> 129 us  [the longest x4 62 us: attend(): pl.pallas_call(functools.partial(attend_kernel, plan, rows, tile), out_sh...]
    ppermute x4 -> x35, starting transfers between devices: 14.5 us -> 74.8 us  [the longest x14 55.9 us: shift(): return lax.ppermute(value, RING, pairs)]
    scatter-add x1 -> x0, other arithmetic: 48.5 us -> none  [body(): partial_value.at[:, slots].add(jnp.stack([key_slots, value_slots]))]
    convert_element_type x17 -> x2, other arithmetic: 40.7 us -> 0.09 us  [the longest x1 0.08 us: body(): table = jnp.stack([value[:3 * rows] for value in lists]).astype(jnp.int32)]
    concatenate x2 -> x0, local copies, waits for them, and re-layouts: 37.7 us -> none  [the longest x1 19 us: body(): jnp.concatenate(head_dks, axis=1).reshape(slot_count, tile_len, lane_width)]
    another operation x3 -> x0, other arithmetic: 31.2 us -> none  [the longest x1 13.6 us: body(): jnp.stack([key_slots, value_slots])]
  transfers between devices with their start and end apart: 6 -> 35, of which waited for: 5 -> 14; matrix products, arithmetic and copies ran while one was open for 2% -> 1% of each run, Pallas kernels for 0% -> 36%
where the time goes in v2:
time: 325 us; the launch traced here: 320 us
  Pallas kernels  129 us (40%)
  waiting for transfers between devices  98.6 us (30%)
  starting transfers between devices  74.8 us (23%)
  local copies, waits for them, and re-layouts  14.6 us (4%)
    ppermute x21, waiting for transfers between devices, swap(): lax.ppermute(value, RING, [(i, i - i % team + (i % team ^ d)) for i in ra...  88.8 us
    pallas_call x4, Pallas kernels, attend(): pl.pallas_call(functools.partial(attend_kernel, plan, rows, tile), out_sh...  62 us
    ppermute x14, starting transfers between devices, shift(): return lax.ppermute(value, RING, pairs)  55.9 us
    pallas_call x4, Pallas kernels, relay(): pl.pallas_call(functools.partial(relay_kernel, rows, tile), out_shape=str...  52.1 us
    ppermute x21, starting transfers between devices, swap(): lax.ppermute(value, RING, [(i, i - i % team + (i % team ^ d)) for i in ra...  19 us
    unnamed x56, local copies, waits for them, and re-layouts  10.8 us
    ppermute x14, waiting for transfers between devices, shift(): return lax.ppermute(value, RING, pairs)  9.87 us
    pallas_call x2, Pallas kernels, pack(): pl.pallas_call(kernel, out_shape=[struct(shape, BF16) for shape in shapes...  8.05 us
  transfers between devices with their start and end apart: 35, of which 14 were waited for; matrix products, arithmetic and copies ran while one was open for 1% of the time, Pallas kernels for 36%

profile of v2, /device:TPU:0, one launch (start us, length us, event | category | flops | bytes accessed | tf_op | source)
XLA Modules:
  0.0 320.3 jit_solution(4734262420892707101)
XLA Ops:
  0.7 0.7 fusion.3
  2.1 1.4 copy-done
  3.5 1.4 copy-done.1
  5.0 1.4 copy-done.2
  6.4 2.4 pack.2
  8.7 5.7 %pack.3 = (bf16[6160,128]{1,0:T(8,128)(2,1)}, bf16[6160,128]{1,0:T(8,128)(2,1)}, bf16[3072,128]{1,0:T(8,128)(2,1)S(1)}, bf16[3072,128]{1,0:T(8,128)(2,1)S(1)}, b...) custom-call(s32[4,4]{1,0:T(4,128)S(1)} %add_multiply_fusion.cols_ref, ...), custom_call_target="tpu_custom_call" | custom-call | bytes 14172160 | tf_op jit(solution)/shard_map/pack/pallas_call | solution.py:67
  14.4 0.5 collective-permute-start
  14.9 2.6 collective-permute-start.11
  17.5 1.7 collective-permute-start.19
  19.3 8.2 %collective-permute-done.11.refs_0_.refs_2_ = bf16[1536,128]{1,0:T(8,128)(2,1)S(1)} collective-permute-done((bf16[1536,128]{1,0:T(8,128)(2,1)S(1)}, bf16[1536,128]{1,0:T(8,128)(2,1)S(1)}, u32[]{:S(2)}, u32[]{:S(2)}) %collective-permute-start.11) | collective-permute-done | bytes 393248 | tf_op jit(solution)/shard_map/ppermute | solution.py:326
  27.4 0.8 collective-permute-start.2
  28.2 7.1 %collective-permute-done.12.refs_1_.refs_3_ = bf16[1536,128]{1,0:T(8,128)(2,1)S(1)} collective-permute-done((bf16[1536,128]{1,0:T(8,128)(2,1)S(1)}, bf16[1536,128]{1,0:T(8,128)(2,1)S(1)}, u32[]{:S(2)}, u32[]{:S(2)}) %collective-permute-start.12) | collective-permute-done | bytes 393248 | tf_op jit(solution)/shard_map/ppermute | solution.py:326
  35.3 1.6 collective-permute-start.27
  36.9 7.4 %collective-permute-done.19.refs_0_.refs_2_ = bf16[1536,128]{1,0:T(8,128)(2,1)S(1)} collective-permute-done((bf16[1536,128]{1,0:T(8,128)(2,1)S(1)}, bf16[1536,128]{1,0:T(8,128)(2,1)S(1)}, u32[]{:S(2)}, u32[]{:S(2)}) %collective-permute-start.19) | collective-permute-done | bytes 393248 | tf_op jit(solution)/shard_map/ppermute | solution.py:326
  44.3 0.8 collective-permute-start.28
  45.0 7.1 %collective-permute-done.20.refs_1_.refs_3_ = bf16[1536,128]{1,0:T(8,128)(2,1)S(1)} collective-permute-done((bf16[1536,128]{1,0:T(8,128)(2,1)S(1)}, bf16[1536,128]{1,0:T(8,128)(2,1)S(1)}, u32[]{:S(2)}, u32[]{:S(2)}) %collective-permute-start.20) | collective-permute-done | bytes 393248 | tf_op jit(solution)/shard_map/ppermute | solution.py:326
  52.2 1.6 collective-permute-start.1
  53.8 1.3 slice_reduce_fusion.3
  55.1 1.3 stack.20
  56.4 13.0 %relay.5 = bf16[1536,128]{1,0:T(8,128)(2,1)} custom-call(bf16[1536,128]{1,0:T(8,128)(2,1)} %copy-done.15, bf16[1536,128]{1,0:T(8,128)(2,1)} %copy-done.17), custom_call_target="tpu_custom_call" | custom-call | bytes 786432 | tf_op jit(solution)/shard_map/relay/pallas_call | solution.py:90
  69.5 13.0 %relay.6 = bf16[1536,128]{1,0:T(8,128)(2,1)} custom-call(bf16[1536,128]{1,0:T(8,128)(2,1)} %copy-done.7, bf16[1536,128]{1,0:T(8,128)(2,1)} %copy-done.9), custom_call_target="tpu_custom_call" | custom-call | bytes 786432 | tf_op jit(solution)/shard_map/relay/pallas_call | solution.py:90
  82.5 1.3 collective-permute-start.3
  83.9 1.3 collective-permute-start.4
  85.2 13.0 %relay.7 = bf16[1536,128]{1,0:T(8,128)(2,1)} custom-call(bf16[1536,128]{1,0:T(8,128)(2,1)} %copy-done.11, bf16[1536,128]{1,0:T(8,128)(2,1)} %copy-done.13), custom_call_target="tpu_custom_call" | custom-call | bytes 786432 | tf_op jit(solution)/shard_map/relay/pallas_call | solution.py:90
  98.2 6.0 %collective-permute-start.13 = (bf16[1536,128]{1,0:T(8,128)(2,1)}, bf16[1536,128]{1,0:T(8,128)(2,1)}, u32[]{:S(2)}, u32[]{:S(2)}) collective-permute-start(bf16[1536,128]{1,0:T(8,128)(2,1)} %relay.5), channel_id=1, source_target_pairs={{0,4},{1,5},{4,8},{5,9},{6,2},{7,3},{8,12},{9,13},{10,6},{11,7},{1... | collective-permute-start | bytes 1179656 | tf_op jit(solution)/shard_map/ppermute | solution.py:338
  104.3 4.0 %collective-permute-start.21 = (bf16[1536,128]{1,0:T(8,128)(2,1)}, bf16[1536,128]{1,0:T(8,128)(2,1)}, u32[]{:S(2)}, u32[]{:S(2)}) collective-permute-start(bf16[1536,128]{1,0:T(8,128)(2,1)} %relay.6), channel_id=1, source_target_pairs={{0,4},{1,5},{4,8},{5,9},{6,2},{7,3},{8,12},{9,13},{10,6},{11,7},{1... | collective-permute-start | bytes 1179656 | tf_op jit(solution)/shard_map/ppermute | solution.py:338
  108.4 13.0 %relay.4 = bf16[1536,128]{1,0:T(8,128)(2,1)} custom-call(bf16[1552,128]{1,0:T(8,128)(2,1)} %copy-done.5, bf16[1552,128]{1,0:T(8,128)(2,1)} %copy-done.3), custom_call_target="tpu_custom_call" | custom-call | bytes 786432 | tf_op jit(solution)/shard_map/relay/pallas_call | solution.py:90
  121.5 3.6 %collective-permute-start.5 = (bf16[1536,128]{1,0:T(8,128)(2,1)}, bf16[1536,128]{1,0:T(8,128)(2,1)S(1)}, u32[]{:S(2)}, u32[]{:S(2)}) collective-permute-start(bf16[1536,128]{1,0:T(8,128)(2,1)} %relay.4), channel_id=1, source_target_pairs={{0,4},{1,5},{4,8},{5,9},{6,2},{7,3},{8,12},{9,13},{10,6},{11,7},{1... | collective-permute-start | bytes 1179656 | tf_op jit(solution)/shard_map/ppermute | solution.py:338
  125.1 0.7 slice_reduce_fusion.2
  126.3 0.9 copy-done.20
  127.2 1.9 collective-permute-start.29
  129.2 5.8 %collective-permute-done.5.refs_6_ = bf16[1536,128]{1,0:T(8,128)(2,1)S(1)} collective-permute-done((bf16[1536,128]{1,0:T(8,128)(2,1)}, bf16[1536,128]{1,0:T(8,128)(2,1)S(1)}, u32[]{:S(2)}, u32[]{:S(2)}) %collective-permute-start.5) | collective-permute-done | bytes 393248 | tf_op jit(solution)/shard_map/ppermute | solution.py:338
  134.9 1.0 copy-done.4
  135.9 1.0 copy-done.6
  136.9 1.1 copy-done.21
  138.1 15.4 %attend.4 = (bf16[4,2,384,128]{3,2,1,0:T(8,128)(2,1)S(1)}, f32[4,2,384,128]{3,2,1,0:T(8,128)S(1)}, bf16[2,2,384,128]{3,2,1,0:T(8,128)(2,1)}, bf16[2,2,384,128]{3,2,1,0:T(8,128)(2,1)}) custom-call(s32[4,6]{1,0:T(4,128)S(1)} %copy.32.live_ref, bf16[6160,128]{1,0:T(8,128)(2,1)} %get-tuple-element.49.refs_0_, bf16[6160,128]{1,0:T(8,128)(2,1)} %collective-permute-done.refs_1_, ...), custom_call_target="tpu_custom_call" | custom-call | flops 5435817984 | bytes 8388608 | tf_op jit(solution)/shard_map/attend/pallas_call | solution.py:227
  153.5 6.6 %collective-permute-start.6 = (bf16[2,2,384,128]{3,2,1,0:T(8,128)(2,1)}, bf16[2,2,384,128]{3,2,1,0:T(8,128)(2,1)S(1)}, u32[]{:S(2)}, u32[]{:S(2)}) collective-permute-start(bf16[2,2,384,128]{3,2,1,0:T(8,128)(2,1)} %get-tuple-element.56), channel_id=1, source_target_pairs={{0,4},{1,5},{4,8},{5,9},{6,2},{7,3},{8,12},{9,13},{10,6},{11,7},{1... | collective-permute-start | bytes 1179656 | tf_op jit(solution)/shard_map/ppermute | solution.py:338
  160.2 1.4 collective-permute-start.7
  161.7 15.7 %attend.5 = (bf16[4,2,384,128]{3,2,1,0:T(8,128)(2,1)S(1)}, f32[4,2,384,128]{3,2,1,0:T(8,128)S(1)}, bf16[2,2,384,128]{3,2,1,0:T(8,128)(2,1)}, bf16[2,2,384,128]{3,2,1,0:T(8,128)(2,1)S(1)}) custom-call(s32[4,6]{1,0:T(4,128)S(1)} %copy.32.live_ref, bf16[6160,128]{1,0:T(8,128)(2,1)} %get-tuple-element.49.refs_0_, ...), custom_call_target="tpu_custom_call" | custom-call | flops 5435817984 | bytes 8388608 | tf_op jit(solution)/shard_map/attend/pallas_call | solution.py:227
  177.4 7.2 %collective-permute-start.14 = (bf16[2,2,384,128]{3,2,1,0:T(8,128)(2,1)}, bf16[2,2,384,128]{3,2,1,0:T(8,128)(2,1)S(1)}, u32[]{:S(2)}, u32[]{:S(2)}) collective-permute-start(bf16[2,2,384,128]{3,2,1,0:T(8,128)(2,1)} %get-tuple-element.66), channel_id=1, source_target_pairs={{0,4},{1,5},{4,8},{5,9},{6,2},{7,3},{8,12},{9,13},{10,6},{11,7},{1... | collective-permute-start | bytes 1179656 | tf_op jit(solution)/shard_map/ppermute | solution.py:338
  184.6 1.4 collective-permute-start.15
  186.0 15.5 %attend.6 = (bf16[4,2,384,128]{3,2,1,0:T(8,128)(2,1)S(1)}, f32[4,2,384,128]{3,2,1,0:T(8,128)S(1)}, bf16[2,2,384,128]{3,2,1,0:T(8,128)(2,1)}, bf16[2,2,384,128]{3,2,1,0:T(8,128)(2,1)S(1)}) custom-call(s32[4,6]{1,0:T(4,128)S(1)} %copy.32.live_ref, bf16[6160,128]{1,0:T(8,128)(2,1)} %get-tuple-element.49.refs_0_, ...), custom_call_target="tpu_custom_call" | custom-call | flops 5435817984 | bytes 8388608 | tf_op jit(solution)/shard_map/attend/pallas_call | solution.py:227
  201.5 0.8 copy-done.24
  202.3 9.4 %collective-permute-start.22 = (bf16[2,2,384,128]{3,2,1,0:T(8,128)(2,1)}, bf16[2,2,384,128]{3,2,1,0:T(8,128)(2,1)S(1)}, u32[]{:S(2)}, u32[]{:S(2)}) collective-permute-start(bf16[2,2,384,128]{3,2,1,0:T(8,128)(2,1)} %get-tuple-element.76), channel_id=1, source_target_pairs={{0,4},{1,5},{4,8},{5,9},{6,2},{7,3},{8,12},{9,13},{10,6},{11,7},{1... | collective-permute-start | bytes 1179656 | tf_op jit(solution)/shard_map/ppermute | solution.py:338
  211.7 1.0 copy-done.25
  212.7 15.4 %attend.7 = (bf16[4,2,384,128]{3,2,1,0:T(8,128)(2,1)S(1)}, f32[4,2,384,128]{3,2,1,0:T(8,128)S(1)}, bf16[2,2,384,128]{3,2,1,0:T(8,128)(2,1)}, bf16[2,2,384,128]{3,2,1,0:T(8,128)(2,1)S(1)}) custom-call(s32[4,6]{1,0:T(4,128)S(1)} %copy.32.live_ref, bf16[6160,128]{1,0:T(8,128)(2,1)} %get-tuple-element.49.refs_0_, ...), custom_call_target="tpu_custom_call" | custom-call | flops 5435817984 | bytes 8388608 | tf_op jit(solution)/shard_map/attend/pallas_call | solution.py:227
  228.1 1.3 collective-permute-start.23
  229.4 9.2 %collective-permute-start.30 = (bf16[2,2,384,128]{3,2,1,0:T(8,128)(2,1)}, bf16[2,2,384,128]{3,2,1,0:T(8,128)(2,1)S(1)}, u32[]{:S(2)}, u32[]{:S(2)}) collective-permute-start(bf16[2,2,384,128]{3,2,1,0:T(8,128)(2,1)} %get-tuple-element.86), channel_id=1, source_target_pairs={{0,4},{1,5},{4,8},{5,9},{6,2},{7,3},{8,12},{9,13},{10,6},{11,7},{1... | collective-permute-start | bytes 1179656 | tf_op jit(solution)/shard_map/ppermute | solution.py:338
  238.8 1.3 collective-permute-start.31
  240.2 5.2 %collective-permute-start.9 = (bf16[4,384,128]{2,1,0:T(8,128)(2,1)S(1)}, bf16[4,384,128]{2,1,0:T(8,128)(2,1)S(1)}, u32[]{:S(2)}, u32[]{:S(2)}) collective-permute-start(bf16[4,384,128]{2,1,0:T(8,128)(2,1)S(1)} %get-tuple-element.60), channel_id=1, source_target_pairs={{0,2},{1,3},{2,0},{3,1},{4,6},{5,7},{6,4},{7,5},{8,10},{9,11},{10,... | collective-permute-start | bytes 1179656 | tf_op jit(solution)/shard_map/ppermute | solution.py:326
  245.4 0.9 finish.5
  246.8 4.1 %collective-permute-done.31.refs_1_ = bf16[2,2,384,128]{3,2,1,0:T(8,128)(2,1)S(1)} collective-permute-done((bf16[2,2,384,128]{3,2,1,0:T(8,128)(2,1)S(1)}, bf16[2,2,384,128]{3,2,1,0:T(8,128)(2,1)S(1)}, u32[]{:S(2)}, u32[]{:S(2)}) %collective-permute-start.31) | collective-permute-done | bytes 393248 | tf_op jit(solution)/shard_map/ppermute | solution.py:338
  250.8 4.5 %collective-permute-done.9.refs_2_ = bf16[4,384,128]{2,1,0:T(8,128)(2,1)S(1)} collective-permute-done((bf16[4,384,128]{2,1,0:T(8,128)(2,1)S(1)}, bf16[4,384,128]{2,1,0:T(8,128)(2,1)S(1)}, u32[]{:S(2)}, u32[]{:S(2)}) %collective-permute-start.9) | collective-permute-done | bytes 393248 | tf_op jit(solution)/shard_map/ppermute | solution.py:326
  255.6 7.7 %collective-permute-done.10.refs_3_ = bf16[4,384,128]{2,1,0:T(8,128)(2,1)S(1)} collective-permute-done((bf16[4,384,128]{2,1,0:T(8,128)(2,1)S(1)}, bf16[4,384,128]{2,1,0:T(8,128)(2,1)S(1)}, u32[]{:S(2)}, u32[]{:S(2)}) %collective-permute-start.10) | collective-permute-done | bytes 393248 | tf_op jit(solution)/shard_map/ppermute | solution.py:326
  263.3 1.6 collective-permute-start.25
  265.2 7.0 %collective-permute-done.17.refs_6_ = bf16[4,384,128]{2,1,0:T(8,128)(2,1)S(1)} collective-permute-done((bf16[4,384,128]{2,1,0:T(8,128)(2,1)S(1)}, bf16[4,384,128]{2,1,0:T(8,128)(2,1)S(1)}, u32[]{:S(2)}, u32[]{:S(2)}) %collective-permute-start.17) | collective-permute-done | bytes 393248 | tf_op jit(solution)/shard_map/ppermute | solution.py:326
  272.2 7.9 %collective-permute-done.18.refs_7_ = bf16[4,384,128]{2,1,0:T(8,128)(2,1)S(1)} collective-permute-done((bf16[4,384,128]{2,1,0:T(8,128)(2,1)S(1)}, bf16[4,384,128]{2,1,0:T(8,128)(2,1)S(1)}, u32[]{:S(2)}, u32[]{:S(2)}) %collective-permute-start.18) | collective-permute-done | bytes 393248 | tf_op jit(solution)/shard_map/ppermute | solution.py:326
  280.1 1.6 collective-permute-start.33
  282.1 7.0 %collective-permute-done.25.refs_10_ = bf16[4,384,128]{2,1,0:T(8,128)(2,1)S(1)} collective-permute-done((bf16[4,384,128]{2,1,0:T(8,128)(2,1)S(1)}, bf16[4,384,128]{2,1,0:T(8,128)(2,1)S(1)}, u32[]{:S(2)}, u32[]{:S(2)}) %collective-permute-start.25) | collective-permute-done | bytes 393248 | tf_op jit(solution)/shard_map/ppermute | solution.py:326
  289.1 7.9 %collective-permute-done.26.refs_11_ = bf16[4,384,128]{2,1,0:T(8,128)(2,1)S(1)} collective-permute-done((bf16[4,384,128]{2,1,0:T(8,128)(2,1)S(1)}, bf16[4,384,128]{2,1,0:T(8,128)(2,1)S(1)}, u32[]{:S(2)}, u32[]{:S(2)}) %collective-permute-start.26) | collective-permute-done | bytes 393248 | tf_op jit(solution)/shard_map/ppermute | solution.py:326
  297.0 8.9 %collective-permute-done.33.refs_14_ = bf16[4,384,128]{2,1,0:T(8,128)(2,1)S(1)} collective-permute-done((bf16[4,384,128]{2,1,0:T(8,128)(2,1)S(1)}, bf16[4,384,128]{2,1,0:T(8,128)(2,1)S(1)}, u32[]{:S(2)}, u32[]{:S(2)}) %collective-permute-start.33) | collective-permute-done | bytes 393248 | tf_op jit(solution)/shard_map/ppermute | solution.py:326
  305.9 7.9 %collective-permute-done.34.refs_15_ = bf16[4,384,128]{2,1,0:T(8,128)(2,1)S(1)} collective-permute-done((bf16[4,384,128]{2,1,0:T(8,128)(2,1)S(1)}, bf16[4,384,128]{2,1,0:T(8,128)(2,1)S(1)}, u32[]{:S(2)}, u32[]{:S(2)}) %collective-permute-start.34) | collective-permute-done | bytes 393248 | tf_op jit(solution)/shard_map/ppermute | solution.py:326
  313.8 0.7 copy-done.26
  314.6 5.3 %unpack.1 = (bf16[1,384,2048]{2,1,0:T(8,128)(2,1)}, bf16[1,384,2048]{2,1,0:T(8,128)(2,1)}, bf16[1,384,2048]{2,1,0:T(8,128)(2,1)}, bf16[1,384,2048]{2,1,0:T(8,128)(2,1)}) custom-call(s32[4,4]{1,0:T(4,128)S(1)} %add_multiply_fusion.cols_ref, bf16[4,384,128]{2,1,0:T(8,128)(2,1)S(1)} %get-tuple-element.58.refs_0_, ...), custom_call_target="tpu_custom_call" | custom-call | bytes 12582912 | tf_op jit(solution)/shard_map/unpack/pallas_call | solution.py:296
  (99 shorter events, 2.7 us)
Async XLA Ops:
  2.1 1.4 copy-start
  3.5 1.4 copy-start.1
  5.0 1.4 copy-start.2
  14.4 37.8 %copy-start.19 = (bf16[3072,128]{1,0:T(8,128)(2,1)}, bf16[3072,128]{1,0:T(8,128)(2,1)S(1)}, u32[]{:S(2)}) copy-start(bf16[3072,128]{1,0:T(8,128)(2,1)S(1)} %get-tuple-element.53) | copy-start | bytes 2359300
  14.4 37.8 %copy-start.23 = (bf16[3072,128]{1,0:T(8,128)(2,1)}, bf16[3072,128]{1,0:T(8,128)(2,1)S(1)}, u32[]{:S(2)}) copy-start(bf16[3072,128]{1,0:T(8,128)(2,1)S(1)} %get-tuple-element.52) | copy-start | bytes 2359300
  14.4 107.0 %collective-permute-start = (bf16[6160,128]{1,0:T(8,128)(2,1)}, bf16[6160,128]{1,0:T(8,128)(2,1)}, u32[]{:S(2)}, u32[]{:S(2)}) collective-permute-start(bf16[6160,128]{1,0:T(8,128)(2,1)} %get-tuple-element.50), channel_id=1, source_target_pairs={{0,1},{1,0},{2,3},{3,2},{4,5},{5,4},{6,7},{7,6},{8,9},{9,8},{10,11... | collective-permute-start | bytes 4730888 | tf_op jit(solution)/shard_map/ppermute | solution.py:326
  14.9 12.5 %collective-permute-start.11 = (bf16[1536,128]{1,0:T(8,128)(2,1)S(1)}, bf16[1536,128]{1,0:T(8,128)(2,1)S(1)}, u32[]{:S(2)}, u32[]{:S(2)}) collective-permute-start(bf16[1536,128]{1,0:T(8,128)(2,1)S(1)} %get-tuple-element.62), channel_id=1, source_target_pairs={{0,2},{1,3},{2,0},{3,1},{4,6},{5,7},{6,4},{7,5},{8,10},{9,11},{10,... | collective-permute-start | bytes 1179656 | tf_op jit(solution)/shard_map/ppermute | solution.py:326
  17.5 17.9 %collective-permute-start.12 = (bf16[1536,128]{1,0:T(8,128)(2,1)S(1)}, bf16[1536,128]{1,0:T(8,128)(2,1)S(1)}, u32[]{:S(2)}, u32[]{:S(2)}) collective-permute-start(bf16[1536,128]{1,0:T(8,128)(2,1)S(1)} %get-tuple-element.63), channel_id=1, source_target_pairs={{0,3},{1,2},{2,1},{3,0},{4,7},{5,6},{6,5},{7,4},{8,11},{9,10},{10,... | collective-permute-start | bytes 1179656 | tf_op jit(solution)/shard_map/ppermute | solution.py:326
  17.5 26.7 %collective-permute-start.19 = (bf16[1536,128]{1,0:T(8,128)(2,1)S(1)}, bf16[1536,128]{1,0:T(8,128)(2,1)S(1)}, u32[]{:S(2)}, u32[]{:S(2)}) collective-permute-start(bf16[1536,128]{1,0:T(8,128)(2,1)S(1)} %get-tuple-element.72), channel_id=1, source_target_pairs={{0,2},{1,3},{2,0},{3,1},{4,6},{5,7},{6,4},{7,5},{8,10},{9,11},{10,... | collective-permute-start | bytes 1179656 | tf_op jit(solution)/shard_map/ppermute | solution.py:326
  19.3 32.9 %collective-permute-start.20 = (bf16[1536,128]{1,0:T(8,128)(2,1)S(1)}, bf16[1536,128]{1,0:T(8,128)(2,1)S(1)}, u32[]{:S(2)}, u32[]{:S(2)}) collective-permute-start(bf16[1536,128]{1,0:T(8,128)(2,1)S(1)} %get-tuple-element.73), channel_id=1, source_target_pairs={{0,3},{1,2},{2,1},{3,0},{4,7},{5,6},{6,5},{7,4},{8,11},{9,10},{10,... | collective-permute-start | bytes 1179656 | tf_op jit(solution)/shard_map/ppermute | solution.py:326
  27.4 29.0 %copy-start.15 = (bf16[1536,128]{1,0:T(8,128)(2,1)}, bf16[1536,128]{1,0:T(8,128)(2,1)S(1)}, u32[]{:S(2)}) copy-start(bf16[1536,128]{1,0:T(8,128)(2,1)S(1)} %collective-permute-done.11.refs_0_.refs_2_) | copy-start | bytes 1179652
  27.4 70.8 %collective-permute-start.2 = (bf16[1552,128]{1,0:T(8,128)(2,1)}, bf16[1552,128]{1,0:T(8,128)(2,1)S(1)}, u32[]{:S(2)}, u32[]{:S(2)}) collective-permute-start(bf16[1552,128]{1,0:T(8,128)(2,1)} %get-tuple-element.51), channel_id=1, source_target_pairs={{0,3},{1,2},{2,1},{3,0},{4,7},{5,6},{6,5},{7,4},{8,11},{9,10},{10,... | collective-permute-start | bytes 1191944 | tf_op jit(solution)/shard_map/ppermute | solution.py:326
  35.3 21.1 %copy-start.17 = (bf16[1536,128]{1,0:T(8,128)(2,1)}, bf16[1536,128]{1,0:T(8,128)(2,1)S(1)}, u32[]{:S(2)}) copy-start(bf16[1536,128]{1,0:T(8,128)(2,1)S(1)} %collective-permute-done.12.refs_1_.refs_3_) | copy-start | bytes 1179652
  35.3 47.2 %collective-permute-start.27 = (bf16[1536,128]{1,0:T(8,128)(2,1)}, bf16[1536,128]{1,0:T(8,128)(2,1)S(1)}, u32[]{:S(2)}, u32[]{:S(2)}) collective-permute-start(bf16[1536,128]{1,0:T(8,128)(2,1)} %get-tuple-element.82), channel_id=1, source_target_pairs={{0,2},{1,3},{2,0},{3,1},{4,6},{5,7},{6,4},{7,5},{8,10},{9,11},{10,... | collective-permute-start | bytes 1179656 | tf_op jit(solution)/shard_map/ppermute | solution.py:326
  44.3 25.2 %copy-start.7 = (bf16[1536,128]{1,0:T(8,128)(2,1)}, bf16[1536,128]{1,0:T(8,128)(2,1)S(1)}, u32[]{:S(2)}) copy-start(bf16[1536,128]{1,0:T(8,128)(2,1)S(1)} %collective-permute-done.19.refs_0_.refs_2_) | copy-start | bytes 1179652
  44.3 39.6 %collective-permute-start.28 = (bf16[1536,128]{1,0:T(8,128)(2,1)}, bf16[1536,128]{1,0:T(8,128)(2,1)S(1)}, u32[]{:S(2)}, u32[]{:S(2)}) collective-permute-start(bf16[1536,128]{1,0:T(8,128)(2,1)} %get-tuple-element.83), channel_id=1, source_target_pairs={{0,3},{1,2},{2,1},{3,0},{4,7},{5,6},{6,5},{7,4},{8,11},{9,10},{10,... | collective-permute-start | bytes 1179656 | tf_op jit(solution)/shard_map/ppermute | solution.py:326
  52.2 17.3 %copy-start.9 = (bf16[1536,128]{1,0:T(8,128)(2,1)}, bf16[1536,128]{1,0:T(8,128)(2,1)S(1)}, u32[]{:S(2)}) copy-start(bf16[1536,128]{1,0:T(8,128)(2,1)S(1)} %collective-permute-done.20.refs_1_.refs_3_) | copy-start | bytes 1179652
  52.2 52.1 %collective-permute-start.1 = (bf16[1552,128]{1,0:T(8,128)(2,1)S(1)}, bf16[1552,128]{1,0:T(8,128)(2,1)S(1)}, u32[]{:S(2)}, u32[]{:S(2)}) collective-permute-start(bf16[1552,128]{1,0:T(8,128)(2,1)S(1)} %get-tuple-element.48.refs_4_), channel_id=1, source_target_pairs={{0,2},{1,3},{2,0},{3,1},{4,6},{5,7},{6,4},{7,5},{8,10},{9,11},{10,... | collective-permute-start | bytes 1191944 | tf_op jit(solution)/shard_map/ppermute | solution.py:326
  69.5 56.4 %copy-start.27 = (bf16[1,3,2]{0,2,1:T(2,128)(2,1)S(1)}, bf16[1,3,2]{0,2,1:T(2,128)(2,1)}, u32[]{:S(2)}) copy-start(bf16[1,3,2]{0,2,1:T(2,128)(2,1)} %stack.20) | copy-start | bytes 40
  82.5 2.6 copy-start.11
  82.5 43.8 %collective-permute-start.3 = (bf16[3072,128]{1,0:T(8,128)(2,1)}, bf16[3072,128]{1,0:T(8,128)(2,1)S(1)}, u32[]{:S(2)}, u32[]{:S(2)}) collective-permute-start(bf16[3072,128]{1,0:T(8,128)(2,1)} %copy-done.23), channel_id=1, source_target_pairs={{2,6},{3,7},{4,0},{5,1},{6,10},{7,11},{8,4},{9,5},{10,14},{11,15},... | collective-permute-start | bytes 2359304 | tf_op jit(solution)/shard_map/ppermute | solution.py:338
  83.9 1.3 copy-start.13
  83.9 45.3 %collective-permute-start.4 = (bf16[3072,128]{1,0:T(8,128)(2,1)}, bf16[3072,128]{1,0:T(8,128)(2,1)}, u32[]{:S(2)}, u32[]{:S(2)}) collective-permute-start(bf16[3072,128]{1,0:T(8,128)(2,1)} %copy-done.19), channel_id=1, source_target_pairs={{2,7},{3,6},{4,1},{5,0},{6,11},{7,10},{8,5},{9,4},{10,15},{11,14},... | collective-permute-start | bytes 2359304 | tf_op jit(solution)/shard_map/ppermute | solution.py:338
  98.2 10.2 %copy-start.3 = (bf16[1552,128]{1,0:T(8,128)(2,1)}, bf16[1552,128]{1,0:T(8,128)(2,1)S(1)}, u32[]{:S(2)}) copy-start(bf16[1552,128]{1,0:T(8,128)(2,1)S(1)} %collective-permute-done.2.refs_1_.refs_3_) | copy-start | bytes 1191940
  98.2 63.4 %collective-permute-start.13 = (bf16[1536,128]{1,0:T(8,128)(2,1)}, bf16[1536,128]{1,0:T(8,128)(2,1)}, u32[]{:S(2)}, u32[]{:S(2)}) collective-permute-start(bf16[1536,128]{1,0:T(8,128)(2,1)} %relay.5), channel_id=1, source_target_pairs={{0,4},{1,5},{4,8},{5,9},{6,2},{7,3},{8,12},{9,13},{10,6},{11,7},{1... | collective-permute-start | bytes 1179656 | tf_op jit(solution)/shard_map/ppermute | solution.py:338
  104.3 4.1 %copy-start.5 = (bf16[1552,128]{1,0:T(8,128)(2,1)}, bf16[1552,128]{1,0:T(8,128)(2,1)S(1)}, u32[]{:S(2)}) copy-start(bf16[1552,128]{1,0:T(8,128)(2,1)S(1)} %collective-permute-done.1.refs_0_.refs_2_) | copy-start | bytes 1191940
  104.3 80.2 %collective-permute-start.21 = (bf16[1536,128]{1,0:T(8,128)(2,1)}, bf16[1536,128]{1,0:T(8,128)(2,1)}, u32[]{:S(2)}, u32[]{:S(2)}) collective-permute-start(bf16[1536,128]{1,0:T(8,128)(2,1)} %relay.6), channel_id=1, source_target_pairs={{0,4},{1,5},{4,8},{5,9},{6,2},{7,3},{8,12},{9,13},{10,6},{11,7},{1... | collective-permute-start | bytes 1179656 | tf_op jit(solution)/shard_map/ppermute | solution.py:338
  121.5 13.5 %collective-permute-start.5 = (bf16[1536,128]{1,0:T(8,128)(2,1)}, bf16[1536,128]{1,0:T(8,128)(2,1)S(1)}, u32[]{:S(2)}, u32[]{:S(2)}) collective-permute-start(bf16[1536,128]{1,0:T(8,128)(2,1)} %relay.4), channel_id=1, source_target_pairs={{0,4},{1,5},{4,8},{5,9},{6,2},{7,3},{8,12},{9,13},{10,6},{11,7},{1... | collective-permute-start | bytes 1179656 | tf_op jit(solution)/shard_map/ppermute | solution.py:338
  126.3 0.9 copy-start.20
  127.2 74.3 %collective-permute-start.29 = (bf16[1536,128]{1,0:T(8,128)(2,1)}, bf16[1536,128]{1,0:T(8,128)(2,1)S(1)}, u32[]{:S(2)}, u32[]{:S(2)}) collective-permute-start(bf16[1536,128]{1,0:T(8,128)(2,1)} %relay.7), channel_id=1, source_target_pairs={{0,4},{1,5},{4,8},{5,9},{6,2},{7,3},{8,12},{9,13},{10,6},{11,7},{1... | collective-permute-start | bytes 1179656 | tf_op jit(solution)/shard_map/ppermute | solution.py:338
  134.9 1.0 copy-start.4
  135.9 1.0 copy-start.6
  136.9 1.1 copy-start.21
  138.1 23.6 %copy-start.16 = (bf16[1536,128]{1,0:T(8,128)(2,1)S(1)}, bf16[1536,128]{1,0:T(8,128)(2,1)}, u32[]{:S(2)}) copy-start(bf16[1536,128]{1,0:T(8,128)(2,1)} %copy-done.15) | copy-start | bytes 1179652
  138.1 23.6 %copy-start.18 = (bf16[1536,128]{1,0:T(8,128)(2,1)S(1)}, bf16[1536,128]{1,0:T(8,128)(2,1)}, u32[]{:S(2)}) copy-start(bf16[1536,128]{1,0:T(8,128)(2,1)} %copy-done.17) | copy-start | bytes 1179652
  138.1 23.6 %copy-start.22 = (bf16[3072,128]{1,0:T(8,128)(2,1)S(1)}, bf16[3072,128]{1,0:T(8,128)(2,1)}, u32[]{:S(2)}) copy-start(bf16[3072,128]{1,0:T(8,128)(2,1)} %copy-done.20) | copy-start | bytes 2359300
  153.5 74.6 %collective-permute-start.6 = (bf16[2,2,384,128]{3,2,1,0:T(8,128)(2,1)}, bf16[2,2,384,128]{3,2,1,0:T(8,128)(2,1)S(1)}, u32[]{:S(2)}, u32[]{:S(2)}) collective-permute-start(bf16[2,2,384,128]{3,2,1,0:T(8,128)(2,1)} %get-tuple-element.56), channel_id=1, source_target_pairs={{0,4},{1,5},{4,8},{5,9},{6,2},{7,3},{8,12},{9,13},{10,6},{11,7},{1... | collective-permute-start | bytes 1179656 | tf_op jit(solution)/shard_map/ppermute | solution.py:338
  160.2 25.8 %copy-start.8 = (bf16[1536,128]{1,0:T(8,128)(2,1)S(1)}, bf16[1536,128]{1,0:T(8,128)(2,1)}, u32[]{:S(2)}) copy-start(bf16[1536,128]{1,0:T(8,128)(2,1)} %copy-done.7) | copy-start | bytes 1179652
  160.2 25.8 %copy-start.10 = (bf16[1536,128]{1,0:T(8,128)(2,1)S(1)}, bf16[1536,128]{1,0:T(8,128)(2,1)}, u32[]{:S(2)}) copy-start(bf16[1536,128]{1,0:T(8,128)(2,1)} %copy-done.9) | copy-start | bytes 1179652
  160.2 69.2 %collective-permute-start.7 = (bf16[2,2,384,128]{3,2,1,0:T(8,128)(2,1)}, bf16[2,2,384,128]{3,2,1,0:T(8,128)(2,1)S(1)}, u32[]{:S(2)}, u32[]{:S(2)}) collective-permute-start(bf16[2,2,384,128]{3,2,1,0:T(8,128)(2,1)} %get-tuple-element.57), channel_id=1, source_target_pairs={{2,6},{3,7},{4,0},{5,1},{6,10},{7,11},{8,4},{9,5},{10,14},{11,15},... | collective-permute-start | bytes 1179656 | tf_op jit(solution)/shard_map/ppermute | solution.py:338
  177.4 61.4 %collective-permute-start.14 = (bf16[2,2,384,128]{3,2,1,0:T(8,128)(2,1)}, bf16[2,2,384,128]{3,2,1,0:T(8,128)(2,1)S(1)}, u32[]{:S(2)}, u32[]{:S(2)}) collective-permute-start(bf16[2,2,384,128]{3,2,1,0:T(8,128)(2,1)} %get-tuple-element.66), channel_id=1, source_target_pairs={{0,4},{1,5},{4,8},{5,9},{6,2},{7,3},{8,12},{9,13},{10,6},{11,7},{1... | collective-permute-start | bytes 1179656 | tf_op jit(solution)/shard_map/ppermute | solution.py:338
  184.6 27.1 %copy-start.12 = (bf16[1536,128]{1,0:T(8,128)(2,1)S(1)}, bf16[1536,128]{1,0:T(8,128)(2,1)}, u32[]{:S(2)}) copy-start(bf16[1536,128]{1,0:T(8,128)(2,1)} %copy-done.11) | copy-start | bytes 1179652
  184.6 27.1 %copy-start.14 = (bf16[1536,128]{1,0:T(8,128)(2,1)S(1)}, bf16[1536,128]{1,0:T(8,128)(2,1)}, u32[]{:S(2)}) copy-start(bf16[1536,128]{1,0:T(8,128)(2,1)} %copy-done.13) | copy-start | bytes 1179652
  184.6 55.5 %collective-permute-start.15 = (bf16[2,2,384,128]{3,2,1,0:T(8,128)(2,1)S(1)}, bf16[2,2,384,128]{3,2,1,0:T(8,128)(2,1)S(1)}, u32[]{:S(2)}, u32[]{:S(2)}) collective-permute-start(bf16[2,2,384,128]{3,2,1,0:T(8,128)(2,1)S(1)} %get-tuple-element.67), channel_id=1, source_target_pairs={{2,6},{3,7},{4,0},{5,1},{6,10},{7,11},{8,4},{9,5},{10,14},{11,15},... | collective-permute-start | bytes 1179656 | tf_op jit(solution)/shard_map/ppermute | solution.py:338
  201.5 0.8 copy-start.24
  202.3 37.9 %collective-permute-start.22 = (bf16[2,2,384,128]{3,2,1,0:T(8,128)(2,1)}, bf16[2,2,384,128]{3,2,1,0:T(8,128)(2,1)S(1)}, u32[]{:S(2)}, u32[]{:S(2)}) collective-permute-start(bf16[2,2,384,128]{3,2,1,0:T(8,128)(2,1)} %get-tuple-element.76), channel_id=1, source_target_pairs={{0,4},{1,5},{4,8},{5,9},{6,2},{7,3},{8,12},{9,13},{10,6},{11,7},{1... | collective-permute-start | bytes 1179656 | tf_op jit(solution)/shard_map/ppermute | solution.py:338
  211.7 1.0 copy-start.25
  228.1 18.2 %collective-permute-start.23 = (bf16[2,2,384,128]{3,2,1,0:T(8,128)(2,1)S(1)}, bf16[2,2,384,128]{3,2,1,0:T(8,128)(2,1)S(1)}, u32[]{:S(2)}, u32[]{:S(2)}) collective-permute-start(bf16[2,2,384,128]{3,2,1,0:T(8,128)(2,1)S(1)} %get-tuple-element.77), channel_id=1, source_target_pairs={{2,6},{3,7},{4,0},{5,1},{6,10},{7,11},{8,4},{9,5},{10,14},{11,15},... | collective-permute-start | bytes 1179656 | tf_op jit(solution)/shard_map/ppermute | solution.py:338
  229.4 17.2 %collective-permute-start.30 = (bf16[2,2,384,128]{3,2,1,0:T(8,128)(2,1)}, bf16[2,2,384,128]{3,2,1,0:T(8,128)(2,1)S(1)}, u32[]{:S(2)}, u32[]{:S(2)}) collective-permute-start(bf16[2,2,384,128]{3,2,1,0:T(8,128)(2,1)} %get-tuple-element.86), channel_id=1, source_target_pairs={{0,4},{1,5},{4,8},{5,9},{6,2},{7,3},{8,12},{9,13},{10,6},{11,7},{1... | collective-permute-start | bytes 1179656 | tf_op jit(solution)/shard_map/ppermute | solution.py:338
  238.8 12.0 %collective-permute-start.31 = (bf16[2,2,384,128]{3,2,1,0:T(8,128)(2,1)S(1)}, bf16[2,2,384,128]{3,2,1,0:T(8,128)(2,1)S(1)}, u32[]{:S(2)}, u32[]{:S(2)}) collective-permute-start(bf16[2,2,384,128]{3,2,1,0:T(8,128)(2,1)S(1)} %get-tuple-element.87), channel_id=1, source_target_pairs={{2,6},{3,7},{4,0},{5,1},{6,10},{7,11},{8,4},{9,5},{10,14},{11,15},... | collective-permute-start | bytes 1179656 | tf_op jit(solution)/shard_map/ppermute | solution.py:338
  240.1 10.7 %collective-permute-start.8 = (bf16[4,384,128]{2,1,0:T(8,128)(2,1)S(1)}, bf16[4,384,128]{2,1,0:T(8,128)(2,1)S(1)}, u32[]{:S(2)}, u32[]{:S(2)}) collective-permute-start(bf16[4,384,128]{2,1,0:T(8,128)(2,1)S(1)} %get-tuple-element.59), channel_id=1, source_target_pairs={{0,1},{1,0},{2,3},{3,2},{4,5},{5,4},{6,7},{7,6},{8,9},{9,8},{10,11... | collective-permute-start | bytes 1179656 | tf_op jit(solution)/shard_map/ppermute | solution.py:326
  240.2 15.2 %collective-permute-start.9 = (bf16[4,384,128]{2,1,0:T(8,128)(2,1)S(1)}, bf16[4,384,128]{2,1,0:T(8,128)(2,1)S(1)}, u32[]{:S(2)}, u32[]{:S(2)}) collective-permute-start(bf16[4,384,128]{2,1,0:T(8,128)(2,1)S(1)} %get-tuple-element.60), channel_id=1, source_target_pairs={{0,2},{1,3},{2,0},{3,1},{4,6},{5,7},{6,4},{7,5},{8,10},{9,11},{10,... | collective-permute-start | bytes 1179656 | tf_op jit(solution)/shard_map/ppermute | solution.py:326
  246.3 16.9 %collective-permute-start.10 = (bf16[4,384,128]{2,1,0:T(8,128)(2,1)S(1)}, bf16[4,384,128]{2,1,0:T(8,128)(2,1)S(1)}, u32[]{:S(2)}, u32[]{:S(2)}) collective-permute-start(bf16[4,384,128]{2,1,0:T(8,128)(2,1)S(1)} %get-tuple-element.61), channel_id=1, source_target_pairs={{0,3},{1,2},{2,1},{3,0},{4,7},{5,6},{6,5},{7,4},{8,11},{9,10},{10,... | collective-permute-start | bytes 1179656 | tf_op jit(solution)/shard_map/ppermute | solution.py:326
  246.6 18.2 %collective-permute-start.16 = (bf16[4,384,128]{2,1,0:T(8,128)(2,1)}, bf16[4,384,128]{2,1,0:T(8,128)(2,1)S(1)}, u32[]{:S(2)}, u32[]{:S(2)}) collective-permute-start(bf16[4,384,128]{2,1,0:T(8,128)(2,1)} %get-tuple-element.69), channel_id=1, source_target_pairs={{0,1},{1,0},{2,3},{3,2},{4,5},{5,4},{6,7},{7,6},{8,9},{9,8},{10,11... | collective-permute-start | bytes 1179656 | tf_op jit(solution)/shard_map/ppermute | solution.py:326
  250.8 21.4 %collective-permute-start.17 = (bf16[4,384,128]{2,1,0:T(8,128)(2,1)S(1)}, bf16[4,384,128]{2,1,0:T(8,128)(2,1)S(1)}, u32[]{:S(2)}, u32[]{:S(2)}) collective-permute-start(bf16[4,384,128]{2,1,0:T(8,128)(2,1)S(1)} %get-tuple-element.70), channel_id=1, source_target_pairs={{0,2},{1,3},{2,0},{3,1},{4,6},{5,7},{6,4},{7,5},{8,10},{9,11},{10,... | collective-permute-start | bytes 1179656 | tf_op jit(solution)/shard_map/ppermute | solution.py:326
  250.8 29.3 %collective-permute-start.18 = (bf16[4,384,128]{2,1,0:T(8,128)(2,1)S(1)}, bf16[4,384,128]{2,1,0:T(8,128)(2,1)S(1)}, u32[]{:S(2)}, u32[]{:S(2)}) collective-permute-start(bf16[4,384,128]{2,1,0:T(8,128)(2,1)S(1)} %get-tuple-element.71), channel_id=1, source_target_pairs={{0,3},{1,2},{2,1},{3,0},{4,7},{5,6},{6,5},{7,4},{8,11},{9,10},{10,... | collective-permute-start | bytes 1179656 | tf_op jit(solution)/shard_map/ppermute | solution.py:326
  255.4 26.3 %collective-permute-start.24 = (bf16[4,384,128]{2,1,0:T(8,128)(2,1)S(1)}, bf16[4,384,128]{2,1,0:T(8,128)(2,1)S(1)}, u32[]{:S(2)}, u32[]{:S(2)}) collective-permute-start(bf16[4,384,128]{2,1,0:T(8,128)(2,1)S(1)} %get-tuple-element.79), channel_id=1, source_target_pairs={{0,1},{1,0},{2,3},{3,2},{4,5},{5,4},{6,7},{7,6},{8,9},{9,8},{10,11... | collective-permute-start | bytes 1179656 | tf_op jit(solution)/shard_map/ppermute | solution.py:326
  263.3 25.8 %collective-permute-start.25 = (bf16[4,384,128]{2,1,0:T(8,128)(2,1)S(1)}, bf16[4,384,128]{2,1,0:T(8,128)(2,1)S(1)}, u32[]{:S(2)}, u32[]{:S(2)}) collective-permute-start(bf16[4,384,128]{2,1,0:T(8,128)(2,1)S(1)} %get-tuple-element.80), channel_id=1, source_target_pairs={{0,2},{1,3},{2,0},{3,1},{4,6},{5,7},{6,4},{7,5},{8,10},{9,11},{10,... | collective-permute-start | bytes 1179656 | tf_op jit(solution)/shard_map/ppermute | solution.py:326
  264.8 32.1 %collective-permute-start.26 = (bf16[4,384,128]{2,1,0:T(8,128)(2,1)S(1)}, bf16[4,384,128]{2,1,0:T(8,128)(2,1)S(1)}, u32[]{:S(2)}, u32[]{:S(2)}) collective-permute-start(bf16[4,384,128]{2,1,0:T(8,128)(2,1)S(1)} %get-tuple-element.81), channel_id=1, source_target_pairs={{0,3},{1,2},{2,1},{3,0},{4,7},{5,6},{6,5},{7,4},{8,11},{9,10},{10,... | collective-permute-start | bytes 1179656 | tf_op jit(solution)/shard_map/ppermute | solution.py:326
  272.2 24.8 %collective-permute-start.32 = (bf16[4,384,128]{2,1,0:T(8,128)(2,1)S(1)}, bf16[4,384,128]{2,1,0:T(8,128)(2,1)S(1)}, u32[]{:S(2)}, u32[]{:S(2)}) collective-permute-start(bf16[4,384,128]{2,1,0:T(8,128)(2,1)S(1)} %get-tuple-element.89), channel_id=1, source_target_pairs={{0,1},{1,0},{2,3},{3,2},{4,5},{5,4},{6,7},{7,6},{8,9},{9,8},{10,11... | collective-permute-start | bytes 1179656 | tf_op jit(solution)/shard_map/ppermute | solution.py:326
  280.1 25.8 %collective-permute-start.33 = (bf16[4,384,128]{2,1,0:T(8,128)(2,1)S(1)}, bf16[4,384,128]{2,1,0:T(8,128)(2,1)S(1)}, u32[]{:S(2)}, u32[]{:S(2)}) collective-permute-start(bf16[4,384,128]{2,1,0:T(8,128)(2,1)S(1)} %get-tuple-element.90), channel_id=1, source_target_pairs={{0,2},{1,3},{2,0},{3,1},{4,6},{5,7},{6,4},{7,5},{8,10},{9,11},{10,... | collective-permute-start | bytes 1179656 | tf_op jit(solution)/shard_map/ppermute | solution.py:326
  281.7 32.1 %collective-permute-start.34 = (bf16[4,384,128]{2,1,0:T(8,128)(2,1)S(1)}, bf16[4,384,128]{2,1,0:T(8,128)(2,1)S(1)}, u32[]{:S(2)}, u32[]{:S(2)}) collective-permute-start(bf16[4,384,128]{2,1,0:T(8,128)(2,1)S(1)} %get-tuple-element.91), channel_id=1, source_target_pairs={{0,3},{1,2},{2,1},{3,0},{4,7},{5,6},{6,5},{7,4},{8,11},{9,10},{10,... | collective-permute-start | bytes 1179656 | tf_op jit(solution)/shard_map/ppermute | solution.py:326
  313.8 0.8 copy-start.26

commit v3 on v2

v3 whole, which is shorter than its diff:
```python
import functools
import math

import jax
import jax.numpy as jnp
from jax import lax
from jax.experimental import pallas as pl
from jax.experimental.pallas import tpu as pltpu
from jax.sharding import PartitionSpec as P

HD = 128
FLAG_ROWS = 16
BLOCKS = 4
RING = ("ctx", "sub")
F32 = jnp.float32
BF16 = jnp.bfloat16
SCALE = 1.0 / math.sqrt(HD)
FACTOR = SCALE * math.log2(math.e)
ANY = pl.BlockSpec(memory_space=pl.ANY)
VMEM = pl.BlockSpec(memory_space=pltpu.VMEM)
SMEM = pl.BlockSpec(memory_space=pltpu.SMEM)
PARAMS = pltpu.CompilerParams(vmem_limit_bytes=48 * 1024 * 1024)


def struct(shape, dtype):
    return jax.ShapeDtypeStruct(shape, dtype)


def moved(nbytes):
    return pl.CostEstimate(flops=0, bytes_accessed=nbytes, transcendentals=0)


def pack_kernel(jobs, step, cols_ref, flags_ref, *refs):
    sources, outs = refs[:4], refs[4 : 4 + len(jobs)]
    lane = lax.broadcasted_iota(jnp.int32, (FLAG_ROWS, HD), 1)
    flags = jnp.zeros((FLAG_ROWS, HD), F32)
    for w in range(flags_ref.shape[0]):
        flags = jnp.where(lane == w, flags_ref[w].astype(F32), flags)
    flags = flags.astype(BF16)
    for out, (d, heads, kinds, flagged) in zip(outs, jobs):
        for m, c in enumerate(heads):
            lanes = pl.ds(pl.multiple_of(cols_ref[c, d], HD), HD)
            for at, n in enumerate(kinds):
                out[m, 0, pl.ds(at * step, step)] = sources[n][0, :, lanes]
            if flagged:
                out[m, 0, pl.ds(len(kinds) * step, FLAG_ROWS)] = flags


def pack(jobs, cols, flags, sources):
    _, tile, lane_width = sources[0].shape
    step = tile // BLOCKS
    shapes = [
        (len(heads), BLOCKS, len(kinds) * step + (FLAG_ROWS if flagged else 0), HD)
        for _, heads, kinds, flagged in jobs
    ]
    return pl.pallas_call(
        functools.partial(pack_kernel, jobs, step),
        grid=(BLOCKS,),
        out_shape=[struct(shape, BF16) for shape in shapes],
        in_specs=[SMEM, SMEM] + [pl.BlockSpec((1, step, lane_width), lambda i: (0, i, 0))] * 4,
        out_specs=[
            pl.BlockSpec((shape[0], 1, shape[2], HD), lambda i: (0, i, 0, 0)) for shape in shapes
        ],
        cost_estimate=moved(sum(4 * HD * math.prod(shape[:3]) for shape in shapes)),
        compiler_params=PARAMS,
        name="pack",
    )(cols, flags, *sources)


def relay_kernel(step, rows, *refs):
    pieces, out = refs[:rows], refs[-1]
    for e, piece in enumerate(pieces):
        out[0, :, pl.ds(2 * step * e, 2 * step)] = piece[0, :, pl.ds(0, 2 * step)]


def relay(step, pieces, passed, spare):
    rows = len(pieces)

    def kernel(*refs):
        relay_kernel(step, rows, *refs[:rows], refs[rows + len(passed) + len(spare)])

    outs = pl.pallas_call(
        kernel,
        out_shape=[struct((1, BLOCKS, rows * 2 * step, HD), BF16)]
        + [struct(value.shape, value.dtype) for value in passed],
        in_specs=[VMEM] * rows + [ANY] * (len(passed) + len(spare)),
        out_specs=[VMEM] + [ANY] * len(passed),
        input_output_aliases={rows + n: 1 + n for n in range(len(passed))},
        cost_estimate=moved(rows * 8 * BLOCKS * step * HD),
        compiler_params=PARAMS,
        name="relay",
    )(*pieces, *passed, *spare)
    return outs[0], outs[1:]


def hold(passed, spare):
    return pl.pallas_call(
        lambda *refs: None,
        out_shape=[struct(value.shape, value.dtype) for value in passed],
        in_specs=[ANY] * (len(passed) + len(spare)),
        out_specs=[ANY] * len(passed),
        input_output_aliases={n: n for n in range(len(passed))},
        cost_estimate=moved(0),
        name="hold",
    )(*passed, *spare)


def nt(a, b):
    return lax.dot_general(a, b, (((1,), (1,)), ((), ())), preferred_element_type=F32)


def nn(a, b):
    return jnp.dot(a, b, preferred_element_type=F32)


def attend_kernel(plan, rows, tile, table_ref, *refs):
    loads, slabs_here, n_in, spare = plan
    inputs = refs[:n_in]
    rest = refs[n_in + spare :]
    done, local, grads_one, grads_two = rest[:4]
    qbuf, gbuf, kbuf, vbuf, kt, vt, dk, dv, s_buf, p_buf, ds_buf, ot = rest[4:]
    targets = {"k": kbuf, "v": vbuf, "q": qbuf, "g": gbuf}
    step = tile // BLOCKS
    for n, at, kind, slab, e in loads:
        for g in range(BLOCKS):
            targets[kind][slab, pl.ds(e * tile + g * step, step)] = inputs[n][
                0, g, pl.ds(at * step, step)
            ]
    width = rows * tile
    team = slabs_here * rows
    places = kbuf.shape[0]

    def prepare(n, carry):
        kt[n] = kbuf[n].T
        vt[n] = vbuf[n].T
        dk[n] = jnp.zeros((width, HD), F32)
        dv[n] = jnp.zeros((width, HD), F32)
        return carry

    lax.fori_loop(0, places, prepare, 0)
    lane = lax.broadcasted_iota(jnp.int32, (1, width), 1)

    def slab_pass(a, carry):
        query = qbuf[a]
        grad = gbuf[a]

        def seen(b):
            count = 0
            for f in range(rows):
                for e in range(rows):
                    count = count + table_ref[a * rows + f, b * rows + e]
            return count > 0

        def scores(b, top):
            def live(top):
                place = table_ref[a * rows, 3 * rows + b]
                for e in range(rows):
                    keep = jnp.zeros((1, width), jnp.int32)
                    for f in range(rows):
                        inside = (lane >= f * tile) & (lane < (f + 1) * tile)
                        keep = jnp.where(inside, table_ref[a * rows + f, b * rows + e], keep)
                    mask = jnp.where(keep > 0, 0.0, -jnp.inf)
                    s = nt(kbuf[place, pl.ds(e * tile, tile)], query) + mask
                    s_buf[b, pl.ds(e * tile, tile)] = s
                    top = jnp.maximum(top, jnp.max(s, axis=0, keepdims=True))
                return top

            return lax.cond(seen(b), live, lambda top: top, top)

        top = lax.fori_loop(0, 3, scores, jnp.full((1, width), -jnp.inf, F32))
        ot[...] = jnp.zeros((HD, width), F32)

        def expo(b, total):
            def live(total):
                place = table_ref[a * rows, 3 * rows + b]
                for e in range(rows):
                    at = pl.ds(e * tile, tile)
                    p = jnp.exp2((s_buf[b, at] - top) * FACTOR)
                    total = total + jnp.sum(p, axis=0, keepdims=True)
                    p_buf[b, at] = p.astype(BF16)
                ot[...] += nn(vt[place], p_buf[b])
                return total

            return lax.cond(seen(b), live, lambda total: total, total)

        total = lax.fori_loop(0, 3, expo, jnp.zeros((1, width), F32))
        inv = 1.0 / total
        low_t = (ot[...] * inv).astype(BF16)
        grad_t = grad.T.astype(F32)
        offset = jnp.sum(grad_t * low_t.astype(F32), axis=0, keepdims=True)
        grad_over = (grad_t * inv).astype(BF16).T
        query_over = (query.T.astype(F32) * (inv * SCALE)).astype(BF16).T
        out = low_t.T
        ot[...] = jnp.zeros((HD, width), F32)

        def backward(b, carry):
            @pl.when(seen(b))
            def _():
                place = table_ref[a * rows, 3 * rows + b]
                for e in range(rows):
                    at = pl.ds(e * tile, tile)
                    p = p_buf[b, at]
                    dp = nt(vbuf[place, at], grad)
                    ds = (p.astype(F32) * (dp - offset)).astype(BF16)
                    ds_buf[at] = ds
                    dv[place, at] += nn(p, grad_over)
                    dk[place, at] += nn(ds, query_over)
                ot[...] += nn(kt[place], ds_buf[...])

            return carry

        lax.fori_loop(0, 3, backward, 0)
        dq = (ot[...] * (inv * SCALE)).astype(BF16).T
        for f in range(rows):
            done[a * rows + f, 0] = out[f * tile : (f + 1) * tile]
            done[a * rows + f, 1] = dq[f * tile : (f + 1) * tile]
        return carry

    lax.fori_loop(0, slabs_here, slab_pass, 0)

    for d in range(team):
        at = pl.ds(d % rows * tile, tile)
        local[d, 0] = dk[d // rows, at]
        local[d, 1] = dv[d // rows, at]
    for n, grads in enumerate((grads_one, grads_two)):
        for e in range(rows):
            at = pl.ds(e * tile, tile)
            grads[e, 0] = dk[slabs_here + n, at].astype(BF16)
            grads[e, 1] = dv[slabs_here + n, at].astype(BF16)


def attend(rows, tile, slabs_here, table, loads, inputs, spare):
    places = slabs_here + 2
    team = slabs_here * rows
    width = rows * tile
    scores = 3 * slabs_here * width * width

    def head_spec(value, c):
        return pl.BlockSpec((1,) + value.shape[1:], lambda i: (c, 0, 0, 0))

    def whole(shape):
        return pl.BlockSpec(shape, lambda i: (0,) * len(shape))

    shapes = [
        struct((team, 2, tile, HD), BF16),
        struct((team, 2, tile, HD), F32),
        struct((rows, 2, tile, HD), BF16),
        struct((rows, 2, tile, HD), BF16),
    ]
    plan = (loads, slabs_here, len(inputs), len(spare))
    return pl.pallas_call(
        functools.partial(attend_kernel, plan, rows, tile),
        grid=(1,),
        out_shape=shapes,
        in_specs=[SMEM] + [head_spec(value, c) for value, c in inputs] + [ANY] * len(spare),
        out_specs=[whole(shape.shape) for shape in shapes],
        scratch_shapes=[
            pltpu.VMEM((slabs_here, width, HD), BF16),
            pltpu.VMEM((slabs_here, width, HD), BF16),
            pltpu.VMEM((places, width, HD), BF16),
            pltpu.VMEM((places, width, HD), BF16),
            pltpu.VMEM((places, HD, width), BF16),
            pltpu.VMEM((places, HD, width), BF16),
            pltpu.VMEM((places, width, HD), F32),
            pltpu.VMEM((places, width, HD), F32),
            pltpu.VMEM((3, width, width), F32),
            pltpu.VMEM((3, width, width), BF16),
            pltpu.VMEM((width, width), BF16),
            pltpu.VMEM((HD, width), F32),
        ],
        cost_estimate=pl.CostEstimate(
            flops=12 * scores * HD, bytes_accessed=8 * 1024 * 1024, transcendentals=scores
        ),
        compiler_params=PARAMS,
        name="attend",
    )(table, *[value for value, _ in inputs], *spare)


def finish_kernel(team, rows, extras, done, local, *refs):
    grads, outs = refs[: len(extras)], refs[-team:]
    for d in range(team):
        for n in range(2):
            outs[d][n] = done[d, n]
            total = local[d, n]
            for grad, slab in zip(grads, extras):
                if d // rows == slab:
                    total = total + grad[d % rows, n].astype(F32)
            outs[d][2 + n] = total.astype(BF16)


def finish(team, rows, extras, done, local, grads, spare):
    tile = done.shape[2]
    return pl.pallas_call(
        functools.partial(finish_kernel, team, rows, extras),
        out_shape=[struct((4, tile, HD), BF16)] * team,
        in_specs=[VMEM] * (2 + len(grads)) + [ANY] * len(spare),
        out_specs=[VMEM] * team,
        cost_estimate=moved(team * 24 * tile * HD),
        compiler_params=PARAMS,
        name="finish",
    )(done, local, *grads, *spare)


def unpack_kernel(team, per, cols_ref, *refs):
    pieces, outs = refs[: team * per], refs[team * per :]
    for c in range(per):
        for d in range(team):
            lanes = pl.ds(pl.multiple_of(cols_ref[c, d], HD), HD)
            for n in range(4):
                outs[n][0, :, lanes] = pieces[c * team + d][n]


def unpack(team, per, cols, pieces, shape):
    tile = shape[1]
    step = tile // 4 if tile % 64 == 0 else tile
    return pl.pallas_call(
        functools.partial(unpack_kernel, team, per),
        grid=(tile // step,),
        out_shape=[struct(shape, BF16)] * 4,
        in_specs=[SMEM] + [pl.BlockSpec((4, step, HD), lambda i: (0, i, 0))] * len(pieces),
        out_specs=[pl.BlockSpec((1, step, shape[2]), lambda i: (0, i, 0))] * 4,
        cost_estimate=moved(len(pieces) * 16 * tile * HD),
        compiler_params=PARAMS,
        name="unpack",
    )(cols, *pieces)


def body(queries, keys, values, grad_out, window_tiles, window_count):
    rows_here, tile, lane_width = queries.shape
    wmax = window_tiles.shape[1]
    heads = lane_width // HD
    rows = lax.axis_size("sub")
    slabs = lax.axis_size("ctx")
    span = 2 if heads % (2 * rows) == 0 and slabs % 2 == 0 else 1
    team = span * rows
    per = heads // team
    size = slabs * rows
    slab = lax.axis_index("ctx")
    row = lax.axis_index("sub")
    odd = slab % span
    me = odd * rows + row

    def swap(value, d):
        if d == 0:
            return value
        return lax.ppermute(value, RING, [(i, i - i % team + (i % team ^ d)) for i in range(size)])

    def shift(value, way, flip=0):
        pairs = []
        for i in range(size):
            place = i % team // rows
            forward = (place == span - 1) if way == 0 else (place == 0)
            if span == 1:
                forward = way == 0
            j = i + team if forward else i - team
            if 0 <= j < size:
                pairs.append((i, j ^ flip))
        return lax.ppermute(value, RING, pairs)

    places = (window_tiles[0] // rows - slab + 1) * rows + window_tiles[0] % rows
    listed = jnp.arange(wmax) < window_count[0]
    flags = jnp.any(
        (places[None, :] == jnp.arange(3 * rows)[:, None]) & listed[None, :], axis=1
    ).astype(jnp.int32)

    partners = jnp.arange(team, dtype=jnp.int32) ^ me
    heads_of = (partners[None, :] * per + jnp.arange(per, dtype=jnp.int32)[:, None]) * HD
    sources = (keys, values, queries, grad_out)
    kinds = (0, 1, 2, 3)
    every = tuple(range(per))
    far = tuple(range(rows, team))
    step = tile // BLOCKS

    jobs = [(d, (c,), kinds, c == 0) for c in every for d in far]
    jobs += [
        (1, every, kinds, True),
        (0, every, (0, 1), False),
        (1, every, (0, 1), False),
        (0, every, kinds, True),
    ]
    packed = pack(jobs, heads_of, flags, sources)
    sent = {(c, d): packed[c * len(far) + n] for c in every for n, d in enumerate(far)}
    beside, own_kv, beside_kv, own = packed[-4:]

    mates = [own, swap(beside, 1)]
    arrived = {(0, d): swap(sent[0, d], d) for d in far}
    held = []
    if span == 2 and per > 1:
        held = hold([sent[1, d] for d in far], [mates[1]])
        arrived.update({(1, d): swap(value, d) for d, value in zip(far, held)})
    near_one = [shift(own_kv, 0), shift(beside_kv, 0, flip=1)]
    if span == 1:
        near_two = [shift(own_kv, 1), shift(beside_kv, 1, flip=1)]

    lists = mates + [arrived[0, d] for d in far]
    table = jnp.stack([value[0, 0, -FLAG_ROWS, : 3 * rows] for value in lists]).astype(jnp.int32)
    table = table.reshape(team, 3, rows)
    table = jnp.where(row == 0, table, table[:, :, ::-1])
    if span == 2:
        turned = table[:, ::-1]
        table = jnp.concatenate(
            [
                jnp.where(odd == 0, table[:rows], turned[:rows]),
                jnp.where(odd == 0, turned[rows:], table[rows:]),
            ]
        )
    if span == 1:
        windows = ((1, 0, 2),)
        extras = (0, 0)
    else:
        windows = ((3, 0, 1), (2, 1, 0))
        extras = (0, 1)
    spots = jnp.repeat(jnp.asarray(windows, jnp.int32), rows, axis=0)
    table = jnp.concatenate([table.reshape(team, 3 * rows), spots], axis=1)

    beyond = {}

    def pass_on(c, spare):
        if span == 1 or c >= per:
            return
        waiting = [(c + 2, d) for d in far if c + 2 < per]
        value, passed = relay(
            step, [arrived[c, d] for d in far], [sent[key] for key in waiting], spare
        )
        beyond[c] = shift(value, 1)
        for key, payload in zip(waiting, passed):
            arrived[key] = swap(payload, key[1])
        ready[c] = value

    ready = {}
    pass_on(0, held[:1])
    pass_on(1, list(ready.values()))
    worked = {}
    homes = {}
    for c in every:
        inputs = []
        loads = []

        def add(value, at, held, wanted, slab_at, e):
            for n, kind in enumerate(wanted):
                loads.append((len(inputs), at + n, kind, slab_at, e))
            inputs.append((value, held))

        for e in range(rows):
            add(mates[e], 0, c, "kvqg", 0, e)
        for d in far:
            add(arrived[c, d], 0, 0, "kvqg", 1, d - rows)
        for e in range(rows):
            add(near_one[e], 0, c, "kv", span, e)
        if span == 1:
            for e in range(rows):
                add(near_two[e], 0, c, "kv", span + 1, e)
        else:
            for n, (kind, e) in enumerate((kind, e) for e in range(rows) for kind in "kv"):
                loads.append((len(inputs), n, kind, span + 1, e))
            inputs.append((beyond[c], 0))
        spare = []
        if c + 1 in ready:
            spare.append(ready[c + 1])
        if c >= 2:
            homes[c - 2] = finish(
                team, rows, extras, *worked[c - 2][:2], worked[c - 2][2], [worked[c - 1][0]]
            )
            spare.append(homes[c - 2][-1])
        done, local, grads_one, grads_two = attend(
            rows, tile, span, table, tuple(loads), inputs, spare
        )
        worked[c] = (done, local, (shift(grads_one, 1), shift(grads_two, 0)))
        pass_on(c + 2, [done])
    for c in every[-2:]:
        homes[c] = finish(team, rows, extras, *worked[c], [])
    pieces = [swap(homes[c][d], d) for c in every for d in range(team)]
    attended, grad_queries, grad_keys, grad_values = unpack(
        team, per, heads_of, pieces, queries.shape
    )
    return (attended, grad_queries, grad_keys, grad_values)


def solution(mesh):
    spec = P(("grp", "ctx", "sub"), None, "head")
    return jax.shard_map(
        body,
        mesh=mesh,
        in_specs=(spec, spec, spec, spec, P(("grp", "ctx", "sub"), None), P(("grp", "ctx", "sub"))),
        out_specs=(spec, spec, spec, spec),
        check_vma=False,
    )
```

time: 325 us -> 226 us (0.70)
  Pallas kernels: 129 us -> 77.4 us
  waiting for transfers between devices: 98.6 us -> 78.8 us
  starting transfers between devices: 74.8 us -> 55.1 us
  local copies, waits for them, and re-layouts: 14.6 us -> 10.3 us
    pallas_call x10, Pallas kernels: 122 us -> 71.4 us  [the longest x4 65 us: attend(): pl.pallas_call(functools.partial(attend_kernel, plan, rows, tile), grid=(...]
    ppermute x21, waiting for transfers between devices: 88.8 us -> 66.1 us  [swap(): lax.ppermute(value, RING, [(i, i - i % team + (i % team ^ d)) for i in ra...]
    ppermute x14, starting transfers between devices: 55.9 us -> 39.4 us  [shift(): return lax.ppermute(value, RING, pairs)]
    unnamed x56 -> x32, local copies, waits for them, and re-layouts: 10.8 us -> 8.26 us
  transfers between devices with their start and end apart: 35 -> 35, of which waited for: 14 -> 12; matrix products, arithmetic and copies ran while one was open for 1% -> 1% of each run, Pallas kernels for 36% -> 29%
where the time goes in v3:
time: 226 us; the launch traced here: 224 us
  waiting for transfers between devices  78.8 us (35%)
  Pallas kernels  77.4 us (34%)
  starting transfers between devices  55.1 us (24%)
  local copies, waits for them, and re-layouts  10.3 us (5%)
    ppermute x21, waiting for transfers between devices, swap(): lax.ppermute(value, RING, [(i, i - i % team + (i % team ^ d)) for i in ra...  66.1 us
    pallas_call x4, Pallas kernels, attend(): pl.pallas_call(functools.partial(attend_kernel, plan, rows, tile), grid=(...  65 us
    ppermute x14, starting transfers between devices, shift(): return lax.ppermute(value, RING, pairs)  39.4 us
    ppermute x21, starting transfers between devices, swap(): lax.ppermute(value, RING, [(i, i - i % team + (i % team ^ d)) for i in ra...  15.7 us
    ppermute x14, waiting for transfers between devices, shift(): return lax.ppermute(value, RING, pairs)  12.7 us
    unnamed x32, local copies, waits for them, and re-layouts  8.26 us
    pallas_call x1, Pallas kernels, pack(): pl.pallas_call(functools.partial(pack_kernel, jobs, step), grid=(BLOCKS,)...  6.28 us
    pallas_call x1, Pallas kernels, unpack(): pl.pallas_call(functools.partial(unpack_kernel, team, per), grid=(tile //...  5.27 us
  transfers between devices with their start and end apart: 35, of which 12 were waited for; matrix products, arithmetic and copies ran while one was open for 1% of the time, Pallas kernels for 29%

profile of v3, /device:TPU:0, one launch (start us, length us, event | category | flops | bytes accessed | tf_op | source)
XLA Modules:
  0.0 224.4 jit_solution(2447570218606870724)
XLA Ops:
  0.7 0.7 fusion.3
  2.0 0.1 fusion.1
  2.1 6.3 %pack.1 = (bf16[1,4,400,128]{3,2,1,0:T(8,128)(2,1)S(1)}, bf16[1,4,400,128]{3,2,1,0:T(8,128)(2,1)S(1)}, bf16[1,4,384,128]{3,2,1,0:T(8,128)(2,1)S(1)}, bf16[1,4,38...) custom-call(s32[4,4]{1,0:T(4,128)S(1)} %add_multiply_fusion.cols_ref, ...), custom_call_target="tpu_custom_call" | custom-call | bytes 16056320 | tf_op jit(solution)/shard_map/pack/pallas_call | solution.py:56
  8.4 0.8 copy-done.4
  9.2 0.7 copy-done.6
  9.9 0.7 copy-done.8
  10.7 0.7 copy-done.11
  11.4 0.5 collective-permute-start
  11.9 2.6 %collective-permute-start.2 = (bf16[1,4,400,128]{3,2,1,0:T(8,128)(2,1)S(1)}, bf16[1,4,400,128]{3,2,1,0:T(8,128)(2,1)S(1)}, u32[]{:S(2)}, u32[]{:S(2)}) collective-permute-start(bf16[1,4,400,128]{3,2,1,0:T(8,128)(2,1)S(1)} %get-tuple-element.59), channel_id=1, source_target_pairs={{0,3},{1,2},{2,1},{3,0},{4,7},{5,6},{6,5},{7,4},{8,11},{9,10},{10,... | collective-permute-start | bytes 1228808 | tf_op jit(solution)/shard_map/ppermute | solution.py:346
  14.5 1.3 collective-permute-start.3
  15.8 1.3 collective-permute-start.4
  17.1 0.7 slice_reduce_fusion.3
  17.9 6.4 %collective-permute-done.2.refs_1_.refs_3_ = bf16[1,4,400,128]{3,2,1,0:T(8,128)(2,1)S(1)} collective-permute-done((bf16[1,4,400,128]{3,2,1,0:T(8,128)(2,1)S(1)}, bf16[1,4,400,128]{3,2,1,0:T(8,128)(2,1)S(1)}, u32[]{:S(2)}, u32[]{:S(2)}) %collective-permute-start.2) | collective-permute-done | bytes 409632 | tf_op jit(solution)/shard_map/ppermute | solution.py:346
  24.3 0.1 stack.19
  24.4 8.9 %collective-permute-done.1.refs_0_.refs_2_ = bf16[1,4,400,128]{3,2,1,0:T(8,128)(2,1)S(1)} collective-permute-done((bf16[1,4,400,128]{3,2,1,0:T(8,128)(2,1)S(1)}, bf16[1,4,400,128]{3,2,1,0:T(8,128)(2,1)S(1)}, u32[]{:S(2)}, u32[]{:S(2)}) %collective-permute-start.1) | collective-permute-done | bytes 409632 | tf_op jit(solution)/shard_map/ppermute | solution.py:346
  33.4 0.7 slice_reduce_fusion.2
  34.3 1.7 collective-permute-start.6
  36.0 1.0 copy-done.5
  37.0 1.0 copy-done.9
  38.0 1.0 copy-done.12
  39.1 0.7 copy-done.10
  39.8 0.7 copy-done.13
  40.5 4.2 %collective-permute-start.5 = (bf16[1,4,384,128]{3,2,1,0:T(8,128)(2,1)S(1)}, bf16[1,4,384,128]{3,2,1,0:T(8,128)(2,1)}, u32[]{:S(2)}, u32[]{:S(2)}) collective-permute-start(bf16[1,4,384,128]{3,2,1,0:T(8,128)(2,1)S(1)} %get-tuple-element.67.refs_4_), channel_id=1, source_target_pairs={{0,4},{1,5},{4,8},{5,9},{6,2},{7,3},{8,12},{9,13},{10,6},{11,7},{1... | collective-permute-start | bytes 1179656 | tf_op jit(solution)/shard_map/ppermute | solution.py:358
  45.0 0.1 copy.30
  45.2 0.4 collective-permute-done.6.refs_0_.refs_2_
  45.6 1.1 collective-permute-start.11
  46.7 9.5 %collective-permute-done.7.refs_1_.refs_3_ = bf16[1,4,384,128]{3,2,1,0:T(8,128)(2,1)S(1)} collective-permute-done((bf16[1,4,384,128]{3,2,1,0:T(8,128)(2,1)S(1)}, bf16[1,4,384,128]{3,2,1,0:T(8,128)(2,1)S(1)}, u32[]{:S(2)}, u32[]{:S(2)}) %collective-permute-start.7) | collective-permute-done | bytes 393248 | tf_op jit(solution)/shard_map/ppermute | solution.py:346
  56.2 0.1 collective-permute-start.12
  56.3 2.8 %collective-permute-start.10 = (bf16[1,4,384,128]{3,2,1,0:T(8,128)(2,1)S(1)}, bf16[1,4,384,128]{3,2,1,0:T(8,128)(2,1)S(1)}, u32[]{:S(2)}, u32[]{:S(2)}) collective-permute-start(bf16[1,4,384,128]{3,2,1,0:T(8,128)(2,1)S(1)} %get-tuple-element.71.refs_7_), channel_id=1, source_target_pairs={{0,4},{1,5},{4,8},{5,9},{6,2},{7,3},{8,12},{9,13},{10,6},{11,7},{1... | collective-permute-start | bytes 1179656 | tf_op jit(solution)/shard_map/ppermute | solution.py:358
  59.1 16.3 %attend.4 = (bf16[4,2,384,128]{3,2,1,0:T(8,128)(2,1)S(1)}, f32[4,2,384,128]{3,2,1,0:T(8,128)}, bf16[2,2,384,128]{3,2,1,0:T(8,128)(2,1)S(1)}, bf16[2,2,384,128]{3,2,1,0:T(8,128)(2,1)S(1)}) custom-call(s32[4,9]{1,0:T(4,128)S(1)} %pad_add_fusion.1.table_ref, bf16[4,4,400,128]{3,2,1,0:T(8,128)(2,1)} %get-tuple-element.56.refs_0_, ...), custom_call_target="tpu_custom_call" | custom-call | flops 5435817984 | bytes 8388608 | tf_op jit(solution)/shard_map/attend/pallas_call | solution.py:251
  75.5 1.3 collective-permute-start.8
  76.8 1.3 collective-permute-start.9
  78.1 7.6 %collective-permute-start.18 = (bf16[1,4,384,128]{3,2,1,0:T(8,128)(2,1)S(1)}, bf16[1,4,384,128]{3,2,1,0:T(8,128)(2,1)S(1)}, u32[]{:S(2)}, u32[]{:S(2)}) collective-permute-start(bf16[1,4,384,128]{3,2,1,0:T(8,128)(2,1)S(1)} %relay.6.refs_7_), channel_id=1, source_target_pairs={{0,4},{1,5},{4,8},{5,9},{6,2},{7,3},{8,12},{9,13},{10,6},{11,7},{1... | collective-permute-start | bytes 1179656 | tf_op jit(solution)/shard_map/ppermute | solution.py:358
  85.8 1.7 collective-permute-start.20
  87.6 16.1 %attend.5 = (bf16[4,2,384,128]{3,2,1,0:T(8,128)(2,1)S(1)}, f32[4,2,384,128]{3,2,1,0:T(8,128)}, bf16[2,2,384,128]{3,2,1,0:T(8,128)(2,1)S(1)}, bf16[2,2,384,128]{3,2,1,0:T(8,128)(2,1)S(1)}) custom-call(s32[4,9]{1,0:T(4,128)S(1)} %pad_add_fusion.1.table_ref, bf16[4,4,400,128]{3,2,1,0:T(8,128)(2,1)} %get-tuple-element.56.refs_0_, ...), custom_call_target="tpu_custom_call" | custom-call | flops 5435817984 | bytes 8388608 | tf_op jit(solution)/shard_map/attend/pallas_call | solution.py:251
  103.8 0.2 finish.4
  103.9 0.4 collective-permute-start.13
  104.4 0.2 collective-permute-start.14
  104.6 1.6 collective-permute-start.16
  106.1 1.3 collective-permute-start.17
  107.5 7.7 %collective-permute-start.29 = (bf16[1,4,384,128]{3,2,1,0:T(8,128)(2,1)S(1)}, bf16[1,4,384,128]{3,2,1,0:T(8,128)(2,1)S(1)}, u32[]{:S(2)}, u32[]{:S(2)}) collective-permute-start(bf16[1,4,384,128]{3,2,1,0:T(8,128)(2,1)S(1)} %relay.7.refs_7_), channel_id=1, source_target_pairs={{0,4},{1,5},{4,8},{5,9},{6,2},{7,3},{8,12},{9,13},{10,6},{11,7},{1... | collective-permute-start | bytes 1179656 | tf_op jit(solution)/shard_map/ppermute | solution.py:358
  115.2 16.3 %attend.6 = (bf16[4,2,384,128]{3,2,1,0:T(8,128)(2,1)S(1)}, f32[4,2,384,128]{3,2,1,0:T(8,128)}, bf16[2,2,384,128]{3,2,1,0:T(8,128)(2,1)S(1)}, bf16[2,2,384,128]{3,2,1,0:T(8,128)(2,1)S(1)}) custom-call(s32[4,9]{1,0:T(4,128)S(1)} %pad_add_fusion.1.table_ref, bf16[4,4,400,128]{3,2,1,0:T(8,128)(2,1)} %get-tuple-element.56.refs_0_, ...), custom_call_target="tpu_custom_call" | custom-call | flops 5435817984 | bytes 8388608 | tf_op jit(solution)/shard_map/attend/pallas_call | solution.py:251
  131.5 1.5 collective-permute-start.24
  133.0 1.3 collective-permute-start.25
  134.3 0.2 finish.5
  134.6 16.3 %attend.7 = (bf16[4,2,384,128]{3,2,1,0:T(8,128)(2,1)S(1)}, f32[4,2,384,128]{3,2,1,0:T(8,128)}, bf16[2,2,384,128]{3,2,1,0:T(8,128)(2,1)S(1)}, bf16[2,2,384,128]{3,2,1,0:T(8,128)(2,1)S(1)}) custom-call(s32[4,9]{1,0:T(4,128)S(1)} %pad_add_fusion.1.table_ref, bf16[4,4,400,128]{3,2,1,0:T(8,128)(2,1)} %get-tuple-element.56.refs_0_, ...), custom_call_target="tpu_custom_call" | custom-call | flops 5435817984 | bytes 8388608 | tf_op jit(solution)/shard_map/attend/pallas_call | solution.py:251
  150.8 4.9 %collective-permute-start.30 = (bf16[2,2,384,128]{3,2,1,0:T(8,128)(2,1)S(1)}, bf16[2,2,384,128]{3,2,1,0:T(8,128)(2,1)S(1)}, u32[]{:S(2)}, u32[]{:S(2)}) collective-permute-start(bf16[2,2,384,128]{3,2,1,0:T(8,128)(2,1)S(1)} %get-tuple-element.102), channel_id=1, source_target_pairs={{0,4},{1,5},{4,8},{5,9},{6,2},{7,3},{8,12},{9,13},{10,6},{11,7},{1... | collective-permute-start | bytes 1179656 | tf_op jit(solution)/shard_map/ppermute | solution.py:358
  155.8 1.3 collective-permute-start.31
  157.1 0.6 collective-permute-start.15
  157.7 1.8 collective-permute-start.21
  159.6 0.2 finish.6
  159.7 3.9 %collective-permute-done.30.refs_0_ = bf16[2,2,384,128]{3,2,1,0:T(8,128)(2,1)S(1)} collective-permute-done((bf16[2,2,384,128]{3,2,1,0:T(8,128)(2,1)S(1)}, bf16[2,2,384,128]{3,2,1,0:T(8,128)(2,1)S(1)}, u32[]{:S(2)}, u32[]{:S(2)}) %collective-permute-start.30) | collective-permute-done | bytes 393248 | tf_op jit(solution)/shard_map/ppermute | solution.py:358
  163.6 8.8 %collective-permute-done.31.refs_1_ = bf16[2,2,384,128]{3,2,1,0:T(8,128)(2,1)S(1)} collective-permute-done((bf16[2,2,384,128]{3,2,1,0:T(8,128)(2,1)S(1)}, bf16[2,2,384,128]{3,2,1,0:T(8,128)(2,1)S(1)}, u32[]{:S(2)}, u32[]{:S(2)}) %collective-permute-start.31) | collective-permute-done | bytes 393248 | tf_op jit(solution)/shard_map/ppermute | solution.py:358
  172.4 0.2 finish.7
  172.7 1.9 collective-permute-start.28
  174.6 3.2 %collective-permute-done.22.refs_6_ = bf16[4,384,128]{2,1,0:T(8,128)(2,1)S(1)} collective-permute-done((bf16[4,384,128]{2,1,0:T(8,128)(2,1)S(1)}, bf16[4,384,128]{2,1,0:T(8,128)(2,1)S(1)}, u32[]{:S(2)}, u32[]{:S(2)}) %collective-permute-start.22) | collective-permute-done | bytes 393248 | tf_op jit(solution)/shard_map/ppermute | solution.py:346
  177.7 6.9 %collective-permute-done.23.refs_7_ = bf16[4,384,128]{2,1,0:T(8,128)(2,1)S(1)} collective-permute-done((bf16[4,384,128]{2,1,0:T(8,128)(2,1)S(1)}, bf16[4,384,128]{2,1,0:T(8,128)(2,1)S(1)}, u32[]{:S(2)}, u32[]{:S(2)}) %collective-permute-start.23) | collective-permute-done | bytes 393248 | tf_op jit(solution)/shard_map/ppermute | solution.py:346
  184.7 3.0 %collective-permute-start.33 = (bf16[4,384,128]{2,1,0:T(8,128)(2,1)S(1)}, bf16[4,384,128]{2,1,0:T(8,128)(2,1)S(1)}, u32[]{:S(2)}, u32[]{:S(2)}) collective-permute-start(bf16[4,384,128]{2,1,0:T(8,128)(2,1)S(1)} %get-tuple-element.106), channel_id=1, source_target_pairs={{0,2},{1,3},{2,0},{3,1},{4,6},{5,7},{6,4},{7,5},{8,10},{9,11},{10,... | collective-permute-start | bytes 1179656 | tf_op jit(solution)/shard_map/ppermute | solution.py:346
  187.6 6.9 %collective-permute-done.27.refs_10_ = bf16[4,384,128]{2,1,0:T(8,128)(2,1)S(1)} collective-permute-done((bf16[4,384,128]{2,1,0:T(8,128)(2,1)S(1)}, bf16[4,384,128]{2,1,0:T(8,128)(2,1)S(1)}, u32[]{:S(2)}, u32[]{:S(2)}) %collective-permute-start.27) | collective-permute-done | bytes 393248 | tf_op jit(solution)/shard_map/ppermute | solution.py:346
  194.6 7.0 %collective-permute-done.28.refs_11_ = bf16[4,384,128]{2,1,0:T(8,128)(2,1)S(1)} collective-permute-done((bf16[4,384,128]{2,1,0:T(8,128)(2,1)S(1)}, bf16[4,384,128]{2,1,0:T(8,128)(2,1)S(1)}, u32[]{:S(2)}, u32[]{:S(2)}) %collective-permute-start.28) | collective-permute-done | bytes 393248 | tf_op jit(solution)/shard_map/ppermute | solution.py:346
  201.5 9.9 %collective-permute-done.33.refs_14_ = bf16[4,384,128]{2,1,0:T(8,128)(2,1)S(1)} collective-permute-done((bf16[4,384,128]{2,1,0:T(8,128)(2,1)S(1)}, bf16[4,384,128]{2,1,0:T(8,128)(2,1)S(1)}, u32[]{:S(2)}, u32[]{:S(2)}) %collective-permute-start.33) | collective-permute-done | bytes 393248 | tf_op jit(solution)/shard_map/ppermute | solution.py:346
  211.4 7.0 %collective-permute-done.34.refs_15_ = bf16[4,384,128]{2,1,0:T(8,128)(2,1)S(1)} collective-permute-done((bf16[4,384,128]{2,1,0:T(8,128)(2,1)S(1)}, bf16[4,384,128]{2,1,0:T(8,128)(2,1)S(1)}, u32[]{:S(2)}, u32[]{:S(2)}) %collective-permute-start.34) | collective-permute-done | bytes 393248 | tf_op jit(solution)/shard_map/ppermute | solution.py:346
  218.4 0.7 copy-done.14
  219.1 5.3 %unpack.1 = (bf16[1,384,2048]{2,1,0:T(8,128)(2,1)}, bf16[1,384,2048]{2,1,0:T(8,128)(2,1)}, bf16[1,384,2048]{2,1,0:T(8,128)(2,1)}, bf16[1,384,2048]{2,1,0:T(8,128)(2,1)}) custom-call(s32[4,4]{1,0:T(4,128)S(1)} %add_multiply_fusion.cols_ref, bf16[4,384,128]{2,1,0:T(8,128)(2,1)S(1)} %get-tuple-element.79.refs_0_, ...), custom_call_target="tpu_custom_call" | custom-call | bytes 12582912 | tf_op jit(solution)/shard_map/unpack/pallas_call | solution.py:316
  (77 shorter events, 1.2 us)
Async XLA Ops:
  8.4 0.8 copy-start.4
  9.2 0.7 copy-start.6
  9.9 0.7 copy-start.8
  10.7 0.7 copy-start.11
  11.4 22.0 %collective-permute-start = (bf16[4,4,400,128]{3,2,1,0:T(8,128)(2,1)}, bf16[4,4,400,128]{3,2,1,0:T(8,128)(2,1)}, u32[]{:S(2)}, u32[]{:S(2)}) collective-permute-start(bf16[4,4,400,128]{3,2,1,0:T(8,128)(2,1)} %get-tuple-element.57), channel_id=1, source_target_pairs={{0,1},{1,0},{2,3},{3,2},{4,5},{5,4},{6,7},{7,6},{8,9},{9,8},{10,11... | collective-permute-start | bytes 4915208 | tf_op jit(solution)/shard_map/ppermute | solution.py:346
  11.9 12.4 %collective-permute-start.2 = (bf16[1,4,400,128]{3,2,1,0:T(8,128)(2,1)S(1)}, bf16[1,4,400,128]{3,2,1,0:T(8,128)(2,1)S(1)}, u32[]{:S(2)}, u32[]{:S(2)}) collective-permute-start(bf16[1,4,400,128]{3,2,1,0:T(8,128)(2,1)S(1)} %get-tuple-element.59), channel_id=1, source_target_pairs={{0,3},{1,2},{2,1},{3,0},{4,7},{5,6},{6,5},{7,4},{8,11},{9,10},{10,... | collective-permute-start | bytes 1228808 | tf_op jit(solution)/shard_map/ppermute | solution.py:346
  14.5 18.8 %collective-permute-start.1 = (bf16[1,4,400,128]{3,2,1,0:T(8,128)(2,1)S(1)}, bf16[1,4,400,128]{3,2,1,0:T(8,128)(2,1)S(1)}, u32[]{:S(2)}, u32[]{:S(2)}) collective-permute-start(bf16[1,4,400,128]{3,2,1,0:T(8,128)(2,1)S(1)} %get-tuple-element.58), channel_id=1, source_target_pairs={{0,2},{1,3},{2,0},{3,1},{4,6},{5,7},{6,4},{7,5},{8,10},{9,11},{10,... | collective-permute-start | bytes 1228808 | tf_op jit(solution)/shard_map/ppermute | solution.py:346
  14.5 41.8 %collective-permute-start.3 = (bf16[4,4,192,128]{3,2,1,0:T(8,128)(2,1)}, bf16[4,4,192,128]{3,2,1,0:T(8,128)(2,1)}, u32[]{:S(2)}, u32[]{:S(2)}) collective-permute-start(bf16[4,4,192,128]{3,2,1,0:T(8,128)(2,1)} %get-tuple-element.60), channel_id=1, source_target_pairs={{2,6},{3,7},{4,0},{5,1},{6,10},{7,11},{8,4},{9,5},{10,14},{11,15},... | collective-permute-start | bytes 2359304 | tf_op jit(solution)/shard_map/ppermute | solution.py:358
  15.8 43.4 %collective-permute-start.4 = (bf16[4,4,192,128]{3,2,1,0:T(8,128)(2,1)}, bf16[4,4,192,128]{3,2,1,0:T(8,128)(2,1)}, u32[]{:S(2)}, u32[]{:S(2)}) collective-permute-start(bf16[4,4,192,128]{3,2,1,0:T(8,128)(2,1)} %get-tuple-element.61), channel_id=1, source_target_pairs={{2,7},{3,6},{4,1},{5,0},{6,11},{7,10},{8,5},{9,4},{10,15},{11,14},... | collective-permute-start | bytes 2359304 | tf_op jit(solution)/shard_map/ppermute | solution.py:358
  34.3 10.8 %copy-start.15 = (s32[2,3]{1,0:T(2,128)S(1)}, s32[2,3]{1,0:T(2,128)}, u32[]{:S(2)}) copy-start(s32[2,3]{1,0:T(2,128)} %constant.51.clone) | copy-start | bytes 76
  34.3 11.3 %collective-permute-start.6 = (bf16[1,4,384,128]{3,2,1,0:T(8,128)(2,1)}, bf16[1,4,384,128]{3,2,1,0:T(8,128)(2,1)S(1)}, u32[]{:S(2)}, u32[]{:S(2)}) collective-permute-start(bf16[1,4,384,128]{3,2,1,0:T(8,128)(2,1)} %get-tuple-element.66.refs_4_), channel_id=1, source_target_pairs={{0,2},{1,3},{2,0},{3,1},{4,6},{5,7},{6,4},{7,5},{8,10},{9,11},{10,... | collective-permute-start | bytes 1179656 | tf_op jit(solution)/shard_map/ppermute | solution.py:346
  36.0 1.0 copy-start.5
  37.0 1.0 copy-start.9
  38.0 1.0 copy-start.12
  39.0 5.7 %copy-start.7 = (bf16[1,4,384,128]{3,2,1,0:T(8,128)(2,1)S(1)}, bf16[1,4,384,128]{3,2,1,0:T(8,128)(2,1)}, u32[]{:S(2)}) copy-start(bf16[1,4,384,128]{3,2,1,0:T(8,128)(2,1)} %get-tuple-element.68) | copy-start | bytes 1179652
  39.1 0.7 copy-start.10
  39.8 0.7 copy-start.13
  40.5 18.6 %collective-permute-start.5 = (bf16[1,4,384,128]{3,2,1,0:T(8,128)(2,1)S(1)}, bf16[1,4,384,128]{3,2,1,0:T(8,128)(2,1)}, u32[]{:S(2)}, u32[]{:S(2)}) collective-permute-start(bf16[1,4,384,128]{3,2,1,0:T(8,128)(2,1)S(1)} %get-tuple-element.67.refs_4_), channel_id=1, source_target_pairs={{0,4},{1,5},{4,8},{5,9},{6,2},{7,3},{8,12},{9,13},{10,6},{11,7},{1... | collective-permute-start | bytes 1179656 | tf_op jit(solution)/shard_map/ppermute | solution.py:358
  44.8 11.4 %collective-permute-start.7 = (bf16[1,4,384,128]{3,2,1,0:T(8,128)(2,1)S(1)}, bf16[1,4,384,128]{3,2,1,0:T(8,128)(2,1)S(1)}, u32[]{:S(2)}, u32[]{:S(2)}) collective-permute-start(bf16[1,4,384,128]{3,2,1,0:T(8,128)(2,1)S(1)} %copy-done.7), channel_id=1, source_target_pairs={{0,3},{1,2},{2,1},{3,0},{4,7},{5,6},{6,5},{7,4},{8,11},{9,10},{10,... | collective-permute-start | bytes 1179656 | tf_op jit(solution)/shard_map/ppermute | solution.py:346
  45.6 32.4 %collective-permute-start.11 = (bf16[1,4,384,128]{3,2,1,0:T(8,128)(2,1)}, bf16[1,4,384,128]{3,2,1,0:T(8,128)(2,1)S(1)}, u32[]{:S(2)}, u32[]{:S(2)}) collective-permute-start(bf16[1,4,384,128]{3,2,1,0:T(8,128)(2,1)} %copy-done.10), channel_id=1, source_target_pairs={{0,2},{1,3},{2,0},{3,1},{4,6},{5,7},{6,4},{7,5},{8,10},{9,11},{10,... | collective-permute-start | bytes 1179656 | tf_op jit(solution)/shard_map/ppermute | solution.py:346
  56.2 21.9 %collective-permute-start.12 = (bf16[1,4,384,128]{3,2,1,0:T(8,128)(2,1)}, bf16[1,4,384,128]{3,2,1,0:T(8,128)(2,1)S(1)}, u32[]{:S(2)}, u32[]{:S(2)}) collective-permute-start(bf16[1,4,384,128]{3,2,1,0:T(8,128)(2,1)} %copy-done.13), channel_id=1, source_target_pairs={{0,3},{1,2},{2,1},{3,0},{4,7},{5,6},{6,5},{7,4},{8,11},{9,10},{10,... | collective-permute-start | bytes 1179656 | tf_op jit(solution)/shard_map/ppermute | solution.py:346
  56.3 29.5 %collective-permute-start.10 = (bf16[1,4,384,128]{3,2,1,0:T(8,128)(2,1)S(1)}, bf16[1,4,384,128]{3,2,1,0:T(8,128)(2,1)S(1)}, u32[]{:S(2)}, u32[]{:S(2)}) collective-permute-start(bf16[1,4,384,128]{3,2,1,0:T(8,128)(2,1)S(1)} %get-tuple-element.71.refs_7_), channel_id=1, source_target_pairs={{0,4},{1,5},{4,8},{5,9},{6,2},{7,3},{8,12},{9,13},{10,6},{11,7},{1... | collective-permute-start | bytes 1179656 | tf_op jit(solution)/shard_map/ppermute | solution.py:358
  75.5 28.3 %collective-permute-start.8 = (bf16[2,2,384,128]{3,2,1,0:T(8,128)(2,1)S(1)}, bf16[2,2,384,128]{3,2,1,0:T(8,128)(2,1)S(1)}, u32[]{:S(2)}, u32[]{:S(2)}) collective-permute-start(bf16[2,2,384,128]{3,2,1,0:T(8,128)(2,1)S(1)} %get-tuple-element.74), channel_id=1, source_target_pairs={{0,4},{1,5},{4,8},{5,9},{6,2},{7,3},{8,12},{9,13},{10,6},{11,7},{1... | collective-permute-start | bytes 1179656 | tf_op jit(solution)/shard_map/ppermute | solution.py:358
  76.8 27.0 %collective-permute-start.9 = (bf16[2,2,384,128]{3,2,1,0:T(8,128)(2,1)S(1)}, bf16[2,2,384,128]{3,2,1,0:T(8,128)(2,1)S(1)}, u32[]{:S(2)}, u32[]{:S(2)}) collective-permute-start(bf16[2,2,384,128]{3,2,1,0:T(8,128)(2,1)S(1)} %get-tuple-element.75), channel_id=1, source_target_pairs={{2,6},{3,7},{4,0},{5,1},{6,10},{7,11},{8,4},{9,5},{10,14},{11,15},... | collective-permute-start | bytes 1179656 | tf_op jit(solution)/shard_map/ppermute | solution.py:358
  78.1 29.4 %collective-permute-start.18 = (bf16[1,4,384,128]{3,2,1,0:T(8,128)(2,1)S(1)}, bf16[1,4,384,128]{3,2,1,0:T(8,128)(2,1)S(1)}, u32[]{:S(2)}, u32[]{:S(2)}) collective-permute-start(bf16[1,4,384,128]{3,2,1,0:T(8,128)(2,1)S(1)} %relay.6.refs_7_), channel_id=1, source_target_pairs={{0,4},{1,5},{4,8},{5,9},{6,2},{7,3},{8,12},{9,13},{10,6},{11,7},{1... | collective-permute-start | bytes 1179656 | tf_op jit(solution)/shard_map/ppermute | solution.py:358
  85.7 18.8 %collective-permute-start.19 = (bf16[1,4,384,128]{3,2,1,0:T(8,128)(2,1)S(1)}, bf16[1,4,384,128]{3,2,1,0:T(8,128)(2,1)S(1)}, u32[]{:S(2)}, u32[]{:S(2)}) collective-permute-start(bf16[1,4,384,128]{3,2,1,0:T(8,128)(2,1)S(1)} %get-tuple-element.86), channel_id=1, source_target_pairs={{0,2},{1,3},{2,0},{3,1},{4,6},{5,7},{6,4},{7,5},{8,10},{9,11},{10,... | collective-permute-start | bytes 1179656 | tf_op jit(solution)/shard_map/ppermute | solution.py:346
  85.8 17.9 %copy-start.3 = (f32[4,2,384,128]{3,2,1,0:T(8,128)S(1)}, f32[4,2,384,128]{3,2,1,0:T(8,128)}, u32[]{:S(2)}) copy-start(f32[4,2,384,128]{3,2,1,0:T(8,128)} %get-tuple-element.73.local) | copy-start | bytes 4718596
  85.8 20.3 %collective-permute-start.20 = (bf16[1,4,384,128]{3,2,1,0:T(8,128)(2,1)S(1)}, bf16[1,4,384,128]{3,2,1,0:T(8,128)(2,1)S(1)}, u32[]{:S(2)}, u32[]{:S(2)}) collective-permute-start(bf16[1,4,384,128]{3,2,1,0:T(8,128)(2,1)S(1)} %get-tuple-element.87), channel_id=1, source_target_pairs={{0,3},{1,2},{2,1},{3,0},{4,7},{5,6},{6,5},{7,4},{8,11},{9,10},{10,... | collective-permute-start | bytes 1179656 | tf_op jit(solution)/shard_map/ppermute | solution.py:346
  103.9 51.8 %collective-permute-start.13 = (bf16[4,384,128]{2,1,0:T(8,128)(2,1)S(1)}, bf16[4,384,128]{2,1,0:T(8,128)(2,1)S(1)}, u32[]{:S(2)}, u32[]{:S(2)}) collective-permute-start(bf16[4,384,128]{2,1,0:T(8,128)(2,1)S(1)} %get-tuple-element.80), channel_id=1, source_target_pairs={{0,1},{1,0},{2,3},{3,2},{4,5},{5,4},{6,7},{7,6},{8,9},{9,8},{10,11... | collective-permute-start | bytes 1179656 | tf_op jit(solution)/shard_map/ppermute | solution.py:346
  104.4 52.7 %collective-permute-start.14 = (bf16[4,384,128]{2,1,0:T(8,128)(2,1)S(1)}, bf16[4,384,128]{2,1,0:T(8,128)(2,1)S(1)}, u32[]{:S(2)}, u32[]{:S(2)}) collective-permute-start(bf16[4,384,128]{2,1,0:T(8,128)(2,1)S(1)} %get-tuple-element.81), channel_id=1, source_target_pairs={{0,2},{1,3},{2,0},{3,1},{4,6},{5,7},{6,4},{7,5},{8,10},{9,11},{10,... | collective-permute-start | bytes 1179656 | tf_op jit(solution)/shard_map/ppermute | solution.py:346
  104.6 26.9 %collective-permute-start.16 = (bf16[2,2,384,128]{3,2,1,0:T(8,128)(2,1)S(1)}, bf16[2,2,384,128]{3,2,1,0:T(8,128)(2,1)S(1)}, u32[]{:S(2)}, u32[]{:S(2)}) collective-permute-start(bf16[2,2,384,128]{3,2,1,0:T(8,128)(2,1)S(1)} %get-tuple-element.84), channel_id=1, source_target_pairs={{0,4},{1,5},{4,8},{5,9},{6,2},{7,3},{8,12},{9,13},{10,6},{11,7},{1... | collective-permute-start | bytes 1179656 | tf_op jit(solution)/shard_map/ppermute | solution.py:358
  106.1 26.9 %collective-permute-start.17 = (bf16[2,2,384,128]{3,2,1,0:T(8,128)(2,1)S(1)}, bf16[2,2,384,128]{3,2,1,0:T(8,128)(2,1)S(1)}, u32[]{:S(2)}, u32[]{:S(2)}) collective-permute-start(bf16[2,2,384,128]{3,2,1,0:T(8,128)(2,1)S(1)} %get-tuple-element.85), channel_id=1, source_target_pairs={{2,6},{3,7},{4,0},{5,1},{6,10},{7,11},{8,4},{9,5},{10,14},{11,15},... | collective-permute-start | bytes 1179656 | tf_op jit(solution)/shard_map/ppermute | solution.py:358
  107.5 27.1 %collective-permute-start.29 = (bf16[1,4,384,128]{3,2,1,0:T(8,128)(2,1)S(1)}, bf16[1,4,384,128]{3,2,1,0:T(8,128)(2,1)S(1)}, u32[]{:S(2)}, u32[]{:S(2)}) collective-permute-start(bf16[1,4,384,128]{3,2,1,0:T(8,128)(2,1)S(1)} %relay.7.refs_7_), channel_id=1, source_target_pairs={{0,4},{1,5},{4,8},{5,9},{6,2},{7,3},{8,12},{9,13},{10,6},{11,7},{1... | collective-permute-start | bytes 1179656 | tf_op jit(solution)/shard_map/ppermute | solution.py:358
  115.2 19.1 %copy-start.2 = (f32[4,2,384,128]{3,2,1,0:T(8,128)S(1)}, f32[4,2,384,128]{3,2,1,0:T(8,128)}, u32[]{:S(2)}) copy-start(f32[4,2,384,128]{3,2,1,0:T(8,128)} %get-tuple-element.83.local) | copy-start | bytes 4718596
  131.5 26.3 %collective-permute-start.24 = (bf16[2,2,384,128]{3,2,1,0:T(8,128)(2,1)S(1)}, bf16[2,2,384,128]{3,2,1,0:T(8,128)(2,1)S(1)}, u32[]{:S(2)}, u32[]{:S(2)}) collective-permute-start(bf16[2,2,384,128]{3,2,1,0:T(8,128)(2,1)S(1)} %get-tuple-element.94), channel_id=1, source_target_pairs={{0,4},{1,5},{4,8},{5,9},{6,2},{7,3},{8,12},{9,13},{10,6},{11,7},{1... | collective-permute-start | bytes 1179656 | tf_op jit(solution)/shard_map/ppermute | solution.py:358
  133.0 26.5 %collective-permute-start.25 = (bf16[2,2,384,128]{3,2,1,0:T(8,128)(2,1)S(1)}, bf16[2,2,384,128]{3,2,1,0:T(8,128)(2,1)S(1)}, u32[]{:S(2)}, u32[]{:S(2)}) collective-permute-start(bf16[2,2,384,128]{3,2,1,0:T(8,128)(2,1)S(1)} %get-tuple-element.95), channel_id=1, source_target_pairs={{2,6},{3,7},{4,0},{5,1},{6,10},{7,11},{8,4},{9,5},{10,14},{11,15},... | collective-permute-start | bytes 1179656 | tf_op jit(solution)/shard_map/ppermute | solution.py:358
  134.5 25.0 %copy-start = (f32[4,2,384,128]{3,2,1,0:T(8,128)S(1)}, f32[4,2,384,128]{3,2,1,0:T(8,128)}, u32[]{:S(2)}) copy-start(f32[4,2,384,128]{3,2,1,0:T(8,128)} %get-tuple-element.93.local) | copy-start | bytes 4718596
  150.8 12.7 %collective-permute-start.30 = (bf16[2,2,384,128]{3,2,1,0:T(8,128)(2,1)S(1)}, bf16[2,2,384,128]{3,2,1,0:T(8,128)(2,1)S(1)}, u32[]{:S(2)}, u32[]{:S(2)}) collective-permute-start(bf16[2,2,384,128]{3,2,1,0:T(8,128)(2,1)S(1)} %get-tuple-element.102), channel_id=1, source_target_pairs={{0,4},{1,5},{4,8},{5,9},{6,2},{7,3},{8,12},{9,13},{10,6},{11,7},{1... | collective-permute-start | bytes 1179656 | tf_op jit(solution)/shard_map/ppermute | solution.py:358
  155.8 16.7 %collective-permute-start.31 = (bf16[2,2,384,128]{3,2,1,0:T(8,128)(2,1)S(1)}, bf16[2,2,384,128]{3,2,1,0:T(8,128)(2,1)S(1)}, u32[]{:S(2)}, u32[]{:S(2)}) collective-permute-start(bf16[2,2,384,128]{3,2,1,0:T(8,128)(2,1)S(1)} %get-tuple-element.103), channel_id=1, source_target_pairs={{2,6},{3,7},{4,0},{5,1},{6,10},{7,11},{8,4},{9,5},{10,14},{11,15},... | collective-permute-start | bytes 1179656 | tf_op jit(solution)/shard_map/ppermute | solution.py:358
  157.1 15.5 %collective-permute-start.15 = (bf16[4,384,128]{2,1,0:T(8,128)(2,1)S(1)}, bf16[4,384,128]{2,1,0:T(8,128)(2,1)S(1)}, u32[]{:S(2)}, u32[]{:S(2)}) collective-permute-start(bf16[4,384,128]{2,1,0:T(8,128)(2,1)S(1)} %get-tuple-element.82.refs_8_), channel_id=1, source_target_pairs={{0,3},{1,2},{2,1},{3,0},{4,7},{5,6},{6,5},{7,4},{8,11},{9,10},{10,... | collective-permute-start | bytes 1179656 | tf_op jit(solution)/shard_map/ppermute | solution.py:346
  157.7 15.0 %collective-permute-start.21 = (bf16[4,384,128]{2,1,0:T(8,128)(2,1)S(1)}, bf16[4,384,128]{2,1,0:T(8,128)(2,1)S(1)}, u32[]{:S(2)}, u32[]{:S(2)}) collective-permute-start(bf16[4,384,128]{2,1,0:T(8,128)(2,1)S(1)} %get-tuple-element.90), channel_id=1, source_target_pairs={{0,1},{1,0},{2,3},{3,2},{4,5},{5,4},{6,7},{7,6},{8,9},{9,8},{10,11... | collective-permute-start | bytes 1179656 | tf_op jit(solution)/shard_map/ppermute | solution.py:346
  159.5 18.2 %collective-permute-start.22 = (bf16[4,384,128]{2,1,0:T(8,128)(2,1)S(1)}, bf16[4,384,128]{2,1,0:T(8,128)(2,1)S(1)}, u32[]{:S(2)}, u32[]{:S(2)}) collective-permute-start(bf16[4,384,128]{2,1,0:T(8,128)(2,1)S(1)} %get-tuple-element.91), channel_id=1, source_target_pairs={{0,2},{1,3},{2,0},{3,1},{4,6},{5,7},{6,4},{7,5},{8,10},{9,11},{10,... | collective-permute-start | bytes 1179656 | tf_op jit(solution)/shard_map/ppermute | solution.py:346
  159.6 12.9 %copy-start.1 = (f32[4,2,384,128]{3,2,1,0:T(8,128)S(1)}, f32[4,2,384,128]{3,2,1,0:T(8,128)}, u32[]{:S(2)}) copy-start(f32[4,2,384,128]{3,2,1,0:T(8,128)} %get-tuple-element.101.local) | copy-start | bytes 4718596
  163.6 21.1 %collective-permute-start.23 = (bf16[4,384,128]{2,1,0:T(8,128)(2,1)S(1)}, bf16[4,384,128]{2,1,0:T(8,128)(2,1)S(1)}, u32[]{:S(2)}, u32[]{:S(2)}) collective-permute-start(bf16[4,384,128]{2,1,0:T(8,128)(2,1)S(1)} %get-tuple-element.92.refs_7_), channel_id=1, source_target_pairs={{0,3},{1,2},{2,1},{3,0},{4,7},{5,6},{6,5},{7,4},{8,11},{9,10},{10,... | collective-permute-start | bytes 1179656 | tf_op jit(solution)/shard_map/ppermute | solution.py:346
  172.4 15.2 %collective-permute-start.26 = (bf16[4,384,128]{2,1,0:T(8,128)(2,1)S(1)}, bf16[4,384,128]{2,1,0:T(8,128)(2,1)S(1)}, u32[]{:S(2)}, u32[]{:S(2)}) collective-permute-start(bf16[4,384,128]{2,1,0:T(8,128)(2,1)S(1)} %get-tuple-element.97), channel_id=1, source_target_pairs={{0,1},{1,0},{2,3},{3,2},{4,5},{5,4},{6,7},{7,6},{8,9},{9,8},{10,11... | collective-permute-start | bytes 1179656 | tf_op jit(solution)/shard_map/ppermute | solution.py:346
  172.6 22.0 %collective-permute-start.27 = (bf16[4,384,128]{2,1,0:T(8,128)(2,1)S(1)}, bf16[4,384,128]{2,1,0:T(8,128)(2,1)S(1)}, u32[]{:S(2)}, u32[]{:S(2)}) collective-permute-start(bf16[4,384,128]{2,1,0:T(8,128)(2,1)S(1)} %get-tuple-element.98), channel_id=1, source_target_pairs={{0,2},{1,3},{2,0},{3,1},{4,6},{5,7},{6,4},{7,5},{8,10},{9,11},{10,... | collective-permute-start | bytes 1179656 | tf_op jit(solution)/shard_map/ppermute | solution.py:346
  172.7 28.8 %collective-permute-start.28 = (bf16[4,384,128]{2,1,0:T(8,128)(2,1)S(1)}, bf16[4,384,128]{2,1,0:T(8,128)(2,1)S(1)}, u32[]{:S(2)}, u32[]{:S(2)}) collective-permute-start(bf16[4,384,128]{2,1,0:T(8,128)(2,1)S(1)} %get-tuple-element.99), channel_id=1, source_target_pairs={{0,3},{1,2},{2,1},{3,0},{4,7},{5,6},{6,5},{7,4},{8,11},{9,10},{10,... | collective-permute-start | bytes 1179656 | tf_op jit(solution)/shard_map/ppermute | solution.py:346
  177.7 23.8 %collective-permute-start.32 = (bf16[4,384,128]{2,1,0:T(8,128)(2,1)S(1)}, bf16[4,384,128]{2,1,0:T(8,128)(2,1)S(1)}, u32[]{:S(2)}, u32[]{:S(2)}) collective-permute-start(bf16[4,384,128]{2,1,0:T(8,128)(2,1)S(1)} %get-tuple-element.105), channel_id=1, source_target_pairs={{0,1},{1,0},{2,3},{3,2},{4,5},{5,4},{6,7},{7,6},{8,9},{9,8},{10,11... | collective-permute-start | bytes 1179656 | tf_op jit(solution)/shard_map/ppermute | solution.py:346
  184.7 26.8 %collective-permute-start.33 = (bf16[4,384,128]{2,1,0:T(8,128)(2,1)S(1)}, bf16[4,384,128]{2,1,0:T(8,128)(2,1)S(1)}, u32[]{:S(2)}, u32[]{:S(2)}) collective-permute-start(bf16[4,384,128]{2,1,0:T(8,128)(2,1)S(1)} %get-tuple-element.106), channel_id=1, source_target_pairs={{0,2},{1,3},{2,0},{3,1},{4,6},{5,7},{6,4},{7,5},{8,10},{9,11},{10,... | collective-permute-start | bytes 1179656 | tf_op jit(solution)/shard_map/ppermute | solution.py:346
  187.6 30.7 %collective-permute-start.34 = (bf16[4,384,128]{2,1,0:T(8,128)(2,1)S(1)}, bf16[4,384,128]{2,1,0:T(8,128)(2,1)S(1)}, u32[]{:S(2)}, u32[]{:S(2)}) collective-permute-start(bf16[4,384,128]{2,1,0:T(8,128)(2,1)S(1)} %get-tuple-element.107), channel_id=1, source_target_pairs={{0,3},{1,2},{2,1},{3,0},{4,7},{5,6},{6,5},{7,4},{8,11},{9,10},{10,... | collective-permute-start | bytes 1179656 | tf_op jit(solution)/shard_map/ppermute | solution.py:346
  218.4 0.7 copy-start.14

commit v4 on v3

v4 whole, which is shorter than its diff:
```python
import functools
import math

import jax
import jax.numpy as jnp
from jax import lax
from jax.experimental import pallas as pl
from jax.experimental.pallas import tpu as pltpu
from jax.sharding import PartitionSpec as P

HD = 128
FLAG_ROWS = 16
BLOCKS = 4
RING = ("ctx", "sub")
F32 = jnp.float32
BF16 = jnp.bfloat16
SCALE = 1.0 / math.sqrt(HD)
FACTOR = SCALE * math.log2(math.e)
ANY = pl.BlockSpec(memory_space=pl.ANY)
SMEM = pl.BlockSpec(memory_space=pltpu.SMEM)
PARAMS = pltpu.CompilerParams(vmem_limit_bytes=48 * 1024 * 1024)


def struct(shape, dtype):
    return jax.ShapeDtypeStruct(shape, dtype)


def moved(nbytes):
    return pl.CostEstimate(flops=0, bytes_accessed=nbytes, transcendentals=0)


def pack_kernel(jobs, step, first, places_ref, flags_ref, *refs):
    sources, outs = refs[:4], refs[-len(jobs) :]
    lane = lax.broadcasted_iota(jnp.int32, (FLAG_ROWS, HD), 1)
    flags = jnp.zeros((FLAG_ROWS, HD), F32)
    for w in range(flags_ref.shape[0]):
        flags = jnp.where(lane == w, flags_ref[w].astype(F32), flags)
    flags = flags.astype(BF16)
    team = places_ref.shape[0]
    for out, (d, heads, kinds, flagged) in zip(outs, jobs):
        for m, c in enumerate(heads):
            lanes = pl.ds(pl.multiple_of(((c - first) * team + places_ref[d]) * HD, HD), HD)
            for at, n in enumerate(kinds):
                out[m, 0, pl.ds(at * step, step)] = sources[n][0, :, lanes]
            if flagged:
                out[m, 0, pl.ds(len(kinds) * step, FLAG_ROWS)] = flags


def pack(jobs, heads, places, flags, sources, spare):
    _, tile, lane_width = sources[0].shape
    step = tile // BLOCKS
    team = places.shape[0]
    first = heads[0]
    count = len(heads)
    wide = count * team * HD if first % count == 0 else lane_width
    block = first // count if first % count == 0 else 0
    start = first if first % count == 0 else 0
    shapes = [
        (len(held), BLOCKS, len(kinds) * step + (FLAG_ROWS if flagged else 0), HD)
        for _, held, kinds, flagged in jobs
    ]
    return pl.pallas_call(
        functools.partial(pack_kernel, jobs, step, start),
        grid=(BLOCKS,),
        out_shape=[struct(shape, BF16) for shape in shapes],
        in_specs=[SMEM, SMEM]
        + [pl.BlockSpec((1, step, wide), lambda i: (0, i, block))] * 4
        + [ANY] * len(spare),
        out_specs=[
            pl.BlockSpec((shape[0], 1, shape[2], HD), lambda i: (0, i, 0, 0)) for shape in shapes
        ],
        cost_estimate=moved(sum(4 * HD * math.prod(shape[:3]) for shape in shapes)),
        compiler_params=PARAMS,
        name="pack",
    )(places, flags, *sources, *spare)


def relay_kernel(step, rows, near, far, grads, outs):
    for out, pieces, grad in zip(outs, (near, far), grads):
        for e, (piece, at) in enumerate(pieces):
            out[0, :, pl.ds(2 * step * e, 2 * step)] = piece[at, :, pl.ds(0, 2 * step)]
        if grad is not None:
            for e in range(rows):
                for n in range(2):
                    for g in range(BLOCKS):
                        at = pl.ds((2 * rows + 2 * e + n) * step, step)
                        out[0, g, at] = grad[e, n, pl.ds(g * step, step)]


def relay(step, held, near, far, grads, passed, spare):
    rows = len(near)
    kinds = 2 if far else 1
    high = (4 if grads else 2) * rows * step

    def kernel(*refs):
        refs = list(refs)
        near_refs = [(refs.pop(0), 0) for _ in range(rows)]
        far_refs = [(refs.pop(0), 0) for _ in far]
        grad_refs = [refs.pop(0) for _ in grads] or [None] * kinds
        outs = refs[len(passed) + len(spare) :][:kinds]
        relay_kernel(step, rows, near_refs, far_refs, grad_refs, outs)

    def whole(shape):
        return pl.BlockSpec(shape, lambda i: (0,) * len(shape))

    before = rows + len(far) + len(grads)
    shape = (1, BLOCKS, high, HD)
    outs = pl.pallas_call(
        kernel,
        grid=(1,),
        out_shape=[struct(shape, BF16)] * kinds
        + [struct(value.shape, value.dtype) for value in passed],
        in_specs=[
            pl.BlockSpec((1, BLOCKS, 2 * step, HD), lambda i, at=at: (at, 0, 0, 0))
            for at in [held] * rows + [0] * len(far)
        ]
        + [whole(value.shape) for value in grads]
        + [ANY] * (len(passed) + len(spare)),
        out_specs=[whole(shape)] * kinds + [ANY] * len(passed),
        input_output_aliases={before + n: kinds + n for n in range(len(passed))},
        cost_estimate=moved(kinds * 4 * BLOCKS * high * HD),
        compiler_params=PARAMS,
        name="relay",
    )(*near, *far, *grads, *passed, *spare)
    return outs[:kinds], outs[kinds:]


def nt(a, b):
    return lax.dot_general(a, b, (((1,), (1,)), ((), ())), preferred_element_type=F32)


def nn(a, b):
    return jnp.dot(a, b, preferred_element_type=F32)


def attend_kernel(plan, rows, tile, table_ref, *refs):
    loads, slabs_here, n_in, spare = plan
    inputs = refs[:n_in]
    rest = refs[n_in + spare :]
    done, local, grads_one, grads_two = rest[:4]
    qbuf, gbuf, kbuf, vbuf, kt, vt, dk_t, dv_t, s_buf, p_buf, ds_buf, ot = rest[4:]
    targets = {"k": kbuf, "v": vbuf, "q": qbuf, "g": gbuf}
    step = tile // BLOCKS
    for n, at, kind, slab, e in loads:
        for g in range(BLOCKS):
            targets[kind][slab, pl.ds(e * tile + g * step, step)] = inputs[n][
                0, g, pl.ds(at * step, step)
            ]
    width = rows * tile
    team = slabs_here * rows
    places = kbuf.shape[0]

    def prepare(n, carry):
        kt[n] = kbuf[n].T
        vt[n] = vbuf[n].T
        dk_t[n] = jnp.zeros((HD, width), F32)
        dv_t[n] = jnp.zeros((HD, width), F32)
        return carry

    lax.fori_loop(0, places, prepare, 0)
    lane = lax.broadcasted_iota(jnp.int32, (1, width), 1)

    def slab_pass(a, carry):
        query = qbuf[a]
        grad = gbuf[a]

        def seen(b):
            count = 0
            for f in range(rows):
                for e in range(rows):
                    count = count + table_ref[a * rows + f, b * rows + e]
            return count > 0

        def scores(b, top):
            def live(top):
                place = table_ref[a * rows, 3 * rows + b]
                for e in range(rows):
                    keep = jnp.zeros((1, width), jnp.int32)
                    for f in range(rows):
                        inside = (lane >= f * tile) & (lane < (f + 1) * tile)
                        keep = jnp.where(inside, table_ref[a * rows + f, b * rows + e], keep)
                    mask = jnp.where(keep > 0, 0.0, -jnp.inf)
                    s = nt(kbuf[place, pl.ds(e * tile, tile)], query) + mask
                    s_buf[b, pl.ds(e * tile, tile)] = s
                    top = jnp.maximum(top, jnp.max(s, axis=0, keepdims=True))
                return top

            return lax.cond(seen(b), live, lambda top: top, top)

        top = lax.fori_loop(0, 3, scores, jnp.full((1, width), -jnp.inf, F32))
        ot[...] = jnp.zeros((HD, width), F32)

        def expo(b, total):
            def live(total):
                place = table_ref[a * rows, 3 * rows + b]
                for e in range(rows):
                    at = pl.ds(e * tile, tile)
                    p = jnp.exp2((s_buf[b, at] - top) * FACTOR)
                    total = total + jnp.sum(p, axis=0, keepdims=True)
                    p_buf[b, at] = p.astype(BF16)
                ot[...] += nn(vt[place], p_buf[b])
                return total

            return lax.cond(seen(b), live, lambda total: total, total)

        total = lax.fori_loop(0, 3, expo, jnp.zeros((1, width), F32))
        inv = 1.0 / total
        low_t = (ot[...] * inv).astype(BF16)
        grad_t = grad.T.astype(F32)
        offset = jnp.sum(grad_t * low_t.astype(F32), axis=0, keepdims=True)
        grad_over = (grad_t * inv).astype(BF16)
        query_over = (query.T.astype(F32) * (inv * SCALE)).astype(BF16)
        out = low_t.T
        ot[...] = jnp.zeros((HD, width), F32)

        def backward(b, carry):
            @pl.when(seen(b))
            def _():
                place = table_ref[a * rows, 3 * rows + b]
                for e in range(rows):
                    at = pl.ds(e * tile, tile)
                    p = p_buf[b, at]
                    dp = nt(vbuf[place, at], grad)
                    ds = (p.astype(F32) * (dp - offset)).astype(BF16)
                    ds_buf[at] = ds
                dv_t[place] += nt(grad_over, p_buf[b])
                dk_t[place] += nt(query_over, ds_buf[...])
                ot[...] += nn(kt[place], ds_buf[...])

            return carry

        lax.fori_loop(0, 3, backward, 0)
        dq = (ot[...] * (inv * SCALE)).astype(BF16).T
        for f in range(rows):
            done[a * rows + f, 0] = out[f * tile : (f + 1) * tile]
            done[a * rows + f, 1] = dq[f * tile : (f + 1) * tile]
        return carry

    lax.fori_loop(0, slabs_here, slab_pass, 0)

    for n, sums in enumerate((dk_t, dv_t)):
        for d in range(team):
            local[d, n] = sums[d // rows, :, pl.ds(d % rows * tile, tile)].T
        for m, grads in enumerate((grads_one, grads_two)):
            for e in range(rows):
                terms = sums[slabs_here + m, :, pl.ds(e * tile, tile)]
                grads[e, n] = terms.astype(BF16).T


def attend(rows, tile, slabs_here, table, loads, inputs, spare):
    places = slabs_here + 2
    team = slabs_here * rows
    width = rows * tile
    scores = 3 * slabs_here * width * width

    def head_spec(value, c):
        return pl.BlockSpec((1,) + value.shape[1:], lambda i: (c, 0, 0, 0))

    def whole(shape):
        return pl.BlockSpec(shape, lambda i: (0,) * len(shape))

    shapes = [
        struct((team, 2, tile, HD), BF16),
        struct((team, 2, tile, HD), F32),
        struct((rows, 2, tile, HD), BF16),
        struct((rows, 2, tile, HD), BF16),
    ]
    plan = (loads, slabs_here, len(inputs), len(spare))
    return pl.pallas_call(
        functools.partial(attend_kernel, plan, rows, tile),
        grid=(1,),
        out_shape=shapes,
        in_specs=[SMEM] + [head_spec(value, c) for value, c in inputs] + [ANY] * len(spare),
        out_specs=[whole(shape.shape) for shape in shapes],
        scratch_shapes=[
            pltpu.VMEM((slabs_here, width, HD), BF16),
            pltpu.VMEM((slabs_here, width, HD), BF16),
            pltpu.VMEM((places, width, HD), BF16),
            pltpu.VMEM((places, width, HD), BF16),
            pltpu.VMEM((places, HD, width), BF16),
            pltpu.VMEM((places, HD, width), BF16),
            pltpu.VMEM((places, HD, width), F32),
            pltpu.VMEM((places, HD, width), F32),
            pltpu.VMEM((3, width, width), F32),
            pltpu.VMEM((3, width, width), BF16),
            pltpu.VMEM((width, width), BF16),
            pltpu.VMEM((HD, width), F32),
        ],
        cost_estimate=pl.CostEstimate(
            flops=12 * scores * HD, bytes_accessed=8 * 1024 * 1024, transcendentals=scores
        ),
        compiler_params=PARAMS,
        name="attend",
    )(table, *[value for value, _ in inputs], *spare)


def finish(rows, extras, done, local, grads, spare):
    team, _, tile, _ = done.shape
    step = tile // BLOCKS

    def kernel(done, local, *refs):
        terms, outs = refs[: len(grads)], refs[-team:]
        for d in range(team):
            out = outs[d].at[0]
            for n in range(2):
                out[n] = done[d, n]
                for g in range(BLOCKS):
                    at = pl.ds(g * step, step)
                    total = local[d, n, at]
                    for term, (_, packed), slab in zip(terms, grads, extras):
                        if d // rows != slab:
                            continue
                        if packed:
                            row = pl.ds((2 * (d % rows) + n) * step, step)
                            total = total + term[0, g, row].astype(F32)
                        else:
                            total = total + term[d % rows, n, at].astype(F32)
                    out[2 + n, at] = total.astype(BF16)

    def whole(shape):
        return pl.BlockSpec(shape, lambda i: (0,) * len(shape))

    def grad_spec(value, packed):
        if not packed:
            return whole(value.shape)
        return pl.BlockSpec((1, BLOCKS, 2 * rows * step, HD), lambda i: (0, 0, 1, 0))

    piece = (1, 4, tile, HD)
    return pl.pallas_call(
        kernel,
        grid=(1,),
        out_shape=[struct(piece, BF16)] * team,
        in_specs=[whole(done.shape), whole(local.shape)]
        + [grad_spec(*grad) for grad in grads]
        + [ANY] * len(spare),
        out_specs=[whole(piece)] * team,
        cost_estimate=moved(team * 24 * tile * HD),
        compiler_params=PARAMS,
        name="finish",
    )(done, local, *[value for value, _ in grads], *spare)


def unpack(c, places, pieces, outs, shape):
    tile = shape[1]
    step = tile // BLOCKS
    team = len(pieces)
    held = [] if outs is None else list(outs)

    def kernel(places_ref, *refs):
        for d in range(team):
            lanes = pl.ds(pl.multiple_of(places_ref[d] * HD, HD), HD)
            for n in range(4):
                refs[n - 4][0, :, lanes] = refs[d][0, n]

    return pl.pallas_call(
        kernel,
        grid=(BLOCKS,),
        out_shape=[struct(shape, BF16)] * 4,
        in_specs=[SMEM]
        + [pl.BlockSpec((1, 4, step, HD), lambda i: (0, 0, i, 0))] * team
        + [ANY] * len(held),
        out_specs=[pl.BlockSpec((1, step, team * HD), lambda i: (0, i, c))] * 4,
        input_output_aliases={1 + team + n: n for n in range(len(held))},
        cost_estimate=moved(16 * tile * team * HD),
        compiler_params=PARAMS,
        name="unpack",
    )(places, *pieces, *held)


def body(queries, keys, values, grad_out, window_tiles, window_count):
    rows_here, tile, lane_width = queries.shape
    wmax = window_tiles.shape[1]
    heads = lane_width // HD
    rows = lax.axis_size("sub")
    slabs = lax.axis_size("ctx")
    span = 2 if heads % (2 * rows) == 0 and slabs % 2 == 0 else 1
    team = span * rows
    per = heads // team
    size = slabs * rows
    slab = lax.axis_index("ctx")
    row = lax.axis_index("sub")
    odd = slab % span
    me = odd * rows + row

    def swap(value, d):
        if d == 0:
            return value
        return lax.ppermute(value, RING, [(i, i - i % team + (i % team ^ d)) for i in range(size)])

    def shift(value, way, flip=0):
        pairs = []
        for i in range(size):
            place = i % team // rows
            forward = (place == span - 1) if way == 0 else (place == 0)
            if span == 1:
                forward = way == 0
            j = i + team if forward else i - team
            if 0 <= j < size:
                pairs.append((i, j ^ flip))
        return lax.ppermute(value, RING, pairs)

    places = (window_tiles[0] // rows - slab + 1) * rows + window_tiles[0] % rows
    listed = jnp.arange(wmax) < window_count[0]
    flags = jnp.any(
        (places[None, :] == jnp.arange(3 * rows)[:, None]) & listed[None, :], axis=1
    ).astype(jnp.int32)

    members = jnp.arange(team, dtype=jnp.int32) ^ me
    sources = (keys, values, queries, grad_out)
    kinds = (0, 1, 2, 3)
    every = tuple(range(per))
    far = tuple(range(rows, team))
    step = tile // BLOCKS

    jobs = [(d, (0,), part, part[0] == 0) for part in ((0, 1), (2, 3)) for d in far]
    jobs += [(1, (0,), kinds, True), (0, (0,), kinds, True)]
    packed = pack(jobs, (0,), members, flags, sources, [])
    count = len(far)
    first_kv = [swap(packed[n], d) for n, d in enumerate(far)]
    first_qg = [swap(packed[count + n], d) for n, d in enumerate(far)]
    mates = {0: (packed[-1], swap(packed[-2], 1), 0)}
    sent = {}
    rest = every[1:]
    if rest:
        jobs = [(d, (c,), kinds, False) for c in rest for d in far]
        jobs += [(1, rest, kinds, False), (0, rest, kinds, False)]
        packed = pack(jobs, rest, members, flags, sources, [mates[0][1]])
        sent = {(c, d): packed[m * count + n] for m, c in enumerate(rest) for n, d in enumerate(far)}
        beside = swap(packed[-2], 1)
        mates.update({c: (packed[-1], beside, m) for m, c in enumerate(rest)})

    lists = list(mates[0][:2]) + first_kv
    table = jnp.stack([value[0, 0, -FLAG_ROWS, : 3 * rows] for value in lists]).astype(jnp.int32)
    table = table.reshape(team, 3, rows)
    table = jnp.where(row == 0, table, table[:, :, ::-1])
    if span == 2:
        turned = table[:, ::-1]
        table = jnp.concatenate(
            [
                jnp.where(odd == 0, table[:rows], turned[:rows]),
                jnp.where(odd == 0, turned[rows:], table[rows:]),
            ]
        )
    if span == 1:
        windows = ((1, 0, 2),)
        extras = (0, 0)
    else:
        windows = ((3, 0, 1), (2, 1, 0))
        extras = (0, 1)
    spots = jnp.repeat(jnp.asarray(windows, jnp.int32), rows, axis=0)
    table = jnp.concatenate([table.reshape(team, 3 * rows), spots], axis=1)

    arrived = {}
    halos = {}
    ready = {}
    worked = {}
    home = {}

    def pass_on(c):
        later = [k for k in ((1, 2) if c == 0 else (c + 2,)) if k < per]
        keys = [(k, d) for k in later for d in far]
        pieces = first_kv if c == 0 else [arrived[c, d] for d in far]
        grads = worked[c - 2][2:] if c >= 2 else []
        payloads, passed = relay(
            step,
            mates[c][2],
            mates[c][:2],
            pieces,
            [grads[1], grads[0]] if grads else [],
            [sent[key] for key in keys],
            [],
        )
        ready[c] = payloads[0]
        halos[c] = (shift(payloads[0], 0), shift(payloads[-1], 1))
        for key, payload in zip(keys, passed):
            arrived[key] = swap(payload, key[1])

    def finished(c, spare):
        done, local, grads_one, grads_two = worked[c]
        if c + 2 < per:
            grads = [(halos[c + 2][1], True), (halos[c + 2][0], True)]
        else:
            grads = [(shift(grads_one, 1), False), (shift(grads_two, 0), False)]
        pieces = finish(rows, extras, done, local, grads, spare)
        home[c] = [swap(piece, d) for d, piece in enumerate(pieces)]
        return pieces[0]

    pass_on(0)
    if per > 1:
        pass_on(1)
    for c in every:
        inputs = []
        loads = []

        def add(value, held, wanted, slab_at, tiles):
            for at, (e, kind) in enumerate((e, kind) for e in tiles for kind in wanted):
                loads.append((len(inputs), at, kind, slab_at, e))
            inputs.append((value, held))

        for e in range(rows):
            add(mates[c][e], mates[c][2], "kvqg", 0, [e])
        for n in range(len(far)):
            if c == 0:
                add(first_kv[n], 0, "kv", 1, [n])
                add(first_qg[n], 0, "qg", 1, [n])
            else:
                add(arrived[c, far[n]], 0, "kvqg", 1, [n])
        for n in range(2):
            add(halos[c][n], 0, "kv", span + n, range(rows))
        spare = [ready[c + 1]] if 1 <= c < per - 1 else []
        if c >= 2:
            spare.append(finished(c - 2, [worked[c - 1][0]]))
        worked[c] = attend(rows, tile, span, table, tuple(loads), inputs, spare)
        if c + 2 < per:
            pass_on(c + 2)
    for c in every[-2:]:
        early = [k for k in (c - 2, c - 1) if k in home and (k == c - 2 or c == per - 1)]
        finished(c, [worked[per - 1][0]] + [home[k][d] for k in early for d in far])
    outs = None
    for c in every:
        outs = unpack(c, members, home[c], outs, queries.shape)
    attended, grad_queries, grad_keys, grad_values = outs
    return (attended, grad_queries, grad_keys, grad_values)


def solution(mesh):
    spec = P(("grp", "ctx", "sub"), None, "head")
    return jax.shard_map(
        body,
        mesh=mesh,
        in_specs=(spec, spec, spec, spec, P(("grp", "ctx", "sub"), None), P(("grp", "ctx", "sub"))),
        out_specs=(spec, spec, spec, spec),
        check_vma=False,
    )
```

time: 226 us -> 221 us (0.978)
  the two profiles are of different devices: /device:TPU:0 before, /device:TPU:13 now
where the time goes in v4:
time: 221 us; the launch traced here: 220 us
  Pallas kernels  98.9 us (45%)
  starting transfers between devices  53.2 us (24%)
  waiting for transfers between devices  42.6 us (19%)
  local copies, waits for them, and re-layouts  22.5 us (10%)
    pallas_call x4, Pallas kernels, attend(): pl.pallas_call(functools.partial(attend_kernel, plan, rows, tile), grid=(...  72.4 us
    ppermute x24, waiting for transfers between devices, swap(): lax.ppermute(value, RING, [(i, i - i % team + (i % team ^ d)) for i in ra...  36.8 us
    ppermute x12, starting transfers between devices, shift(): return lax.ppermute(value, RING, pairs)  32.1 us
    unnamed x66, local copies, waits for them, and re-layouts  21.2 us
    ppermute x24, starting transfers between devices, swap(): lax.ppermute(value, RING, [(i, i - i % team + (i % team ^ d)) for i in ra...  21.1 us
    pallas_call x4, Pallas kernels, unpack(): pl.pallas_call(kernel, grid=(BLOCKS,), out_shape=[struct(shape, BF16)] *...  9.58 us
    pallas_call x2, Pallas kernels, pack(): pl.pallas_call(functools.partial(pack_kernel, jobs, step, start), grid=(B...  8.26 us
    pallas_call x4, Pallas kernels, finish(): pl.pallas_call(kernel, grid=(1,), out_shape=[struct(piece, BF16)] * team,...  6.4 us
  transfers between devices with their start and end apart: 36, of which 9 were waited for; matrix products, arithmetic and copies ran while one was open for 1% of the time, Pallas kernels for 42%

profile of v4, /device:TPU:13, one launch (start us, length us, event | category | flops | bytes accessed | tf_op | source)
XLA Modules:
  0.0 220.0 jit_solution(12586804266135697359)
XLA Ops:
  2.1 1.4 copy-done.4
  3.5 1.4 copy-done.5
  4.9 3.4 %pack.2 = (bf16[1,4,208,128]{3,2,1,0:T(8,128)(2,1)S(1)}, bf16[1,4,208,128]{3,2,1,0:T(8,128)(2,1)}, bf16[1,4,192,128]{3,2,1,0:T(8,128)(2,1)}, bf16[1,4,192,128]{3...) custom-call(s32[4]{0:T(128)S(1)} %iota_xor_fusion.places_ref, ...), custom_call_target="tpu_custom_call" | custom-call | bytes 3276800 | tf_op jit(solution)/shard_map/pack/pallas_call | solution.py:62
  9.0 1.2 collective-permute-start.1
  10.8 5.0 %collective-permute-done.1.refs_2_ = bf16[1,4,208,128]{3,2,1,0:T(8,128)(2,1)S(1)} collective-permute-done((bf16[1,4,208,128]{3,2,1,0:T(8,128)(2,1)S(1)}, bf16[1,4,208,128]{3,2,1,0:T(8,128)(2,1)S(1)}, u32[]{:S(2)}, u32[]{:S(2)}) %collective-permute-start.1) | collective-permute-done | bytes 213024 | tf_op jit(solution)/shard_map/ppermute | solution.py:388
  15.9 4.9 %pack.3 = (bf16[1,4,384,128]{3,2,1,0:T(8,128)(2,1)S(1)}, bf16[1,4,384,128]{3,2,1,0:T(8,128)(2,1)S(1)}, bf16[1,4,384,128]{3,2,1,0:T(8,128)(2,1)S(1)}, bf16[1,4,38...) custom-call(s32[4]{0:T(128)S(1)} %iota_xor_fusion.places_ref, ...), custom_call_target="tpu_custom_call" | custom-call | bytes 9437184 | tf_op jit(solution)/shard_map/pack/pallas_call | solution.py:62
  22.3 0.8 copy-done.11
  23.8 0.8 copy-done.24
  24.6 0.7 copy-done.28
  25.3 1.3 collective-permute-start.3
  27.6 1.0 copy-done.8
  28.6 1.0 copy-done.10
  29.6 1.0 copy-done.12
  30.6 1.0 copy-done.15
  31.6 1.9 relay.4
  33.5 0.8 copy-done.13
  35.0 1.2 collective-permute-start.4
  36.6 2.1 collective-permute-start.14
  38.7 3.2 %collective-permute-start.15 = (bf16[1,4,384,128]{3,2,1,0:T(8,128)(2,1)}, bf16[1,4,384,128]{3,2,1,0:T(8,128)(2,1)}, u32[]{:S(2)}, u32[]{:S(2)}) collective-permute-start(bf16[1,4,384,128]{3,2,1,0:T(8,128)(2,1)} %get-tuple-element.99), channel_id=1, source_target_pairs={{0,4},{1,5},{4,8},{5,9},{6,2},{7,3},{8,12},{9,13},{10,6},{11,7},{1... | collective-permute-start | bytes 1179656 | tf_op jit(solution)/shard_map/ppermute | solution.py:400
  42.1 3.7 %collective-permute-done.4.refs_2_ = bf16[1,4,384,128]{3,2,1,0:T(8,128)(2,1)S(1)} collective-permute-done((bf16[1,4,384,128]{3,2,1,0:T(8,128)(2,1)S(1)}, bf16[1,4,384,128]{3,2,1,0:T(8,128)(2,1)S(1)}, u32[]{:S(2)}, u32[]{:S(2)}) %collective-permute-start.4) | collective-permute-done | bytes 393248 | tf_op jit(solution)/shard_map/ppermute | solution.py:388
  46.6 1.2 collective-permute-start.12
  47.8 6.9 %collective-permute-done.5.refs_3_ = bf16[1,4,384,128]{3,2,1,0:T(8,128)(2,1)S(1)} collective-permute-done((bf16[1,4,384,128]{3,2,1,0:T(8,128)(2,1)S(1)}, bf16[1,4,384,128]{3,2,1,0:T(8,128)(2,1)S(1)}, u32[]{:S(2)}, u32[]{:S(2)}) %collective-permute-start.5) | collective-permute-done | bytes 393248 | tf_op jit(solution)/shard_map/ppermute | solution.py:388
  54.7 0.8 copy-done.21
  55.4 1.0 collective-permute-start.13
  57.0 1.1 copy-done.19
  58.1 1.0 copy-done.22
  59.1 1.0 copy-done.25
  60.1 1.0 copy-done.29
  62.0 0.8 copy-done.30
  62.8 1.8 collective-permute-start.11
  64.6 2.1 collective-permute-start.8
  66.7 3.2 %collective-permute-start.9 = (bf16[1,4,384,128]{3,2,1,0:T(8,128)(2,1)S(1)}, bf16[1,4,384,128]{3,2,1,0:T(8,128)(2,1)S(1)}, u32[]{:S(2)}, u32[]{:S(2)}) collective-permute-start(bf16[1,4,384,128]{3,2,1,0:T(8,128)(2,1)S(1)} %get-tuple-element.93), channel_id=1, source_target_pairs={{0,4},{1,5},{4,8},{5,9},{6,2},{7,3},{8,12},{9,13},{10,6},{11,7},{1... | collective-permute-start | bytes 1179656 | tf_op jit(solution)/shard_map/ppermute | solution.py:400
  69.9 17.6 %attend.4 = (bf16[4,2,384,128]{3,2,1,0:T(8,128)(2,1)S(1)}, f32[4,2,384,128]{3,2,1,0:T(8,128)S(1)}, bf16[2,2,384,128]{3,2,1,0:T(8,128)(2,1)S(1)}, bf16[2,2,384,128]{3,2,1,0:T(8,128)(2,1)S(1)}) custom-call(s32[4,9]{1,0:T(4,128)S(1)} %pad_add_fusion.1.table_ref, bf16[1,4,400,128]{3,2,1,0:T(8,128)(2,1)S(1)} %get-tuple-element.76.refs_0_, ...), custom_call_target="tpu_custom_call" | custom-call | flops 5435817984 | bytes 8388608 | tf_op jit(solution)/shard_map/attend/pallas_call | solution.py:269
  87.5 1.1 copy-done.6
  88.8 2.1 collective-permute-start.19
  90.9 3.4 %collective-permute-start.18 = (bf16[1,4,768,128]{3,2,1,0:T(8,128)(2,1)S(1)}, bf16[1,4,768,128]{3,2,1,0:T(8,128)(2,1)S(1)}, u32[]{:S(2)}, u32[]{:S(2)}) collective-permute-start(bf16[1,4,768,128]{3,2,1,0:T(8,128)(2,1)S(1)} %get-tuple-element.102.refs_6_), channel_id=1, source_target_pairs={{2,6},{3,7},{4,0},{5,1},{6,10},{7,11},{8,4},{9,5},{10,14},{11,15},... | collective-permute-start | bytes 2359304 | tf_op jit(solution)/shard_map/ppermute | solution.py:400
  94.6 2.2 %collective-permute-start.7 = (bf16[1,4,384,128]{3,2,1,0:T(8,128)(2,1)S(1)}, bf16[1,4,384,128]{3,2,1,0:T(8,128)(2,1)S(1)}, u32[]{:S(2)}, u32[]{:S(2)}) collective-permute-start(bf16[1,4,384,128]{3,2,1,0:T(8,128)(2,1)S(1)} %copy-done.31), channel_id=1, source_target_pairs={{0,3},{1,2},{2,1},{3,0},{4,7},{5,6},{6,5},{7,4},{8,11},{9,10},{10,... | collective-permute-start | bytes 1179656 | tf_op jit(solution)/shard_map/ppermute | solution.py:388
  96.8 18.2 %attend.5 = (bf16[4,2,384,128]{3,2,1,0:T(8,128)(2,1)S(1)}, f32[4,2,384,128]{3,2,1,0:T(8,128)}, bf16[2,2,384,128]{3,2,1,0:T(8,128)(2,1)S(1)}, bf16[2,2,384,128]{3,2,1,0:T(8,128)(2,1)S(1)}) custom-call(s32[4,9]{1,0:T(4,128)S(1)} %pad_add_fusion.1.table_ref, bf16[3,4,384,128]{3,2,1,0:T(8,128)(2,1)S(1)} %get-tuple-element.80.refs_0_, ...), custom_call_target="tpu_custom_call" | custom-call | flops 5435817984 | bytes 8388608 | tf_op jit(solution)/shard_map/attend/pallas_call | solution.py:269
  115.3 1.9 collective-permute-start.17
  117.2 3.6 %collective-permute-start.16 = (bf16[1,4,768,128]{3,2,1,0:T(8,128)(2,1)S(1)}, bf16[1,4,768,128]{3,2,1,0:T(8,128)(2,1)S(1)}, u32[]{:S(2)}, u32[]{:S(2)}) collective-permute-start(bf16[1,4,768,128]{3,2,1,0:T(8,128)(2,1)S(1)} %get-tuple-element.105.refs_6_), channel_id=1, source_target_pairs={{2,6},{3,7},{4,0},{5,1},{6,10},{7,11},{8,4},{9,5},{10,14},{11,15},... | collective-permute-start | bytes 2359304 | tf_op jit(solution)/shard_map/ppermute | solution.py:400
  120.8 1.6 finish.4
  122.9 1.2 collective-permute-start.27
  124.1 18.4 %attend.6 = (bf16[4,2,384,128]{3,2,1,0:T(8,128)(2,1)S(1)}, f32[4,2,384,128]{3,2,1,0:T(8,128)}, bf16[2,2,384,128]{3,2,1,0:T(8,128)(2,1)S(1)}, bf16[2,2,384,128]{3,2,1,0:T(8,128)(2,1)S(1)}) custom-call(s32[4,9]{1,0:T(4,128)S(1)} %pad_add_fusion.1.table_ref, bf16[3,4,384,128]{3,2,1,0:T(8,128)(2,1)} %copy-done, bf16[3,4,384,128]{3,2,1,0:T(8,128)(2,1)} %copy-done.2, ...), custom_call_target="tpu_custom_call" | custom-call | flops 5435817984 | bytes 8388608 | tf_op jit(solution)/shard_map/attend/pallas_call | solution.py:269
  142.5 1.9 collective-permute-start.24
  144.4 3.4 %collective-permute-start.25 = (bf16[2,2,384,128]{3,2,1,0:T(8,128)(2,1)S(1)}, bf16[2,2,384,128]{3,2,1,0:T(8,128)(2,1)S(1)}, u32[]{:S(2)}, u32[]{:S(2)}) collective-permute-start(bf16[2,2,384,128]{3,2,1,0:T(8,128)(2,1)S(1)} %get-tuple-element.123), channel_id=1, source_target_pairs={{2,6},{3,7},{4,0},{5,1},{6,10},{7,11},{8,4},{9,5},{10,14},{11,15},... | collective-permute-start | bytes 1179656 | tf_op jit(solution)/shard_map/ppermute | solution.py:400
  147.8 1.7 finish.5
  150.2 1.7 collective-permute-start.23
  151.9 18.2 %attend.7 = (bf16[4,2,384,128]{3,2,1,0:T(8,128)(2,1)S(1)}, f32[4,2,384,128]{3,2,1,0:T(8,128)}, bf16[2,2,384,128]{3,2,1,0:T(8,128)(2,1)S(1)}, bf16[2,2,384,128]{3,2,1,0:T(8,128)(2,1)S(1)}) custom-call(s32[4,9]{1,0:T(4,128)S(1)} %pad_add_fusion.1.table_ref, bf16[3,4,384,128]{3,2,1,0:T(8,128)(2,1)S(1)} %copy-done.1, bf16[3,4,384,128]{3,2,1,0:T(8,128)(2,1)} %copy-done.2, ...), custom_call_target="tpu_custom_call" | custom-call | flops 5435817984 | bytes 8388608 | tf_op jit(solution)/shard_map/attend/pallas_call | solution.py:269
  170.2 1.9 collective-permute-start.20
  172.1 3.4 %collective-permute-start.21 = (bf16[2,2,384,128]{3,2,1,0:T(8,128)(2,1)S(1)}, bf16[2,2,384,128]{3,2,1,0:T(8,128)(2,1)S(1)}, u32[]{:S(2)}, u32[]{:S(2)}) collective-permute-start(bf16[2,2,384,128]{3,2,1,0:T(8,128)(2,1)S(1)} %get-tuple-element.118), channel_id=1, source_target_pairs={{2,6},{3,7},{4,0},{5,1},{6,10},{7,11},{8,4},{9,5},{10,14},{11,15},... | collective-permute-start | bytes 1179656 | tf_op jit(solution)/shard_map/ppermute | solution.py:400
  175.5 1.6 finish.6
  177.6 1.3 collective-permute-start.29
  179.0 4.1 %collective-permute-done.20.refs_0_ = bf16[2,2,384,128]{3,2,1,0:T(8,128)(2,1)S(1)} collective-permute-done((bf16[2,2,384,128]{3,2,1,0:T(8,128)(2,1)S(1)}, bf16[2,2,384,128]{3,2,1,0:T(8,128)(2,1)S(1)}, u32[]{:S(2)}, u32[]{:S(2)}) %collective-permute-start.20) | collective-permute-done | bytes 393248 | tf_op jit(solution)/shard_map/ppermute | solution.py:400
  183.5 1.6 collective-permute-done.21.refs_1_
  185.4 2.5 %collective-permute-done.28.refs_5_.refs_2_ = bf16[1,4,384,128]{3,2,1,0:T(8,128)(2,1)S(1)} collective-permute-done((bf16[1,4,384,128]{3,2,1,0:T(8,128)(2,1)S(1)}, bf16[1,4,384,128]{3,2,1,0:T(8,128)(2,1)S(1)}, u32[]{:S(2)}, u32[]{:S(2)}) %collective-permute-start.28) | collective-permute-done | bytes 393248 | tf_op jit(solution)/shard_map/ppermute | solution.py:388
  187.9 8.6 %collective-permute-done.29.refs_6_.refs_3_ = bf16[1,4,384,128]{3,2,1,0:T(8,128)(2,1)S(1)} collective-permute-done((bf16[1,4,384,128]{3,2,1,0:T(8,128)(2,1)S(1)}, bf16[1,4,384,128]{3,2,1,0:T(8,128)(2,1)S(1)}, u32[]{:S(2)}, u32[]{:S(2)}) %collective-permute-start.29) | collective-permute-done | bytes 393248 | tf_op jit(solution)/shard_map/ppermute | solution.py:388
  196.4 1.6 finish.7
  198.6 1.7 collective-permute-start.32
  200.2 2.4 %unpack.4 = (bf16[1,384,2048]{2,1,0:T(8,128)(2,1)}, bf16[1,384,2048]{2,1,0:T(8,128)(2,1)}, bf16[1,384,2048]{2,1,0:T(8,128)(2,1)}, bf16[1,384,2048]{2,1,0:T(8,128)(2,1)}) custom-call(s32[4]{0:T(128)S(1)} %iota_xor_fusion.places_ref, bf16[1,4,384,128]{3,2,1,0:T(8,128)(2,1)S(1)} %get-tuple-element.112.refs_7_.refs_0_, ...), custom_call_target="tpu_custom_call" | custom-call | bytes 3145728 | tf_op jit(solution)/shard_map/unpack/pallas_call | solution.py:355
  202.6 2.4 %unpack.5 = (bf16[1,384,2048]{2,1,0:T(8,128)(2,1)}, bf16[1,384,2048]{2,1,0:T(8,128)(2,1)}, bf16[1,384,2048]{2,1,0:T(8,128)(2,1)}, bf16[1,384,2048]{2,1,0:T(8,128)(2,1)}) custom-call(s32[4]{0:T(128)S(1)} %iota_xor_fusion.places_ref, ...), custom_call_target="tpu_custom_call", output_to_operand_aliasing={{0}: (5, {}), {1}: (6, {}), {2}: (7, {}), {3}: (8, {})} | custom-call | bytes 3145728 | tf_op jit(solution)/shard_map/unpack/pallas_call | solution.py:355
  205.0 2.4 %unpack.6 = (bf16[1,384,2048]{2,1,0:T(8,128)(2,1)}, bf16[1,384,2048]{2,1,0:T(8,128)(2,1)}, bf16[1,384,2048]{2,1,0:T(8,128)(2,1)}, bf16[1,384,2048]{2,1,0:T(8,128)(2,1)}) custom-call(s32[4]{0:T(128)S(1)} %iota_xor_fusion.places_ref, ...), custom_call_target="tpu_custom_call", output_to_operand_aliasing={{0}: (5, {}), {1}: (6, {}), {2}: (7, {}), {3}: (8, {})} | custom-call | bytes 3145728 | tf_op jit(solution)/shard_map/unpack/pallas_call | solution.py:355
  207.4 1.4 collective-permute-done.31.refs_2_
  208.8 8.8 %collective-permute-done.32.refs_3_ = bf16[1,4,384,128]{3,2,1,0:T(8,128)(2,1)S(1)} collective-permute-done((bf16[1,4,384,128]{3,2,1,0:T(8,128)(2,1)S(1)}, bf16[1,4,384,128]{3,2,1,0:T(8,128)(2,1)S(1)}, u32[]{:S(2)}, u32[]{:S(2)}) %collective-permute-start.32) | collective-permute-done | bytes 393248 | tf_op jit(solution)/shard_map/ppermute | solution.py:388
  217.6 2.4 %unpack.7 = (bf16[1,384,2048]{2,1,0:T(8,128)(2,1)}, bf16[1,384,2048]{2,1,0:T(8,128)(2,1)}, bf16[1,384,2048]{2,1,0:T(8,128)(2,1)}, bf16[1,384,2048]{2,1,0:T(8,128)(2,1)}) custom-call(s32[4]{0:T(128)S(1)} %iota_xor_fusion.places_ref, ...), custom_call_target="tpu_custom_call", output_to_operand_aliasing={{0}: (5, {}), {1}: (6, {}), {2}: (7, {}), {3}: (8, {})} | custom-call | bytes 3145728 | tf_op jit(solution)/shard_map/unpack/pallas_call | solution.py:355
  (115 shorter events, 12.8 us)
Async XLA Ops:
  2.1 1.4 copy-start.4
  3.5 1.4 copy-start.5
  8.3 7.6 %collective-permute-start = (bf16[1,4,400,128]{3,2,1,0:T(8,128)(2,1)S(1)}, bf16[1,4,400,128]{3,2,1,0:T(8,128)(2,1)S(1)}, u32[]{:S(2)}, u32[]{:S(2)}) collective-permute-start(bf16[1,4,400,128]{3,2,1,0:T(8,128)(2,1)S(1)} %get-tuple-element.77), channel_id=1, source_target_pairs={{0,1},{1,0},{2,3},{3,2},{4,5},{5,4},{6,7},{7,6},{8,9},{9,8},{10,11... | collective-permute-start | bytes 1228808 | tf_op jit(solution)/shard_map/ppermute | solution.py:388
  9.0 6.8 %collective-permute-start.1 = (bf16[1,4,208,128]{3,2,1,0:T(8,128)(2,1)S(1)}, bf16[1,4,208,128]{3,2,1,0:T(8,128)(2,1)S(1)}, u32[]{:S(2)}, u32[]{:S(2)}) collective-permute-start(bf16[1,4,208,128]{3,2,1,0:T(8,128)(2,1)S(1)} %get-tuple-element.78), channel_id=1, source_target_pairs={{0,2},{1,3},{2,0},{3,1},{4,6},{5,7},{6,4},{7,5},{8,10},{9,11},{10,... | collective-permute-start | bytes 638984 | tf_op jit(solution)/shard_map/ppermute | solution.py:388
  10.2 16.5 %collective-permute-start.2 = (bf16[1,4,208,128]{3,2,1,0:T(8,128)(2,1)}, bf16[1,4,208,128]{3,2,1,0:T(8,128)(2,1)}, u32[]{:S(2)}, u32[]{:S(2)}) collective-permute-start(bf16[1,4,208,128]{3,2,1,0:T(8,128)(2,1)} %get-tuple-element.79), channel_id=1, source_target_pairs={{0,3},{1,2},{2,1},{3,0},{4,7},{5,6},{6,5},{7,4},{8,11},{9,10},{10,... | collective-permute-start | bytes 638984 | tf_op jit(solution)/shard_map/ppermute | solution.py:388
  22.3 0.8 copy-start.11
  23.8 0.8 copy-start.24
  24.6 0.8 copy-start.28
  25.3 89.8 %copy-start = (bf16[3,4,384,128]{3,2,1,0:T(8,128)(2,1)}, bf16[3,4,384,128]{3,2,1,0:T(8,128)(2,1)S(1)}, u32[]{:S(2)}) copy-start(bf16[3,4,384,128]{3,2,1,0:T(8,128)(2,1)S(1)} %get-tuple-element.80.refs_0_) | copy-start | bytes 3538948
  25.3 31.3 %copy-start.32 = (s32[2,3]{1,0:T(2,128)S(1)}, s32[2,3]{1,0:T(2,128)}, u32[]{:S(2)}) copy-start(s32[2,3]{1,0:T(2,128)} %constant.47.clone) | copy-start | bytes 76
  25.3 31.4 %collective-permute-start.3 = (bf16[3,4,384,128]{3,2,1,0:T(8,128)(2,1)}, bf16[3,4,384,128]{3,2,1,0:T(8,128)(2,1)S(1)}, u32[]{:S(2)}, u32[]{:S(2)}) collective-permute-start(bf16[3,4,384,128]{3,2,1,0:T(8,128)(2,1)} %get-tuple-element.81), channel_id=1, source_target_pairs={{0,1},{1,0},{2,3},{3,2},{4,5},{5,4},{6,7},{7,6},{8,9},{9,8},{10,11... | collective-permute-start | bytes 3538952 | tf_op jit(solution)/shard_map/ppermute | solution.py:388
  27.6 1.0 copy-start.8
  28.6 1.0 copy-start.10
  29.6 1.0 copy-start.12
  30.6 1.0 copy-start.15
  33.5 0.8 copy-start.13
  34.3 0.8 copy-start.16
  35.0 10.8 %collective-permute-start.4 = (bf16[1,4,384,128]{3,2,1,0:T(8,128)(2,1)S(1)}, bf16[1,4,384,128]{3,2,1,0:T(8,128)(2,1)S(1)}, u32[]{:S(2)}, u32[]{:S(2)}) collective-permute-start(bf16[1,4,384,128]{3,2,1,0:T(8,128)(2,1)S(1)} %get-tuple-element.86), channel_id=1, source_target_pairs={{0,2},{1,3},{2,0},{3,1},{4,6},{5,7},{6,4},{7,5},{8,10},{9,11},{10,... | collective-permute-start | bytes 1179656 | tf_op jit(solution)/shard_map/ppermute | solution.py:388
  36.2 18.4 %collective-permute-start.5 = (bf16[1,4,384,128]{3,2,1,0:T(8,128)(2,1)S(1)}, bf16[1,4,384,128]{3,2,1,0:T(8,128)(2,1)S(1)}, u32[]{:S(2)}, u32[]{:S(2)}) collective-permute-start(bf16[1,4,384,128]{3,2,1,0:T(8,128)(2,1)S(1)} %get-tuple-element.87), channel_id=1, source_target_pairs={{0,3},{1,2},{2,1},{3,0},{4,7},{5,6},{6,5},{7,4},{8,11},{9,10},{10,... | collective-permute-start | bytes 1179656 | tf_op jit(solution)/shard_map/ppermute | solution.py:388
  36.6 30.0 %collective-permute-start.14 = (bf16[1,4,384,128]{3,2,1,0:T(8,128)(2,1)}, bf16[1,4,384,128]{3,2,1,0:T(8,128)(2,1)}, u32[]{:S(2)}, u32[]{:S(2)}) collective-permute-start(bf16[1,4,384,128]{3,2,1,0:T(8,128)(2,1)} %get-tuple-element.98), channel_id=1, source_target_pairs={{2,6},{3,7},{4,0},{5,1},{6,10},{7,11},{8,4},{9,5},{10,14},{11,15},... | collective-permute-start | bytes 1179656 | tf_op jit(solution)/shard_map/ppermute | solution.py:400
  38.7 31.2 %collective-permute-start.15 = (bf16[1,4,384,128]{3,2,1,0:T(8,128)(2,1)}, bf16[1,4,384,128]{3,2,1,0:T(8,128)(2,1)}, u32[]{:S(2)}, u32[]{:S(2)}) collective-permute-start(bf16[1,4,384,128]{3,2,1,0:T(8,128)(2,1)} %get-tuple-element.99), channel_id=1, source_target_pairs={{0,4},{1,5},{4,8},{5,9},{6,2},{7,3},{8,12},{9,13},{10,6},{11,7},{1... | collective-permute-start | bytes 1179656 | tf_op jit(solution)/shard_map/ppermute | solution.py:400
  46.6 16.2 %collective-permute-start.12 = (bf16[1,4,192,128]{3,2,1,0:T(8,128)(2,1)}, bf16[1,4,192,128]{3,2,1,0:T(8,128)(2,1)}, u32[]{:S(2)}, u32[]{:S(2)}) collective-permute-start(bf16[1,4,192,128]{3,2,1,0:T(8,128)(2,1)} %get-tuple-element.96), channel_id=1, source_target_pairs={{0,2},{1,3},{2,0},{3,1},{4,6},{5,7},{6,4},{7,5},{8,10},{9,11},{10,... | collective-permute-start | bytes 589832 | tf_op jit(solution)/shard_map/ppermute | solution.py:388
  54.7 0.8 copy-start.21
  55.4 9.1 %collective-permute-start.13 = (bf16[1,4,192,128]{3,2,1,0:T(8,128)(2,1)}, bf16[1,4,192,128]{3,2,1,0:T(8,128)(2,1)}, u32[]{:S(2)}, u32[]{:S(2)}) collective-permute-start(bf16[1,4,192,128]{3,2,1,0:T(8,128)(2,1)} %get-tuple-element.97), channel_id=1, source_target_pairs={{0,3},{1,2},{2,1},{3,0},{4,7},{5,6},{6,5},{7,4},{8,11},{9,10},{10,... | collective-permute-start | bytes 589832 | tf_op jit(solution)/shard_map/ppermute | solution.py:388
  56.7 31.9 %copy-start.2 = (bf16[3,4,384,128]{3,2,1,0:T(8,128)(2,1)}, bf16[3,4,384,128]{3,2,1,0:T(8,128)(2,1)S(1)}, u32[]{:S(2)}) copy-start(bf16[3,4,384,128]{3,2,1,0:T(8,128)(2,1)S(1)} %collective-permute-done.3.refs_1_) | copy-start | bytes 3538948
  56.7 31.9 %collective-permute-start.10 = (bf16[1,4,384,128]{3,2,1,0:T(8,128)(2,1)}, bf16[1,4,384,128]{3,2,1,0:T(8,128)(2,1)S(1)}, u32[]{:S(2)}, u32[]{:S(2)}) collective-permute-start(bf16[1,4,384,128]{3,2,1,0:T(8,128)(2,1)} %copy-done.13), channel_id=1, source_target_pairs={{0,2},{1,3},{2,0},{3,1},{4,6},{5,7},{6,4},{7,5},{8,10},{9,11},{10,... | collective-permute-start | bytes 1179656 | tf_op jit(solution)/shard_map/ppermute | solution.py:388
  57.0 1.1 copy-start.19
  58.1 1.0 copy-start.22
  59.1 1.0 copy-start.25
  60.1 1.0 copy-start.29
  61.1 1.6 copy-start.17
  62.0 0.8 copy-start.30
  62.8 25.9 %collective-permute-start.11 = (bf16[1,4,384,128]{3,2,1,0:T(8,128)(2,1)S(1)}, bf16[1,4,384,128]{3,2,1,0:T(8,128)(2,1)S(1)}, u32[]{:S(2)}, u32[]{:S(2)}) collective-permute-start(bf16[1,4,384,128]{3,2,1,0:T(8,128)(2,1)S(1)} %copy-done.17), channel_id=1, source_target_pairs={{0,3},{1,2},{2,1},{3,0},{4,7},{5,6},{6,5},{7,4},{8,11},{9,10},{10,... | collective-permute-start | bytes 1179656 | tf_op jit(solution)/shard_map/ppermute | solution.py:388
  64.6 30.0 %collective-permute-start.8 = (bf16[1,4,384,128]{3,2,1,0:T(8,128)(2,1)S(1)}, bf16[1,4,384,128]{3,2,1,0:T(8,128)(2,1)S(1)}, u32[]{:S(2)}, u32[]{:S(2)}) collective-permute-start(bf16[1,4,384,128]{3,2,1,0:T(8,128)(2,1)S(1)} %get-tuple-element.92), channel_id=1, source_target_pairs={{2,6},{3,7},{4,0},{5,1},{6,10},{7,11},{8,4},{9,5},{10,14},{11,15},... | collective-permute-start | bytes 1179656 | tf_op jit(solution)/shard_map/ppermute | solution.py:400
  66.7 30.1 %collective-permute-start.9 = (bf16[1,4,384,128]{3,2,1,0:T(8,128)(2,1)S(1)}, bf16[1,4,384,128]{3,2,1,0:T(8,128)(2,1)S(1)}, u32[]{:S(2)}, u32[]{:S(2)}) collective-permute-start(bf16[1,4,384,128]{3,2,1,0:T(8,128)(2,1)S(1)} %get-tuple-element.93), channel_id=1, source_target_pairs={{0,4},{1,5},{4,8},{5,9},{6,2},{7,3},{8,12},{9,13},{10,6},{11,7},{1... | collective-permute-start | bytes 1179656 | tf_op jit(solution)/shard_map/ppermute | solution.py:400
  87.5 1.1 copy-start.6
  88.6 5.7 %copy-start.27 = (bf16[1,4,384,128]{3,2,1,0:T(8,128)(2,1)S(1)}, bf16[1,4,384,128]{3,2,1,0:T(8,128)(2,1)}, u32[]{:S(2)}) copy-start(bf16[1,4,384,128]{3,2,1,0:T(8,128)(2,1)} %copy-done.26) | copy-start | bytes 1179652
  88.6 6.0 %copy-start.31 = (bf16[1,4,384,128]{3,2,1,0:T(8,128)(2,1)S(1)}, bf16[1,4,384,128]{3,2,1,0:T(8,128)(2,1)}, u32[]{:S(2)}) copy-start(bf16[1,4,384,128]{3,2,1,0:T(8,128)(2,1)} %copy-done.30) | copy-start | bytes 1179652
  88.6 8.2 %copy-start.20 = (bf16[1,4,384,128]{3,2,1,0:T(8,128)(2,1)S(1)}, bf16[1,4,384,128]{3,2,1,0:T(8,128)(2,1)}, u32[]{:S(2)}) copy-start(bf16[1,4,384,128]{3,2,1,0:T(8,128)(2,1)} %copy-done.18) | copy-start | bytes 1179652
  88.6 8.2 %copy-start.23 = (bf16[1,4,384,128]{3,2,1,0:T(8,128)(2,1)S(1)}, bf16[1,4,384,128]{3,2,1,0:T(8,128)(2,1)}, u32[]{:S(2)}) copy-start(bf16[1,4,384,128]{3,2,1,0:T(8,128)(2,1)} %copy-done.21) | copy-start | bytes 1179652
  88.8 32.0 %collective-permute-start.19 = (bf16[1,4,768,128]{3,2,1,0:T(8,128)(2,1)S(1)}, bf16[1,4,768,128]{3,2,1,0:T(8,128)(2,1)S(1)}, u32[]{:S(2)}, u32[]{:S(2)}) collective-permute-start(bf16[1,4,768,128]{3,2,1,0:T(8,128)(2,1)S(1)} %get-tuple-element.109), channel_id=1, source_target_pairs={{0,4},{1,5},{4,8},{5,9},{6,2},{7,3},{8,12},{9,13},{10,6},{11,7},{1... | collective-permute-start | bytes 2359304 | tf_op jit(solution)/shard_map/ppermute | solution.py:400
  90.9 29.9 %collective-permute-start.18 = (bf16[1,4,768,128]{3,2,1,0:T(8,128)(2,1)S(1)}, bf16[1,4,768,128]{3,2,1,0:T(8,128)(2,1)S(1)}, u32[]{:S(2)}, u32[]{:S(2)}) collective-permute-start(bf16[1,4,768,128]{3,2,1,0:T(8,128)(2,1)S(1)} %get-tuple-element.102.refs_6_), channel_id=1, source_target_pairs={{2,6},{3,7},{4,0},{5,1},{6,10},{7,11},{8,4},{9,5},{10,14},{11,15},... | collective-permute-start | bytes 2359304 | tf_op jit(solution)/shard_map/ppermute | solution.py:400
  94.3 20.8 %collective-permute-start.6 = (bf16[1,4,384,128]{3,2,1,0:T(8,128)(2,1)S(1)}, bf16[1,4,384,128]{3,2,1,0:T(8,128)(2,1)S(1)}, u32[]{:S(2)}, u32[]{:S(2)}) collective-permute-start(bf16[1,4,384,128]{3,2,1,0:T(8,128)(2,1)S(1)} %copy-done.27), channel_id=1, source_target_pairs={{0,2},{1,3},{2,0},{3,1},{4,6},{5,7},{6,4},{7,5},{8,10},{9,11},{10,... | collective-permute-start | bytes 1179656 | tf_op jit(solution)/shard_map/ppermute | solution.py:388
  94.6 20.5 %copy-start.3 = (bf16[3,4,384,128]{3,2,1,0:T(8,128)(2,1)S(1)}, bf16[3,4,384,128]{3,2,1,0:T(8,128)(2,1)}, u32[]{:S(2)}) copy-start(bf16[3,4,384,128]{3,2,1,0:T(8,128)(2,1)} %copy-done.2) | copy-start | bytes 3538948
  94.6 20.5 %collective-permute-start.7 = (bf16[1,4,384,128]{3,2,1,0:T(8,128)(2,1)S(1)}, bf16[1,4,384,128]{3,2,1,0:T(8,128)(2,1)S(1)}, u32[]{:S(2)}, u32[]{:S(2)}) collective-permute-start(bf16[1,4,384,128]{3,2,1,0:T(8,128)(2,1)S(1)} %copy-done.31), channel_id=1, source_target_pairs={{0,3},{1,2},{2,1},{3,0},{4,7},{5,6},{6,5},{7,4},{8,11},{9,10},{10,... | collective-permute-start | bytes 1179656 | tf_op jit(solution)/shard_map/ppermute | solution.py:388
  115.3 29.1 %collective-permute-start.17 = (bf16[1,4,768,128]{3,2,1,0:T(8,128)(2,1)S(1)}, bf16[1,4,768,128]{3,2,1,0:T(8,128)(2,1)S(1)}, u32[]{:S(2)}, u32[]{:S(2)}) collective-permute-start(bf16[1,4,768,128]{3,2,1,0:T(8,128)(2,1)S(1)} %get-tuple-element.106), channel_id=1, source_target_pairs={{0,4},{1,5},{4,8},{5,9},{6,2},{7,3},{8,12},{9,13},{10,6},{11,7},{1... | collective-permute-start | bytes 2359304 | tf_op jit(solution)/shard_map/ppermute | solution.py:400
  117.2 30.6 %collective-permute-start.16 = (bf16[1,4,768,128]{3,2,1,0:T(8,128)(2,1)S(1)}, bf16[1,4,768,128]{3,2,1,0:T(8,128)(2,1)S(1)}, u32[]{:S(2)}, u32[]{:S(2)}) collective-permute-start(bf16[1,4,768,128]{3,2,1,0:T(8,128)(2,1)S(1)} %get-tuple-element.105.refs_6_), channel_id=1, source_target_pairs={{2,6},{3,7},{4,0},{5,1},{6,10},{7,11},{8,4},{9,5},{10,14},{11,15},... | collective-permute-start | bytes 2359304 | tf_op jit(solution)/shard_map/ppermute | solution.py:400
  122.4 27.9 %collective-permute-start.26 = (bf16[1,4,384,128]{3,2,1,0:T(8,128)(2,1)S(1)}, bf16[1,4,384,128]{3,2,1,0:T(8,128)(2,1)S(1)}, u32[]{:S(2)}, u32[]{:S(2)}) collective-permute-start(bf16[1,4,384,128]{3,2,1,0:T(8,128)(2,1)S(1)} %get-tuple-element.124), channel_id=1, source_target_pairs={{0,2},{1,3},{2,0},{3,1},{4,6},{5,7},{6,4},{7,5},{8,10},{9,11},{10,... | collective-permute-start | bytes 1179656 | tf_op jit(solution)/shard_map/ppermute | solution.py:388
  122.9 47.3 %collective-permute-start.27 = (bf16[1,4,384,128]{3,2,1,0:T(8,128)(2,1)S(1)}, bf16[1,4,384,128]{3,2,1,0:T(8,128)(2,1)S(1)}, u32[]{:S(2)}, u32[]{:S(2)}) collective-permute-start(bf16[1,4,384,128]{3,2,1,0:T(8,128)(2,1)S(1)} %get-tuple-element.125), channel_id=1, source_target_pairs={{0,3},{1,2},{2,1},{3,0},{4,7},{5,6},{6,5},{7,4},{8,11},{9,10},{10,... | collective-permute-start | bytes 1179656 | tf_op jit(solution)/shard_map/ppermute | solution.py:388
  142.5 29.6 %collective-permute-start.24 = (bf16[2,2,384,128]{3,2,1,0:T(8,128)(2,1)S(1)}, bf16[2,2,384,128]{3,2,1,0:T(8,128)(2,1)S(1)}, u32[]{:S(2)}, u32[]{:S(2)}) collective-permute-start(bf16[2,2,384,128]{3,2,1,0:T(8,128)(2,1)S(1)} %get-tuple-element.122), channel_id=1, source_target_pairs={{0,4},{1,5},{4,8},{5,9},{6,2},{7,3},{8,12},{9,13},{10,6},{11,7},{1... | collective-permute-start | bytes 1179656 | tf_op jit(solution)/shard_map/ppermute | solution.py:400
  144.4 31.1 %collective-permute-start.25 = (bf16[2,2,384,128]{3,2,1,0:T(8,128)(2,1)S(1)}, bf16[2,2,384,128]{3,2,1,0:T(8,128)(2,1)S(1)}, u32[]{:S(2)}, u32[]{:S(2)}) collective-permute-start(bf16[2,2,384,128]{3,2,1,0:T(8,128)(2,1)S(1)} %get-tuple-element.123), channel_id=1, source_target_pairs={{2,6},{3,7},{4,0},{5,1},{6,10},{7,11},{8,4},{9,5},{10,14},{11,15},... | collective-permute-start | bytes 1179656 | tf_op jit(solution)/shard_map/ppermute | solution.py:400
  147.8 4.1 %copy-start.1 = (bf16[3,4,384,128]{3,2,1,0:T(8,128)(2,1)S(1)}, bf16[3,4,384,128]{3,2,1,0:T(8,128)(2,1)}, u32[]{:S(2)}) copy-start(bf16[3,4,384,128]{3,2,1,0:T(8,128)(2,1)} %copy-done) | copy-start | bytes 3538948
  149.5 28.1 %collective-permute-start.22 = (bf16[1,4,384,128]{3,2,1,0:T(8,128)(2,1)S(1)}, bf16[1,4,384,128]{3,2,1,0:T(8,128)(2,1)S(1)}, u32[]{:S(2)}, u32[]{:S(2)}) collective-permute-start(bf16[1,4,384,128]{3,2,1,0:T(8,128)(2,1)S(1)} %get-tuple-element.119), channel_id=1, source_target_pairs={{0,2},{1,3},{2,0},{3,1},{4,6},{5,7},{6,4},{7,5},{8,10},{9,11},{10,... | collective-permute-start | bytes 1179656 | tf_op jit(solution)/shard_map/ppermute | solution.py:388
  150.2 28.6 %collective-permute-start.23 = (bf16[1,4,384,128]{3,2,1,0:T(8,128)(2,1)S(1)}, bf16[1,4,384,128]{3,2,1,0:T(8,128)(2,1)S(1)}, u32[]{:S(2)}, u32[]{:S(2)}) collective-permute-start(bf16[1,4,384,128]{3,2,1,0:T(8,128)(2,1)S(1)} %get-tuple-element.120), channel_id=1, source_target_pairs={{0,3},{1,2},{2,1},{3,0},{4,7},{5,6},{6,5},{7,4},{8,11},{9,10},{10,... | collective-permute-start | bytes 1179656 | tf_op jit(solution)/shard_map/ppermute | solution.py:388
  170.2 13.0 %collective-permute-start.20 = (bf16[2,2,384,128]{3,2,1,0:T(8,128)(2,1)S(1)}, bf16[2,2,384,128]{3,2,1,0:T(8,128)(2,1)S(1)}, u32[]{:S(2)}, u32[]{:S(2)}) collective-permute-start(bf16[2,2,384,128]{3,2,1,0:T(8,128)(2,1)S(1)} %get-tuple-element.117), channel_id=1, source_target_pairs={{0,4},{1,5},{4,8},{5,9},{6,2},{7,3},{8,12},{9,13},{10,6},{11,7},{1... | collective-permute-start | bytes 1179656 | tf_op jit(solution)/shard_map/ppermute | solution.py:400
  172.1 13.0 %collective-permute-start.21 = (bf16[2,2,384,128]{3,2,1,0:T(8,128)(2,1)S(1)}, bf16[2,2,384,128]{3,2,1,0:T(8,128)(2,1)S(1)}, u32[]{:S(2)}, u32[]{:S(2)}) collective-permute-start(bf16[2,2,384,128]{3,2,1,0:T(8,128)(2,1)S(1)} %get-tuple-element.118), channel_id=1, source_target_pairs={{2,6},{3,7},{4,0},{5,1},{6,10},{7,11},{8,4},{9,5},{10,14},{11,15},... | collective-permute-start | bytes 1179656 | tf_op jit(solution)/shard_map/ppermute | solution.py:400
  177.1 10.8 %collective-permute-start.28 = (bf16[1,4,384,128]{3,2,1,0:T(8,128)(2,1)S(1)}, bf16[1,4,384,128]{3,2,1,0:T(8,128)(2,1)S(1)}, u32[]{:S(2)}, u32[]{:S(2)}) collective-permute-start(bf16[1,4,384,128]{3,2,1,0:T(8,128)(2,1)S(1)} %get-tuple-element.126), channel_id=1, source_target_pairs={{0,2},{1,3},{2,0},{3,1},{4,6},{5,7},{6,4},{7,5},{8,10},{9,11},{10,... | collective-permute-start | bytes 1179656 | tf_op jit(solution)/shard_map/ppermute | solution.py:388
  177.6 18.9 %collective-permute-start.29 = (bf16[1,4,384,128]{3,2,1,0:T(8,128)(2,1)S(1)}, bf16[1,4,384,128]{3,2,1,0:T(8,128)(2,1)S(1)}, u32[]{:S(2)}, u32[]{:S(2)}) collective-permute-start(bf16[1,4,384,128]{3,2,1,0:T(8,128)(2,1)S(1)} %get-tuple-element.127), channel_id=1, source_target_pairs={{0,3},{1,2},{2,1},{3,0},{4,7},{5,6},{6,5},{7,4},{8,11},{9,10},{10,... | collective-permute-start | bytes 1179656 | tf_op jit(solution)/shard_map/ppermute | solution.py:388
  178.8 19.7 %collective-permute-start.35 = (bf16[1,4,384,128]{3,2,1,0:T(8,128)(2,1)S(1)}, bf16[1,4,384,128]{3,2,1,0:T(8,128)(2,1)S(1)}, u32[]{:S(2)}, u32[]{:S(2)}) collective-permute-start(bf16[1,4,384,128]{3,2,1,0:T(8,128)(2,1)S(1)} %get-tuple-element.135), channel_id=1, source_target_pairs={{0,1},{1,0},{2,3},{3,2},{4,5},{5,4},{6,7},{7,6},{8,9},{9,8},{10,11... | collective-permute-start | bytes 1179656 | tf_op jit(solution)/shard_map/ppermute | solution.py:388
  183.1 19.5 %collective-permute-start.34 = (bf16[1,4,384,128]{3,2,1,0:T(8,128)(2,1)S(1)}, bf16[1,4,384,128]{3,2,1,0:T(8,128)(2,1)S(1)}, u32[]{:S(2)}, u32[]{:S(2)}) collective-permute-start(bf16[1,4,384,128]{3,2,1,0:T(8,128)(2,1)S(1)} %get-tuple-element.134), channel_id=1, source_target_pairs={{0,1},{1,0},{2,3},{3,2},{4,5},{5,4},{6,7},{7,6},{8,9},{9,8},{10,11... | collective-permute-start | bytes 1179656 | tf_op jit(solution)/shard_map/ppermute | solution.py:388
  185.1 19.9 %collective-permute-start.33 = (bf16[1,4,384,128]{3,2,1,0:T(8,128)(2,1)S(1)}, bf16[1,4,384,128]{3,2,1,0:T(8,128)(2,1)S(1)}, u32[]{:S(2)}, u32[]{:S(2)}) collective-permute-start(bf16[1,4,384,128]{3,2,1,0:T(8,128)(2,1)S(1)} %get-tuple-element.133), channel_id=1, source_target_pairs={{0,1},{1,0},{2,3},{3,2},{4,5},{5,4},{6,7},{7,6},{8,9},{9,8},{10,11... | collective-permute-start | bytes 1179656 | tf_op jit(solution)/shard_map/ppermute | solution.py:388
  198.0 9.4 %collective-permute-start.30 = (bf16[1,4,384,128]{3,2,1,0:T(8,128)(2,1)S(1)}, bf16[1,4,384,128]{3,2,1,0:T(8,128)(2,1)S(1)}, u32[]{:S(2)}, u32[]{:S(2)}) collective-permute-start(bf16[1,4,384,128]{3,2,1,0:T(8,128)(2,1)S(1)} %get-tuple-element.129), channel_id=1, source_target_pairs={{0,1},{1,0},{2,3},{3,2},{4,5},{5,4},{6,7},{7,6},{8,9},{9,8},{10,11... | collective-permute-start | bytes 1179656 | tf_op jit(solution)/shard_map/ppermute | solution.py:388
  198.3 10.5 %collective-permute-start.31 = (bf16[1,4,384,128]{3,2,1,0:T(8,128)(2,1)S(1)}, bf16[1,4,384,128]{3,2,1,0:T(8,128)(2,1)S(1)}, u32[]{:S(2)}, u32[]{:S(2)}) collective-permute-start(bf16[1,4,384,128]{3,2,1,0:T(8,128)(2,1)S(1)} %get-tuple-element.130), channel_id=1, source_target_pairs={{0,2},{1,3},{2,0},{3,1},{4,6},{5,7},{6,4},{7,5},{8,10},{9,11},{10,... | collective-permute-start | bytes 1179656 | tf_op jit(solution)/shard_map/ppermute | solution.py:388
  198.6 19.0 %collective-permute-start.32 = (bf16[1,4,384,128]{3,2,1,0:T(8,128)(2,1)S(1)}, bf16[1,4,384,128]{3,2,1,0:T(8,128)(2,1)S(1)}, u32[]{:S(2)}, u32[]{:S(2)}) collective-permute-start(bf16[1,4,384,128]{3,2,1,0:T(8,128)(2,1)S(1)} %get-tuple-element.131), channel_id=1, source_target_pairs={{0,3},{1,2},{2,1},{3,0},{4,7},{5,6},{6,5},{7,4},{8,11},{9,10},{10,... | collective-permute-start | bytes 1179656 | tf_op jit(solution)/shard_map/ppermute | solution.py:388
  (5 other events, 3.7 us)

commit v5 on v4

--- a/solution.py
+++ b/solution.py
@@ -18,11 +18,16 @@
 FACTOR = SCALE * math.log2(math.e)
 ANY = pl.BlockSpec(memory_space=pl.ANY)
 SMEM = pl.BlockSpec(memory_space=pltpu.SMEM)
-PARAMS = pltpu.CompilerParams(vmem_limit_bytes=48 * 1024 * 1024)
+PARAMS = pltpu.CompilerParams(vmem_limit_bytes=34 * 1024 * 1024)
+LIGHT = pltpu.CompilerParams(vmem_limit_bytes=20 * 1024 * 1024)
 
 
 def struct(shape, dtype):
     return jax.ShapeDtypeStruct(shape, dtype)
+
+
+def hbm(values):
+    return [pltpu.with_memory_space_constraint(value, pltpu.HBM) for value in values]
 
 
 def moved(nbytes):
@@ -70,9 +75,9 @@
             pl.BlockSpec((shape[0], 1, shape[2], HD), lambda i: (0, i, 0, 0)) for shape in shapes
         ],
         cost_estimate=moved(sum(4 * HD * math.prod(shape[:3]) for shape in shapes)),
-        compiler_params=PARAMS,
+        compiler_params=LIGHT,
         name="pack",
-    )(places, flags, *sources, *spare)
+    )(places, flags, *hbm(sources), *spare)
 
 
 def relay_kernel(step, rows, near, far, grads, outs):
@@ -87,7 +92,7 @@
                         out[0, g, at] = grad[e, n, pl.ds(g * step, step)]
 
 
-def relay(step, held, near, far, grads, passed, spare):
+def relay(step, held, near, far, grads, spare):
     rows = len(near)
     kinds = 2 if far else 1
     high = (4 if grads else 2) * rows * step
@@ -97,32 +102,28 @@
         near_refs = [(refs.pop(0), 0) for _ in range(rows)]
         far_refs = [(refs.pop(0), 0) for _ in far]
         grad_refs = [refs.pop(0) for _ in grads] or [None] * kinds
-        outs = refs[len(passed) + len(spare) :][:kinds]
+        outs = refs[len(spare) :]
         relay_kernel(step, rows, near_refs, far_refs, grad_refs, outs)
 
     def whole(shape):
         return pl.BlockSpec(shape, lambda i: (0,) * len(shape))
 
-    before = rows + len(far) + len(grads)
     shape = (1, BLOCKS, high, HD)
-    outs = pl.pallas_call(
+    return pl.pallas_call(
         kernel,
         grid=(1,),
-        out_shape=[struct(shape, BF16)] * kinds
-        + [struct(value.shape, value.dtype) for value in passed],
+        out_shape=[struct(shape, BF16)] * kinds,
         in_specs=[
             pl.BlockSpec((1, BLOCKS, 2 * step, HD), lambda i, at=at: (at, 0, 0, 0))
             for at in [held] * rows + [0] * len(far)
         ]
         + [whole(value.shape) for value in grads]
-        + [ANY] * (len(passed) + len(spare)),
-        out_specs=[whole(shape)] * kinds + [ANY] * len(passed),
-        input_output_aliases={before + n: kinds + n for n in range(len(passed))},
+        + [ANY] * len(spare),
+        out_specs=[whole(shape)] * kinds,
         cost_estimate=moved(kinds * 4 * BLOCKS * high * HD),
-        compiler_params=PARAMS,
+        compiler_params=LIGHT,
         name="relay",
-    )(*near, *far, *grads, *passed, *spare)
-    return outs[:kinds], outs[kinds:]
+    )(*near, *far, *grads, *spare)
 
 
 def nt(a, b):
@@ -335,7 +336,7 @@
         + [ANY] * len(spare),
         out_specs=[whole(piece)] * team,
         cost_estimate=moved(team * 24 * tile * HD),
-        compiler_params=PARAMS,
+        compiler_params=LIGHT,
         name="finish",
     )(done, local, *[value for value, _ in grads], *spare)
 
@@ -362,7 +363,7 @@
         out_specs=[pl.BlockSpec((1, step, team * HD), lambda i: (0, i, c))] * 4,
         input_output_aliases={1 + team + n: n for n in range(len(held))},
         cost_estimate=moved(16 * tile * team * HD),
-        compiler_params=PARAMS,
+        compiler_params=LIGHT,
         name="unpack",
     )(places, *pieces, *held)
 
@@ -450,30 +451,20 @@
     spots = jnp.repeat(jnp.asarray(windows, jnp.int32), rows, axis=0)
     table = jnp.concatenate([table.reshape(team, 3 * rows), spots], axis=1)
 
-    arrived = {}
+    arrived = {key: swap(value, key[1]) for key, value in sent.items()}
     halos = {}
     ready = {}
     worked = {}
     home = {}
 
-    def pass_on(c):
-        later = [k for k in ((1, 2) if c == 0 else (c + 2,)) if k < per]
-        keys = [(k, d) for k in later for d in far]
+    def pass_on(c, spare):
         pieces = first_kv if c == 0 else [arrived[c, d] for d in far]
         grads = worked[c - 2][2:] if c >= 2 else []
-        payloads, passed = relay(
-            step,
-            mates[c][2],
-            mates[c][:2],
-            pieces,
-            [grads[1], grads[0]] if grads else [],
-            [sent[key] for key in keys],
-            [],
+        payloads = relay(
+            step, mates[c][2], mates[c][:2], pieces, [grads[1], grads[0]] if grads else [], spare
         )
         ready[c] = payloads[0]
         halos[c] = (shift(payloads[0], 0), shift(payloads[-1], 1))
-        for key, payload in zip(keys, passed):
-            arrived[key] = swap(payload, key[1])
 
     def finished(c, spare):
         done, local, grads_one, grads_two = worked[c]
@@ -485,9 +476,7 @@
         home[c] = [swap(piece, d) for d, piece in enumerate(pieces)]
         return pieces[0]
 
-    pass_on(0)
-    if per > 1:
-        pass_on(1)
+    pass_on(0, [])
     for c in every:
         inputs = []
         loads = []
@@ -511,8 +500,10 @@
         if c >= 2:
             spare.append(finished(c - 2, [worked[c - 1][0]]))
         worked[c] = attend(rows, tile, span, table, tuple(loads), inputs, spare)
+        if c == 0 and per > 1:
+            pass_on(1, [worked[0][0]])
         if c + 2 < per:
-            pass_on(c + 2)
+            pass_on(c + 2, [])
     for c in every[-2:]:
         early = [k for k in (c - 2, c - 1) if k in home and (k == c - 2 or c == per - 1)]
         finished(c, [worked[per - 1][0]] + [home[k][d] for k in early for d in far])

time: 221 us -> 202 us (0.914)
  the two profiles are of different devices: /device:TPU:13 before, /device:TPU:0 now
where the time goes in v5:
time: 202 us; the launch traced here: 201 us
  Pallas kernels  79.8 us (40%)
  starting transfers between devices  62.9 us (31%)
  waiting for transfers between devices  49.3 us (24%)
  local copies, waits for them, and re-layouts  6.11 us (3%)
    pallas_call x4, Pallas kernels, attend(): pl.pallas_call(functools.partial(attend_kernel, plan, rows, tile), grid=(...  59.4 us
    ppermute x12, starting transfers between devices, shift(): return lax.ppermute(value, RING, pairs)  42.5 us
    ppermute x24, waiting for transfers between devices, swap(): lax.ppermute(value, RING, [(i, i - i % team + (i % team ^ d)) for i in ra...  40.7 us
    ppermute x24, starting transfers between devices, swap(): lax.ppermute(value, RING, [(i, i - i % team + (i % team ^ d)) for i in ra...  20.5 us
    pallas_call x4, Pallas kernels, unpack(): pl.pallas_call(kernel, grid=(BLOCKS,), out_shape=[struct(shape, BF16)] *...  9.6 us
    ppermute x12, waiting for transfers between devices, shift(): return lax.ppermute(value, RING, pairs)  8.66 us
    pallas_call x2, Pallas kernels, pack(): pl.pallas_call(functools.partial(pack_kernel, jobs, step, start), grid=(B...  8.46 us
    unnamed x22, local copies, waits for them, and re-layouts  5.46 us
  transfers between devices with their start and end apart: 36, of which 9 were waited for; matrix products, arithmetic and copies ran while one was open for 0% of the time, Pallas kernels for 37%

profile of v5, /device:TPU:0, one launch (start us, length us, event | category | flops | bytes accessed | tf_op | source)
XLA Modules:
  0.0 200.9 jit_solution(6661451241643665073)
XLA Ops:
  1.3 0.7 fusion.3
  2.0 0.1 fusion.1
  2.1 3.6 %pack.2 = (bf16[1,4,208,128]{3,2,1,0:T(8,128)(2,1)S(1)}, bf16[1,4,208,128]{3,2,1,0:T(8,128)(2,1)S(1)}, bf16[1,4,192,128]{3,2,1,0:T(8,128)(2,1)}, bf16[1,4,192,12...) custom-call(s32[4]{0:T(128)S(1)} %iota_xor_fusion.places_ref, ...), custom_call_target="tpu_custom_call" | custom-call | bytes 3276800 | tf_op jit(solution)/shard_map/pack/pallas_call | solution.py:67
  5.7 2.9 %collective-permute-start.1 = (bf16[1,4,208,128]{3,2,1,0:T(8,128)(2,1)S(1)}, bf16[1,4,208,128]{3,2,1,0:T(8,128)(2,1)S(1)}, u32[]{:S(2)}, u32[]{:S(2)}) collective-permute-start(bf16[1,4,208,128]{3,2,1,0:T(8,128)(2,1)S(1)} %get-tuple-element.72), channel_id=1, source_target_pairs={{0,2},{1,3},{2,0},{3,1},{4,6},{5,7},{6,4},{7,5},{8,10},{9,11},{10,... | collective-permute-start | bytes 638984 | tf_op jit(solution)/shard_map/ppermute | solution.py:389
  8.6 0.1 collective-permute-start.8
  8.8 1.7 collective-permute-start.9
  10.7 4.1 %collective-permute-done.1.refs_2_ = bf16[1,4,208,128]{3,2,1,0:T(8,128)(2,1)S(1)} collective-permute-done((bf16[1,4,208,128]{3,2,1,0:T(8,128)(2,1)S(1)}, bf16[1,4,208,128]{3,2,1,0:T(8,128)(2,1)S(1)}, u32[]{:S(2)}, u32[]{:S(2)}) %collective-permute-start.1) | collective-permute-done | bytes 213024 | tf_op jit(solution)/shard_map/ppermute | solution.py:389
  14.8 11.3 %collective-permute-done.2.refs_3_.refs_4_ = bf16[1,4,208,128]{3,2,1,0:T(8,128)(2,1)S(1)} collective-permute-done((bf16[1,4,208,128]{3,2,1,0:T(8,128)(2,1)S(1)}, bf16[1,4,208,128]{3,2,1,0:T(8,128)(2,1)S(1)}, u32[]{:S(2)}, u32[]{:S(2)}) %collective-permute-start.2) | collective-permute-done | bytes 213024 | tf_op jit(solution)/shard_map/ppermute | solution.py:389
  26.5 1.0 relay.4
  27.5 1.3 collective-permute-start.10
  28.8 5.3 %collective-permute-start.11 = (bf16[1,4,384,128]{3,2,1,0:T(8,128)(2,1)}, bf16[1,4,384,128]{3,2,1,0:T(8,128)(2,1)}, u32[]{:S(2)}, u32[]{:S(2)}) collective-permute-start(bf16[1,4,384,128]{3,2,1,0:T(8,128)(2,1)} %get-tuple-element.83), channel_id=1, source_target_pairs={{0,4},{1,5},{4,8},{5,9},{6,2},{7,3},{8,12},{9,13},{10,6},{11,7},{1... | collective-permute-start | bytes 1179656 | tf_op jit(solution)/shard_map/ppermute | solution.py:401
  34.1 4.9 %pack.3 = (bf16[1,4,384,128]{3,2,1,0:T(8,128)(2,1)S(1)}, bf16[1,4,384,128]{3,2,1,0:T(8,128)(2,1)S(1)}, bf16[1,4,384,128]{3,2,1,0:T(8,128)(2,1)S(1)}, bf16[1,4,38...) custom-call(s32[4]{0:T(128)S(1)} %iota_xor_fusion.places_ref, ...), custom_call_target="tpu_custom_call" | custom-call | bytes 9437184 | tf_op jit(solution)/shard_map/pack/pallas_call | solution.py:67
  39.0 0.7 copy-done.2
  39.7 0.7 copy-done.4
  40.5 0.7 copy-done.6
  41.2 0.8 copy-done.7
  42.0 0.7 copy-done.8
  42.8 0.7 copy-done.9
  44.0 1.0 collective-permute-start.6
  45.0 0.8 collective-permute-start.7
  45.8 0.6 collective-permute-start.14
  46.4 1.1 collective-permute-start.15
  47.5 0.9 copy-done.1
  48.5 15.4 %attend.4 = (bf16[4,2,384,128]{3,2,1,0:T(8,128)(2,1)S(1)}, f32[4,2,384,128]{3,2,1,0:T(8,128)S(1)}, bf16[2,2,384,128]{3,2,1,0:T(8,128)(2,1)S(1)}, bf16[2,2,384,128]{3,2,1,0:T(8,128)(2,1)S(1)}) custom-call(s32[4,9]{1,0:T(4,128)S(1)} %pad_add_fusion.1.table_ref, bf16[1,4,400,128]{3,2,1,0:T(8,128)(2,1)S(1)} %get-tuple-element.70.refs_0_, ...), custom_call_target="tpu_custom_call" | custom-call | flops 5435817984 | bytes 8388608 | tf_op jit(solution)/shard_map/attend/pallas_call | solution.py:270
  64.1 1.3 collective-permute-start.12
  65.4 6.6 %collective-permute-start.13 = (bf16[1,4,384,128]{3,2,1,0:T(8,128)(2,1)S(1)}, bf16[1,4,384,128]{3,2,1,0:T(8,128)(2,1)S(1)}, u32[]{:S(2)}, u32[]{:S(2)}) collective-permute-start(bf16[1,4,384,128]{3,2,1,0:T(8,128)(2,1)S(1)} %get-tuple-element.86), channel_id=1, source_target_pairs={{0,4},{1,5},{4,8},{5,9},{6,2},{7,3},{8,12},{9,13},{10,6},{11,7},{1... | collective-permute-start | bytes 1179656 | tf_op jit(solution)/shard_map/ppermute | solution.py:401
  72.0 1.1 collective-permute-start.4
  73.1 7.5 %collective-permute-done.15.refs_3_ = bf16[1,4,384,128]{3,2,1,0:T(8,128)(2,1)S(1)} collective-permute-done((bf16[1,4,384,128]{3,2,1,0:T(8,128)(2,1)}, bf16[1,4,384,128]{3,2,1,0:T(8,128)(2,1)S(1)}, u32[]{:S(2)}, u32[]{:S(2)}) %collective-permute-start.15) | collective-permute-done | bytes 393248 | tf_op jit(solution)/shard_map/ppermute | solution.py:389
  80.5 0.2 relay.6
  80.7 3.9 %collective-permute-start.19 = (bf16[1,4,768,128]{3,2,1,0:T(8,128)(2,1)S(1)}, bf16[1,4,768,128]{3,2,1,0:T(8,128)(2,1)S(1)}, u32[]{:S(2)}, u32[]{:S(2)}) collective-permute-start(bf16[1,4,768,128]{3,2,1,0:T(8,128)(2,1)S(1)} %get-tuple-element.98), channel_id=1, source_target_pairs={{0,4},{1,5},{4,8},{5,9},{6,2},{7,3},{8,12},{9,13},{10,6},{11,7},{1... | collective-permute-start | bytes 2359304 | tf_op jit(solution)/shard_map/ppermute | solution.py:401
  84.6 1.3 collective-permute-start.18
  85.9 2.3 %collective-permute-start.5 = (bf16[1,4,384,128]{3,2,1,0:T(8,128)(2,1)S(1)}, bf16[1,4,384,128]{3,2,1,0:T(8,128)(2,1)S(1)}, u32[]{:S(2)}, u32[]{:S(2)}) collective-permute-start(bf16[1,4,384,128]{3,2,1,0:T(8,128)(2,1)S(1)} %copy-done.3), channel_id=1, source_target_pairs={{0,3},{1,2},{2,1},{3,0},{4,7},{5,6},{6,5},{7,4},{8,11},{9,10},{10,... | collective-permute-start | bytes 1179656 | tf_op jit(solution)/shard_map/ppermute | solution.py:389
  88.3 14.7 %attend.5 = (bf16[4,2,384,128]{3,2,1,0:T(8,128)(2,1)S(1)}, f32[4,2,384,128]{3,2,1,0:T(8,128)S(1)}, bf16[2,2,384,128]{3,2,1,0:T(8,128)(2,1)S(1)}, bf16[2,2,384,128]{3,2,1,0:T(8,128)(2,1)S(1)}) custom-call(s32[4,9]{1,0:T(4,128)S(1)} %pad_add_fusion.1.table_ref, bf16[3,4,384,128]{3,2,1,0:T(8,128)(2,1)S(1)} %get-tuple-element.74.refs_0_, ...), custom_call_target="tpu_custom_call" | custom-call | flops 5435817984 | bytes 8388608 | tf_op jit(solution)/shard_map/attend/pallas_call | solution.py:270
  103.0 0.2 relay.7
  103.1 5.9 %collective-permute-start.17 = (bf16[1,4,768,128]{3,2,1,0:T(8,128)(2,1)S(1)}, bf16[1,4,768,128]{3,2,1,0:T(8,128)(2,1)S(1)}, u32[]{:S(2)}, u32[]{:S(2)}) collective-permute-start(bf16[1,4,768,128]{3,2,1,0:T(8,128)(2,1)S(1)} %get-tuple-element.95), channel_id=1, source_target_pairs={{0,4},{1,5},{4,8},{5,9},{6,2},{7,3},{8,12},{9,13},{10,6},{11,7},{1... | collective-permute-start | bytes 2359304 | tf_op jit(solution)/shard_map/ppermute | solution.py:401
  109.1 1.5 collective-permute-start.16
  110.6 0.3 finish.4
  110.8 1.2 collective-permute-start.26
  112.1 14.7 %attend.6 = (bf16[4,2,384,128]{3,2,1,0:T(8,128)(2,1)S(1)}, f32[4,2,384,128]{3,2,1,0:T(8,128)S(1)}, bf16[2,2,384,128]{3,2,1,0:T(8,128)(2,1)S(1)}, bf16[2,2,384,128]{3,2,1,0:T(8,128)(2,1)S(1)}) custom-call(s32[4,9]{1,0:T(4,128)S(1)} %pad_add_fusion.1.table_ref, bf16[3,4,384,128]{3,2,1,0:T(8,128)(2,1)S(1)} %get-tuple-element.74.refs_0_, ...), custom_call_target="tpu_custom_call" | custom-call | flops 5435817984 | bytes 8388608 | tf_op jit(solution)/shard_map/attend/pallas_call | solution.py:270
  126.7 6.2 %collective-permute-start.24 = (bf16[2,2,384,128]{3,2,1,0:T(8,128)(2,1)S(1)}, bf16[2,2,384,128]{3,2,1,0:T(8,128)(2,1)S(1)}, u32[]{:S(2)}, u32[]{:S(2)}) collective-permute-start(bf16[2,2,384,128]{3,2,1,0:T(8,128)(2,1)S(1)} %get-tuple-element.110), channel_id=1, source_target_pairs={{0,4},{1,5},{4,8},{5,9},{6,2},{7,3},{8,12},{9,13},{10,6},{11,7},{1... | collective-permute-start | bytes 1179656 | tf_op jit(solution)/shard_map/ppermute | solution.py:401
  133.0 1.3 collective-permute-start.25
  134.3 0.3 finish.5
  134.5 2.2 %collective-permute-start.22 = (bf16[1,4,384,128]{3,2,1,0:T(8,128)(2,1)S(1)}, bf16[1,4,384,128]{3,2,1,0:T(8,128)(2,1)S(1)}, u32[]{:S(2)}, u32[]{:S(2)}) collective-permute-start(bf16[1,4,384,128]{3,2,1,0:T(8,128)(2,1)S(1)} %get-tuple-element.107), channel_id=1, source_target_pairs={{0,2},{1,3},{2,0},{3,1},{4,6},{5,7},{6,4},{7,5},{8,10},{9,11},{10,... | collective-permute-start | bytes 1179656 | tf_op jit(solution)/shard_map/ppermute | solution.py:389
  136.8 0.6 collective-permute-start.23
  137.3 14.7 %attend.7 = (bf16[4,2,384,128]{3,2,1,0:T(8,128)(2,1)S(1)}, f32[4,2,384,128]{3,2,1,0:T(8,128)S(1)}, bf16[2,2,384,128]{3,2,1,0:T(8,128)(2,1)S(1)}, bf16[2,2,384,128]{3,2,1,0:T(8,128)(2,1)S(1)}) custom-call(s32[4,9]{1,0:T(4,128)S(1)} %pad_add_fusion.1.table_ref, bf16[3,4,384,128]{3,2,1,0:T(8,128)(2,1)S(1)} %get-tuple-element.74.refs_0_, ...), custom_call_target="tpu_custom_call" | custom-call | flops 5435817984 | bytes 8388608 | tf_op jit(solution)/shard_map/attend/pallas_call | solution.py:270
  152.0 6.6 %collective-permute-start.20 = (bf16[2,2,384,128]{3,2,1,0:T(8,128)(2,1)S(1)}, bf16[2,2,384,128]{3,2,1,0:T(8,128)(2,1)S(1)}, u32[]{:S(2)}, u32[]{:S(2)}) collective-permute-start(bf16[2,2,384,128]{3,2,1,0:T(8,128)(2,1)S(1)} %get-tuple-element.105), channel_id=1, source_target_pairs={{0,4},{1,5},{4,8},{5,9},{6,2},{7,3},{8,12},{9,13},{10,6},{11,7},{1... | collective-permute-start | bytes 1179656 | tf_op jit(solution)/shard_map/ppermute | solution.py:401
  158.6 1.3 collective-permute-start.21
  159.9 0.2 finish.6
  160.1 1.2 collective-permute-start.28
  161.3 0.2 collective-permute-start.29
  161.5 0.9 collective-permute-start.35
  162.3 4.5 %collective-permute-done.20.refs_0_ = bf16[2,2,384,128]{3,2,1,0:T(8,128)(2,1)S(1)} collective-permute-done((bf16[2,2,384,128]{3,2,1,0:T(8,128)(2,1)S(1)}, bf16[2,2,384,128]{3,2,1,0:T(8,128)(2,1)S(1)}, u32[]{:S(2)}, u32[]{:S(2)}) %collective-permute-start.20) | collective-permute-done | bytes 393248 | tf_op jit(solution)/shard_map/ppermute | solution.py:401
  166.8 4.1 %collective-permute-done.21.refs_1_ = bf16[2,2,384,128]{3,2,1,0:T(8,128)(2,1)S(1)} collective-permute-done((bf16[2,2,384,128]{3,2,1,0:T(8,128)(2,1)S(1)}, bf16[2,2,384,128]{3,2,1,0:T(8,128)(2,1)S(1)}, u32[]{:S(2)}, u32[]{:S(2)}) %collective-permute-start.21) | collective-permute-done | bytes 393248 | tf_op jit(solution)/shard_map/ppermute | solution.py:401
  171.0 1.2 collective-permute-done.28.refs_5_.refs_2_
  172.2 6.5 %collective-permute-done.29.refs_6_.refs_3_ = bf16[1,4,384,128]{3,2,1,0:T(8,128)(2,1)S(1)} collective-permute-done((bf16[1,4,384,128]{3,2,1,0:T(8,128)(2,1)S(1)}, bf16[1,4,384,128]{3,2,1,0:T(8,128)(2,1)S(1)}, u32[]{:S(2)}, u32[]{:S(2)}) %collective-permute-start.29) | collective-permute-done | bytes 393248 | tf_op jit(solution)/shard_map/ppermute | solution.py:389
  178.7 0.2 finish.7
  178.9 0.6 collective-permute-start.30
  179.5 1.7 collective-permute-start.31
  181.3 2.4 %unpack.4 = (bf16[1,384,2048]{2,1,0:T(8,128)(2,1)}, bf16[1,384,2048]{2,1,0:T(8,128)(2,1)}, bf16[1,384,2048]{2,1,0:T(8,128)(2,1)}, bf16[1,384,2048]{2,1,0:T(8,128)(2,1)}) custom-call(s32[4]{0:T(128)S(1)} %iota_xor_fusion.places_ref, bf16[1,4,384,128]{3,2,1,0:T(8,128)(2,1)S(1)} %get-tuple-element.100.refs_7_.refs_0_, ...), custom_call_target="tpu_custom_call" | custom-call | bytes 3145728 | tf_op jit(solution)/shard_map/unpack/pallas_call | solution.py:356
  183.7 2.4 %unpack.5 = (bf16[1,384,2048]{2,1,0:T(8,128)(2,1)}, bf16[1,384,2048]{2,1,0:T(8,128)(2,1)}, bf16[1,384,2048]{2,1,0:T(8,128)(2,1)}, bf16[1,384,2048]{2,1,0:T(8,128)(2,1)}) custom-call(s32[4]{0:T(128)S(1)} %iota_xor_fusion.places_ref, ...), custom_call_target="tpu_custom_call", output_to_operand_aliasing={{0}: (5, {}), {1}: (6, {}), {2}: (7, {}), {3}: (8, {})} | custom-call | bytes 3145728 | tf_op jit(solution)/shard_map/unpack/pallas_call | solution.py:356
  186.1 2.4 %unpack.6 = (bf16[1,384,2048]{2,1,0:T(8,128)(2,1)}, bf16[1,384,2048]{2,1,0:T(8,128)(2,1)}, bf16[1,384,2048]{2,1,0:T(8,128)(2,1)}, bf16[1,384,2048]{2,1,0:T(8,128)(2,1)}) custom-call(s32[4]{0:T(128)S(1)} %iota_xor_fusion.places_ref, ...), custom_call_target="tpu_custom_call", output_to_operand_aliasing={{0}: (5, {}), {1}: (6, {}), {2}: (7, {}), {3}: (8, {})} | custom-call | bytes 3145728 | tf_op jit(solution)/shard_map/unpack/pallas_call | solution.py:356
  188.5 3.0 %collective-permute-done.31.refs_2_ = bf16[1,4,384,128]{3,2,1,0:T(8,128)(2,1)S(1)} collective-permute-done((bf16[1,4,384,128]{3,2,1,0:T(8,128)(2,1)S(1)}, bf16[1,4,384,128]{3,2,1,0:T(8,128)(2,1)S(1)}, u32[]{:S(2)}, u32[]{:S(2)}) %collective-permute-start.31) | collective-permute-done | bytes 393248 | tf_op jit(solution)/shard_map/ppermute | solution.py:389
  191.5 7.1 %collective-permute-done.32.refs_3_ = bf16[1,4,384,128]{3,2,1,0:T(8,128)(2,1)S(1)} collective-permute-done((bf16[1,4,384,128]{3,2,1,0:T(8,128)(2,1)S(1)}, bf16[1,4,384,128]{3,2,1,0:T(8,128)(2,1)S(1)}, u32[]{:S(2)}, u32[]{:S(2)}) %collective-permute-start.32) | collective-permute-done | bytes 393248 | tf_op jit(solution)/shard_map/ppermute | solution.py:389
  198.5 2.4 %unpack.7 = (bf16[1,384,2048]{2,1,0:T(8,128)(2,1)}, bf16[1,384,2048]{2,1,0:T(8,128)(2,1)}, bf16[1,384,2048]{2,1,0:T(8,128)(2,1)}, bf16[1,384,2048]{2,1,0:T(8,128)(2,1)}) custom-call(s32[4]{0:T(128)S(1)} %iota_xor_fusion.places_ref, ...), custom_call_target="tpu_custom_call", output_to_operand_aliasing={{0}: (5, {}), {1}: (6, {}), {2}: (7, {}), {3}: (8, {})} | custom-call | bytes 3145728 | tf_op jit(solution)/shard_map/unpack/pallas_call | solution.py:356
  (71 shorter events, 1.4 us)
Async XLA Ops:
  5.7 9.0 %collective-permute-start.1 = (bf16[1,4,208,128]{3,2,1,0:T(8,128)(2,1)S(1)}, bf16[1,4,208,128]{3,2,1,0:T(8,128)(2,1)S(1)}, u32[]{:S(2)}, u32[]{:S(2)}) collective-permute-start(bf16[1,4,208,128]{3,2,1,0:T(8,128)(2,1)S(1)} %get-tuple-element.72), channel_id=1, source_target_pairs={{0,2},{1,3},{2,0},{3,1},{4,6},{5,7},{6,4},{7,5},{8,10},{9,11},{10,... | collective-permute-start | bytes 638984 | tf_op jit(solution)/shard_map/ppermute | solution.py:389
  8.6 17.6 %collective-permute-start = (bf16[1,4,400,128]{3,2,1,0:T(8,128)(2,1)S(1)}, bf16[1,4,400,128]{3,2,1,0:T(8,128)(2,1)S(1)}, u32[]{:S(2)}, u32[]{:S(2)}) collective-permute-start(bf16[1,4,400,128]{3,2,1,0:T(8,128)(2,1)S(1)} %get-tuple-element.71), channel_id=1, source_target_pairs={{0,1},{1,0},{2,3},{3,2},{4,5},{5,4},{6,7},{7,6},{8,9},{9,8},{10,11... | collective-permute-start | bytes 1228808 | tf_op jit(solution)/shard_map/ppermute | solution.py:389
  8.6 35.4 %collective-permute-start.8 = (bf16[1,4,192,128]{3,2,1,0:T(8,128)(2,1)}, bf16[1,4,192,128]{3,2,1,0:T(8,128)(2,1)}, u32[]{:S(2)}, u32[]{:S(2)}) collective-permute-start(bf16[1,4,192,128]{3,2,1,0:T(8,128)(2,1)} %get-tuple-element.80), channel_id=1, source_target_pairs={{0,2},{1,3},{2,0},{3,1},{4,6},{5,7},{6,4},{7,5},{8,10},{9,11},{10,... | collective-permute-start | bytes 589832 | tf_op jit(solution)/shard_map/ppermute | solution.py:389
  8.8 36.3 %collective-permute-start.9 = (bf16[1,4,192,128]{3,2,1,0:T(8,128)(2,1)}, bf16[1,4,192,128]{3,2,1,0:T(8,128)(2,1)}, u32[]{:S(2)}, u32[]{:S(2)}) collective-permute-start(bf16[1,4,192,128]{3,2,1,0:T(8,128)(2,1)} %get-tuple-element.81), channel_id=1, source_target_pairs={{0,3},{1,2},{2,1},{3,0},{4,7},{5,6},{6,5},{7,4},{8,11},{9,10},{10,... | collective-permute-start | bytes 589832 | tf_op jit(solution)/shard_map/ppermute | solution.py:389
  10.5 15.6 %collective-permute-start.2 = (bf16[1,4,208,128]{3,2,1,0:T(8,128)(2,1)S(1)}, bf16[1,4,208,128]{3,2,1,0:T(8,128)(2,1)S(1)}, u32[]{:S(2)}, u32[]{:S(2)}) collective-permute-start(bf16[1,4,208,128]{3,2,1,0:T(8,128)(2,1)S(1)} %get-tuple-element.73), channel_id=1, source_target_pairs={{0,3},{1,2},{2,1},{3,0},{4,7},{5,6},{6,5},{7,4},{8,11},{9,10},{10,... | collective-permute-start | bytes 638984 | tf_op jit(solution)/shard_map/ppermute | solution.py:389
  26.1 2.6 %copy-start = (bf16[1,4,208,128]{3,2,1,0:T(8,128)(2,1)}, bf16[1,4,208,128]{3,2,1,0:T(8,128)(2,1)S(1)}, u32[]{:S(2)}) copy-start(bf16[1,4,208,128]{3,2,1,0:T(8,128)(2,1)S(1)} %collective-permute-done.2.refs_3_.refs_4_) | copy-start | bytes 638980
  27.5 18.4 %collective-permute-start.10 = (bf16[1,4,384,128]{3,2,1,0:T(8,128)(2,1)}, bf16[1,4,384,128]{3,2,1,0:T(8,128)(2,1)}, u32[]{:S(2)}, u32[]{:S(2)}) collective-permute-start(bf16[1,4,384,128]{3,2,1,0:T(8,128)(2,1)} %get-tuple-element.82), channel_id=1, source_target_pairs={{2,6},{3,7},{4,0},{5,1},{6,10},{7,11},{8,4},{9,5},{10,14},{11,15},... | collective-permute-start | bytes 1179656 | tf_op jit(solution)/shard_map/ppermute | solution.py:401
  28.8 15.2 %copy-start.10 = (s32[2,3]{1,0:T(2,128)S(1)}, s32[2,3]{1,0:T(2,128)}, u32[]{:S(2)}) copy-start(s32[2,3]{1,0:T(2,128)} %constant.47.clone) | copy-start | bytes 76
  28.8 17.6 %collective-permute-start.11 = (bf16[1,4,384,128]{3,2,1,0:T(8,128)(2,1)}, bf16[1,4,384,128]{3,2,1,0:T(8,128)(2,1)}, u32[]{:S(2)}, u32[]{:S(2)}) collective-permute-start(bf16[1,4,384,128]{3,2,1,0:T(8,128)(2,1)} %get-tuple-element.83), channel_id=1, source_target_pairs={{0,4},{1,5},{4,8},{5,9},{6,2},{7,3},{8,12},{9,13},{10,6},{11,7},{1... | collective-permute-start | bytes 1179656 | tf_op jit(solution)/shard_map/ppermute | solution.py:401
  39.0 0.7 copy-start.2
  39.7 0.7 copy-start.4
  40.5 0.7 copy-start.6
  41.2 0.8 copy-start.7
  42.0 0.7 copy-start.8
  42.8 0.7 copy-start.9
  43.5 20.4 %collective-permute-start.3 = (bf16[3,4,384,128]{3,2,1,0:T(8,128)(2,1)}, bf16[3,4,384,128]{3,2,1,0:T(8,128)(2,1)S(1)}, u32[]{:S(2)}, u32[]{:S(2)}) collective-permute-start(bf16[3,4,384,128]{3,2,1,0:T(8,128)(2,1)} %get-tuple-element.75), channel_id=1, source_target_pairs={{0,1},{1,0},{2,3},{3,2},{4,5},{5,4},{6,7},{7,6},{8,9},{9,8},{10,11... | collective-permute-start | bytes 3538952 | tf_op jit(solution)/shard_map/ppermute | solution.py:389
  44.0 19.9 %collective-permute-start.6 = (bf16[1,4,384,128]{3,2,1,0:T(8,128)(2,1)}, bf16[1,4,384,128]{3,2,1,0:T(8,128)(2,1)S(1)}, u32[]{:S(2)}, u32[]{:S(2)}) collective-permute-start(bf16[1,4,384,128]{3,2,1,0:T(8,128)(2,1)} %copy-done.9), channel_id=1, source_target_pairs={{0,2},{1,3},{2,0},{3,1},{4,6},{5,7},{6,4},{7,5},{8,10},{9,11},{10,... | collective-permute-start | bytes 1179656 | tf_op jit(solution)/shard_map/ppermute | solution.py:389
  45.0 18.9 %collective-permute-start.7 = (bf16[1,4,384,128]{3,2,1,0:T(8,128)(2,1)}, bf16[1,4,384,128]{3,2,1,0:T(8,128)(2,1)S(1)}, u32[]{:S(2)}, u32[]{:S(2)}) collective-permute-start(bf16[1,4,384,128]{3,2,1,0:T(8,128)(2,1)} %copy-done.8), channel_id=1, source_target_pairs={{0,3},{1,2},{2,1},{3,0},{4,7},{5,6},{6,5},{7,4},{8,11},{9,10},{10,... | collective-permute-start | bytes 1179656 | tf_op jit(solution)/shard_map/ppermute | solution.py:389
  45.8 27.2 %collective-permute-start.14 = (bf16[1,4,384,128]{3,2,1,0:T(8,128)(2,1)}, bf16[1,4,384,128]{3,2,1,0:T(8,128)(2,1)S(1)}, u32[]{:S(2)}, u32[]{:S(2)}) collective-permute-start(bf16[1,4,384,128]{3,2,1,0:T(8,128)(2,1)} %copy-done.7), channel_id=1, source_target_pairs={{0,2},{1,3},{2,0},{3,1},{4,6},{5,7},{6,4},{7,5},{8,10},{9,11},{10,... | collective-permute-start | bytes 1179656 | tf_op jit(solution)/shard_map/ppermute | solution.py:389
  46.4 34.1 %collective-permute-start.15 = (bf16[1,4,384,128]{3,2,1,0:T(8,128)(2,1)}, bf16[1,4,384,128]{3,2,1,0:T(8,128)(2,1)S(1)}, u32[]{:S(2)}, u32[]{:S(2)}) collective-permute-start(bf16[1,4,384,128]{3,2,1,0:T(8,128)(2,1)} %copy-done.6), channel_id=1, source_target_pairs={{0,3},{1,2},{2,1},{3,0},{4,7},{5,6},{6,5},{7,4},{8,11},{9,10},{10,... | collective-permute-start | bytes 1179656 | tf_op jit(solution)/shard_map/ppermute | solution.py:389
  47.5 0.9 copy-start.1
  63.9 8.0 %copy-start.5 = (bf16[1,4,384,128]{3,2,1,0:T(8,128)(2,1)S(1)}, bf16[1,4,384,128]{3,2,1,0:T(8,128)(2,1)}, u32[]{:S(2)}) copy-start(bf16[1,4,384,128]{3,2,1,0:T(8,128)(2,1)} %copy-done.4) | copy-start | bytes 1179652
  64.1 21.8 %collective-permute-start.12 = (bf16[1,4,384,128]{3,2,1,0:T(8,128)(2,1)S(1)}, bf16[1,4,384,128]{3,2,1,0:T(8,128)(2,1)S(1)}, u32[]{:S(2)}, u32[]{:S(2)}) collective-permute-start(bf16[1,4,384,128]{3,2,1,0:T(8,128)(2,1)S(1)} %get-tuple-element.85), channel_id=1, source_target_pairs={{2,6},{3,7},{4,0},{5,1},{6,10},{7,11},{8,4},{9,5},{10,14},{11,15},... | collective-permute-start | bytes 1179656 | tf_op jit(solution)/shard_map/ppermute | solution.py:401
  65.4 22.9 %collective-permute-start.13 = (bf16[1,4,384,128]{3,2,1,0:T(8,128)(2,1)S(1)}, bf16[1,4,384,128]{3,2,1,0:T(8,128)(2,1)S(1)}, u32[]{:S(2)}, u32[]{:S(2)}) collective-permute-start(bf16[1,4,384,128]{3,2,1,0:T(8,128)(2,1)S(1)} %get-tuple-element.86), channel_id=1, source_target_pairs={{0,4},{1,5},{4,8},{5,9},{6,2},{7,3},{8,12},{9,13},{10,6},{11,7},{1... | collective-permute-start | bytes 1179656 | tf_op jit(solution)/shard_map/ppermute | solution.py:401
  72.0 31.0 %collective-permute-start.4 = (bf16[1,4,384,128]{3,2,1,0:T(8,128)(2,1)S(1)}, bf16[1,4,384,128]{3,2,1,0:T(8,128)(2,1)S(1)}, u32[]{:S(2)}, u32[]{:S(2)}) collective-permute-start(bf16[1,4,384,128]{3,2,1,0:T(8,128)(2,1)S(1)} %copy-done.5), channel_id=1, source_target_pairs={{0,2},{1,3},{2,0},{3,1},{4,6},{5,7},{6,4},{7,5},{8,10},{9,11},{10,... | collective-permute-start | bytes 1179656 | tf_op jit(solution)/shard_map/ppermute | solution.py:389
  80.5 5.4 %copy-start.3 = (bf16[1,4,384,128]{3,2,1,0:T(8,128)(2,1)S(1)}, bf16[1,4,384,128]{3,2,1,0:T(8,128)(2,1)}, u32[]{:S(2)}) copy-start(bf16[1,4,384,128]{3,2,1,0:T(8,128)(2,1)} %copy-done.2) | copy-start | bytes 1179652
  80.7 29.9 %collective-permute-start.19 = (bf16[1,4,768,128]{3,2,1,0:T(8,128)(2,1)S(1)}, bf16[1,4,768,128]{3,2,1,0:T(8,128)(2,1)S(1)}, u32[]{:S(2)}, u32[]{:S(2)}) collective-permute-start(bf16[1,4,768,128]{3,2,1,0:T(8,128)(2,1)S(1)} %get-tuple-element.98), channel_id=1, source_target_pairs={{0,4},{1,5},{4,8},{5,9},{6,2},{7,3},{8,12},{9,13},{10,6},{11,7},{1... | collective-permute-start | bytes 2359304 | tf_op jit(solution)/shard_map/ppermute | solution.py:401
  84.6 26.0 %collective-permute-start.18 = (bf16[1,4,768,128]{3,2,1,0:T(8,128)(2,1)S(1)}, bf16[1,4,768,128]{3,2,1,0:T(8,128)(2,1)S(1)}, u32[]{:S(2)}, u32[]{:S(2)}) collective-permute-start(bf16[1,4,768,128]{3,2,1,0:T(8,128)(2,1)S(1)} %get-tuple-element.91.refs_6_), channel_id=1, source_target_pairs={{2,6},{3,7},{4,0},{5,1},{6,10},{7,11},{8,4},{9,5},{10,14},{11,15},... | collective-permute-start | bytes 2359304 | tf_op jit(solution)/shard_map/ppermute | solution.py:401
  85.9 17.0 %collective-permute-start.5 = (bf16[1,4,384,128]{3,2,1,0:T(8,128)(2,1)S(1)}, bf16[1,4,384,128]{3,2,1,0:T(8,128)(2,1)S(1)}, u32[]{:S(2)}, u32[]{:S(2)}) collective-permute-start(bf16[1,4,384,128]{3,2,1,0:T(8,128)(2,1)S(1)} %copy-done.3), channel_id=1, source_target_pairs={{0,3},{1,2},{2,1},{3,0},{4,7},{5,6},{6,5},{7,4},{8,11},{9,10},{10,... | collective-permute-start | bytes 1179656 | tf_op jit(solution)/shard_map/ppermute | solution.py:389
  103.1 29.8 %collective-permute-start.17 = (bf16[1,4,768,128]{3,2,1,0:T(8,128)(2,1)S(1)}, bf16[1,4,768,128]{3,2,1,0:T(8,128)(2,1)S(1)}, u32[]{:S(2)}, u32[]{:S(2)}) collective-permute-start(bf16[1,4,768,128]{3,2,1,0:T(8,128)(2,1)S(1)} %get-tuple-element.95), channel_id=1, source_target_pairs={{0,4},{1,5},{4,8},{5,9},{6,2},{7,3},{8,12},{9,13},{10,6},{11,7},{1... | collective-permute-start | bytes 2359304 | tf_op jit(solution)/shard_map/ppermute | solution.py:401
  109.1 25.2 %collective-permute-start.16 = (bf16[1,4,768,128]{3,2,1,0:T(8,128)(2,1)S(1)}, bf16[1,4,768,128]{3,2,1,0:T(8,128)(2,1)S(1)}, u32[]{:S(2)}, u32[]{:S(2)}) collective-permute-start(bf16[1,4,768,128]{3,2,1,0:T(8,128)(2,1)S(1)} %get-tuple-element.94.refs_6_), channel_id=1, source_target_pairs={{2,6},{3,7},{4,0},{5,1},{6,10},{7,11},{8,4},{9,5},{10,14},{11,15},... | collective-permute-start | bytes 2359304 | tf_op jit(solution)/shard_map/ppermute | solution.py:401
  110.8 25.9 %collective-permute-start.26 = (bf16[1,4,384,128]{3,2,1,0:T(8,128)(2,1)S(1)}, bf16[1,4,384,128]{3,2,1,0:T(8,128)(2,1)S(1)}, u32[]{:S(2)}, u32[]{:S(2)}) collective-permute-start(bf16[1,4,384,128]{3,2,1,0:T(8,128)(2,1)S(1)} %get-tuple-element.112), channel_id=1, source_target_pairs={{0,2},{1,3},{2,0},{3,1},{4,6},{5,7},{6,4},{7,5},{8,10},{9,11},{10,... | collective-permute-start | bytes 1179656 | tf_op jit(solution)/shard_map/ppermute | solution.py:389
  112.1 39.9 %collective-permute-start.27 = (bf16[1,4,384,128]{3,2,1,0:T(8,128)(2,1)S(1)}, bf16[1,4,384,128]{3,2,1,0:T(8,128)(2,1)S(1)}, u32[]{:S(2)}, u32[]{:S(2)}) collective-permute-start(bf16[1,4,384,128]{3,2,1,0:T(8,128)(2,1)S(1)} %get-tuple-element.113), channel_id=1, source_target_pairs={{0,3},{1,2},{2,1},{3,0},{4,7},{5,6},{6,5},{7,4},{8,11},{9,10},{10,... | collective-permute-start | bytes 1179656 | tf_op jit(solution)/shard_map/ppermute | solution.py:389
  126.7 31.9 %collective-permute-start.24 = (bf16[2,2,384,128]{3,2,1,0:T(8,128)(2,1)S(1)}, bf16[2,2,384,128]{3,2,1,0:T(8,128)(2,1)S(1)}, u32[]{:S(2)}, u32[]{:S(2)}) collective-permute-start(bf16[2,2,384,128]{3,2,1,0:T(8,128)(2,1)S(1)} %get-tuple-element.110), channel_id=1, source_target_pairs={{0,4},{1,5},{4,8},{5,9},{6,2},{7,3},{8,12},{9,13},{10,6},{11,7},{1... | collective-permute-start | bytes 1179656 | tf_op jit(solution)/shard_map/ppermute | solution.py:401
  133.0 27.0 %collective-permute-start.25 = (bf16[2,2,384,128]{3,2,1,0:T(8,128)(2,1)S(1)}, bf16[2,2,384,128]{3,2,1,0:T(8,128)(2,1)S(1)}, u32[]{:S(2)}, u32[]{:S(2)}) collective-permute-start(bf16[2,2,384,128]{3,2,1,0:T(8,128)(2,1)S(1)} %get-tuple-element.111), channel_id=1, source_target_pairs={{2,6},{3,7},{4,0},{5,1},{6,10},{7,11},{8,4},{9,5},{10,14},{11,15},... | collective-permute-start | bytes 1179656 | tf_op jit(solution)/shard_map/ppermute | solution.py:401
  134.5 26.8 %collective-permute-start.22 = (bf16[1,4,384,128]{3,2,1,0:T(8,128)(2,1)S(1)}, bf16[1,4,384,128]{3,2,1,0:T(8,128)(2,1)S(1)}, u32[]{:S(2)}, u32[]{:S(2)}) collective-permute-start(bf16[1,4,384,128]{3,2,1,0:T(8,128)(2,1)S(1)} %get-tuple-element.107), channel_id=1, source_target_pairs={{0,2},{1,3},{2,0},{3,1},{4,6},{5,7},{6,4},{7,5},{8,10},{9,11},{10,... | collective-permute-start | bytes 1179656 | tf_op jit(solution)/shard_map/ppermute | solution.py:389
  136.8 24.7 %collective-permute-start.23 = (bf16[1,4,384,128]{3,2,1,0:T(8,128)(2,1)S(1)}, bf16[1,4,384,128]{3,2,1,0:T(8,128)(2,1)S(1)}, u32[]{:S(2)}, u32[]{:S(2)}) collective-permute-start(bf16[1,4,384,128]{3,2,1,0:T(8,128)(2,1)S(1)} %get-tuple-element.108), channel_id=1, source_target_pairs={{0,3},{1,2},{2,1},{3,0},{4,7},{5,6},{6,5},{7,4},{8,11},{9,10},{10,... | collective-permute-start | bytes 1179656 | tf_op jit(solution)/shard_map/ppermute | solution.py:389
  152.0 14.8 %collective-permute-start.20 = (bf16[2,2,384,128]{3,2,1,0:T(8,128)(2,1)S(1)}, bf16[2,2,384,128]{3,2,1,0:T(8,128)(2,1)S(1)}, u32[]{:S(2)}, u32[]{:S(2)}) collective-permute-start(bf16[2,2,384,128]{3,2,1,0:T(8,128)(2,1)S(1)} %get-tuple-element.105), channel_id=1, source_target_pairs={{0,4},{1,5},{4,8},{5,9},{6,2},{7,3},{8,12},{9,13},{10,6},{11,7},{1... | collective-permute-start | bytes 1179656 | tf_op jit(solution)/shard_map/ppermute | solution.py:401
  158.6 12.3 %collective-permute-start.21 = (bf16[2,2,384,128]{3,2,1,0:T(8,128)(2,1)S(1)}, bf16[2,2,384,128]{3,2,1,0:T(8,128)(2,1)S(1)}, u32[]{:S(2)}, u32[]{:S(2)}) collective-permute-start(bf16[2,2,384,128]{3,2,1,0:T(8,128)(2,1)S(1)} %get-tuple-element.106), channel_id=1, source_target_pairs={{2,6},{3,7},{4,0},{5,1},{6,10},{7,11},{8,4},{9,5},{10,14},{11,15},... | collective-permute-start | bytes 1179656 | tf_op jit(solution)/shard_map/ppermute | solution.py:401
  160.1 12.1 %collective-permute-start.28 = (bf16[1,4,384,128]{3,2,1,0:T(8,128)(2,1)S(1)}, bf16[1,4,384,128]{3,2,1,0:T(8,128)(2,1)S(1)}, u32[]{:S(2)}, u32[]{:S(2)}) collective-permute-start(bf16[1,4,384,128]{3,2,1,0:T(8,128)(2,1)S(1)} %get-tuple-element.114), channel_id=1, source_target_pairs={{0,2},{1,3},{2,0},{3,1},{4,6},{5,7},{6,4},{7,5},{8,10},{9,11},{10,... | collective-permute-start | bytes 1179656 | tf_op jit(solution)/shard_map/ppermute | solution.py:389
  161.3 17.4 %collective-permute-start.29 = (bf16[1,4,384,128]{3,2,1,0:T(8,128)(2,1)S(1)}, bf16[1,4,384,128]{3,2,1,0:T(8,128)(2,1)S(1)}, u32[]{:S(2)}, u32[]{:S(2)}) collective-permute-start(bf16[1,4,384,128]{3,2,1,0:T(8,128)(2,1)S(1)} %get-tuple-element.115), channel_id=1, source_target_pairs={{0,3},{1,2},{2,1},{3,0},{4,7},{5,6},{6,5},{7,4},{8,11},{9,10},{10,... | collective-permute-start | bytes 1179656 | tf_op jit(solution)/shard_map/ppermute | solution.py:389
  161.5 19.8 %collective-permute-start.35 = (bf16[1,4,384,128]{3,2,1,0:T(8,128)(2,1)S(1)}, bf16[1,4,384,128]{3,2,1,0:T(8,128)(2,1)S(1)}, u32[]{:S(2)}, u32[]{:S(2)}) collective-permute-start(bf16[1,4,384,128]{3,2,1,0:T(8,128)(2,1)S(1)} %get-tuple-element.123), channel_id=1, source_target_pairs={{0,1},{1,0},{2,3},{3,2},{4,5},{5,4},{6,7},{7,6},{8,9},{9,8},{10,11... | collective-permute-start | bytes 1179656 | tf_op jit(solution)/shard_map/ppermute | solution.py:389
  166.8 16.9 %collective-permute-start.34 = (bf16[1,4,384,128]{3,2,1,0:T(8,128)(2,1)S(1)}, bf16[1,4,384,128]{3,2,1,0:T(8,128)(2,1)S(1)}, u32[]{:S(2)}, u32[]{:S(2)}) collective-permute-start(bf16[1,4,384,128]{3,2,1,0:T(8,128)(2,1)S(1)} %get-tuple-element.122), channel_id=1, source_target_pairs={{0,1},{1,0},{2,3},{3,2},{4,5},{5,4},{6,7},{7,6},{8,9},{9,8},{10,11... | collective-permute-start | bytes 1179656 | tf_op jit(solution)/shard_map/ppermute | solution.py:389
  171.0 15.1 %collective-permute-start.33 = (bf16[1,4,384,128]{3,2,1,0:T(8,128)(2,1)S(1)}, bf16[1,4,384,128]{3,2,1,0:T(8,128)(2,1)S(1)}, u32[]{:S(2)}, u32[]{:S(2)}) collective-permute-start(bf16[1,4,384,128]{3,2,1,0:T(8,128)(2,1)S(1)} %get-tuple-element.121), channel_id=1, source_target_pairs={{0,1},{1,0},{2,3},{3,2},{4,5},{5,4},{6,7},{7,6},{8,9},{9,8},{10,11... | collective-permute-start | bytes 1179656 | tf_op jit(solution)/shard_map/ppermute | solution.py:389
  178.9 9.6 %collective-permute-start.30 = (bf16[1,4,384,128]{3,2,1,0:T(8,128)(2,1)S(1)}, bf16[1,4,384,128]{3,2,1,0:T(8,128)(2,1)S(1)}, u32[]{:S(2)}, u32[]{:S(2)}) collective-permute-start(bf16[1,4,384,128]{3,2,1,0:T(8,128)(2,1)S(1)} %get-tuple-element.117), channel_id=1, source_target_pairs={{0,1},{1,0},{2,3},{3,2},{4,5},{5,4},{6,7},{7,6},{8,9},{9,8},{10,11... | collective-permute-start | bytes 1179656 | tf_op jit(solution)/shard_map/ppermute | solution.py:389
  179.5 11.9 %collective-permute-start.31 = (bf16[1,4,384,128]{3,2,1,0:T(8,128)(2,1)S(1)}, bf16[1,4,384,128]{3,2,1,0:T(8,128)(2,1)S(1)}, u32[]{:S(2)}, u32[]{:S(2)}) collective-permute-start(bf16[1,4,384,128]{3,2,1,0:T(8,128)(2,1)S(1)} %get-tuple-element.118), channel_id=1, source_target_pairs={{0,2},{1,3},{2,0},{3,1},{4,6},{5,7},{6,4},{7,5},{8,10},{9,11},{10,... | collective-permute-start | bytes 1179656 | tf_op jit(solution)/shard_map/ppermute | solution.py:389
  181.3 17.3 %collective-permute-start.32 = (bf16[1,4,384,128]{3,2,1,0:T(8,128)(2,1)S(1)}, bf16[1,4,384,128]{3,2,1,0:T(8,128)(2,1)S(1)}, u32[]{:S(2)}, u32[]{:S(2)}) collective-permute-start(bf16[1,4,384,128]{3,2,1,0:T(8,128)(2,1)S(1)} %get-tuple-element.119), channel_id=1, source_target_pairs={{0,3},{1,2},{2,1},{3,0},{4,7},{5,6},{6,5},{7,4},{8,11},{9,10},{10,... | collective-permute-start | bytes 1179656 | tf_op jit(solution)/shard_map/ppermute | solution.py:389

commit v6 on v5

--- a/solution.py
+++ b/solution.py
@@ -18,7 +18,7 @@
 FACTOR = SCALE * math.log2(math.e)
 ANY = pl.BlockSpec(memory_space=pl.ANY)
 SMEM = pl.BlockSpec(memory_space=pltpu.SMEM)
-PARAMS = pltpu.CompilerParams(vmem_limit_bytes=34 * 1024 * 1024)
+PARAMS = pltpu.CompilerParams(vmem_limit_bytes=36 * 1024 * 1024)
 LIGHT = pltpu.CompilerParams(vmem_limit_bytes=20 * 1024 * 1024)
 
 
@@ -51,7 +51,7 @@
                 out[m, 0, pl.ds(len(kinds) * step, FLAG_ROWS)] = flags
 
 
-def pack(jobs, heads, places, flags, sources, spare):
+def pack(jobs, heads, places, flags, sources, spare, kept=jax.ShapeDtypeStruct):
     _, tile, lane_width = sources[0].shape
     step = tile // BLOCKS
     team = places.shape[0]
@@ -67,7 +67,7 @@
     return pl.pallas_call(
         functools.partial(pack_kernel, jobs, step, start),
         grid=(BLOCKS,),
-        out_shape=[struct(shape, BF16) for shape in shapes],
+        out_shape=[kept(shape, BF16) for shape in shapes],
         in_specs=[SMEM, SMEM]
         + [pl.BlockSpec((1, step, wide), lambda i: (0, i, block))] * 4
         + [ANY] * len(spare),
@@ -92,18 +92,22 @@
                         out[0, g, at] = grad[e, n, pl.ds(g * step, step)]
 
 
-def relay(step, held, near, far, grads, spare):
+def relay(step, held, near, far, grads, spare, flagged=False):
     rows = len(near)
     kinds = 2 if far else 1
     high = (4 if grads else 2) * rows * step
+    flag_sources = [*near, *far] if flagged else []
 
     def kernel(*refs):
         refs = list(refs)
         near_refs = [(refs.pop(0), 0) for _ in range(rows)]
         far_refs = [(refs.pop(0), 0) for _ in far]
         grad_refs = [refs.pop(0) for _ in grads] or [None] * kinds
+        flag_refs = [refs.pop(0) for _ in flag_sources]
         outs = refs[len(spare) :]
-        relay_kernel(step, rows, near_refs, far_refs, grad_refs, outs)
+        relay_kernel(step, rows, near_refs, far_refs, grad_refs, outs[:kinds])
+        for d, ref in enumerate(flag_refs):
+            outs[kinds][d] = ref[0, 0]
 
     def whole(shape):
         return pl.BlockSpec(shape, lambda i: (0,) * len(shape))
@@ -112,18 +116,27 @@
     return pl.pallas_call(
         kernel,
         grid=(1,),
-        out_shape=[struct(shape, BF16)] * kinds,
+        out_shape=[struct(shape, BF16)] * kinds
+        + ([struct((len(flag_sources), FLAG_ROWS, HD), BF16)] if flagged else []),
         in_specs=[
             pl.BlockSpec((1, BLOCKS, 2 * step, HD), lambda i, at=at: (at, 0, 0, 0))
             for at in [held] * rows + [0] * len(far)
         ]
         + [whole(value.shape) for value in grads]
+        + [
+            pl.BlockSpec(
+                (1, 1, FLAG_ROWS, HD),
+                lambda i, at=value.shape[2] // FLAG_ROWS - 1: (0, 0, at, 0),
+            )
+            for value in flag_sources
+        ]
         + [ANY] * len(spare),
-        out_specs=[whole(shape)] * kinds,
+        out_specs=[whole(shape)] * kinds
+        + ([whole((len(flag_sources), FLAG_ROWS, HD))] if flagged else []),
         cost_estimate=moved(kinds * 4 * BLOCKS * high * HD),
         compiler_params=LIGHT,
         name="relay",
-    )(*near, *far, *grads, *spare)
+    )(*near, *far, *grads, *flag_sources, *spare)
 
 
 def nt(a, b):
@@ -165,46 +178,30 @@
         query = qbuf[a]
         grad = gbuf[a]
 
-        def seen(b):
-            count = 0
-            for f in range(rows):
-                for e in range(rows):
-                    count = count + table_ref[a * rows + f, b * rows + e]
-            return count > 0
-
-        def scores(b, top):
-            def live(top):
-                place = table_ref[a * rows, 3 * rows + b]
-                for e in range(rows):
-                    keep = jnp.zeros((1, width), jnp.int32)
-                    for f in range(rows):
-                        inside = (lane >= f * tile) & (lane < (f + 1) * tile)
-                        keep = jnp.where(inside, table_ref[a * rows + f, b * rows + e], keep)
-                    mask = jnp.where(keep > 0, 0.0, -jnp.inf)
-                    s = nt(kbuf[place, pl.ds(e * tile, tile)], query) + mask
-                    s_buf[b, pl.ds(e * tile, tile)] = s
-                    top = jnp.maximum(top, jnp.max(s, axis=0, keepdims=True))
-                return top
-
-            return lax.cond(seen(b), live, lambda top: top, top)
-
-        top = lax.fori_loop(0, 3, scores, jnp.full((1, width), -jnp.inf, F32))
-        ot[...] = jnp.zeros((HD, width), F32)
-
-        def expo(b, total):
-            def live(total):
-                place = table_ref[a * rows, 3 * rows + b]
-                for e in range(rows):
-                    at = pl.ds(e * tile, tile)
-                    p = jnp.exp2((s_buf[b, at] - top) * FACTOR)
-                    total = total + jnp.sum(p, axis=0, keepdims=True)
-                    p_buf[b, at] = p.astype(BF16)
-                ot[...] += nn(vt[place], p_buf[b])
-                return total
-
-            return lax.cond(seen(b), live, lambda total: total, total)
-
-        total = lax.fori_loop(0, 3, expo, jnp.zeros((1, width), F32))
+        blocks = range(3)
+        spots = [table_ref[a * rows, 3 * rows + b] for b in blocks]
+        top = jnp.full((1, width), -jnp.inf, F32)
+        for b in blocks:
+            for e in range(rows):
+                at = pl.ds(e * tile, tile)
+                keep = jnp.zeros((1, width), jnp.int32)
+                for f in range(rows):
+                    inside = (lane >= f * tile) & (lane < (f + 1) * tile)
+                    keep = jnp.where(inside, table_ref[a * rows + f, b * rows + e], keep)
+                mask = jnp.where(keep > 0, 0.0, -jnp.inf)
+                s = nt(kbuf[spots[b], at], query) + mask
+                s_buf[b, at] = s
+                top = jnp.maximum(top, jnp.max(s, axis=0, keepdims=True))
+
+        total = jnp.zeros((1, width), F32)
+        for b in blocks:
+            for e in range(rows):
+                at = pl.ds(e * tile, tile)
+                p = jnp.exp2((s_buf[b, at] - top) * FACTOR)
+                total = total + jnp.sum(p, axis=0, keepdims=True)
+                p_buf[b, at] = p.astype(BF16)
+            term = nn(vt[spots[b]], p_buf[b])
+            ot[...] = term if b == 0 else ot[...] + term
         inv = 1.0 / total
         low_t = (ot[...] * inv).astype(BF16)
         grad_t = grad.T.astype(F32)
@@ -212,25 +209,16 @@
         grad_over = (grad_t * inv).astype(BF16)
         query_over = (query.T.astype(F32) * (inv * SCALE)).astype(BF16)
         out = low_t.T
-        ot[...] = jnp.zeros((HD, width), F32)
-
-        def backward(b, carry):
-            @pl.when(seen(b))
-            def _():
-                place = table_ref[a * rows, 3 * rows + b]
-                for e in range(rows):
-                    at = pl.ds(e * tile, tile)
-                    p = p_buf[b, at]
-                    dp = nt(vbuf[place, at], grad)
-                    ds = (p.astype(F32) * (dp - offset)).astype(BF16)
-                    ds_buf[at] = ds
-                dv_t[place] += nt(grad_over, p_buf[b])
-                dk_t[place] += nt(query_over, ds_buf[...])
-                ot[...] += nn(kt[place], ds_buf[...])
-
-            return carry
-
-        lax.fori_loop(0, 3, backward, 0)
+
+        for b in blocks:
+            for e in range(rows):
+                at = pl.ds(e * tile, tile)
+                dp = nt(vbuf[spots[b], at], grad)
+                ds_buf[b, at] = p_buf[b, at] * (dp - offset).astype(BF16)
+            dv_t[spots[b]] += nt(grad_over, p_buf[b])
+            dk_t[spots[b]] += nt(query_over, ds_buf[b])
+            term = nn(kt[spots[b]], ds_buf[b])
+            ot[...] = term if b == 0 else ot[...] + term
         dq = (ot[...] * (inv * SCALE)).astype(BF16).T
         for f in range(rows):
             done[a * rows + f, 0] = out[f * tile : (f + 1) * tile]
@@ -284,7 +272,7 @@
             pltpu.VMEM((places, HD, width), F32),
             pltpu.VMEM((3, width, width), F32),
             pltpu.VMEM((3, width, width), BF16),
-            pltpu.VMEM((width, width), BF16),
+            pltpu.VMEM((3, width, width), BF16),
             pltpu.VMEM((HD, width), F32),
         ],
         cost_estimate=pl.CostEstimate(
@@ -413,25 +401,50 @@
     far = tuple(range(rows, team))
     step = tile // BLOCKS
 
-    jobs = [(d, (0,), part, part[0] == 0) for part in ((0, 1), (2, 3)) for d in far]
-    jobs += [(1, (0,), kinds, True), (0, (0,), kinds, True)]
+    jobs = [(d, (0,), kinds, True) for d in (*far, 1, 0)]
     packed = pack(jobs, (0,), members, flags, sources, [])
     count = len(far)
-    first_kv = [swap(packed[n], d) for n, d in enumerate(far)]
-    first_qg = [swap(packed[count + n], d) for n, d in enumerate(far)]
     mates = {0: (packed[-1], swap(packed[-2], 1), 0)}
-    sent = {}
+    sent = {(0, d): packed[n] for n, d in enumerate(far)}
     rest = every[1:]
     if rest:
         jobs = [(d, (c,), kinds, False) for c in rest for d in far]
         jobs += [(1, rest, kinds, False), (0, rest, kinds, False)]
-        packed = pack(jobs, rest, members, flags, sources, [mates[0][1]])
-        sent = {(c, d): packed[m * count + n] for m, c in enumerate(rest) for n, d in enumerate(far)}
+        packed = pack(jobs, rest, members, flags, sources, [mates[0][1]], pltpu.HBM)
+        sent.update(
+            {(c, d): packed[m * count + n] for m, c in enumerate(rest) for n, d in enumerate(far)}
+        )
         beside = swap(packed[-2], 1)
         mates.update({c: (packed[-1], beside, m) for m, c in enumerate(rest)})
 
-    lists = list(mates[0][:2]) + first_kv
-    table = jnp.stack([value[0, 0, -FLAG_ROWS, : 3 * rows] for value in lists]).astype(jnp.int32)
+    arrived = {key: swap(value, key[1]) for key, value in sent.items()}
+    halos = {}
+    ready = {}
+    worked = {}
+    home = {}
+
+    def pass_on(c, spare):
+        pieces = [arrived[c, d] for d in far]
+        grads = [worked[c - 2][3], worked[c - 2][2]] if c >= 2 else []
+        outs = relay(step, mates[c][2], mates[c][:2], pieces, grads, spare, c == 0)
+        ready[c] = outs[0]
+        halos[c] = (shift(outs[0], 0), shift(outs[span - 1], 1))
+        return outs[-1]
+
+    def finished(c, spare):
+        done, local, grads_one, grads_two = worked[c]
+        if c + 2 < per:
+            grads = [(halos[c + 2][1], True), (halos[c + 2][0], True)]
+        else:
+            grads = [(shift(grads_one, 1), False), (shift(grads_two, 0), False)]
+        pieces = finish(rows, extras, done, local, grads, spare)
+        home[c] = [swap(piece, d) for d, piece in enumerate(pieces)]
+        return pieces[0]
+
+    all_flags = pass_on(0, hbm([packed[0]]))
+    if per > 1:
+        pass_on(1, [ready[0]])
+    table = all_flags[:, 0, : 3 * rows].astype(jnp.int32)
     table = table.reshape(team, 3, rows)
     table = jnp.where(row == 0, table, table[:, :, ::-1])
     if span == 2:
@@ -451,32 +464,6 @@
     spots = jnp.repeat(jnp.asarray(windows, jnp.int32), rows, axis=0)
     table = jnp.concatenate([table.reshape(team, 3 * rows), spots], axis=1)
 
-    arrived = {key: swap(value, key[1]) for key, value in sent.items()}
-    halos = {}
-    ready = {}
-    worked = {}
-    home = {}
-
-    def pass_on(c, spare):
-        pieces = first_kv if c == 0 else [arrived[c, d] for d in far]
-        grads = worked[c - 2][2:] if c >= 2 else []
-        payloads = relay(
-            step, mates[c][2], mates[c][:2], pieces, [grads[1], grads[0]] if grads else [], spare
-        )
-        ready[c] = payloads[0]
-        halos[c] = (shift(payloads[0], 0), shift(payloads[-1], 1))
-
-    def finished(c, spare):
-        done, local, grads_one, grads_two = worked[c]
-        if c + 2 < per:
-            grads = [(halos[c + 2][1], True), (halos[c + 2][0], True)]
-        else:
-            grads = [(shift(grads_one, 1), False), (shift(grads_two, 0), False)]
-        pieces = finish(rows, extras, done, local, grads, spare)
-        home[c] = [swap(piece, d) for d, piece in enumerate(pieces)]
-        return pieces[0]
-
-    pass_on(0, [])
     for c in every:
         inputs = []
         loads = []
@@ -489,19 +476,13 @@
         for e in range(rows):
             add(mates[c][e], mates[c][2], "kvqg", 0, [e])
         for n in range(len(far)):
-            if c == 0:
-                add(first_kv[n], 0, "kv", 1, [n])
-                add(first_qg[n], 0, "qg", 1, [n])
-            else:
-                add(arrived[c, far[n]], 0, "kvqg", 1, [n])
+            add(arrived[c, far[n]], 0, "kvqg", 1, [n])
         for n in range(2):
             add(halos[c][n], 0, "kv", span + n, range(rows))
-        spare = [ready[c + 1]] if 1 <= c < per - 1 else []
+        spare = [ready[c + 1]] if c < per - 1 else []
         if c >= 2:
             spare.append(finished(c - 2, [worked[c - 1][0]]))
         worked[c] = attend(rows, tile, span, table, tuple(loads), inputs, spare)
-        if c == 0 and per > 1:
-            pass_on(1, [worked[0][0]])
         if c + 2 < per:
             pass_on(c + 2, [])
     for c in every[-2:]:

time: 202 us -> 188 us (0.931)
  starting transfers between devices: 62.9 us -> 52.5 us
  waiting for transfers between devices: 49.3 us -> 42.8 us
  Pallas kernels: 79.8 us -> 83 us
    ppermute x12, starting transfers between devices: 42.5 us -> 33.7 us  [shift(): return lax.ppermute(value, RING, pairs)]
    ppermute x24 -> x22, waiting for transfers between devices: 40.7 us -> 33.3 us  [swap(): lax.ppermute(value, RING, [(i, i - i % team + (i % team ^ d)) for i in ra...]
    pallas_call x4, Pallas kernels: 59.4 us -> 61.7 us  [attend(): pl.pallas_call(functools.partial(attend_kernel, plan, rows, tile), grid=(...]
    ppermute x24 -> x22, starting transfers between devices: 20.5 us -> 18.7 us  [swap(): lax.ppermute(value, RING, [(i, i - i % team + (i % team ^ d)) for i in ra...]
    unnamed x22 -> x26, local copies, waits for them, and re-layouts: 5.46 us -> 6.03 us
  transfers between devices with their start and end apart: 36 -> 34, of which waited for: 9 -> 10; matrix products, arithmetic and copies ran while one was open for 0% -> 0% of each run, Pallas kernels for 37% -> 41%
where the time goes in v6:
time: 188 us; the launch traced here: 187 us
  Pallas kernels  83 us (44%)
  starting transfers between devices  52.5 us (28%)
  waiting for transfers between devices  42.8 us (23%)
  local copies, waits for them, and re-layouts  6.35 us (3%)
    pallas_call x4, Pallas kernels, attend(): pl.pallas_call(functools.partial(attend_kernel, plan, rows, tile), grid=(...  61.7 us
    ppermute x12, starting transfers between devices, shift(): return lax.ppermute(value, RING, pairs)  33.7 us
    ppermute x22, waiting for transfers between devices, swap(): lax.ppermute(value, RING, [(i, i - i % team + (i % team ^ d)) for i in ra...  33.3 us
    ppermute x22, starting transfers between devices, swap(): lax.ppermute(value, RING, [(i, i - i % team + (i % team ^ d)) for i in ra...  18.7 us
    pallas_call x4, Pallas kernels, unpack(): pl.pallas_call(kernel, grid=(BLOCKS,), out_shape=[struct(shape, BF16)] *...  9.58 us
    ppermute x12, waiting for transfers between devices, shift(): return lax.ppermute(value, RING, pairs)  9.51 us
    pallas_call x2, Pallas kernels, pack(): pl.pallas_call(functools.partial(pack_kernel, jobs, step, start), grid=(B...  9.27 us
    unnamed x26, local copies, waits for them, and re-layouts  6.03 us
  transfers between devices with their start and end apart: 34, of which 10 were waited for; matrix products, arithmetic and copies ran while one was open for 0% of the time, Pallas kernels for 41%

profile of v6, /device:TPU:0, one launch (start us, length us, event | category | flops | bytes accessed | tf_op | source)
XLA Modules:
  0.0 187.3 jit_solution(13500435944754815042)
XLA Ops:
  1.3 0.7 fusion.3
  2.1 3.6 %pack.2 = (bf16[1,4,400,128]{3,2,1,0:T(8,128)(2,1)}, bf16[1,4,400,128]{3,2,1,0:T(8,128)(2,1)}, bf16[1,4,400,128]{3,2,1,0:T(8,128)(2,1)S(1)}, bf16[1,4,400,128]{3,2,1,0:T(8,128)(2,1)S(1)}) custom-call(s32[4]{0:T(128)S(1)} %iota_xor_fusion.places_ref, s32[6]{0:T(128)S(1)} %convert_element_type.10.flags_ref, bf16[1,384,2048]{2,1,0:T(8,128)(2,1)} %refs_0_.3, ...), custom_call_target="tpu_custom_call" | custom-call | bytes 3276800 | tf_op jit(solution)/shard_map/pack/pallas_call | solution.py:67
  5.8 0.5 collective-permute-start
  6.2 2.6 %collective-permute-start.1 = (bf16[1,4,400,128]{3,2,1,0:T(8,128)(2,1)}, bf16[1,4,400,128]{3,2,1,0:T(8,128)(2,1)S(1)}, u32[]{:S(2)}, u32[]{:S(2)}) collective-permute-start(bf16[1,4,400,128]{3,2,1,0:T(8,128)(2,1)} %get-tuple-element.71), channel_id=1, source_target_pairs={{0,2},{1,3},{2,0},{3,1},{4,6},{5,7},{6,4},{7,5},{8,10},{9,11},{10,... | collective-permute-start | bytes 1228808 | tf_op jit(solution)/shard_map/ppermute | solution.py:377
  8.9 5.6 %pack.3 = (bf16[1,4,384,128]{3,2,1,0:T(8,128)(2,1)}, bf16[1,4,384,128]{3,2,1,0:T(8,128)(2,1)}, bf16[1,4,384,128]{3,2,1,0:T(8,128)(2,1)}, bf16[1,4,384,128]{3,2,1...) custom-call(s32[4]{0:T(128)S(1)} %iota_xor_fusion.places_ref, ...), custom_call_target="tpu_custom_call" | custom-call | bytes 9437184 | tf_op jit(solution)/shard_map/pack/pallas_call | solution.py:67
  14.5 0.2 collective-permute-start.3
  14.7 1.7 collective-permute-start.7
  16.4 0.3 collective-permute-start.6
  16.7 2.6 %collective-permute-done.1.refs_2_.refs_6_ = bf16[1,4,400,128]{3,2,1,0:T(8,128)(2,1)S(1)} collective-permute-done((bf16[1,4,400,128]{3,2,1,0:T(8,128)(2,1)}, bf16[1,4,400,128]{3,2,1,0:T(8,128)(2,1)S(1)}, u32[]{:S(2)}, u32[]{:S(2)}) %collective-permute-start.1) | collective-permute-done | bytes 409632 | tf_op jit(solution)/shard_map/ppermute | solution.py:377
  19.3 0.7 copy-done.1
  20.1 7.6 %collective-permute-done.2.refs_3_.refs_7_ = bf16[1,4,400,128]{3,2,1,0:T(8,128)(2,1)S(1)} collective-permute-done((bf16[1,4,400,128]{3,2,1,0:T(8,128)(2,1)}, bf16[1,4,400,128]{3,2,1,0:T(8,128)(2,1)S(1)}, u32[]{:S(2)}, u32[]{:S(2)}) %collective-permute-start.2) | collective-permute-done | bytes 409632 | tf_op jit(solution)/shard_map/ppermute | solution.py:377
  27.7 0.7 copy-done.4
  28.4 1.0 copy-done.2
  29.4 1.0 copy-done.5
  30.5 0.7 copy-done.7
  31.3 0.8 copy-done.9
  32.2 4.2 %collective-permute-start.13 = (bf16[1,4,384,128]{3,2,1,0:T(8,128)(2,1)}, bf16[1,4,384,128]{3,2,1,0:T(8,128)(2,1)}, u32[]{:S(2)}, u32[]{:S(2)}) collective-permute-start(bf16[1,4,384,128]{3,2,1,0:T(8,128)(2,1)} %copy-done.9), channel_id=1, source_target_pairs={{0,4},{1,5},{4,8},{5,9},{6,2},{7,3},{8,12},{9,13},{10,6},{11,7},{1... | collective-permute-start | bytes 1179656 | tf_op jit(solution)/shard_map/ppermute | solution.py:389
  36.4 1.3 collective-permute-start.12
  38.1 2.5 %collective-permute-start.10 = (bf16[1,4,384,128]{3,2,1,0:T(8,128)(2,1)}, bf16[1,4,384,128]{3,2,1,0:T(8,128)(2,1)S(1)}, u32[]{:S(2)}, u32[]{:S(2)}) collective-permute-start(bf16[1,4,384,128]{3,2,1,0:T(8,128)(2,1)} %get-tuple-element.83), channel_id=1, source_target_pairs={{0,2},{1,3},{2,0},{3,1},{4,6},{5,7},{6,4},{7,5},{8,10},{9,11},{10,... | collective-permute-start | bytes 1179656 | tf_op jit(solution)/shard_map/ppermute | solution.py:377
  40.6 4.4 %collective-permute-done.6.refs_2_ = bf16[1,4,384,128]{3,2,1,0:T(8,128)(2,1)} collective-permute-done((bf16[1,4,384,128]{3,2,1,0:T(8,128)(2,1)}, bf16[1,4,384,128]{3,2,1,0:T(8,128)(2,1)}, u32[]{:S(2)}, u32[]{:S(2)}) %collective-permute-start.6) | collective-permute-done | bytes 393248 | tf_op jit(solution)/shard_map/ppermute | solution.py:377
  45.0 0.7 collective-permute-start.11
  45.8 1.0 copy-done.8
  46.8 1.2 relay.5
  48.0 3.5 %collective-permute-start.9 = (bf16[1,4,384,128]{3,2,1,0:T(8,128)(2,1)S(1)}, bf16[1,4,384,128]{3,2,1,0:T(8,128)(2,1)S(1)}, u32[]{:S(2)}, u32[]{:S(2)}) collective-permute-start(bf16[1,4,384,128]{3,2,1,0:T(8,128)(2,1)S(1)} %get-tuple-element.82), channel_id=1, source_target_pairs={{0,4},{1,5},{4,8},{5,9},{6,2},{7,3},{8,12},{9,13},{10,6},{11,7},{1... | collective-permute-start | bytes 1179656 | tf_op jit(solution)/shard_map/ppermute | solution.py:389
  51.5 1.3 collective-permute-start.8
  52.8 15.7 %attend.4 = (bf16[4,2,384,128]{3,2,1,0:T(8,128)(2,1)S(1)}, f32[4,2,384,128]{3,2,1,0:T(8,128)S(1)}, bf16[2,2,384,128]{3,2,1,0:T(8,128)(2,1)S(1)}, bf16[2,2,384,128]{3,2,1,0:T(8,128)(2,1)S(1)}) custom-call(s32[4,9]{1,0:T(4,128)S(1)} %pad_add_fusion.1.table_ref, bf16[1,4,400,128]{3,2,1,0:T(8,128)(2,1)S(1)} %get-tuple-element.69.refs_0_.refs_4_, ...), custom_call_target="tpu_custom_call" | custom-call | flops 5435817984 | bytes 8388608 | tf_op jit(solution)/shard_map/attend/pallas_call | solution.py:258
  68.6 0.2 relay.6
  68.7 4.7 %collective-permute-start.17 = (bf16[1,4,768,128]{3,2,1,0:T(8,128)(2,1)S(1)}, bf16[1,4,768,128]{3,2,1,0:T(8,128)(2,1)S(1)}, u32[]{:S(2)}, u32[]{:S(2)}) collective-permute-start(bf16[1,4,768,128]{3,2,1,0:T(8,128)(2,1)S(1)} %get-tuple-element.95), channel_id=1, source_target_pairs={{0,4},{1,5},{4,8},{5,9},{6,2},{7,3},{8,12},{9,13},{10,6},{11,7},{1... | collective-permute-start | bytes 2359304 | tf_op jit(solution)/shard_map/ppermute | solution.py:389
  73.5 1.5 collective-permute-start.16
  75.0 2.3 %collective-permute-start.4 = (bf16[1,4,384,128]{3,2,1,0:T(8,128)(2,1)S(1)}, bf16[1,4,384,128]{3,2,1,0:T(8,128)(2,1)S(1)}, u32[]{:S(2)}, u32[]{:S(2)}) collective-permute-start(bf16[1,4,384,128]{3,2,1,0:T(8,128)(2,1)S(1)} %copy-done.12), channel_id=1, source_target_pairs={{0,2},{1,3},{2,0},{3,1},{4,6},{5,7},{6,4},{7,5},{8,10},{9,11},{10,... | collective-permute-start | bytes 1179656 | tf_op jit(solution)/shard_map/ppermute | solution.py:377
  77.3 15.7 %attend.5 = (bf16[4,2,384,128]{3,2,1,0:T(8,128)(2,1)S(1)}, f32[4,2,384,128]{3,2,1,0:T(8,128)S(1)}, bf16[2,2,384,128]{3,2,1,0:T(8,128)(2,1)S(1)}, bf16[2,2,384,128]{3,2,1,0:T(8,128)(2,1)S(1)}) custom-call(s32[4,9]{1,0:T(4,128)S(1)} %pad_add_fusion.1.table_ref, bf16[3,4,384,128]{3,2,1,0:T(8,128)(2,1)S(1)} %copy-done, ...), custom_call_target="tpu_custom_call" | custom-call | flops 5435817984 | bytes 8388608 | tf_op jit(solution)/shard_map/attend/pallas_call | solution.py:258
  93.0 1.2 collective-permute-done.5.refs_3_
  94.2 0.2 relay.7
  94.4 4.3 %collective-permute-start.15 = (bf16[1,4,768,128]{3,2,1,0:T(8,128)(2,1)S(1)}, bf16[1,4,768,128]{3,2,1,0:T(8,128)(2,1)S(1)}, u32[]{:S(2)}, u32[]{:S(2)}) collective-permute-start(bf16[1,4,768,128]{3,2,1,0:T(8,128)(2,1)S(1)} %get-tuple-element.92), channel_id=1, source_target_pairs={{0,4},{1,5},{4,8},{5,9},{6,2},{7,3},{8,12},{9,13},{10,6},{11,7},{1... | collective-permute-start | bytes 2359304 | tf_op jit(solution)/shard_map/ppermute | solution.py:389
  98.7 1.5 collective-permute-start.14
  100.2 0.3 finish.4
  100.5 1.0 collective-permute-start.24
  101.5 0.7 collective-permute-start.25
  102.2 15.1 %attend.6 = (bf16[4,2,384,128]{3,2,1,0:T(8,128)(2,1)S(1)}, f32[4,2,384,128]{3,2,1,0:T(8,128)S(1)}, bf16[2,2,384,128]{3,2,1,0:T(8,128)(2,1)S(1)}, bf16[2,2,384,128]{3,2,1,0:T(8,128)(2,1)S(1)}) custom-call(s32[4,9]{1,0:T(4,128)S(1)} %pad_add_fusion.1.table_ref, bf16[3,4,384,128]{3,2,1,0:T(8,128)(2,1)S(1)} %copy-done, ...), custom_call_target="tpu_custom_call" | custom-call | flops 5435817984 | bytes 8388608 | tf_op jit(solution)/shard_map/attend/pallas_call | solution.py:258
  117.3 4.3 %collective-permute-start.22 = (bf16[2,2,384,128]{3,2,1,0:T(8,128)(2,1)S(1)}, bf16[2,2,384,128]{3,2,1,0:T(8,128)(2,1)S(1)}, u32[]{:S(2)}, u32[]{:S(2)}) collective-permute-start(bf16[2,2,384,128]{3,2,1,0:T(8,128)(2,1)S(1)} %get-tuple-element.108), channel_id=1, source_target_pairs={{0,4},{1,5},{4,8},{5,9},{6,2},{7,3},{8,12},{9,13},{10,6},{11,7},{1... | collective-permute-start | bytes 1179656 | tf_op jit(solution)/shard_map/ppermute | solution.py:389
  121.6 1.6 collective-permute-start.23
  123.2 0.3 finish.5
  123.5 1.5 collective-permute-start.20
  125.0 0.4 collective-permute-start.21
  125.4 15.1 %attend.7 = (bf16[4,2,384,128]{3,2,1,0:T(8,128)(2,1)S(1)}, f32[4,2,384,128]{3,2,1,0:T(8,128)S(1)}, bf16[2,2,384,128]{3,2,1,0:T(8,128)(2,1)S(1)}, bf16[2,2,384,128]{3,2,1,0:T(8,128)(2,1)S(1)}) custom-call(s32[4,9]{1,0:T(4,128)S(1)} %pad_add_fusion.1.table_ref, bf16[3,4,384,128]{3,2,1,0:T(8,128)(2,1)S(1)} %copy-done, ...), custom_call_target="tpu_custom_call" | custom-call | flops 5435817984 | bytes 8388608 | tf_op jit(solution)/shard_map/attend/pallas_call | solution.py:258
  140.6 4.3 %collective-permute-start.18 = (bf16[2,2,384,128]{3,2,1,0:T(8,128)(2,1)S(1)}, bf16[2,2,384,128]{3,2,1,0:T(8,128)(2,1)S(1)}, u32[]{:S(2)}, u32[]{:S(2)}) collective-permute-start(bf16[2,2,384,128]{3,2,1,0:T(8,128)(2,1)S(1)} %get-tuple-element.103), channel_id=1, source_target_pairs={{0,4},{1,5},{4,8},{5,9},{6,2},{7,3},{8,12},{9,13},{10,6},{11,7},{1... | collective-permute-start | bytes 1179656 | tf_op jit(solution)/shard_map/ppermute | solution.py:389
  144.9 1.3 collective-permute-start.19
  146.2 0.2 finish.6
  146.4 1.2 collective-permute-start.26
  147.6 0.5 collective-permute-start.27
  148.1 0.5 collective-permute-start.33
  148.6 5.3 %collective-permute-done.18.refs_0_ = bf16[2,2,384,128]{3,2,1,0:T(8,128)(2,1)S(1)} collective-permute-done((bf16[2,2,384,128]{3,2,1,0:T(8,128)(2,1)S(1)}, bf16[2,2,384,128]{3,2,1,0:T(8,128)(2,1)S(1)}, u32[]{:S(2)}, u32[]{:S(2)}) %collective-permute-start.18) | collective-permute-done | bytes 393248 | tf_op jit(solution)/shard_map/ppermute | solution.py:389
  153.9 4.1 %collective-permute-done.19.refs_1_ = bf16[2,2,384,128]{3,2,1,0:T(8,128)(2,1)S(1)} collective-permute-done((bf16[2,2,384,128]{3,2,1,0:T(8,128)(2,1)S(1)}, bf16[2,2,384,128]{3,2,1,0:T(8,128)(2,1)S(1)}, u32[]{:S(2)}, u32[]{:S(2)}) %collective-permute-start.19) | collective-permute-done | bytes 393248 | tf_op jit(solution)/shard_map/ppermute | solution.py:389
  158.1 0.3 collective-permute-done.26.refs_5_.refs_2_
  158.4 7.1 %collective-permute-done.27.refs_6_.refs_3_ = bf16[1,4,384,128]{3,2,1,0:T(8,128)(2,1)S(1)} collective-permute-done((bf16[1,4,384,128]{3,2,1,0:T(8,128)(2,1)S(1)}, bf16[1,4,384,128]{3,2,1,0:T(8,128)(2,1)S(1)}, u32[]{:S(2)}, u32[]{:S(2)}) %collective-permute-start.27) | collective-permute-done | bytes 393248 | tf_op jit(solution)/shard_map/ppermute | solution.py:377
  165.5 0.2 finish.7
  165.7 0.5 collective-permute-start.28
  166.2 1.3 collective-permute-start.29
  167.7 2.4 %unpack.4 = (bf16[1,384,2048]{2,1,0:T(8,128)(2,1)}, bf16[1,384,2048]{2,1,0:T(8,128)(2,1)}, bf16[1,384,2048]{2,1,0:T(8,128)(2,1)}, bf16[1,384,2048]{2,1,0:T(8,128)(2,1)}) custom-call(s32[4]{0:T(128)S(1)} %iota_xor_fusion.places_ref, bf16[1,4,384,128]{3,2,1,0:T(8,128)(2,1)S(1)} %get-tuple-element.98.refs_7_.refs_0_, ...), custom_call_target="tpu_custom_call" | custom-call | bytes 3145728 | tf_op jit(solution)/shard_map/unpack/pallas_call | solution.py:344
  170.1 2.4 %unpack.5 = (bf16[1,384,2048]{2,1,0:T(8,128)(2,1)}, bf16[1,384,2048]{2,1,0:T(8,128)(2,1)}, bf16[1,384,2048]{2,1,0:T(8,128)(2,1)}, bf16[1,384,2048]{2,1,0:T(8,128)(2,1)}) custom-call(s32[4]{0:T(128)S(1)} %iota_xor_fusion.places_ref, ...), custom_call_target="tpu_custom_call", output_to_operand_aliasing={{0}: (5, {}), {1}: (6, {}), {2}: (7, {}), {3}: (8, {})} | custom-call | bytes 3145728 | tf_op jit(solution)/shard_map/unpack/pallas_call | solution.py:344
  172.5 2.4 %unpack.6 = (bf16[1,384,2048]{2,1,0:T(8,128)(2,1)}, bf16[1,384,2048]{2,1,0:T(8,128)(2,1)}, bf16[1,384,2048]{2,1,0:T(8,128)(2,1)}, bf16[1,384,2048]{2,1,0:T(8,128)(2,1)}) custom-call(s32[4]{0:T(128)S(1)} %iota_xor_fusion.places_ref, ...), custom_call_target="tpu_custom_call", output_to_operand_aliasing={{0}: (5, {}), {1}: (6, {}), {2}: (7, {}), {3}: (8, {})} | custom-call | bytes 3145728 | tf_op jit(solution)/shard_map/unpack/pallas_call | solution.py:344
  174.9 3.3 %collective-permute-done.29.refs_2_ = bf16[1,4,384,128]{3,2,1,0:T(8,128)(2,1)S(1)} collective-permute-done((bf16[1,4,384,128]{3,2,1,0:T(8,128)(2,1)S(1)}, bf16[1,4,384,128]{3,2,1,0:T(8,128)(2,1)S(1)}, u32[]{:S(2)}, u32[]{:S(2)}) %collective-permute-start.29) | collective-permute-done | bytes 393248 | tf_op jit(solution)/shard_map/ppermute | solution.py:377
  178.2 6.7 %collective-permute-done.30.refs_3_ = bf16[1,4,384,128]{3,2,1,0:T(8,128)(2,1)S(1)} collective-permute-done((bf16[1,4,384,128]{3,2,1,0:T(8,128)(2,1)S(1)}, bf16[1,4,384,128]{3,2,1,0:T(8,128)(2,1)S(1)}, u32[]{:S(2)}, u32[]{:S(2)}) %collective-permute-start.30) | collective-permute-done | bytes 393248 | tf_op jit(solution)/shard_map/ppermute | solution.py:377
  184.9 2.4 %unpack.7 = (bf16[1,384,2048]{2,1,0:T(8,128)(2,1)}, bf16[1,384,2048]{2,1,0:T(8,128)(2,1)}, bf16[1,384,2048]{2,1,0:T(8,128)(2,1)}, bf16[1,384,2048]{2,1,0:T(8,128)(2,1)}) custom-call(s32[4]{0:T(128)S(1)} %iota_xor_fusion.places_ref, ...), custom_call_target="tpu_custom_call", output_to_operand_aliasing={{0}: (5, {}), {1}: (6, {}), {2}: (7, {}), {3}: (8, {})} | custom-call | bytes 3145728 | tf_op jit(solution)/shard_map/unpack/pallas_call | solution.py:344
  (65 shorter events, 1.0 us)
Async XLA Ops:
  5.8 3.1 %collective-permute-start = (bf16[1,4,400,128]{3,2,1,0:T(8,128)(2,1)S(1)}, bf16[1,4,400,128]{3,2,1,0:T(8,128)(2,1)S(1)}, u32[]{:S(2)}, u32[]{:S(2)}) collective-permute-start(bf16[1,4,400,128]{3,2,1,0:T(8,128)(2,1)S(1)} %get-tuple-element.70), channel_id=1, source_target_pairs={{0,1},{1,0},{2,3},{3,2},{4,5},{5,4},{6,7},{7,6},{8,9},{9,8},{10,11... | collective-permute-start | bytes 1228808 | tf_op jit(solution)/shard_map/ppermute | solution.py:377
  6.2 13.1 %collective-permute-start.1 = (bf16[1,4,400,128]{3,2,1,0:T(8,128)(2,1)}, bf16[1,4,400,128]{3,2,1,0:T(8,128)(2,1)S(1)}, u32[]{:S(2)}, u32[]{:S(2)}) collective-permute-start(bf16[1,4,400,128]{3,2,1,0:T(8,128)(2,1)} %get-tuple-element.71), channel_id=1, source_target_pairs={{0,2},{1,3},{2,0},{3,1},{4,6},{5,7},{6,4},{7,5},{8,10},{9,11},{10,... | collective-permute-start | bytes 1228808 | tf_op jit(solution)/shard_map/ppermute | solution.py:377
  8.8 18.9 %collective-permute-start.2 = (bf16[1,4,400,128]{3,2,1,0:T(8,128)(2,1)}, bf16[1,4,400,128]{3,2,1,0:T(8,128)(2,1)S(1)}, u32[]{:S(2)}, u32[]{:S(2)}) collective-permute-start(bf16[1,4,400,128]{3,2,1,0:T(8,128)(2,1)} %get-tuple-element.72), channel_id=1, source_target_pairs={{0,3},{1,2},{2,1},{3,0},{4,7},{5,6},{6,5},{7,4},{8,11},{9,10},{10,... | collective-permute-start | bytes 1228808 | tf_op jit(solution)/shard_map/ppermute | solution.py:377
  14.5 31.3 %collective-permute-start.3 = (bf16[3,4,384,128]{3,2,1,0:T(8,128)(2,1)}, bf16[3,4,384,128]{3,2,1,0:T(8,128)(2,1)S(1)}, u32[]{:S(2)}, u32[]{:S(2)}) collective-permute-start(bf16[3,4,384,128]{3,2,1,0:T(8,128)(2,1)} %get-tuple-element.76), channel_id=1, source_target_pairs={{0,1},{1,0},{2,3},{3,2},{4,5},{5,4},{6,7},{7,6},{8,9},{9,8},{10,11... | collective-permute-start | bytes 3538952 | tf_op jit(solution)/shard_map/ppermute | solution.py:377
  14.7 23.4 %collective-permute-start.7 = (bf16[1,4,384,128]{3,2,1,0:T(8,128)(2,1)}, bf16[1,4,384,128]{3,2,1,0:T(8,128)(2,1)}, u32[]{:S(2)}, u32[]{:S(2)}) collective-permute-start(bf16[1,4,384,128]{3,2,1,0:T(8,128)(2,1)} %get-tuple-element.79), channel_id=1, source_target_pairs={{0,3},{1,2},{2,1},{3,0},{4,7},{5,6},{6,5},{7,4},{8,11},{9,10},{10,... | collective-permute-start | bytes 1179656 | tf_op jit(solution)/shard_map/ppermute | solution.py:377
  16.4 28.7 %collective-permute-start.6 = (bf16[1,4,384,128]{3,2,1,0:T(8,128)(2,1)}, bf16[1,4,384,128]{3,2,1,0:T(8,128)(2,1)}, u32[]{:S(2)}, u32[]{:S(2)}) collective-permute-start(bf16[1,4,384,128]{3,2,1,0:T(8,128)(2,1)} %get-tuple-element.73.refs_8_), channel_id=1, source_target_pairs={{0,2},{1,3},{2,0},{3,1},{4,6},{5,7},{6,4},{7,5},{8,10},{9,11},{10,... | collective-permute-start | bytes 1179656 | tf_op jit(solution)/shard_map/ppermute | solution.py:377
  19.3 0.8 copy-start.1
  27.7 0.8 copy-start.4
  28.4 1.0 copy-start.2
  29.4 1.0 copy-start.5
  30.4 7.6 %copy-start.10 = (s32[2,3]{1,0:T(2,128)S(1)}, s32[2,3]{1,0:T(2,128)}, u32[]{:S(2)}) copy-start(s32[2,3]{1,0:T(2,128)} %constant.47.clone) | copy-start | bytes 76
  30.4 15.4 %copy-start = (bf16[3,4,384,128]{3,2,1,0:T(8,128)(2,1)S(1)}, bf16[3,4,384,128]{3,2,1,0:T(8,128)(2,1)}, u32[]{:S(2)}) copy-start(bf16[3,4,384,128]{3,2,1,0:T(8,128)(2,1)} %get-tuple-element.75.refs_0_) | copy-start | bytes 3538948
  30.5 0.8 copy-start.7
  31.3 0.8 copy-start.9
  32.2 19.3 %collective-permute-start.13 = (bf16[1,4,384,128]{3,2,1,0:T(8,128)(2,1)}, bf16[1,4,384,128]{3,2,1,0:T(8,128)(2,1)}, u32[]{:S(2)}, u32[]{:S(2)}) collective-permute-start(bf16[1,4,384,128]{3,2,1,0:T(8,128)(2,1)} %copy-done.9), channel_id=1, source_target_pairs={{0,4},{1,5},{4,8},{5,9},{6,2},{7,3},{8,12},{9,13},{10,6},{11,7},{1... | collective-permute-start | bytes 1179656 | tf_op jit(solution)/shard_map/ppermute | solution.py:389
  36.4 16.4 %collective-permute-start.12 = (bf16[1,4,384,128]{3,2,1,0:T(8,128)(2,1)}, bf16[1,4,384,128]{3,2,1,0:T(8,128)(2,1)}, u32[]{:S(2)}, u32[]{:S(2)}) collective-permute-start(bf16[1,4,384,128]{3,2,1,0:T(8,128)(2,1)} %copy-done.7), channel_id=1, source_target_pairs={{2,6},{3,7},{4,0},{5,1},{6,10},{7,11},{8,4},{9,5},{10,14},{11,15},... | collective-permute-start | bytes 1179656 | tf_op jit(solution)/shard_map/ppermute | solution.py:389
  38.1 30.5 %collective-permute-start.10 = (bf16[1,4,384,128]{3,2,1,0:T(8,128)(2,1)}, bf16[1,4,384,128]{3,2,1,0:T(8,128)(2,1)S(1)}, u32[]{:S(2)}, u32[]{:S(2)}) collective-permute-start(bf16[1,4,384,128]{3,2,1,0:T(8,128)(2,1)} %get-tuple-element.83), channel_id=1, source_target_pairs={{0,2},{1,3},{2,0},{3,1},{4,6},{5,7},{6,4},{7,5},{8,10},{9,11},{10,... | collective-permute-start | bytes 1179656 | tf_op jit(solution)/shard_map/ppermute | solution.py:377
  45.0 23.5 %collective-permute-start.11 = (bf16[1,4,384,128]{3,2,1,0:T(8,128)(2,1)}, bf16[1,4,384,128]{3,2,1,0:T(8,128)(2,1)S(1)}, u32[]{:S(2)}, u32[]{:S(2)}) collective-permute-start(bf16[1,4,384,128]{3,2,1,0:T(8,128)(2,1)} %get-tuple-element.84), channel_id=1, source_target_pairs={{0,3},{1,2},{2,1},{3,0},{4,7},{5,6},{6,5},{7,4},{8,11},{9,10},{10,... | collective-permute-start | bytes 1179656 | tf_op jit(solution)/shard_map/ppermute | solution.py:377
  45.8 1.0 copy-start.8
  46.8 6.0 %copy-start.3 = (bf16[1,4,400,128]{3,2,1,0:T(8,128)(2,1)S(1)}, bf16[1,4,400,128]{3,2,1,0:T(8,128)(2,1)}, u32[]{:S(2)}) copy-start(bf16[1,4,400,128]{3,2,1,0:T(8,128)(2,1)} %copy-done.1) | copy-start | bytes 1228804
  46.8 6.0 %copy-start.6 = (bf16[1,4,400,128]{3,2,1,0:T(8,128)(2,1)S(1)}, bf16[1,4,400,128]{3,2,1,0:T(8,128)(2,1)}, u32[]{:S(2)}) copy-start(bf16[1,4,400,128]{3,2,1,0:T(8,128)(2,1)} %copy-done.4) | copy-start | bytes 1228804
  48.0 29.3 %collective-permute-start.9 = (bf16[1,4,384,128]{3,2,1,0:T(8,128)(2,1)S(1)}, bf16[1,4,384,128]{3,2,1,0:T(8,128)(2,1)S(1)}, u32[]{:S(2)}, u32[]{:S(2)}) collective-permute-start(bf16[1,4,384,128]{3,2,1,0:T(8,128)(2,1)S(1)} %get-tuple-element.82), channel_id=1, source_target_pairs={{0,4},{1,5},{4,8},{5,9},{6,2},{7,3},{8,12},{9,13},{10,6},{11,7},{1... | collective-permute-start | bytes 1179656 | tf_op jit(solution)/shard_map/ppermute | solution.py:389
  51.5 25.8 %collective-permute-start.8 = (bf16[1,4,384,128]{3,2,1,0:T(8,128)(2,1)S(1)}, bf16[1,4,384,128]{3,2,1,0:T(8,128)(2,1)S(1)}, u32[]{:S(2)}, u32[]{:S(2)}) collective-permute-start(bf16[1,4,384,128]{3,2,1,0:T(8,128)(2,1)S(1)} %get-tuple-element.81.refs_6_), channel_id=1, source_target_pairs={{2,6},{3,7},{4,0},{5,1},{6,10},{7,11},{8,4},{9,5},{10,14},{11,15},... | collective-permute-start | bytes 1179656 | tf_op jit(solution)/shard_map/ppermute | solution.py:389
  68.5 6.4 %copy-start.12 = (bf16[1,4,384,128]{3,2,1,0:T(8,128)(2,1)S(1)}, bf16[1,4,384,128]{3,2,1,0:T(8,128)(2,1)}, u32[]{:S(2)}) copy-start(bf16[1,4,384,128]{3,2,1,0:T(8,128)(2,1)} %get-tuple-element.77) | copy-start | bytes 1179652
  68.6 8.8 %copy-start.11 = (bf16[1,4,384,128]{3,2,1,0:T(8,128)(2,1)S(1)}, bf16[1,4,384,128]{3,2,1,0:T(8,128)(2,1)}, u32[]{:S(2)}) copy-start(bf16[1,4,384,128]{3,2,1,0:T(8,128)(2,1)} %get-tuple-element.78) | copy-start | bytes 1179652
  68.7 31.5 %collective-permute-start.17 = (bf16[1,4,768,128]{3,2,1,0:T(8,128)(2,1)S(1)}, bf16[1,4,768,128]{3,2,1,0:T(8,128)(2,1)S(1)}, u32[]{:S(2)}, u32[]{:S(2)}) collective-permute-start(bf16[1,4,768,128]{3,2,1,0:T(8,128)(2,1)S(1)} %get-tuple-element.95), channel_id=1, source_target_pairs={{0,4},{1,5},{4,8},{5,9},{6,2},{7,3},{8,12},{9,13},{10,6},{11,7},{1... | collective-permute-start | bytes 2359304 | tf_op jit(solution)/shard_map/ppermute | solution.py:389
  73.5 26.8 %collective-permute-start.16 = (bf16[1,4,768,128]{3,2,1,0:T(8,128)(2,1)S(1)}, bf16[1,4,768,128]{3,2,1,0:T(8,128)(2,1)S(1)}, u32[]{:S(2)}, u32[]{:S(2)}) collective-permute-start(bf16[1,4,768,128]{3,2,1,0:T(8,128)(2,1)S(1)} %get-tuple-element.88.refs_6_), channel_id=1, source_target_pairs={{2,6},{3,7},{4,0},{5,1},{6,10},{7,11},{8,4},{9,5},{10,14},{11,15},... | collective-permute-start | bytes 2359304 | tf_op jit(solution)/shard_map/ppermute | solution.py:389
  75.0 18.1 %collective-permute-start.4 = (bf16[1,4,384,128]{3,2,1,0:T(8,128)(2,1)S(1)}, bf16[1,4,384,128]{3,2,1,0:T(8,128)(2,1)S(1)}, u32[]{:S(2)}, u32[]{:S(2)}) collective-permute-start(bf16[1,4,384,128]{3,2,1,0:T(8,128)(2,1)S(1)} %copy-done.12), channel_id=1, source_target_pairs={{0,2},{1,3},{2,0},{3,1},{4,6},{5,7},{6,4},{7,5},{8,10},{9,11},{10,... | collective-permute-start | bytes 1179656 | tf_op jit(solution)/shard_map/ppermute | solution.py:377
  77.3 16.9 %collective-permute-start.5 = (bf16[1,4,384,128]{3,2,1,0:T(8,128)(2,1)S(1)}, bf16[1,4,384,128]{3,2,1,0:T(8,128)(2,1)S(1)}, u32[]{:S(2)}, u32[]{:S(2)}) collective-permute-start(bf16[1,4,384,128]{3,2,1,0:T(8,128)(2,1)S(1)} %copy-done.11), channel_id=1, source_target_pairs={{0,3},{1,2},{2,1},{3,0},{4,7},{5,6},{6,5},{7,4},{8,11},{9,10},{10,... | collective-permute-start | bytes 1179656 | tf_op jit(solution)/shard_map/ppermute | solution.py:377
  94.4 27.2 %collective-permute-start.15 = (bf16[1,4,768,128]{3,2,1,0:T(8,128)(2,1)S(1)}, bf16[1,4,768,128]{3,2,1,0:T(8,128)(2,1)S(1)}, u32[]{:S(2)}, u32[]{:S(2)}) collective-permute-start(bf16[1,4,768,128]{3,2,1,0:T(8,128)(2,1)S(1)} %get-tuple-element.92), channel_id=1, source_target_pairs={{0,4},{1,5},{4,8},{5,9},{6,2},{7,3},{8,12},{9,13},{10,6},{11,7},{1... | collective-permute-start | bytes 2359304 | tf_op jit(solution)/shard_map/ppermute | solution.py:389
  98.7 24.5 %collective-permute-start.14 = (bf16[1,4,768,128]{3,2,1,0:T(8,128)(2,1)S(1)}, bf16[1,4,768,128]{3,2,1,0:T(8,128)(2,1)S(1)}, u32[]{:S(2)}, u32[]{:S(2)}) collective-permute-start(bf16[1,4,768,128]{3,2,1,0:T(8,128)(2,1)S(1)} %get-tuple-element.91.refs_6_), channel_id=1, source_target_pairs={{2,6},{3,7},{4,0},{5,1},{6,10},{7,11},{8,4},{9,5},{10,14},{11,15},... | collective-permute-start | bytes 2359304 | tf_op jit(solution)/shard_map/ppermute | solution.py:389
  100.5 24.5 %collective-permute-start.24 = (bf16[1,4,384,128]{3,2,1,0:T(8,128)(2,1)S(1)}, bf16[1,4,384,128]{3,2,1,0:T(8,128)(2,1)S(1)}, u32[]{:S(2)}, u32[]{:S(2)}) collective-permute-start(bf16[1,4,384,128]{3,2,1,0:T(8,128)(2,1)S(1)} %get-tuple-element.110), channel_id=1, source_target_pairs={{0,2},{1,3},{2,0},{3,1},{4,6},{5,7},{6,4},{7,5},{8,10},{9,11},{10,... | collective-permute-start | bytes 1179656 | tf_op jit(solution)/shard_map/ppermute | solution.py:377
  101.5 39.1 %collective-permute-start.25 = (bf16[1,4,384,128]{3,2,1,0:T(8,128)(2,1)S(1)}, bf16[1,4,384,128]{3,2,1,0:T(8,128)(2,1)S(1)}, u32[]{:S(2)}, u32[]{:S(2)}) collective-permute-start(bf16[1,4,384,128]{3,2,1,0:T(8,128)(2,1)S(1)} %get-tuple-element.111), channel_id=1, source_target_pairs={{0,3},{1,2},{2,1},{3,0},{4,7},{5,6},{6,5},{7,4},{8,11},{9,10},{10,... | collective-permute-start | bytes 1179656 | tf_op jit(solution)/shard_map/ppermute | solution.py:377
  117.3 27.5 %collective-permute-start.22 = (bf16[2,2,384,128]{3,2,1,0:T(8,128)(2,1)S(1)}, bf16[2,2,384,128]{3,2,1,0:T(8,128)(2,1)S(1)}, u32[]{:S(2)}, u32[]{:S(2)}) collective-permute-start(bf16[2,2,384,128]{3,2,1,0:T(8,128)(2,1)S(1)} %get-tuple-element.108), channel_id=1, source_target_pairs={{0,4},{1,5},{4,8},{5,9},{6,2},{7,3},{8,12},{9,13},{10,6},{11,7},{1... | collective-permute-start | bytes 1179656 | tf_op jit(solution)/shard_map/ppermute | solution.py:389
  121.6 24.5 %collective-permute-start.23 = (bf16[2,2,384,128]{3,2,1,0:T(8,128)(2,1)S(1)}, bf16[2,2,384,128]{3,2,1,0:T(8,128)(2,1)S(1)}, u32[]{:S(2)}, u32[]{:S(2)}) collective-permute-start(bf16[2,2,384,128]{3,2,1,0:T(8,128)(2,1)S(1)} %get-tuple-element.109), channel_id=1, source_target_pairs={{2,6},{3,7},{4,0},{5,1},{6,10},{7,11},{8,4},{9,5},{10,14},{11,15},... | collective-permute-start | bytes 1179656 | tf_op jit(solution)/shard_map/ppermute | solution.py:389
  123.5 24.1 %collective-permute-start.20 = (bf16[1,4,384,128]{3,2,1,0:T(8,128)(2,1)S(1)}, bf16[1,4,384,128]{3,2,1,0:T(8,128)(2,1)S(1)}, u32[]{:S(2)}, u32[]{:S(2)}) collective-permute-start(bf16[1,4,384,128]{3,2,1,0:T(8,128)(2,1)S(1)} %get-tuple-element.105), channel_id=1, source_target_pairs={{0,2},{1,3},{2,0},{3,1},{4,6},{5,7},{6,4},{7,5},{8,10},{9,11},{10,... | collective-permute-start | bytes 1179656 | tf_op jit(solution)/shard_map/ppermute | solution.py:377
  125.0 23.1 %collective-permute-start.21 = (bf16[1,4,384,128]{3,2,1,0:T(8,128)(2,1)S(1)}, bf16[1,4,384,128]{3,2,1,0:T(8,128)(2,1)S(1)}, u32[]{:S(2)}, u32[]{:S(2)}) collective-permute-start(bf16[1,4,384,128]{3,2,1,0:T(8,128)(2,1)S(1)} %get-tuple-element.106), channel_id=1, source_target_pairs={{0,3},{1,2},{2,1},{3,0},{4,7},{5,6},{6,5},{7,4},{8,11},{9,10},{10,... | collective-permute-start | bytes 1179656 | tf_op jit(solution)/shard_map/ppermute | solution.py:377
  140.6 13.3 %collective-permute-start.18 = (bf16[2,2,384,128]{3,2,1,0:T(8,128)(2,1)S(1)}, bf16[2,2,384,128]{3,2,1,0:T(8,128)(2,1)S(1)}, u32[]{:S(2)}, u32[]{:S(2)}) collective-permute-start(bf16[2,2,384,128]{3,2,1,0:T(8,128)(2,1)S(1)} %get-tuple-element.103), channel_id=1, source_target_pairs={{0,4},{1,5},{4,8},{5,9},{6,2},{7,3},{8,12},{9,13},{10,6},{11,7},{1... | collective-permute-start | bytes 1179656 | tf_op jit(solution)/shard_map/ppermute | solution.py:389
  144.9 13.2 %collective-permute-start.19 = (bf16[2,2,384,128]{3,2,1,0:T(8,128)(2,1)S(1)}, bf16[2,2,384,128]{3,2,1,0:T(8,128)(2,1)S(1)}, u32[]{:S(2)}, u32[]{:S(2)}) collective-permute-start(bf16[2,2,384,128]{3,2,1,0:T(8,128)(2,1)S(1)} %get-tuple-element.104), channel_id=1, source_target_pairs={{2,6},{3,7},{4,0},{5,1},{6,10},{7,11},{8,4},{9,5},{10,14},{11,15},... | collective-permute-start | bytes 1179656 | tf_op jit(solution)/shard_map/ppermute | solution.py:389
  146.4 12.0 %collective-permute-start.26 = (bf16[1,4,384,128]{3,2,1,0:T(8,128)(2,1)S(1)}, bf16[1,4,384,128]{3,2,1,0:T(8,128)(2,1)S(1)}, u32[]{:S(2)}, u32[]{:S(2)}) collective-permute-start(bf16[1,4,384,128]{3,2,1,0:T(8,128)(2,1)S(1)} %get-tuple-element.112), channel_id=1, source_target_pairs={{0,2},{1,3},{2,0},{3,1},{4,6},{5,7},{6,4},{7,5},{8,10},{9,11},{10,... | collective-permute-start | bytes 1179656 | tf_op jit(solution)/shard_map/ppermute | solution.py:377
  147.6 17.9 %collective-permute-start.27 = (bf16[1,4,384,128]{3,2,1,0:T(8,128)(2,1)S(1)}, bf16[1,4,384,128]{3,2,1,0:T(8,128)(2,1)S(1)}, u32[]{:S(2)}, u32[]{:S(2)}) collective-permute-start(bf16[1,4,384,128]{3,2,1,0:T(8,128)(2,1)S(1)} %get-tuple-element.113), channel_id=1, source_target_pairs={{0,3},{1,2},{2,1},{3,0},{4,7},{5,6},{6,5},{7,4},{8,11},{9,10},{10,... | collective-permute-start | bytes 1179656 | tf_op jit(solution)/shard_map/ppermute | solution.py:377
  148.1 19.5 %collective-permute-start.33 = (bf16[1,4,384,128]{3,2,1,0:T(8,128)(2,1)S(1)}, bf16[1,4,384,128]{3,2,1,0:T(8,128)(2,1)S(1)}, u32[]{:S(2)}, u32[]{:S(2)}) collective-permute-start(bf16[1,4,384,128]{3,2,1,0:T(8,128)(2,1)S(1)} %get-tuple-element.121), channel_id=1, source_target_pairs={{0,1},{1,0},{2,3},{3,2},{4,5},{5,4},{6,7},{7,6},{8,9},{9,8},{10,11... | collective-permute-start | bytes 1179656 | tf_op jit(solution)/shard_map/ppermute | solution.py:377
  153.9 16.1 %collective-permute-start.32 = (bf16[1,4,384,128]{3,2,1,0:T(8,128)(2,1)S(1)}, bf16[1,4,384,128]{3,2,1,0:T(8,128)(2,1)S(1)}, u32[]{:S(2)}, u32[]{:S(2)}) collective-permute-start(bf16[1,4,384,128]{3,2,1,0:T(8,128)(2,1)S(1)} %get-tuple-element.120), channel_id=1, source_target_pairs={{0,1},{1,0},{2,3},{3,2},{4,5},{5,4},{6,7},{7,6},{8,9},{9,8},{10,11... | collective-permute-start | bytes 1179656 | tf_op jit(solution)/shard_map/ppermute | solution.py:377
  158.1 14.4 %collective-permute-start.31 = (bf16[1,4,384,128]{3,2,1,0:T(8,128)(2,1)S(1)}, bf16[1,4,384,128]{3,2,1,0:T(8,128)(2,1)S(1)}, u32[]{:S(2)}, u32[]{:S(2)}) collective-permute-start(bf16[1,4,384,128]{3,2,1,0:T(8,128)(2,1)S(1)} %get-tuple-element.119), channel_id=1, source_target_pairs={{0,1},{1,0},{2,3},{3,2},{4,5},{5,4},{6,7},{7,6},{8,9},{9,8},{10,11... | collective-permute-start | bytes 1179656 | tf_op jit(solution)/shard_map/ppermute | solution.py:377
  165.7 9.2 %collective-permute-start.28 = (bf16[1,4,384,128]{3,2,1,0:T(8,128)(2,1)S(1)}, bf16[1,4,384,128]{3,2,1,0:T(8,128)(2,1)S(1)}, u32[]{:S(2)}, u32[]{:S(2)}) collective-permute-start(bf16[1,4,384,128]{3,2,1,0:T(8,128)(2,1)S(1)} %get-tuple-element.115), channel_id=1, source_target_pairs={{0,1},{1,0},{2,3},{3,2},{4,5},{5,4},{6,7},{7,6},{8,9},{9,8},{10,11... | collective-permute-start | bytes 1179656 | tf_op jit(solution)/shard_map/ppermute | solution.py:377
  166.2 12.0 %collective-permute-start.29 = (bf16[1,4,384,128]{3,2,1,0:T(8,128)(2,1)S(1)}, bf16[1,4,384,128]{3,2,1,0:T(8,128)(2,1)S(1)}, u32[]{:S(2)}, u32[]{:S(2)}) collective-permute-start(bf16[1,4,384,128]{3,2,1,0:T(8,128)(2,1)S(1)} %get-tuple-element.116), channel_id=1, source_target_pairs={{0,2},{1,3},{2,0},{3,1},{4,6},{5,7},{6,4},{7,5},{8,10},{9,11},{10,... | collective-permute-start | bytes 1179656 | tf_op jit(solution)/shard_map/ppermute | solution.py:377
  167.5 17.3 %collective-permute-start.30 = (bf16[1,4,384,128]{3,2,1,0:T(8,128)(2,1)S(1)}, bf16[1,4,384,128]{3,2,1,0:T(8,128)(2,1)S(1)}, u32[]{:S(2)}, u32[]{:S(2)}) collective-permute-start(bf16[1,4,384,128]{3,2,1,0:T(8,128)(2,1)S(1)} %get-tuple-element.117), channel_id=1, source_target_pairs={{0,3},{1,2},{2,1},{3,0},{4,7},{5,6},{6,5},{7,4},{8,11},{9,10},{10,... | collective-permute-start | bytes 1179656 | tf_op jit(solution)/shard_map/ppermute | solution.py:377
